TPU v7x, 32 devices: a whole 2x2x4 slice. The times are simulated.
32 devices in a mesh: dp: 8 (over z, x), rows: 4 (over y, core).
Axes of the slice: x: 2, y: 2, z: 4, core: 2. Of those that a mesh axis runs over, the one named last changes fastest.
Arguments:
- tokens: bfloat16 [4096, 1024], P(('dp', 'rows')), parts along dimension 0, may hold values from -6 to 6
- timestep: int32 [8], P('dp'), parts along dimension 0, may hold values from 0 to 999
- timestep_gain_map: float32 [256, 1024], replicated, may hold values from -0.25 to 0.25
- query_key_value_weight: bfloat16 [1024, 3072], P('rows'), may hold values from -0.1875 to 0.1875
- adapter_down_weight: bfloat16 [1024, 16], replicated, may hold values from -0.1875 to 0.1875
- adapter_up_weight: bfloat16 [16, 3072], replicated, may hold values from -1.5 to 1.5
- head_score_scale: float32 [16], P('rows'), may hold values from 4 to 12
- heads_output_grad: bfloat16 [4096, 1024], P(('dp', 'rows')), parts along dimension 0, may hold values from -6 to 6
Outputs:
- input_grad: bfloat16 [4096, 1024], P(('dp', 'rows')), parts along dimension 0
- down_grad: float32 [8192, 16], P('dp'), parts along dimension 0
- up_grad: float32 [128, 3072], P('dp'), parts along dimension 0
There are 8 independent parts, one for each index of `dp`. A program takes and returns all parts, laid end to end along the dimension named above; an argument that names none is the same for every part. Nothing has to cross between parts.
All inputs are finite; a program needn't handle non-finite values.
Results may differ from a plain program's by a relative error of at most 0.012.
Values may be sent and summed in bfloat16 or wider, within the bound.
No kernel may reach another device: no remote copies, remote signals or barrier semaphores. Data moves between devices by JAX's collectives and lax.ppermute only.
A program may use at most 64 MiB of HBM per device.

v0:
```python
import math

import jax
import jax.numpy as jnp
from jax import lax
from jax.sharding import PartitionSpec as P

HEAD = 64
EMB = 256


eps = 1e-06


def time_features(timestep):
    half_emb = EMB // 2
    frequency = jnp.exp(-math.log(10000.0) * jnp.arange(half_emb, dtype=jnp.float32) / half_emb)
    phases = timestep.astype(jnp.float32)[0] * frequency
    return jnp.concatenate([jnp.cos(phases), jnp.sin(phases)])


def head_backward(query_rows, key_rows, value_rows, grad_out, scaling):
    seq_len = query_rows.shape[0]
    block_rows = math.gcd(512, seq_len)
    query_f = query_rows.astype(jnp.float32)
    key_f = key_rows.astype(jnp.float32)
    query_inv = lax.rsqrt(jnp.sum(query_f * query_f, -1, keepdims=True) + eps)
    key_inv = lax.rsqrt(jnp.sum(key_f * key_f, -1, keepdims=True) + eps)
    query_unit = query_f * query_inv
    key_unit = key_f * key_inv
    query_low = query_unit.astype(jnp.bfloat16)
    key_low = key_unit.astype(jnp.bfloat16)

    def step_block(carry, block_index):
        key_acc, value_acc = carry
        row_start = block_index * block_rows
        query_block = lax.dynamic_slice_in_dim(query_low, row_start, block_rows, 0)
        grad_block = lax.dynamic_slice_in_dim(grad_out, row_start, block_rows, 0)
        scores = scaling * jnp.dot(query_block, key_low.T, preferred_element_type=jnp.float32)
        exponent = jnp.exp(scores)
        attention = exponent / jnp.sum(exponent, -1, keepdims=True)
        value_acc = value_acc + jnp.dot(
            attention.astype(jnp.bfloat16).T, grad_block, preferred_element_type=jnp.float32
        )
        grad_probs = jnp.dot(grad_block, value_rows.T, preferred_element_type=jnp.float32)
        row_delta = jnp.sum(attention * grad_probs, -1, keepdims=True)
        grad_scores = (attention * (grad_probs - row_delta)).astype(jnp.bfloat16)
        grad_qunit = scaling * jnp.dot(grad_scores, key_low, preferred_element_type=jnp.float32)
        key_acc = key_acc + scaling * jnp.dot(
            grad_scores.T, query_block, preferred_element_type=jnp.float32
        )
        unit_block = lax.dynamic_slice_in_dim(query_unit, row_start, block_rows, 0)
        inv_block = lax.dynamic_slice_in_dim(query_inv, row_start, block_rows, 0)
        grad_query = inv_block * (
            grad_qunit - unit_block * jnp.sum(unit_block * grad_qunit, -1, keepdims=True)
        )
        return ((key_acc, value_acc), grad_query.astype(jnp.bfloat16))

    zeros_acc = jnp.zeros((seq_len, query_rows.shape[1]), jnp.float32)
    (key_acc, value_acc), query_blocks = lax.scan(
        step_block, (zeros_acc, zeros_acc), jnp.arange(seq_len // block_rows, dtype=jnp.int32)
    )
    grad_query = query_blocks.reshape(seq_len, query_rows.shape[1])
    grad_key = key_inv * (key_acc - key_unit * jnp.sum(key_unit * key_acc, -1, keepdims=True))
    return (grad_query, grad_key.astype(jnp.bfloat16), value_acc.astype(jnp.bfloat16))


def one_head(head_cols, scaling):
    return head_backward(
        head_cols[:, :HEAD],
        head_cols[:, HEAD : 2 * HEAD],
        head_cols[:, 2 * HEAD : 3 * HEAD],
        head_cols[:, 3 * HEAD :],
        scaling,
    )


def per_device(
    tokens,
    timestep,
    timestep_gain_map,
    query_key_value_weight,
    adapter_down_weight,
    adapter_up_weight,
    head_score_scale,
    heads_output_grad,
):
    tok_rows = tokens.shape[0]
    model_width = tokens.shape[1]
    heads_all = model_width // HEAD
    heads_here = head_score_scale.shape[0]
    features = time_features(timestep)
    ada_gain = 1.0 + jnp.dot(features, timestep_gain_map, precision=lax.Precision.HIGHEST)
    tokens_f = tokens.astype(jnp.float32)
    inv_rms = lax.rsqrt(jnp.mean(tokens_f * tokens_f, -1, keepdims=True) + eps)
    normalized_input = (tokens_f * inv_rms * ada_gain).astype(jnp.bfloat16)
    low_rank_output = jnp.dot(
        normalized_input, adapter_down_weight, preferred_element_type=jnp.float32
    ).astype(jnp.bfloat16)
    full_weight = lax.all_gather(query_key_value_weight, "rows", axis=0, tiled=True)
    base_output = jnp.dot(normalized_input, full_weight, preferred_element_type=jnp.float32)
    projected_rows = (
        base_output
        + 0.5 * jnp.dot(low_rank_output, adapter_up_weight, preferred_element_type=jnp.float32)
    ).astype(jnp.bfloat16)
    packed = jnp.concatenate(
        [
            projected_rows.reshape(tok_rows, heads_all, 3 * HEAD),
            heads_output_grad.reshape(tok_rows, heads_all, HEAD),
        ],
        axis=2,
    )
    packed = packed.reshape(tok_rows, heads_all * 4 * HEAD)
    arrived = lax.all_to_all(packed, "rows", split_axis=1, concat_axis=0, tiled=True)
    seq_len = arrived.shape[0]
    arrived = arrived.reshape(seq_len, heads_here, 4 * HEAD)
    grad_q, grad_k, grad_v = jax.vmap(one_head, in_axes=(1, 0), out_axes=1)(
        arrived, head_score_scale
    )
    grad_heads = jnp.concatenate([grad_q, grad_k, grad_v], axis=2).reshape(
        seq_len, heads_here * 3 * HEAD
    )
    projected_grad = lax.all_to_all(grad_heads, "rows", split_axis=0, concat_axis=1, tiled=True)
    low_rank_grad = (
        0.5 * jnp.dot(projected_grad, adapter_up_weight.T, preferred_element_type=jnp.float32)
    ).astype(jnp.bfloat16)
    base_output_grad = lax.dot_general(
        projected_grad, full_weight, (((1,), (1,)), ((), ())), preferred_element_type=jnp.float32
    )
    normalized_grad = base_output_grad + jnp.dot(
        low_rank_grad, adapter_down_weight.T, preferred_element_type=jnp.float32
    )
    up_part = 0.5 * jnp.dot(low_rank_output.T, projected_grad, preferred_element_type=jnp.float32)
    down_part = jnp.dot(normalized_input.T, low_rank_grad, preferred_element_type=jnp.float32)
    down_grad, up_grad = lax.psum((down_part, up_part), "rows")
    scaled = normalized_grad * ada_gain
    input_grad = inv_rms * (
        scaled - tokens_f * inv_rms * inv_rms * jnp.mean(scaled * tokens_f, -1, keepdims=True)
    )
    return (input_grad.astype(jnp.bfloat16), down_grad, up_grad)


def solution(mesh):
    in_specs = (
        P(("dp", "rows"), None),
        P("dp"),
        P(),
        P("rows", None),
        P(),
        P(),
        P("rows"),
        P(("dp", "rows"), None),
    )
    out_specs = (P(("dp", "rows"), None), P("dp", None), P("dp", None))
    return jax.shard_map(
        per_device, mesh=mesh, in_specs=in_specs, out_specs=out_specs, check_vma=False
    )
```

profile of v0, /device:TPU:0, one launch (start us, length us, event | category | flops | bytes accessed | tf_op | source)
XLA Modules:
  0.0 153.7 jit_solution(7110613297571394688)
XLA Ops:
  7.2 0.7 all-gather.2.cloned.1.call-update
  8.6 1.1 copy.23
  9.8 1.1 fusion.30
  10.9 0.6 fusion.60
  11.5 1.2 convolution_convert_fusion
  12.7 1.3 convolution_multiply_fusion
  14.0 44.7 %all-gather.2.cloned.1.call-done = bf16[1024,3072]{1,0:T(8,128)(2,1)} async-done(((bf16[256,3072]{1,0:T(8,128)(2,1)}), bf16[1024,3072]{1,0:T(8,128)(2,1)}) %all-gather.2.cloned.1.call-update) | async-done | bytes 6291472 | tf_op jit(solution)/shard_map/all_gather | solution.py:100
  58.7 4.7 %fusion.2 = bf16[128,3072]{1,0:T(8,128)(2,1)} fusion(f32[128,3072]{1,0:T(8,128)S(1)} %convolution_multiply_fusion, bf16[1024,3072]{1,0:T(8,128)(2,1)} %all-gather.2.cloned.1.call-done, bf16[128,1024]{1,0:T(8,128)(2,1)S(1)} %copy-done.1, f32[1024]{0:T(1024)S(1)} %broadcast_add_fusion, f32[128]{0:T(128)S(1)} %add_rsqrt_fusion.2), kind=kOutput, calls=%fused_computation.7 | convolution fusion | flops 806617088 | bytes 8917504 | tf_op jit(solution)/shard_map/dot_general | solution.py:101
  63.4 1.5 copy.22
  65.0 16.9 %all_to_all.35 = bf16[128,4,1024]{0,2,1:T(8,128)(2,1)S(1)} all-to-all(bf16[128,4,1024]{0,2,1:T(8,128)(2,1)S(1)} %bitcast.107), channel_id=1, replica_groups=mesh['dp'=8,'rows'=4] {'rows'}, dimensions={1} | all-to-all | bytes 2097152 | tf_op jit(solution)/shard_map/all_to_all | solution.py:114
  81.9 0.8 copy.24
  82.7 0.4 reshape.53
  83.2 0.1 fusion.20
  83.4 1.0 fusion.1
  84.4 1.4 multiply_reduce_fusion
  85.8 0.9 fusion.9
  86.7 1.3 multiply_convert_fusion
  88.0 0.8 convolution_multiply_fusion.3
  88.8 0.6 fusion.25
  89.4 0.2 fusion.29
  89.7 0.2 all_to_all.29
  89.8 0.1 copy.28
  90.0 14.1 %all_to_all.36 = bf16[4,128,768]{1,2,0:T(8,128)(2,1)S(1)} all-to-all(bf16[4,128,768]{1,2,0:T(8,128)(2,1)S(1)} %copy.28), channel_id=1, replica_groups=mesh['dp'=8,'rows'=4] {'rows'}, dimensions={0} | all-to-all | bytes 1572864 | tf_op jit(solution)/shard_map/all_to_all | solution.py:123
  104.0 1.0 convolution_multiply_fusion.1
  105.0 0.2 fusion.12
  105.2 0.9 fusion.55
  106.1 5.0 %fusion.61 = f32[128,1024]{1,0:T(8,128)S(1)} fusion(bf16[128,3072]{0,1:T(8,128)(2,1)S(1)} %bitcast.106, bf16[1024,3072]{1,0:T(8,128)(2,1)} %all-gather.2.cloned.1.call-done), kind=kOutput, calls=%fused_computation.79 | convolution fusion | flops 805306368 | bytes 7602176 | tf_op jit(solution)/shard_map/dot_general | solution.py:127
  111.1 0.4 fusion.31
  111.5 0.9 fusion.19
  112.4 31.3 %all-reduce.3.cloned.1.call-done = (f32[1024,16]{0,1:T(8,128)}, f32[16,3072]{1,0:T(8,128)}) async-done(((f32[1024,16]{0,1:T(8,128)}, f32[16,3072]{1,0:T(8,128)}), (f32[1024,16]{0,1:T(8,128)}, f32[16,3072]{1,0:T(8,128)})) %all-reduce.3.cloned.1.call-update) | async-done | bytes 262160 | tf_op jit(solution)/shard_map/psum | solution.py:135
  143.7 1.5 copy.35
  145.2 1.6 %copy.36 = f32[16,3072]{1,0:T(8,128)} copy(f32[16,3072]{1,0:T(8,128)} %get-tuple-element.59) | data formatting | bytes 393216
  (22 shorter events, 0.4 us)
Async XLA Ops:
  7.2 3.7 %copy-start = (f32[256,1024]{1,0:T(8,128)S(1)}, f32[256,1024]{1,0:T(8,128)}, u32[]{:S(2)}) copy-start(f32[256,1024]{1,0:T(8,128)} %param.10) | copy-start | bytes 3145732
  7.2 51.5 %copy-start.1 = (bf16[128,1024]{1,0:T(8,128)(2,1)S(1)}, bf16[128,1024]{1,0:T(8,128)(2,1)}, u32[]{:S(2)}) copy-start(bf16[128,1024]{1,0:T(8,128)(2,1)} %param.8) | copy-start | bytes 786436
  7.2 51.5 %all-gather.2.cloned.1.call-start = ((), (), s32[]{:S(2)}) async-start(), calls=%async_computation.2 | async-start | bytes 7864320 | tf_op jit(solution)/shard_map/all_gather | solution.py:100
  7.9 135.8 %all-reduce.3.cloned.1.call-start = ((), (), s32[]{:S(2)}) async-start(), calls=%async_computation.3 | async-start | bytes 524288 | tf_op jit(solution)/shard_map/psum | solution.py:135
  65.0 18.4 %copy-start.4 = (f32[4]{0:T(128)S(1)}, f32[4]{0:T(128)}, u32[]{:S(2)}) copy-start(f32[4]{0:T(128)} %param.14) | copy-start | bytes 52
  89.4 15.7 %copy-start.2 = (bf16[16,3072]{1,0:T(8,128)(2,1)S(1)}, bf16[16,3072]{1,0:T(8,128)(2,1)}, u32[]{:S(2)}) copy-start(bf16[16,3072]{1,0:T(8,128)(2,1)} %param.13) | copy-start | bytes 294916
  105.2 5.9 %copy-start.3 = (bf16[1024,16]{0,1:T(8,128)(2,1)S(1)}, bf16[1024,16]{0,1:T(8,128)(2,1)}, u32[]{:S(2)}) copy-start(bf16[1024,16]{0,1:T(8,128)(2,1)} %param.12) | copy-start | bytes 98308
Sparse Core Ops, SparseCore 0:
  9.6 49.0 all-gather.1
  111.6 32.0 all-reduce.2
where the time goes:
time: 154 us
  waiting for transfers between devices  76.7 us (50%)
  blocking collectives  31 us (20%)
  matrix products  20 us (13%)
  between operations  14.9 us (10%)
  local copies, waits for them, and re-layouts  7.28 us (5%)
  other arithmetic  3.82 us (2%)
    all_gather x1, waiting for transfers between devices, per_device(): lax.all_gather(query_key_value_weight, 'rows', axis=0, tiled=True)  44.7 us
    psum x1, waiting for transfers between devices, per_device(): down_grad, up_grad = lax.psum((down_part, up_part), 'rows')  31.3 us
    all_to_all x1, blocking collectives, per_device(): lax.all_to_all(packed, 'rows', split_axis=1, concat_axis=0, tiled=True)  16.9 us
    all_to_all x1, blocking collectives, per_device(): lax.all_to_all(grad_heads, 'rows', split_axis=0, concat_axis=1, tiled=True)  14.1 us
    dot_general x1, matrix products, per_device(): lax.dot_general(projected_grad, full_weight, (((1,), (1,)), ((), ())), pr...  5 us
    dot_general x1, matrix products, per_device(): jnp.dot(normalized_input, full_weight, preferred_element_type=jnp.float32)  4.73 us
    unnamed x13, local copies, waits for them, and re-layouts  4.24 us
  transfers between devices with their start and end apart: 2, of which 2 were waited for; matrix products, arithmetic and copies ran while one was open for 4% of the time, Pallas kernels for 0%

commit v1 on v0

v1 whole, which is shorter than its diff:
```python
import functools
import math

import jax
import jax.numpy as jnp
from jax import lax
from jax.experimental import pallas as pl
from jax.experimental.pallas import tpu as pltpu
from jax.sharding import PartitionSpec as P

HEAD = 64
EMB = 256
EPS = 1e-06
LOG2E = 1.4426950408889634
BF = jnp.bfloat16
F32 = jnp.float32


def time_features(timestep):
    half_emb = EMB // 2
    frequency = jnp.exp(-math.log(10000.0) * jnp.arange(half_emb, dtype=F32) / half_emb)
    phases = timestep.astype(F32)[0] * frequency
    return jnp.concatenate([jnp.cos(phases), jnp.sin(phases)])


def contract(a, b, a_dim, b_dim):
    return lax.dot_general(a, b, (((a_dim,), (b_dim,)), ((), ())), preferred_element_type=F32)


def attention_kernel(n, heads, piece_rows, *refs):
    pieces = len(piece_rows)
    refs = list(refs)
    bases, scale = refs.pop(0), refs.pop(0)
    normed_in = [refs.pop(0) for _ in range(n)]
    weight_in = [refs.pop(0) for _ in range(pieces)]
    cot_in = [refs.pop(0) for _ in range(n)]
    down, up = refs.pop(0), refs.pop(0)
    parts = [refs.pop(0) for _ in range(n)]
    pack = refs.pop(0)
    normed, weight, cot, qkv_t, cot_t, grad_t, sems = refs

    tok = normed_in[0].shape[0]
    seq = n * tok
    cols = weight.shape[1]
    copies = []
    for j in range(n):
        copies.append((normed_in[j], normed.at[pl.ds(j * tok, tok)]))
        copies.append((cot_in[j], cot.at[pl.ds(j * tok, tok)]))
    for i, rows in enumerate(piece_rows):
        base = pl.multiple_of(bases[i], 16)
        copies.append((weight_in[i], weight.at[pl.ds(base, rows)]))
    copies = [pltpu.make_async_copy(a, b, sems.at[i]) for i, (a, b) in enumerate(copies)]
    for c in copies:
        c.start()
    for c in copies:
        c.wait()

    step = math.gcd(512, seq)
    up_all = up[...]
    low_t = []
    for s in range(0, seq, step):
        x = normed[pl.ds(s, step), :]
        low = jnp.dot(x, down[...], preferred_element_type=F32).astype(BF)
        low_t.append(low.T)
        qkv = jnp.dot(x, weight[...], preferred_element_type=F32)
        qkv = qkv + 0.5 * jnp.dot(low, up_all, preferred_element_type=F32)
        qkv_t[:, pl.ds(s, step)] = qkv.astype(BF).T
        cot_t[:, pl.ds(s, step)] = cot[pl.ds(s, step), :].T

    for h in range(heads):
        o = 3 * HEAD * h
        kf = qkv_t[pl.ds(o + HEAD, HEAD), :].astype(F32)
        k_inv = lax.rsqrt(jnp.sum(kf * kf, 0, keepdims=True) + EPS)
        k_unit = kf * k_inv
        k_low = k_unit.astype(BF)
        v = qkv_t[pl.ds(o + 2 * HEAD, HEAD), :]
        sc = scale[h]
        gk = gv = None
        for s in range(0, seq, step):
            qf = qkv_t[pl.ds(o, HEAD), pl.ds(s, step)].astype(F32)
            q_inv = lax.rsqrt(jnp.sum(qf * qf, 0, keepdims=True) + EPS)
            q_unit = qf * q_inv
            q_low = q_unit.astype(BF)
            g = cot_t[pl.ds(HEAD * h, HEAD), pl.ds(s, step)]
            e = jnp.exp2(contract(k_low, q_low, 0, 0) * (sc * LOG2E))
            attention = e * (1.0 / jnp.sum(e, 0, keepdims=True))
            grad_probs = contract(v, g, 0, 0)
            delta = jnp.sum(attention * grad_probs, 0, keepdims=True)
            grad_scores = (attention * (grad_probs - delta)).astype(BF)
            gv_s = contract(g, attention.astype(BF), 1, 1)
            gk_s = sc * contract(q_low, grad_scores, 1, 1)
            gq = sc * jnp.dot(k_low, grad_scores, preferred_element_type=F32)
            gq = q_inv * (gq - q_unit * jnp.sum(q_unit * gq, 0, keepdims=True))
            grad_t[pl.ds(o, HEAD), pl.ds(s, step)] = gq.astype(BF)
            gv = gv_s if gv is None else gv + gv_s
            gk = gk_s if gk is None else gk + gk_s
        gk = k_inv * (gk - k_unit * jnp.sum(k_unit * gk, 0, keepdims=True))
        grad_t[pl.ds(o + HEAD, HEAD), :] = gk.astype(BF)
        grad_t[pl.ds(o + 2 * HEAD, HEAD), :] = gv.astype(BF)

    up_part = None
    for i, s in enumerate(range(0, seq, step)):
        gt = grad_t[:, pl.ds(s, step)]
        term = contract(low_t[i], gt, 1, 1)
        up_part = term if up_part is None else up_part + term
        low_grad_t = 0.5 * jnp.dot(up_all, gt, preferred_element_type=F32)
        pack[pl.ds(up.shape[0], up.shape[0]), pl.ds(s, step)] = low_grad_t
        grad = gt.T
        part = contract(grad, weight[...], 1, 1)
        part = part + contract(low_grad_t.astype(BF).T, down[...], 1, 1)
        for b in range(step // tok):
            j = s // tok + b
            parts[j][...] = part[b * tok : (b + 1) * tok].astype(parts[j].dtype)
    pack[pl.ds(0, up.shape[0]), pl.ds(0, cols)] = 0.5 * up_part


def attention_call(bases, scale, normed, pieces, cot, down, up):
    n = len(normed)
    tok, width = normed[0].shape
    seq = n * tok
    cols = pieces[0].shape[1]
    heads = cols // (3 * HEAD)
    rank = up.shape[0]
    any_ = pl.BlockSpec(memory_space=pl.ANY)
    smem = pl.BlockSpec(memory_space=pltpu.SMEM)
    vmem = pl.BlockSpec(memory_space=pltpu.VMEM)
    total = 2 * n + len(pieces)
    out_shape = [jax.ShapeDtypeStruct((tok, width), BF if j % 2 else F32) for j in range(n)]
    out_shape.append(jax.ShapeDtypeStruct((2 * rank, max(cols, seq)), F32))
    return pl.pallas_call(
        functools.partial(attention_kernel, n, heads, tuple(p.shape[0] for p in pieces)),
        out_shape=out_shape,
        in_specs=[smem, smem] + [any_] * total + [vmem, vmem],
        out_specs=[vmem] * (n + 1),
        scratch_shapes=[
            pltpu.VMEM((seq, width), BF),
            pltpu.VMEM((width, cols), BF),
            pltpu.VMEM((seq, cols // 3), BF),
            pltpu.VMEM((cols, seq), BF),
            pltpu.VMEM((cols // 3, seq), BF),
            pltpu.VMEM((cols, seq), BF),
            pltpu.SemaphoreType.DMA((total,)),
        ],
        compiler_params=pltpu.CompilerParams(vmem_limit_bytes=48 * 1024 * 1024),
        name="attention_grads",
    )(bases, scale, *normed, *pieces, *cot, down, up)


def per_device(
    mesh_shape,
    tokens,
    timestep,
    timestep_gain_map,
    query_key_value_weight,
    adapter_down_weight,
    adapter_up_weight,
    head_score_scale,
    heads_output_grad,
):
    dp, n = mesh_shape
    axes = ("dp", "rows")
    r, d = lax.axis_index("rows"), lax.axis_index("dp")
    odd = d % 2

    def send(x, target):
        perm = []
        for a in range(dp):
            for b in range(n):
                a2, b2 = target(a, b)
                perm.append((a * n + b, a2 * n + b2))
        return lax.ppermute(x, axes, perm)

    def to_row(x, j):
        return send(x, lambda a, b: (a, b ^ j))

    tok = tokens.shape[0]
    weight = query_key_value_weight
    k_rows = weight.shape[0]
    cols = weight.shape[1] // n
    head_cols = heads_output_grad.shape[1] // n
    half = k_rows // 2

    def weight_slice(row, rows, owner):
        return lax.dynamic_slice(weight, (row, owner * cols), (rows, cols))

    def cot_slice(owner):
        return lax.dynamic_slice(heads_output_grad, (0, owner * head_cols), (tok, head_cols))

    pieces, bases = [], []
    fetched = []
    for j in range(2, n, 2):
        for c in range(2):
            piece = weight_slice(c * half, half, r ^ (j + odd))
            piece = send(piece, lambda a, b, j=j: (a, b ^ (j + a % 2)))
            fetched.append((piece, j, c))
    for piece, j, c in fetched:
        pieces.append(piece)
        bases.append((r ^ (j + odd)) * k_rows + c * half)
        pieces.append(send(piece, lambda a, b: (a ^ 1, b)))
        bases.append((r ^ (j + 1 - odd)) * k_rows + c * half)
    pieces.append(weight_slice(0, k_rows, r))
    bases.append(r * k_rows)
    pieces.append(to_row(weight_slice(0, k_rows, r ^ 1), 1))
    bases.append((r ^ 1) * k_rows)

    ada_gain = 1.0 + jnp.dot(time_features(timestep), timestep_gain_map, precision=lax.Precision.HIGHEST)
    tokens_f = tokens.astype(F32)
    inv_rms = lax.rsqrt(jnp.mean(tokens_f * tokens_f, -1, keepdims=True) + EPS)
    normed = [(tokens_f * inv_rms * ada_gain).astype(BF)]
    normed.append(to_row(normed[0], 1))
    for j in range(2, n, 2):
        normed.append(to_row(normed[0], j))
        normed.append(to_row(normed[j], 1))
    cot = [cot_slice(r)] + [to_row(cot_slice(r ^ j), j) for j in range(1, n)]

    up_here = lax.dynamic_slice(adapter_up_weight, (0, r * cols), (adapter_up_weight.shape[0], cols))
    *parts, pack = attention_call(
        jnp.stack(bases).astype(jnp.int32), head_score_scale, normed, pieces, cot, adapter_down_weight, up_here
    )

    rank = adapter_up_weight.shape[0]
    grad = None
    for j in list(range(2, n, 2)) + [0]:
        summed = parts[j] + to_row(parts[j ^ 1], 1).astype(F32)
        if j:
            summed = to_row(summed.astype(BF), j).astype(F32)
        grad = summed if grad is None else grad + summed

    packs = [pack, to_row(pack, 1)]
    for j in range(2, n, 2):
        packs.append(to_row(pack, j))
        packs.append(to_row(packs[j], 1))
    low_grad_t = None
    for j in range(n):
        blocks = [packs[j][rank:, (q ^ j) * tok : (q ^ j) * tok + tok] for q in range(n)]
        term = jnp.concatenate(blocks, axis=1)
        low_grad_t = term if low_grad_t is None else low_grad_t + term
    low_grad_t = low_grad_t.astype(BF)
    down_t = None
    for j in range(n):
        term = jnp.dot(low_grad_t[:, j * tok : (j + 1) * tok], normed[j], preferred_element_type=F32)
        down_t = term if down_t is None else down_t + term
    up_grad = jnp.zeros(adapter_up_weight.shape, F32)
    for j in range(n):
        up_grad = lax.dynamic_update_slice(up_grad, packs[j][:rank, :cols], (0, (r ^ j) * cols))

    scaled = grad * ada_gain
    input_grad = inv_rms * (
        scaled - tokens_f * inv_rms * inv_rms * jnp.mean(scaled * tokens_f, -1, keepdims=True)
    )
    return (input_grad.astype(BF), down_t.T, up_grad)


def solution(mesh):
    in_specs = (
        P(("dp", "rows"), None),
        P("dp"),
        P(),
        P("rows", None),
        P(),
        P(),
        P("rows"),
        P(("dp", "rows"), None),
    )
    out_specs = (P(("dp", "rows"), None), P("dp", None), P("dp", None))
    shape = (mesh.shape["dp"], mesh.shape["rows"])
    return jax.shard_map(
        functools.partial(per_device, shape), mesh=mesh, in_specs=in_specs, out_specs=out_specs, check_vma=False
    )
```

time: 154 us -> 63.3 us (0.41)
  waiting for transfers between devices: 76.7 us -> 26.5 us
  blocking collectives: 31 us -> 0 us
  matrix products: 20 us -> 1.85 us
  starting transfers between devices: 0.08 us -> 14.3 us
  between operations: 14.9 us -> 1.49 us
  Pallas kernels: 0 us -> 9.23 us
  other arithmetic: 3.82 us -> 1.56 us
    all_gather x1 -> x0, waiting for transfers between devices: 44.7 us -> none  [per_device(): lax.all_gather(query_key_value_weight, 'rows', axis=0, tiled=True)]
    psum x1 -> x0, waiting for transfers between devices: 31.3 us -> none  [per_device(): down_grad, up_grad = lax.psum((down_part, up_part), 'rows')]
    all_to_all x2 -> x0, blocking collectives: 31 us -> none  [the longest x1 16.9 us: per_device(): lax.all_to_all(packed, 'rows', split_axis=1, concat_axis=0, tiled=True)]
    ppermute x0 -> x17, waiting for transfers between devices: none -> 26.5 us  [send(): return lax.ppermute(x, axes, perm)]
    dot_general x14 -> x5, matrix products: 20 us -> 1.85 us  [the longest x4 1.24 us: per_device(): jnp.dot(low_grad_t[:, j * tok:(j + 1) * tok], normed[j], preferred_elemen...]
    ppermute x0 -> x17, starting transfers between devices: none -> 14.3 us  [send(): return lax.ppermute(x, axes, perm)]
    pallas_call x0 -> x1, Pallas kernels: none -> 9.23 us  [attention_call(): pl.pallas_call(functools.partial(attention_kernel, n, heads, tuple((p.sha...]
    dynamic_slice x0 -> x4, local copies, waits for them, and re-layouts: none -> 5.44 us  [the longest x2 3.74 us: weight_slice(): return lax.dynamic_slice(weight, (row, owner * cols), (rows, cols))]
  transfers between devices with their start and end apart: 2 -> 17, of which waited for: 2 -> 7; matrix products, arithmetic and copies ran while one was open for 4% -> 11% of each run, Pallas kernels for 0% -> 0%
where the time goes in v1:
time: 63.3 us; the launch traced here: 62.9 us
  waiting for transfers between devices  26.5 us (42%)
  starting transfers between devices  14.3 us (23%)
  Pallas kernels  9.23 us (15%)
  local copies, waits for them, and re-layouts  8.01 us (13%)
  matrix products  1.85 us (3%)
  other arithmetic  1.56 us (2%)
  between operations  1.49 us (2%)
    ppermute x17, waiting for transfers between devices, send(): return lax.ppermute(x, axes, perm)  26.5 us
    ppermute x17, starting transfers between devices, send(): return lax.ppermute(x, axes, perm)  14.3 us
    pallas_call x1, Pallas kernels, attention_call(): pl.pallas_call(functools.partial(attention_kernel, n, heads, tuple((p.sha...  9.23 us
    dynamic_slice x2, local copies, waits for them, and re-layouts, weight_slice(): return lax.dynamic_slice(weight, (row, owner * cols), (rows, cols))  3.74 us
    unnamed x15, local copies, waits for them, and re-layouts  2.42 us
  transfers between devices with their start and end apart: 17, of which 7 were waited for; matrix products, arithmetic and copies ran while one was open for 11% of the time, Pallas kernels for 0%

profile of v1, /device:TPU:0, one launch (start us, length us, event | category | flops | bytes accessed | tf_op | source)
XLA Modules:
  0.0 62.9 jit_solution(6690774545873660352)
XLA Ops:
  0.7 1.8 %constant_dynamic-slice_fusion.8 = (bf16[128,768]{1,0:T(8,128)(2,1)S(1)}, bf16[128,768]{1,0:T(8,128)(2,1)}) fusion(bf16[256,3072]{1,0:T(8,128)(2,1)} %param.11, s32[]{:T(128)S(6)} %select_n.39), kind=kLoop, calls=%fused_computation.44 | loop fusion | bytes 786436 | tf_op jit(solution)/shard_map/dynamic_slice | solution.py:184
  2.5 3.0 %collective-permute-start.3 = (bf16[128,768]{1,0:T(8,128)(2,1)}, bf16[128,768]{1,0:T(8,128)(2,1)S(1)}, u32[]{:S(2)}, u32[]{:S(2)}) collective-permute-start(bf16[128,768]{1,0:T(8,128)(2,1)} %get-tuple-element.16), channel_id=1, source_target_pairs={{0,2},{1,3},{2,0},{3,1},{4,7},{5,6},{6,5},{7,4},{8,10},{9,11},{10,... | collective-permute-start | bytes 589832 | tf_op jit(solution)/shard_map/ppermute | solution.py:171
  5.5 1.0 %constant_dynamic-slice_fusion.1 = (bf16[128,256]{1,0:T(8,128)(2,1)S(1)}, bf16[128,256]{1,0:T(8,128)(2,1)S(1)}, bf16[128,256]{1,0:T(8,128)(2,1)S(1)}, bf16[128,256]{1,0:T(8,128)(2,1)S(1)}) fusion(bf16[128,1024]{1,0:T(8,128)(2,1)} %param.15, s32[]{:T(128)S(6)} %select_n.45, s32[]{:T(128)S(6)} %select_n.43, s32[]{:T(128)S(6)} %select_n.42, s32[]{:T(128)S(6)} %select_n.44), kind=kLoop, calls=%fused_computation.31 | loop fusion | bytes 524304 | tf_op jit(solution)/shard_map/dynamic_slice | solution.py:187
  6.5 0.9 %collective-permute-start.10 = (bf16[128,256]{1,0:T(8,128)(2,1)S(1)}, bf16[128,256]{1,0:T(8,128)(2,1)S(1)}, u32[]{:S(2)}, u32[]{:S(2)}) collective-permute-start(bf16[128,256]{1,0:T(8,128)(2,1)S(1)} %get-tuple-element.17), channel_id=1, source_target_pairs={{0,3},{1,2},{2,1},{3,0},{4,7},{5,6},{6,5},{7,4},{8,11},{9,10},{10,... | collective-permute-start | bytes 196616 | tf_op jit(solution)/shard_map/ppermute | solution.py:171
  7.4 1.2 %collective-permute-start.8 = (bf16[128,256]{1,0:T(8,128)(2,1)S(1)}, bf16[128,256]{1,0:T(8,128)(2,1)S(1)}, u32[]{:S(2)}, u32[]{:S(2)}) collective-permute-start(bf16[128,256]{1,0:T(8,128)(2,1)S(1)} %get-tuple-element.18), channel_id=1, source_target_pairs={{0,1},{1,0},{2,3},{3,2},{4,5},{5,4},{6,7},{7,6},{8,9},{9,8},{10,11... | collective-permute-start | bytes 196616 | tf_op jit(solution)/shard_map/ppermute | solution.py:171
  9.4 0.6 fusion.22
  10.4 1.9 %constant_dynamic-slice_fusion.5 = (bf16[256,768]{1,0:T(8,128)(2,1)}, bf16[256,768]{1,0:T(8,128)(2,1)S(1)}) fusion(bf16[256,3072]{1,0:T(8,128)(2,1)} %param.11, s32[]{:T(128)S(6)} %select_n.41, s32[]{:T(128)S(6)} %select_n.40), kind=kLoop, calls=%fused_computation.35 | loop fusion | bytes 1572872 | tf_op jit(solution)/shard_map/dynamic_slice | solution.py:184
  12.3 4.3 %collective-permute-done.10.refs_15_ = bf16[128,256]{1,0:T(8,128)(2,1)S(1)} collective-permute-done((bf16[128,256]{1,0:T(8,128)(2,1)S(1)}, bf16[128,256]{1,0:T(8,128)(2,1)S(1)}, u32[]{:S(2)}, u32[]{:S(2)}) %collective-permute-start.10) | collective-permute-done | bytes 65568 | tf_op jit(solution)/shard_map/ppermute | solution.py:171
  16.6 0.2 collective-permute-start.7
  16.8 2.1 %collective-permute-start.9 = (bf16[128,256]{1,0:T(8,128)(2,1)S(1)}, bf16[128,256]{1,0:T(8,128)(2,1)S(1)}, u32[]{:S(2)}, u32[]{:S(2)}) collective-permute-start(bf16[128,256]{1,0:T(8,128)(2,1)S(1)} %get-tuple-element.20), channel_id=1, source_target_pairs={{0,2},{1,3},{2,0},{3,1},{4,6},{5,7},{6,4},{7,5},{8,10},{9,11},{10,... | collective-permute-start | bytes 196616 | tf_op jit(solution)/shard_map/ppermute | solution.py:171
  18.9 4.3 %collective-permute-done.9.refs_14_ = bf16[128,256]{1,0:T(8,128)(2,1)S(1)} collective-permute-done((bf16[128,256]{1,0:T(8,128)(2,1)S(1)}, bf16[128,256]{1,0:T(8,128)(2,1)S(1)}, u32[]{:S(2)}, u32[]{:S(2)}) %collective-permute-start.9) | collective-permute-done | bytes 65568 | tf_op jit(solution)/shard_map/ppermute | solution.py:171
  23.2 0.6 copy-done.1
  23.9 0.5 collective-permute-start.2
  24.4 2.3 %collective-permute-start.4 = (bf16[128,768]{1,0:T(8,128)(2,1)S(1)}, bf16[128,768]{1,0:T(8,128)(2,1)}, u32[]{:S(2)}, u32[]{:S(2)}) collective-permute-start(bf16[128,768]{1,0:T(8,128)(2,1)S(1)} %collective-permute-done.3.refs_6_), channel_id=1, source_target_pairs={{0,4},{1,5},{2,6},{3,7},{4,0},{5,1},{6,2},{7,3},{8,12},{9,13},{10,... | collective-permute-start | bytes 589832 | tf_op jit(solution)/shard_map/ppermute | solution.py:171
  26.7 0.9 %copy.11.refs_16_ = bf16[1024,16]{1,0:T(8,128)(2,1)S(1)} copy(bf16[1024,16]{0,1:T(8,128)(2,1)} %param.12) | data formatting | bytes 65536 | tf_op args[4]
  27.8 0.7 %constant_dynamic-slice_fusion.refs_17_ = bf16[16,768]{1,0:T(8,128)(2,1)S(1)} fusion(bf16[16,3072]{1,0:T(8,128)(2,1)} %param.13, s32[]{:T(128)S(6)} %select_n.40), kind=kLoop, calls=%fused_computation.30 | loop fusion | bytes 49156 | tf_op jit(solution)/shard_map/dynamic_slice | solution.py:216
  28.5 3.9 %collective-permute-done.4.refs_7_ = bf16[128,768]{1,0:T(8,128)(2,1)} collective-permute-done((bf16[128,768]{1,0:T(8,128)(2,1)S(1)}, bf16[128,768]{1,0:T(8,128)(2,1)}, u32[]{:S(2)}, u32[]{:S(2)}) %collective-permute-start.4) | collective-permute-done | bytes 196640 | tf_op jit(solution)/shard_map/ppermute | solution.py:171
  32.4 3.7 %collective-permute-done.6.refs_9_ = bf16[128,768]{1,0:T(8,128)(2,1)} collective-permute-done((bf16[128,768]{1,0:T(8,128)(2,1)}, bf16[128,768]{1,0:T(8,128)(2,1)}, u32[]{:S(2)}, u32[]{:S(2)}) %collective-permute-start.6) | collective-permute-done | bytes 196640 | tf_op jit(solution)/shard_map/ppermute | solution.py:171
  36.1 0.8 %copy-done.2 = bf16[128,256]{1,0:T(8,128)(2,1)S(1)} copy-done((bf16[128,256]{1,0:T(8,128)(2,1)S(1)}, bf16[128,256]{1,0:T(8,128)(2,1)}, u32[]{:S(2)}) %copy-start.2) | copy-done | bytes 65560
  37.0 9.2 %attention_grads.1 = (f32[128,1024]{1,0:T(8,128)S(1)}, bf16[128,1024]{1,0:T(8,128)(2,1)S(1)}, f32[128,1024]{1,0:T(8,128)S(1)}, bf16[128,1024]{1,0:T(8,128)(2,1)S(1)}, f32[32,768]{1,0:T(8,128)S(1)}) custom-call(s32[6]{0:T(128)S(1)} %stack.27.refs_0_, f32[4]{0:T(128)S(1)} %copy-done.3, bf16[128,1024]{1,0:T(8,128)(2,1)S(1)} %fusion.2.refs_2_, ...), custom_call_target="tpu_custom_call" | custom-call | tf_op jit(solution)/shard_map/attention_grads/pallas_call | solution.py:130
  46.3 1.6 %collective-permute-start.15 = (f32[32,768]{1,0:T(8,128)S(1)}, f32[32,768]{1,0:T(8,128)S(1)}, u32[]{:S(2)}, u32[]{:S(2)}) collective-permute-start(f32[32,768]{1,0:T(8,128)S(1)} %get-tuple-element.12), channel_id=1, source_target_pairs={{0,2},{1,3},{2,0},{3,1},{4,6},{5,7},{6,4},{7,5},{8,10},{9,11},{10,... | collective-permute-start | bytes 294920 | tf_op jit(solution)/shard_map/ppermute | solution.py:171
  47.9 0.2 collective-permute-start.11
  48.2 0.3 collective-permute-start.13
  48.5 3.0 %collective-permute-done.15 = f32[32,768]{1,0:T(8,128)S(1)} collective-permute-done((f32[32,768]{1,0:T(8,128)S(1)}, f32[32,768]{1,0:T(8,128)S(1)}, u32[]{:S(2)}, u32[]{:S(2)}) %collective-permute-start.15) | collective-permute-done | bytes 98336 | tf_op jit(solution)/shard_map/ppermute | solution.py:171
  51.6 1.2 %collective-permute-done.16 = f32[32,768]{1,0:T(8,128)S(1)} collective-permute-done((f32[32,768]{1,0:T(8,128)S(1)}, f32[32,768]{1,0:T(8,128)S(1)}, u32[]{:S(2)}, u32[]{:S(2)}) %collective-permute-start.16) | collective-permute-done | bytes 98336 | tf_op jit(solution)/shard_map/ppermute | solution.py:171
  53.0 0.2 convolution_add_fusion.2
  53.1 0.2 convolution_add_fusion.1
  53.3 1.6 %collective-permute-start.12 = (bf16[128,1024]{1,0:T(8,128)(2,1)S(1)}, bf16[128,1024]{1,0:T(8,128)(2,1)S(1)}, u32[]{:S(2)}, u32[]{:S(2)}) collective-permute-start(bf16[128,1024]{1,0:T(8,128)(2,1)S(1)} %add_convert_fusion), channel_id=1, source_target_pairs={{0,2},{1,3},{2,0},{3,1},{4,6},{5,7},{6,4},{7,5},{8,10},{9,11},{10,... | collective-permute-start | bytes 786440 | tf_op jit(solution)/shard_map/ppermute | solution.py:171
  55.0 0.8 %convolution_add_fusion = f32[1024,16]{0,1:T(8,128)} fusion(f32[1024,16]{0,1:T(8,128)S(1)} %convolution_add_fusion.1, bf16[128,1024]{1,0:T(8,128)(2,1)S(1)} %collective-permute-done.2.refs_5_, bf16[16,512]{1,0:T(8,128)(2,1)S(1)} %fusion.11), kind=kOutput, calls=%fused_computation | convolution fusion | flops 4210688 | bytes 397312 | tf_op jit(solution)/shard_map/dot_general | solution.py:241
  55.7 6.0 %collective-permute-done.12 = bf16[128,1024]{1,0:T(8,128)(2,1)S(1)} collective-permute-done((bf16[128,1024]{1,0:T(8,128)(2,1)S(1)}, bf16[128,1024]{1,0:T(8,128)(2,1)S(1)}, u32[]{:S(2)}, u32[]{:S(2)}) %collective-permute-start.12) | collective-permute-done | bytes 262176 | tf_op jit(solution)/shard_map/ppermute | solution.py:171
  61.8 0.2 fusion.8
  62.0 0.9 %fusion.6 = bf16[128,1024]{1,0:T(8,128)(2,1)} fusion(bf16[128,1024]{1,0:T(8,128)(2,1)S(1)} %copy-done.5, f32[128]{0:T(128)S(1)} %broadcast_multiply_fusion, f32[128]{0:T(128)S(1)} %add_rsqrt_fusion, f32[1024]{0:T(1024)S(1)} %broadcast_add_fusion, f32[128,1024]{1,0:T(8,128)S(1)} %get-tuple-element.10, bf16[128,1024]{1,0:T(8,128)(2,1)S(1)} %collective-permute-done.13, ...), kind=kLoop, calls=%fused_computation.12 | loop fusion | flops 1572864 | bytes 1577984 | tf_op jit(solution)/shard_map/convert_element_type | solution.py:251
  (47 shorter events, 1.1 us)
Async XLA Ops:
  0.6 8.7 %copy-start = (f32[256,1024]{1,0:T(8,128)S(1)}, f32[256,1024]{1,0:T(8,128)}, u32[]{:S(2)}) copy-start(f32[256,1024]{1,0:T(8,128)} %param.10) | copy-start | bytes 3145732
  0.6 9.3 %copy-start.4 = (bf16[128,1024]{1,0:T(8,128)(2,1)S(1)}, bf16[128,1024]{1,0:T(8,128)(2,1)}, u32[]{:S(2)}) copy-start(bf16[128,1024]{1,0:T(8,128)(2,1)} %param.8) | copy-start | bytes 786436
  2.5 21.9 %collective-permute-start.3 = (bf16[128,768]{1,0:T(8,128)(2,1)}, bf16[128,768]{1,0:T(8,128)(2,1)S(1)}, u32[]{:S(2)}, u32[]{:S(2)}) collective-permute-start(bf16[128,768]{1,0:T(8,128)(2,1)} %get-tuple-element.16), channel_id=1, source_target_pairs={{0,2},{1,3},{2,0},{3,1},{4,7},{5,6},{6,5},{7,4},{8,10},{9,11},{10,... | collective-permute-start | bytes 589832 | tf_op jit(solution)/shard_map/ppermute | solution.py:171
  5.5 21.2 %collective-permute-start.5 = (bf16[128,768]{1,0:T(8,128)(2,1)S(1)}, bf16[128,768]{1,0:T(8,128)(2,1)}, u32[]{:S(2)}, u32[]{:S(2)}) collective-permute-start(bf16[128,768]{1,0:T(8,128)(2,1)S(1)} %get-tuple-element.15), channel_id=1, source_target_pairs={{0,2},{1,3},{2,0},{3,1},{4,7},{5,6},{6,5},{7,4},{8,10},{9,11},{10,... | collective-permute-start | bytes 589832 | tf_op jit(solution)/shard_map/ppermute | solution.py:171
  6.5 10.1 %collective-permute-start.10 = (bf16[128,256]{1,0:T(8,128)(2,1)S(1)}, bf16[128,256]{1,0:T(8,128)(2,1)S(1)}, u32[]{:S(2)}, u32[]{:S(2)}) collective-permute-start(bf16[128,256]{1,0:T(8,128)(2,1)S(1)} %get-tuple-element.17), channel_id=1, source_target_pairs={{0,3},{1,2},{2,1},{3,0},{4,7},{5,6},{6,5},{7,4},{8,11},{9,10},{10,... | collective-permute-start | bytes 196616 | tf_op jit(solution)/shard_map/ppermute | solution.py:171
  7.4 9.4 %collective-permute-start.8 = (bf16[128,256]{1,0:T(8,128)(2,1)S(1)}, bf16[128,256]{1,0:T(8,128)(2,1)S(1)}, u32[]{:S(2)}, u32[]{:S(2)}) collective-permute-start(bf16[128,256]{1,0:T(8,128)(2,1)S(1)} %get-tuple-element.18), channel_id=1, source_target_pairs={{0,1},{1,0},{2,3},{3,2},{4,5},{5,4},{6,7},{7,6},{8,9},{9,8},{10,11... | collective-permute-start | bytes 196616 | tf_op jit(solution)/shard_map/ppermute | solution.py:171
  10.0 26.1 %copy-start.3 = (f32[4]{0:T(128)S(1)}, f32[4]{0:T(128)}, u32[]{:S(2)}) copy-start(f32[4]{0:T(128)} %refs_1_.1) | copy-start | bytes 52
  10.3 13.6 %collective-permute-start.1 = (bf16[128,1024]{1,0:T(8,128)(2,1)S(1)}, bf16[128,1024]{1,0:T(8,128)(2,1)S(1)}, u32[]{:S(2)}, u32[]{:S(2)}) collective-permute-start(bf16[128,1024]{1,0:T(8,128)(2,1)S(1)} %fusion.2.refs_2_), channel_id=1, source_target_pairs={{0,2},{1,3},{2,0},{3,1},{4,6},{5,7},{6,4},{7,5},{8,10},{9,11},{10,... | collective-permute-start | bytes 786440 | tf_op jit(solution)/shard_map/ppermute | solution.py:171
  16.6 19.5 %collective-permute-start.7 = (bf16[256,768]{1,0:T(8,128)(2,1)}, bf16[256,768]{1,0:T(8,128)(2,1)S(1)}, u32[]{:S(2)}, u32[]{:S(2)}) collective-permute-start(bf16[256,768]{1,0:T(8,128)(2,1)} %get-tuple-element.13), channel_id=1, source_target_pairs={{0,1},{1,0},{2,3},{3,2},{4,5},{5,4},{6,7},{7,6},{8,9},{9,8},{10,11... | collective-permute-start | bytes 1179656 | tf_op jit(solution)/shard_map/ppermute | solution.py:171
  16.8 6.4 %collective-permute-start.9 = (bf16[128,256]{1,0:T(8,128)(2,1)S(1)}, bf16[128,256]{1,0:T(8,128)(2,1)S(1)}, u32[]{:S(2)}, u32[]{:S(2)}) collective-permute-start(bf16[128,256]{1,0:T(8,128)(2,1)S(1)} %get-tuple-element.20), channel_id=1, source_target_pairs={{0,2},{1,3},{2,0},{3,1},{4,6},{5,7},{6,4},{7,5},{8,10},{9,11},{10,... | collective-permute-start | bytes 196616 | tf_op jit(solution)/shard_map/ppermute | solution.py:171
  23.2 0.6 %copy-start.1 = (bf16[128,256]{1,0:T(8,128)(2,1)}, bf16[128,256]{1,0:T(8,128)(2,1)S(1)}, u32[]{:S(2)}) copy-start(bf16[128,256]{1,0:T(8,128)(2,1)S(1)} %collective-permute-done.9.refs_14_) | copy-start | bytes 196612
  23.8 4.7 %collective-permute-start = (bf16[128,1024]{1,0:T(8,128)(2,1)S(1)}, bf16[128,1024]{1,0:T(8,128)(2,1)S(1)}, u32[]{:S(2)}, u32[]{:S(2)}) collective-permute-start(bf16[128,1024]{1,0:T(8,128)(2,1)S(1)} %fusion.2.refs_2_), channel_id=1, source_target_pairs={{0,1},{1,0},{2,3},{3,2},{4,5},{5,4},{6,7},{7,6},{8,9},{9,8},{10,11... | collective-permute-start | bytes 786440 | tf_op jit(solution)/shard_map/ppermute | solution.py:171
  23.9 12.2 %collective-permute-start.2 = (bf16[128,1024]{1,0:T(8,128)(2,1)S(1)}, bf16[128,1024]{1,0:T(8,128)(2,1)S(1)}, u32[]{:S(2)}, u32[]{:S(2)}) collective-permute-start(bf16[128,1024]{1,0:T(8,128)(2,1)S(1)} %collective-permute-done.1.refs_4_), channel_id=1, source_target_pairs={{0,1},{1,0},{2,3},{3,2},{4,5},{5,4},{6,7},{7,6},{8,9},{9,8},{10,11... | collective-permute-start | bytes 786440 | tf_op jit(solution)/shard_map/ppermute | solution.py:171
  24.4 8.1 %collective-permute-start.4 = (bf16[128,768]{1,0:T(8,128)(2,1)S(1)}, bf16[128,768]{1,0:T(8,128)(2,1)}, u32[]{:S(2)}, u32[]{:S(2)}) collective-permute-start(bf16[128,768]{1,0:T(8,128)(2,1)S(1)} %collective-permute-done.3.refs_6_), channel_id=1, source_target_pairs={{0,4},{1,5},{2,6},{3,7},{4,0},{5,1},{6,2},{7,3},{8,12},{9,13},{10,... | collective-permute-start | bytes 589832 | tf_op jit(solution)/shard_map/ppermute | solution.py:171
  26.6 9.5 %collective-permute-start.6 = (bf16[128,768]{1,0:T(8,128)(2,1)}, bf16[128,768]{1,0:T(8,128)(2,1)}, u32[]{:S(2)}, u32[]{:S(2)}) collective-permute-start(bf16[128,768]{1,0:T(8,128)(2,1)} %collective-permute-done.5.refs_8_), channel_id=1, source_target_pairs={{0,4},{1,5},{2,6},{3,7},{4,0},{5,1},{6,2},{7,3},{8,12},{9,13},{10,... | collective-permute-start | bytes 589832 | tf_op jit(solution)/shard_map/ppermute | solution.py:171
  36.1 0.8 %copy-start.2 = (bf16[128,256]{1,0:T(8,128)(2,1)S(1)}, bf16[128,256]{1,0:T(8,128)(2,1)}, u32[]{:S(2)}) copy-start(bf16[128,256]{1,0:T(8,128)(2,1)} %copy-done.1) | copy-start | bytes 196612
  46.2 5.3 %collective-permute-start.14 = (f32[32,768]{1,0:T(8,128)S(1)}, f32[32,768]{1,0:T(8,128)S(1)}, u32[]{:S(2)}, u32[]{:S(2)}) collective-permute-start(f32[32,768]{1,0:T(8,128)S(1)} %get-tuple-element.12), channel_id=1, source_target_pairs={{0,1},{1,0},{2,3},{3,2},{4,5},{5,4},{6,7},{7,6},{8,9},{9,8},{10,11... | collective-permute-start | bytes 294920 | tf_op jit(solution)/shard_map/ppermute | solution.py:171
  46.3 5.2 %collective-permute-start.15 = (f32[32,768]{1,0:T(8,128)S(1)}, f32[32,768]{1,0:T(8,128)S(1)}, u32[]{:S(2)}, u32[]{:S(2)}) collective-permute-start(f32[32,768]{1,0:T(8,128)S(1)} %get-tuple-element.12), channel_id=1, source_target_pairs={{0,2},{1,3},{2,0},{3,1},{4,6},{5,7},{6,4},{7,5},{8,10},{9,11},{10,... | collective-permute-start | bytes 294920 | tf_op jit(solution)/shard_map/ppermute | solution.py:171
  47.9 5.3 %collective-permute-start.11 = (bf16[128,1024]{1,0:T(8,128)(2,1)S(1)}, bf16[128,1024]{1,0:T(8,128)(2,1)S(1)}, u32[]{:S(2)}, u32[]{:S(2)}) collective-permute-start(bf16[128,1024]{1,0:T(8,128)(2,1)S(1)} %get-tuple-element.9), channel_id=1, source_target_pairs={{0,1},{1,0},{2,3},{3,2},{4,5},{5,4},{6,7},{7,6},{8,9},{9,8},{10,11... | collective-permute-start | bytes 786440 | tf_op jit(solution)/shard_map/ppermute | solution.py:171
  48.2 7.6 %collective-permute-start.13 = (bf16[128,1024]{1,0:T(8,128)(2,1)S(1)}, bf16[128,1024]{1,0:T(8,128)(2,1)S(1)}, u32[]{:S(2)}, u32[]{:S(2)}) collective-permute-start(bf16[128,1024]{1,0:T(8,128)(2,1)S(1)} %get-tuple-element.11), channel_id=1, source_target_pairs={{0,1},{1,0},{2,3},{3,2},{4,5},{5,4},{6,7},{7,6},{8,9},{9,8},{10,11... | collective-permute-start | bytes 786440 | tf_op jit(solution)/shard_map/ppermute | solution.py:171
  51.5 1.3 %collective-permute-start.16 = (f32[32,768]{1,0:T(8,128)S(1)}, f32[32,768]{1,0:T(8,128)S(1)}, u32[]{:S(2)}, u32[]{:S(2)}) collective-permute-start(f32[32,768]{1,0:T(8,128)S(1)} %collective-permute-done.15), channel_id=1, source_target_pairs={{0,1},{1,0},{2,3},{3,2},{4,5},{5,4},{6,7},{7,6},{8,9},{9,8},{10,11... | collective-permute-start | bytes 294920 | tf_op jit(solution)/shard_map/ppermute | solution.py:171
  51.5 10.3 %copy-start.5 = (bf16[128,1024]{1,0:T(8,128)(2,1)S(1)}, bf16[128,1024]{1,0:T(8,128)(2,1)}, u32[]{:S(2)}) copy-start(bf16[128,1024]{1,0:T(8,128)(2,1)} %param.8) | copy-start | bytes 786436
  53.3 8.4 %collective-permute-start.12 = (bf16[128,1024]{1,0:T(8,128)(2,1)S(1)}, bf16[128,1024]{1,0:T(8,128)(2,1)S(1)}, u32[]{:S(2)}, u32[]{:S(2)}) collective-permute-start(bf16[128,1024]{1,0:T(8,128)(2,1)S(1)} %add_convert_fusion), channel_id=1, source_target_pairs={{0,2},{1,3},{2,0},{3,1},{4,6},{5,7},{6,4},{7,5},{8,10},{9,11},{10,... | collective-permute-start | bytes 786440 | tf_op jit(solution)/shard_map/ppermute | solution.py:171
  55.0 8.0 %copy-start.6 = (f32[16,3072]{1,0:T(8,128)}, f32[16,3072]{1,0:T(8,128)S(1)}, u32[]{:S(2)}) copy-start(f32[16,3072]{1,0:T(8,128)S(1)} %slice_dynamic-update-slice_fusion) | copy-start | bytes 589828

commit v2 on v1

v2 whole, which is shorter than its diff:
```python
import functools
import math

import jax
import jax.numpy as jnp
from jax import lax
from jax.experimental import pallas as pl
from jax.experimental.pallas import tpu as pltpu
from jax.sharding import PartitionSpec as P

HEAD = 64
EMB = 256
EPS = 1e-06
LOG2E = 1.4426950408889634
BF = jnp.bfloat16
F32 = jnp.float32
VMEM = 32 * 1024 * 1024
SMALL = pl.CostEstimate(flops=1, bytes_accessed=1, transcendentals=0)


def time_features(timestep):
    half_emb = EMB // 2
    frequency = jnp.exp(-math.log(10000.0) * jnp.arange(half_emb, dtype=F32) / half_emb)
    phases = timestep.astype(F32)[0] * frequency
    return jnp.stack([jnp.cos(phases), jnp.sin(phases)])


def contract(a, b, a_dim, b_dim):
    return lax.dot_general(a, b, (((a_dim,), (b_dim,)), ((), ())), preferred_element_type=F32)


def norm_kernel(features, gain_map, tokens, normed, gain, inv_rms):
    half = features.shape[1]
    col = features[...].T
    total = jnp.sum(col[:, :1] * gain_map[:half, :], 0, keepdims=True)
    total = total + jnp.sum(col[:, 1:] * gain_map[half:, :], 0, keepdims=True)
    gain[...] = 1.0 + total
    x = tokens[...].astype(F32)
    inv = lax.rsqrt(jnp.mean(x * x, -1, keepdims=True) + EPS)
    inv_rms[...] = inv
    normed[...] = (x * inv * gain[...]).astype(BF)


def norm_call(features, gain_map, tokens):
    rows, width = tokens.shape
    vmem = pl.BlockSpec(memory_space=pltpu.VMEM)
    return pl.pallas_call(
        norm_kernel,
        out_shape=[
            jax.ShapeDtypeStruct((rows, width), BF),
            jax.ShapeDtypeStruct((1, width), F32),
            jax.ShapeDtypeStruct((rows, 1), F32),
        ],
        in_specs=[vmem] * 3,
        out_specs=[vmem] * 3,
        cost_estimate=SMALL,
        name="norm",
    )(features, gain_map, tokens)


def qkv_kernel(x_from, w_from, *refs):
    bases, refs = refs[0], refs[1:]
    down_t, up = refs[-6:-4]
    x_all, w_all, qkv_t, low_t = refs[-4:]
    at = 0
    for i, row, rows, col in x_from:
        x_all[pl.ds(at, rows), :] = refs[i][pl.ds(row, rows), pl.ds(col, x_all.shape[1])]
        at += rows
    for k, (i, row, rows, col, cols, to) in enumerate(w_from):
        base = pl.multiple_of(bases[k], 16)
        w_all[pl.ds(base, rows), pl.ds(to, cols)] = refs[i][pl.ds(row, rows), pl.ds(col, cols)]
    seq = x_all.shape[0]
    step = math.gcd(512, seq)
    for s in range(0, seq, step):
        x = x_all[pl.ds(s, step), :]
        low = contract(x, down_t[...], 1, 1).astype(BF)
        low_t[:, pl.ds(s, step)] = low.T
        qkv = jnp.dot(x, w_all[...], preferred_element_type=F32)
        qkv = qkv + 0.5 * jnp.dot(low, up[...], preferred_element_type=F32)
        qkv_t[:, pl.ds(s, step)] = qkv.astype(BF).T


def whole_vmem(count):
    return [pl.BlockSpec(memory_space=pltpu.VMEM)] * count


def qkv_call(bases, arrays, x_from, w_from, down_t, up, seq):
    rank, width = down_t.shape
    cols = up.shape[1]
    return pl.pallas_call(
        functools.partial(qkv_kernel, x_from, w_from),
        out_shape=[
            jax.ShapeDtypeStruct((seq, width), BF),
            jax.ShapeDtypeStruct((width, cols), BF),
            jax.ShapeDtypeStruct((cols, seq), BF),
            jax.ShapeDtypeStruct((rank, seq), BF),
        ],
        in_specs=[pl.BlockSpec(memory_space=pltpu.SMEM)] + whole_vmem(len(arrays) + 2),
        out_specs=whole_vmem(4),
        compiler_params=pltpu.CompilerParams(vmem_limit_bytes=VMEM),
        cost_estimate=SMALL,
        name="qkv",
    )(bases, *arrays, down_t, up)


def token_grads(low_grad_t, grad_t, w_all, down_t, at, rows):
    grad = grad_t[:, pl.ds(at, rows)].T
    part = contract(grad, w_all[...], 1, 1)
    return part + contract(low_grad_t[:, pl.ds(at, rows)].astype(BF), down_t[...], 0, 0)


def attention_kernel(heads, tok, c_from, first, outs, *refs):
    refs = list(refs)
    scale, half = refs.pop(0), refs.pop(0)
    cots = [refs.pop(0) for _ in range(1 + max(i for i, *_ in c_from))]
    qkv_t, low_t, w_all, down_t, up = (refs.pop(0) for _ in range(5))
    parts = [refs.pop(0) for _ in range(outs)]
    grad_t, pack, cot_t = refs

    seq = qkv_t.shape[1]
    cols = up.shape[1]
    step = math.gcd(512, seq)
    width = cot_t.shape[0]
    for j, (i, col, choose) in enumerate(c_from):
        if choose and width % 128 == 0:
            block = cots[i][:, pl.ds(pl.multiple_of(half[0] * width, 128), width)]
        elif choose:
            block = jnp.where(half[0] == 0, cots[i][:, pl.ds(0, width)], cots[i][:, pl.ds(width, width)])
        else:
            block = cots[i][:, pl.ds(col, width)]
        cot_t[:, pl.ds(j * tok, tok)] = block.T

    for h in range(heads):
        o = 3 * HEAD * h
        kf = qkv_t[pl.ds(o + HEAD, HEAD), :].astype(F32)
        k_inv = lax.rsqrt(jnp.sum(kf * kf, 0, keepdims=True) + EPS)
        k_unit = kf * k_inv
        k_low = k_unit.astype(BF)
        v = qkv_t[pl.ds(o + 2 * HEAD, HEAD), :]
        sc = scale[h]
        gk = gv = None
        for s in range(0, seq, step):
            qf = qkv_t[pl.ds(o, HEAD), pl.ds(s, step)].astype(F32)
            q_inv = lax.rsqrt(jnp.sum(qf * qf, 0, keepdims=True) + EPS)
            q_unit = qf * q_inv
            q_low = q_unit.astype(BF)
            g = cot_t[pl.ds(HEAD * h, HEAD), pl.ds(s, step)]
            e = jnp.exp2(contract(k_low, q_low, 0, 0) * (sc * LOG2E))
            attention = e * (1.0 / jnp.sum(e, 0, keepdims=True))
            grad_probs = contract(v, g, 0, 0)
            delta = jnp.sum(attention * grad_probs, 0, keepdims=True)
            grad_scores = (attention * (grad_probs - delta)).astype(BF)
            gv_s = contract(g, attention.astype(BF), 1, 1)
            gk_s = sc * contract(q_low, grad_scores, 1, 1)
            gq = sc * jnp.dot(k_low, grad_scores, preferred_element_type=F32)
            gq = q_inv * (gq - q_unit * jnp.sum(q_unit * gq, 0, keepdims=True))
            grad_t[pl.ds(o, HEAD), pl.ds(s, step)] = gq.astype(BF)
            gv = gv_s if gv is None else gv + gv_s
            gk = gk_s if gk is None else gk + gk_s
        gk = k_inv * (gk - k_unit * jnp.sum(k_unit * gk, 0, keepdims=True))
        grad_t[pl.ds(o + HEAD, HEAD), :] = gk.astype(BF)
        grad_t[pl.ds(o + 2 * HEAD, HEAD), :] = gv.astype(BF)

    rank = up.shape[0]
    pack[pl.ds(0, rank), pl.ds(0, cols)] = 0.5 * contract(low_t[...], grad_t[...], 1, 1)
    low_grad_t = pack.at[pl.ds(rank, rank), pl.ds(0, seq)]
    low_grad_t[...] = 0.5 * jnp.dot(up[...], grad_t[...], preferred_element_type=F32)
    for p in range(outs):
        part = token_grads(low_grad_t, grad_t, w_all, down_t, (first + p) * tok, tok)
        parts[p][...] = part.astype(parts[p].dtype)


def attention_call(scale, half, cots, c_from, qkv_t, low_t, w_all, down_t, up, tok, first, dtypes):
    cols, seq = qkv_t.shape
    rank, width = down_t.shape
    smem = pl.BlockSpec(memory_space=pltpu.SMEM)
    outs = len(dtypes)
    return pl.pallas_call(
        functools.partial(attention_kernel, cols // (3 * HEAD), tok, c_from, first, outs),
        out_shape=[jax.ShapeDtypeStruct((tok, width), t) for t in dtypes]
        + [jax.ShapeDtypeStruct((cols, seq), BF), jax.ShapeDtypeStruct((2 * rank, max(cols, seq)), F32)],
        in_specs=[smem, smem] + whole_vmem(len(cots) + 5),
        out_specs=whole_vmem(outs + 2),
        scratch_shapes=[pltpu.VMEM((cols // 3, seq), BF)],
        compiler_params=pltpu.CompilerParams(vmem_limit_bytes=VMEM),
        cost_estimate=SMALL,
        name="attention_grads",
    )(scale, half, *cots, qkv_t, low_t, w_all, down_t, up)


def own_kernel(grad_t, pack, w_all, down_t, *parts):
    tok = parts[0].shape[0]
    rank = down_t.shape[0]
    low_grad_t = pack.at[pl.ds(rank, rank), :]
    for p, out in enumerate(parts):
        out[...] = token_grads(low_grad_t, grad_t, w_all, down_t, p * tok, tok).astype(out.dtype)


def own_call(grad_t, pack, w_all, down_t, tok, dtypes):
    return pl.pallas_call(
        own_kernel,
        out_shape=[jax.ShapeDtypeStruct((tok, down_t.shape[1]), t) for t in dtypes],
        in_specs=whole_vmem(4),
        out_specs=whole_vmem(len(dtypes)),
        compiler_params=pltpu.CompilerParams(vmem_limit_bytes=VMEM),
        cost_estimate=SMALL,
        name="own_grads",
    )(grad_t, pack, w_all, down_t)


def prepare_kernel(layout, features, gain_map, tokens, weight, cot, normed, to_core, own_w, own_cot, chip_cot, gain, inv_rms, sems):
    r = lax.axis_index("rows")
    tok, cols, head_cols, stack, width = layout
    core = r ^ 1
    copies = []
    for i in range(stack):
        src = weight.at[pl.ds(i * tok, tok), pl.ds(pl.multiple_of(core * cols, 128), cols)]
        copies.append((src, to_core.at[:, pl.ds(i * cols, cols)]))
    at = stack * cols + width
    copies.append(
        (cot.at[:, pl.ds(pl.multiple_of(core * head_cols, 128), head_cols)], to_core.at[:, pl.ds(at, head_cols)])
    )
    copies.append((weight.at[:, pl.ds(pl.multiple_of(r * cols, 128), cols)], own_w))
    copies.append((cot.at[:, pl.ds(pl.multiple_of(r * head_cols, 128), head_cols)], own_cot))
    chip = lax.div(r ^ 2, 2) * 2
    copies.append((cot.at[:, pl.ds(pl.multiple_of(chip * head_cols, 128), 2 * head_cols)], chip_cot))
    copies = [pltpu.make_async_copy(a, b, sems.at[i]) for i, (a, b) in enumerate(copies)]
    for c in copies:
        c.start()
    half = features.shape[1]
    col = features[...].T
    total = jnp.sum(col[:, :1] * gain_map[:half, :], 0, keepdims=True)
    total = total + jnp.sum(col[:, 1:] * gain_map[half:, :], 0, keepdims=True)
    gain[...] = 1.0 + total
    x = tokens[...].astype(F32)
    inv = lax.rsqrt(jnp.mean(x * x, -1, keepdims=True) + EPS)
    inv_rms[...] = inv
    y = (x * inv * gain[...]).astype(BF)
    normed[...] = y
    to_core[:, pl.ds(stack * cols, width)] = y
    for c in copies:
        c.wait()


def prepare_call(features, gain_map, tokens, weight, cot, n):
    tok, width = tokens.shape
    cols, head_cols = weight.shape[1] // n, cot.shape[1] // n
    stack = weight.shape[0] // tok
    any_ = pl.BlockSpec(memory_space=pl.ANY)
    shapes = [
        ((tok, width), BF),
        ((tok, stack * cols + width + head_cols), BF),
        ((weight.shape[0], cols), BF),
        ((tok, head_cols), BF),
        ((tok, 2 * head_cols), BF),
        ((1, width), F32),
        ((tok, 1), F32),
    ]
    return pl.pallas_call(
        functools.partial(prepare_kernel, (tok, cols, head_cols, stack, width)),
        out_shape=[jax.ShapeDtypeStruct(*shape) for shape in shapes],
        in_specs=whole_vmem(3) + [any_, any_],
        out_specs=whole_vmem(7),
        scratch_shapes=[pltpu.SemaphoreType.DMA((stack + 4,))],
        cost_estimate=SMALL,
        name="prepare",
    )(features, gain_map, tokens, weight, cot)


def per_device(
    mesh_shape,
    tokens,
    timestep,
    timestep_gain_map,
    query_key_value_weight,
    adapter_down_weight,
    adapter_up_weight,
    head_score_scale,
    heads_output_grad,
):
    dp, n = mesh_shape
    axes = ("dp", "rows")
    r, d = lax.axis_index("rows"), lax.axis_index("dp")

    def send(x, target):
        perm = []
        for a in range(dp):
            for b in range(n):
                a2, b2 = target(a, b)
                perm.append((a * n + b, a2 * n + b2))
        return lax.ppermute(x, axes, perm)

    def to_row(x, j):
        return send(x, lambda a, b: (a, b ^ j))

    tok, width = tokens.shape
    weight, cot_all = query_key_value_weight, heads_output_grad
    k_rows = weight.shape[0]
    cols = weight.shape[1] // n
    head_cols = cot_all.shape[1] // n
    chips = list(range(2, n, 2))

    cuts = 2 if cols % 256 == 0 else 1
    part_cols = cols // cuts
    odd = d % 2
    fetched = []
    for j in chips:
        for c in range(cuts):
            x = lax.dynamic_slice(weight, (0, (r ^ (j + odd)) * cols + c * part_cols), (k_rows, part_cols))
            fetched.append((send(x, lambda a, b, j=j: (a, b ^ (j + a % 2))), j, c))

    features = time_features(timestep)
    if cols % 128 == 0 and head_cols % 128 == 0 and k_rows % tok == 0 and n == 4:
        normed, to_core, own_w, own_cot, chip_cot, gain, inv_rms = prepare_call(
            features, timestep_gain_map, tokens, weight, cot_all, n
        )
        chip_cot = [chip_cot]
        core = to_row(to_core, 1)
        stack = k_rows // tok
        arrays = [own_w, core, normed]
        x_from = [(2, 0, tok, 0), (1, 0, tok, stack * cols)]
        w_from = [(0, 0, k_rows, 0, cols, 0)] + [(1, 0, tok, i * cols, cols, 0) for i in range(stack)]
        bases = [r * k_rows] + [(r ^ 1) * k_rows + i * tok for i in range(stack)]
        cots = [own_cot, core]
        c_from = [(0, 0, False), (1, stack * cols + width, False)]
    else:
        normed, gain, inv_rms = norm_call(features, timestep_gain_map, tokens)

        def columns(x, at, count):
            return lax.dynamic_slice(x, (0, at), (x.shape[0], count))

        chip_cot = [columns(cot_all, (r ^ j) // 2 * (2 * head_cols), 2 * head_cols) for j in chips]
        arrays = [columns(weight, r * cols, cols), to_row(columns(weight, (r ^ 1) * cols, cols), 1)]
        arrays += [normed, to_row(normed, 1)]
        x_from = [(2, 0, tok, 0), (3, 0, tok, 0)]
        w_from = [(i, 0, k_rows, 0, cols, 0) for i in range(2)]
        bases = [(r ^ i) * k_rows for i in range(2)]
        cots = [columns(cot_all, r * head_cols, head_cols), to_row(columns(cot_all, (r ^ 1) * head_cols, head_cols), 1)]
        c_from = [(0, 0, False), (1, 0, False)]

    for x, j, c in fetched:
        for other in range(2):
            w_from.append((len(arrays), 0, k_rows, 0, part_cols, c * part_cols))
            bases.append((r ^ (j + (odd ^ other))) * k_rows)
            arrays.append(send(x, lambda a, b: (a ^ 1, b)) if other else x)

    chip_normed = [to_row(normed, j) for j in chips]
    chip_cot = [to_row(x, j) for j, x in zip(chips, chip_cot)]
    rows = tok // 2 if tok % 32 == 0 else tok
    for x in chip_normed:
        x_from.append((len(arrays), 0, tok, 0))
        arrays.append(x)
        for at in range(0, tok, rows):
            x_from.append((len(arrays), 0, rows, 0))
            arrays.append(to_row(x[at : at + rows], 1))
    for x in chip_cot:
        other = lax.dynamic_slice(x, (0, (r ^ 1) % 2 * head_cols), (tok, head_cols))
        c_from += [(len(cots), 0, True), (len(cots) + 1, 0, False)]
        cots += [x, to_row(other, 1)]

    rank = adapter_up_weight.shape[0]
    down_t = adapter_down_weight.T
    up = lax.dynamic_slice(adapter_up_weight, (0, r * cols), (rank, cols))
    x_all, w_all, qkv_t, low_t = qkv_call(
        jnp.stack(bases).astype(jnp.int32), arrays, tuple(x_from), tuple(w_from), down_t, up, n * tok
    )
    half = (r % 2).astype(jnp.int32)[None]
    *others, grad_t, pack = attention_call(
        head_score_scale, half, cots, tuple(c_from), qkv_t, low_t, w_all, down_t, up, tok, 2, (F32, BF) * len(chips)
    )

    sums = []
    for i, j in enumerate(chips):
        total = others[2 * i] + to_row(others[2 * i + 1], 1).astype(F32)
        sums.append(to_row(total.astype(BF), j))
    mine, core_part = own_call(grad_t, pack, w_all, down_t, tok, (F32, BF))
    grad = mine + to_row(core_part, 1).astype(F32)
    for x in sums:
        grad = grad + x.astype(F32)

    packs = [pack, to_row(pack, 1)]
    for j in chips:
        packs.append(to_row(pack, j))
        packs.append(to_row(packs[j], 1))
    low_grad_t = None
    for j in range(n):
        blocks = [packs[j][rank:, (q ^ j) * tok : (q ^ j) * tok + tok] for q in range(n)]
        term = jnp.concatenate(blocks, axis=1)
        low_grad_t = term if low_grad_t is None else low_grad_t + term
    down_grad_t = jnp.dot(low_grad_t.astype(BF), x_all, preferred_element_type=F32)
    up_grad = jnp.zeros(adapter_up_weight.shape, F32)
    for j in range(n):
        up_grad = lax.dynamic_update_slice(up_grad, packs[j][:rank, :cols], (0, (r ^ j) * cols))

    x = tokens.astype(F32)
    scaled = grad * gain
    input_grad = inv_rms * (scaled - x * inv_rms * inv_rms * jnp.mean(scaled * x, -1, keepdims=True))
    return (input_grad.astype(BF), down_grad_t.T, up_grad)


def solution(mesh):
    in_specs = (
        P(("dp", "rows"), None),
        P("dp"),
        P(),
        P("rows", None),
        P(),
        P(),
        P("rows"),
        P(("dp", "rows"), None),
    )
    out_specs = (P(("dp", "rows"), None), P("dp", None), P("dp", None))
    shape = (mesh.shape["dp"], mesh.shape["rows"])
    return jax.shard_map(
        functools.partial(per_device, shape), mesh=mesh, in_specs=in_specs, out_specs=out_specs, check_vma=False
    )
```

time: 63.3 us -> 57.1 us (0.902)
  local copies, waits for them, and re-layouts: 8.01 us -> 1.3 us
  Pallas kernels: 9.23 us -> 13.8 us
  starting transfers between devices: 14.3 us -> 11.8 us
  waiting for transfers between devices: 26.5 us -> 24.6 us
  other arithmetic: 1.56 us -> 2.78 us
  matrix products: 1.85 us -> 0.89 us
    pallas_call x1 -> x4, Pallas kernels: 9.23 us -> 13.8 us  [the longest x1 6.13 us: attention_call(): pl.pallas_call(functools.partial(attention_kernel, cols // (3 * HEAD), to...]
    dynamic_slice x4 -> x3, local copies, waits for them, and re-layouts: 5.44 us -> 1.07 us  [the longest x1 1.06 us: per_device(): lax.dynamic_slice(weight, (0, (r ^ j + odd) * cols + c * part_cols), (k_r...]
    ppermute x17 -> x16, starting transfers between devices: 14.3 us -> 11.8 us  [send(): return lax.ppermute(x, axes, perm)]
    unnamed x15 -> x18, local copies, waits for them, and re-layouts: 2.42 us -> 0.05 us
    ppermute x17 -> x16, waiting for transfers between devices: 26.5 us -> 24.6 us  [send(): return lax.ppermute(x, axes, perm)]
    dot_general x5 -> x1, matrix products: 1.85 us -> 0.89 us  [per_device(): jnp.dot(low_grad_t.astype(BF), x_all, preferred_element_type=F32)]
    pallas_call x0 -> x1, other arithmetic: none -> 0.94 us  [prepare_call(): pl.pallas_call(functools.partial(prepare_kernel, (tok, cols, head_cols, s...]
  transfers between devices with their start and end apart: 17 -> 16, of which waited for: 7 -> 9; matrix products, arithmetic and copies ran while one was open for 11% -> 5% of each run, Pallas kernels for 0% -> 7%
where the time goes in v2:
time: 57.1 us; the launch traced here: 56.9 us
  waiting for transfers between devices  24.6 us (43%)
  Pallas kernels  13.8 us (24%)
  starting transfers between devices  11.8 us (21%)
  other arithmetic  2.78 us (5%)
  between operations  1.64 us (3%)
  local copies, waits for them, and re-layouts  1.3 us (2%)
  matrix products  0.89 us (2%)
    ppermute x16, waiting for transfers between devices, send(): return lax.ppermute(x, axes, perm)  24.6 us
    ppermute x16, starting transfers between devices, send(): return lax.ppermute(x, axes, perm)  11.8 us
    pallas_call x1, Pallas kernels, attention_call(): pl.pallas_call(functools.partial(attention_kernel, cols // (3 * HEAD), to...  6.13 us
    pallas_call x1, Pallas kernels, prepare_call(): pl.pallas_call(functools.partial(prepare_kernel, (tok, cols, head_cols, s...  3.74 us
    pallas_call x1, Pallas kernels, qkv_call(): pl.pallas_call(functools.partial(qkv_kernel, x_from, w_from), out_shape=[...  2.64 us
    pallas_call x1, Pallas kernels, own_call(): pl.pallas_call(own_kernel, out_shape=[jax.ShapeDtypeStruct((tok, down_t.s...  1.31 us
  transfers between devices with their start and end apart: 16, of which 9 were waited for; matrix products, arithmetic and copies ran while one was open for 5% of the time, Pallas kernels for 7%

profile of v2, /device:TPU:0, one launch (start us, length us, event | category | flops | bytes accessed | tf_op | source)
XLA Modules:
  0.0 56.9 jit_solution(11663397215150841700)
XLA Ops:
  1.4 0.6 %pad_maximum_fusion.features = f32[2,128]{1,0:T(2,128)} fusion(f32[1,128]{1,0:T(1,128)S(1)} %get-tuple-element.51, f32[1,128]{1,0:T(1,128)S(1)} %get-tuple-element.52), kind=kLoop, calls=%fused_computation.23 | loop fusion | flops 256 | bytes 2048 | tf_op jit(solution)/shard_map/stack | solution.py:25
  2.0 3.7 %prepare.1 = (bf16[128,1024]{1,0:T(8,128)(2,1)}, bf16[128,2816]{1,0:T(8,128)(2,1)}, bf16[256,768]{1,0:T(8,128)(2,1)}, bf16[128,256]{1,0:T(8,128)(2,1)}, bf16[128...) custom-call(f32[2,128]{1,0:T(2,128)} %pad_maximum_fusion.features, f32[256,1024]{1,0:T(8,128)} %gain_map.1, ...), custom_call_target="tpu_custom_call" | custom-call | flops 1 | bytes 1 | tf_op jit(solution)/shard_map/prepare/pallas_call | solution.py:259
  5.8 3.0 %collective-permute-start.7 = (bf16[128,1024]{1,0:T(8,128)(2,1)}, bf16[128,1024]{1,0:T(8,128)(2,1)S(1)}, u32[]{:S(2)}, u32[]{:S(2)}) collective-permute-start(bf16[128,1024]{1,0:T(8,128)(2,1)} %get-tuple-element.25.refs_3_), channel_id=1, source_target_pairs={{0,2},{1,3},{2,0},{3,1},{4,6},{5,7},{6,4},{7,5},{8,10},{9,11},{10,... | collective-permute-start | bytes 786440 | tf_op jit(solution)/shard_map/ppermute | solution.py:291
  8.8 1.1 %constant_dynamic-slice_fusion.1 = (bf16[256,384]{1,0:T(8,128)(2,1)S(1)}, bf16[256,384]{1,0:T(8,128)(2,1)S(1)}) fusion(bf16[256,3072]{1,0:T(8,128)(2,1)} %weight.1, s32[]{:T(128)S(6)} %select_n.42, s32[]{:T(128)S(6)} %select_n.41), kind=kLoop, calls=%fused_computation.20 | loop fusion | bytes 786440 | tf_op jit(solution)/shard_map/dynamic_slice | solution.py:309
  9.9 0.2 collective-permute-start.3
  10.0 1.9 %collective-permute-start.5 = (bf16[256,384]{1,0:T(8,128)(2,1)S(1)}, bf16[256,384]{1,0:T(8,128)(2,1)S(1)}, u32[]{:S(2)}, u32[]{:S(2)}) collective-permute-start(bf16[256,384]{1,0:T(8,128)(2,1)S(1)} %get-tuple-element.37), channel_id=1, source_target_pairs={{0,2},{1,3},{2,0},{3,1},{4,7},{5,6},{6,5},{7,4},{8,10},{9,11},{10,... | collective-permute-start | bytes 589832 | tf_op jit(solution)/shard_map/ppermute | solution.py:291
  11.9 0.1 collective-permute-start.1
  12.1 4.0 %collective-permute-done.7.refs_8_ = bf16[128,1024]{1,0:T(8,128)(2,1)S(1)} collective-permute-done((bf16[128,1024]{1,0:T(8,128)(2,1)}, bf16[128,1024]{1,0:T(8,128)(2,1)S(1)}, u32[]{:S(2)}, u32[]{:S(2)}) %collective-permute-start.7) | collective-permute-done | bytes 262176 | tf_op jit(solution)/shard_map/ppermute | solution.py:291
  16.2 0.1 collective-permute-start.8
  16.3 0.9 %reduce = f32[128]{0:T(128)S(1)} reduce(f32[128,1]{1,0:T(8,128)} %get-tuple-element.20, f32[]{:T(128)} %constant.61), dimensions={1}, to_apply=%get-tuple-element.20.reduce_sub_computation | reduce | bytes 1028 | tf_op jit(solution)/shard_map/prepare/pallas_call | solution.py:259
  17.3 0.1 stack.31.refs_0_
  17.4 3.0 %collective-permute-done.3.refs_4_ = bf16[256,384]{1,0:T(8,128)(2,1)S(1)} collective-permute-done((bf16[256,384]{1,0:T(8,128)(2,1)S(1)}, bf16[256,384]{1,0:T(8,128)(2,1)S(1)}, u32[]{:S(2)}, u32[]{:S(2)}) %collective-permute-start.3) | collective-permute-done | bytes 196640 | tf_op jit(solution)/shard_map/ppermute | solution.py:291
  20.3 1.1 %collective-permute-start.4 = (bf16[256,384]{1,0:T(8,128)(2,1)S(1)}, bf16[256,384]{1,0:T(8,128)(2,1)S(1)}, u32[]{:S(2)}, u32[]{:S(2)}) collective-permute-start(bf16[256,384]{1,0:T(8,128)(2,1)S(1)} %collective-permute-done.3.refs_4_), channel_id=1, source_target_pairs={{0,4},{1,5},{2,6},{3,7},{4,0},{5,1},{6,2},{7,3},{8,12},{9,13},{10,... | collective-permute-start | bytes 589832 | tf_op jit(solution)/shard_map/ppermute | solution.py:291
  21.4 3.1 %collective-permute-done.5.refs_6_ = bf16[256,384]{1,0:T(8,128)(2,1)S(1)} collective-permute-done((bf16[256,384]{1,0:T(8,128)(2,1)S(1)}, bf16[256,384]{1,0:T(8,128)(2,1)S(1)}, u32[]{:S(2)}, u32[]{:S(2)}) %collective-permute-start.5) | collective-permute-done | bytes 196640 | tf_op jit(solution)/shard_map/ppermute | solution.py:291
  24.6 1.1 %collective-permute-start.6 = (bf16[256,384]{1,0:T(8,128)(2,1)S(1)}, bf16[256,384]{1,0:T(8,128)(2,1)S(1)}, u32[]{:S(2)}, u32[]{:S(2)}) collective-permute-start(bf16[256,384]{1,0:T(8,128)(2,1)S(1)} %collective-permute-done.5.refs_6_), channel_id=1, source_target_pairs={{0,4},{1,5},{2,6},{3,7},{4,0},{5,1},{6,2},{7,3},{8,12},{9,13},{10,... | collective-permute-start | bytes 589832 | tf_op jit(solution)/shard_map/ppermute | solution.py:291
  25.6 0.9 %collective-permute-done.1.refs_4_ = bf16[128,512]{1,0:T(8,128)(2,1)S(1)} collective-permute-done((bf16[128,512]{1,0:T(8,128)(2,1)}, bf16[128,512]{1,0:T(8,128)(2,1)S(1)}, u32[]{:S(2)}, u32[]{:S(2)}) %collective-permute-start.1) | collective-permute-done | bytes 131104 | tf_op jit(solution)/shard_map/ppermute | solution.py:291
  26.6 0.6 collective-permute-start.2
  27.1 0.8 %collective-permute-done.9.refs_10_ = bf16[64,1024]{1,0:T(8,128)(2,1)S(1)} collective-permute-done((bf16[64,1024]{1,0:T(8,128)(2,1)S(1)}, bf16[64,1024]{1,0:T(8,128)(2,1)S(1)}, u32[]{:S(2)}, u32[]{:S(2)}) %collective-permute-start.9) | collective-permute-done | bytes 131104 | tf_op jit(solution)/shard_map/ppermute | solution.py:291
  27.9 3.9 %collective-permute-done.6.refs_7_ = bf16[256,384]{1,0:T(8,128)(2,1)S(1)} collective-permute-done((bf16[256,384]{1,0:T(8,128)(2,1)S(1)}, bf16[256,384]{1,0:T(8,128)(2,1)S(1)}, u32[]{:S(2)}, u32[]{:S(2)}) %collective-permute-start.6) | collective-permute-done | bytes 196640 | tf_op jit(solution)/shard_map/ppermute | solution.py:291
  31.8 2.6 %qkv.1 = (bf16[512,1024]{1,0:T(8,128)(2,1)S(1)}, bf16[1024,768]{1,0:T(8,128)(2,1)S(1)}, bf16[768,512]{1,0:T(8,128)(2,1)S(1)}, bf16[16,512]{1,0:T(8,128)(2,1)S(1)}) custom-call(s32[7]{0:T(128)S(1)} %stack.31.refs_0_, bf16[256,768]{1,0:T(8,128)(2,1)S(1)} %copy-done.1, bf16[128,2816]{1,0:T(8,128)(2,1)S(1)} %collective-permute-done.refs_2_.refs_3_, ...), custom_call_target="tpu_custom_call" | custom-call | flops 1 | bytes 1 | tf_op jit(solution)/shard_map/qkv/pallas_call | solution.py:90
  34.5 6.1 %attention_grads.1 = (f32[128,1024]{1,0:T(8,128)S(1)}, bf16[128,1024]{1,0:T(8,128)(2,1)S(1)}, bf16[768,512]{1,0:T(8,128)(2,1)S(1)}, f32[32,768]{1,0:T(8,128)S(1)}) custom-call(f32[4]{0:T(128)S(1)} %copy-done.5, s32[1]{0:T(128)} %bitcast.1.refs_1_, bf16[128,256]{1,0:T(8,128)(2,1)S(1)} %copy-done.4, ...), custom_call_target="tpu_custom_call" | custom-call | flops 1 | bytes 1 | tf_op jit(solution)/shard_map/attention_grads/pallas_call | solution.py:178
  40.7 1.6 %collective-permute-start.14 = (f32[32,768]{1,0:T(8,128)S(1)}, f32[32,768]{1,0:T(8,128)S(1)}, u32[]{:S(2)}, u32[]{:S(2)}) collective-permute-start(f32[32,768]{1,0:T(8,128)S(1)} %get-tuple-element.30.pack), channel_id=1, source_target_pairs={{0,2},{1,3},{2,0},{3,1},{4,6},{5,7},{6,4},{7,5},{8,10},{9,11},{10,... | collective-permute-start | bytes 294920 | tf_op jit(solution)/shard_map/ppermute | solution.py:291
  42.3 1.3 %own_grads.1 = (f32[128,1024]{1,0:T(8,128)S(1)}, bf16[128,1024]{1,0:T(8,128)(2,1)S(1)}) custom-call(bf16[768,512]{1,0:T(8,128)(2,1)S(1)} %get-tuple-element.29.grad_t, f32[32,768]{1,0:T(8,128)S(1)} %get-tuple-element.30.pack, bf16[1024,768]{1,0:T(8,128)(2,1)S(1)} %get-tuple-element.28.refs_8_.w_all, bf16[16,1024]{1,0:T(8,128)(2,1)S(1)} %bitcast.12), custom_call_target="tpu_custom_call" | custom-call | flops 1 | bytes 1 | tf_op jit(solution)/shard_map/own_grads/pallas_call | solution.py:200
  43.6 0.2 collective-permute-start.10
  43.9 0.3 collective-permute-start.11
  44.2 1.7 %collective-permute-done.14 = f32[32,768]{1,0:T(8,128)S(1)} collective-permute-done((f32[32,768]{1,0:T(8,128)S(1)}, f32[32,768]{1,0:T(8,128)S(1)}, u32[]{:S(2)}, u32[]{:S(2)}) %collective-permute-start.14) | collective-permute-done | bytes 98336 | tf_op jit(solution)/shard_map/ppermute | solution.py:291
  46.0 1.2 %collective-permute-done.15 = f32[32,768]{1,0:T(8,128)S(1)} collective-permute-done((f32[32,768]{1,0:T(8,128)S(1)}, f32[32,768]{1,0:T(8,128)S(1)}, u32[]{:S(2)}, u32[]{:S(2)}) %collective-permute-start.15) | collective-permute-done | bytes 98336 | tf_op jit(solution)/shard_map/ppermute | solution.py:291
  47.3 1.6 %collective-permute-start.12 = (bf16[128,1024]{1,0:T(8,128)(2,1)S(1)}, bf16[128,1024]{1,0:T(8,128)(2,1)S(1)}, u32[]{:S(2)}, u32[]{:S(2)}) collective-permute-start(bf16[128,1024]{1,0:T(8,128)(2,1)S(1)} %add_convert_fusion), channel_id=1, source_target_pairs={{0,2},{1,3},{2,0},{3,1},{4,6},{5,7},{6,4},{7,5},{8,10},{9,11},{10,... | collective-permute-start | bytes 786440 | tf_op jit(solution)/shard_map/ppermute | solution.py:291
  48.8 0.9 %fusion.9 = f32[1024,16]{0,1:T(8,128)} fusion(bf16[512,1024]{1,0:T(8,128)(2,1)S(1)} %get-tuple-element.36, f32[16,128]{1,0:T(8,128)S(1)} %get-tuple-element.48, f32[16,128]{1,0:T(8,128)S(1)} %get-tuple-element.49, f32[16,128]{1,0:T(8,128)S(1)} %get-tuple-element.50, f32[16,128]{1,0:T(8,128)S(1)} %get-tuple-element.47, f32[16,256]{1,0:T(8,128)S(1)} %get-tuple-element.46, ...), kind=kOutput, calls=%fused_computation.18 | convolution fusion | flops 16867328 | bytes 1245184 | tf_op jit(solution)/shard_map/dot_general | solution.py:390
  49.7 6.0 %collective-permute-done.12 = bf16[128,1024]{1,0:T(8,128)(2,1)S(1)} collective-permute-done((bf16[128,1024]{1,0:T(8,128)(2,1)S(1)}, bf16[128,1024]{1,0:T(8,128)(2,1)S(1)}, u32[]{:S(2)}, u32[]{:S(2)}) %collective-permute-start.12) | collective-permute-done | bytes 262176 | tf_op jit(solution)/shard_map/ppermute | solution.py:291
  55.7 0.2 fusion.5
  55.9 0.9 %fusion.4 = bf16[128,1024]{1,0:T(8,128)(2,1)} fusion(bf16[128,1024]{1,0:T(8,128)(2,1)S(1)} %copy-done.6, f32[128]{0:T(128)S(1)} %broadcast_multiply_fusion, f32[128]{0:T(128)S(1)} %reduce, f32[1024]{0:T(1024)S(1)} %bitcast.14, bf16[128,1024]{1,0:T(8,128)(2,1)S(1)} %collective-permute-done.12, f32[128,1024]{1,0:T(8,128)S(1)} %get-tuple-element.31, ...), kind=kLoop, calls=%fused_computation.6 | loop fusion | flops 1572864 | bytes 1577984 | tf_op jit(solution)/shard_map/convert_element_type | solution.py:398
  (43 shorter events, 0.3 us)
Async XLA Ops:
  0.6 26.5 %copy-start = (bf16[16,3072]{1,0:T(8,128)(2,1)S(1)}, bf16[16,3072]{1,0:T(8,128)(2,1)}, u32[]{:S(2)}) copy-start(bf16[16,3072]{1,0:T(8,128)(2,1)} %param.13) | copy-start | bytes 294916
  5.7 26.1 %copy-start.1 = (bf16[256,768]{1,0:T(8,128)(2,1)S(1)}, bf16[256,768]{1,0:T(8,128)(2,1)}, u32[]{:S(2)}) copy-start(bf16[256,768]{1,0:T(8,128)(2,1)} %get-tuple-element.24.refs_1_) | copy-start | bytes 1179652
  5.7 26.0 %copy-start.2 = (bf16[1024,16]{0,1:T(8,128)(2,1)S(1)}, bf16[1024,16]{0,1:T(8,128)(2,1)}, u32[]{:S(2)}) copy-start(bf16[1024,16]{0,1:T(8,128)(2,1)} %param.12) | copy-start | bytes 98308
  5.7 26.0 %copy-start.3 = (bf16[128,1024]{1,0:T(8,128)(2,1)S(1)}, bf16[128,1024]{1,0:T(8,128)(2,1)}, u32[]{:S(2)}) copy-start(bf16[128,1024]{1,0:T(8,128)(2,1)} %get-tuple-element.25.refs_3_) | copy-start | bytes 786436
  5.8 10.4 %collective-permute-start.7 = (bf16[128,1024]{1,0:T(8,128)(2,1)}, bf16[128,1024]{1,0:T(8,128)(2,1)S(1)}, u32[]{:S(2)}, u32[]{:S(2)}) collective-permute-start(bf16[128,1024]{1,0:T(8,128)(2,1)} %get-tuple-element.25.refs_3_), channel_id=1, source_target_pairs={{0,2},{1,3},{2,0},{3,1},{4,6},{5,7},{6,4},{7,5},{8,10},{9,11},{10,... | collective-permute-start | bytes 786440 | tf_op jit(solution)/shard_map/ppermute | solution.py:291
  8.8 23.0 %collective-permute-start = (bf16[128,2816]{1,0:T(8,128)(2,1)}, bf16[128,2816]{1,0:T(8,128)(2,1)S(1)}, u32[]{:S(2)}, u32[]{:S(2)}) collective-permute-start(bf16[128,2816]{1,0:T(8,128)(2,1)} %get-tuple-element.22), channel_id=1, source_target_pairs={{0,1},{1,0},{2,3},{3,2},{4,5},{5,4},{6,7},{7,6},{8,9},{9,8},{10,11... | collective-permute-start | bytes 2162696 | tf_op jit(solution)/shard_map/ppermute | solution.py:291
  9.9 10.5 %collective-permute-start.3 = (bf16[256,384]{1,0:T(8,128)(2,1)S(1)}, bf16[256,384]{1,0:T(8,128)(2,1)S(1)}, u32[]{:S(2)}, u32[]{:S(2)}) collective-permute-start(bf16[256,384]{1,0:T(8,128)(2,1)S(1)} %get-tuple-element.38), channel_id=1, source_target_pairs={{0,2},{1,3},{2,0},{3,1},{4,7},{5,6},{6,5},{7,4},{8,10},{9,11},{10,... | collective-permute-start | bytes 589832 | tf_op jit(solution)/shard_map/ppermute | solution.py:291
  10.0 14.5 %collective-permute-start.5 = (bf16[256,384]{1,0:T(8,128)(2,1)S(1)}, bf16[256,384]{1,0:T(8,128)(2,1)S(1)}, u32[]{:S(2)}, u32[]{:S(2)}) collective-permute-start(bf16[256,384]{1,0:T(8,128)(2,1)S(1)} %get-tuple-element.37), channel_id=1, source_target_pairs={{0,2},{1,3},{2,0},{3,1},{4,7},{5,6},{6,5},{7,4},{8,10},{9,11},{10,... | collective-permute-start | bytes 589832 | tf_op jit(solution)/shard_map/ppermute | solution.py:291
  11.9 14.6 %collective-permute-start.1 = (bf16[128,512]{1,0:T(8,128)(2,1)}, bf16[128,512]{1,0:T(8,128)(2,1)S(1)}, u32[]{:S(2)}, u32[]{:S(2)}) collective-permute-start(bf16[128,512]{1,0:T(8,128)(2,1)} %get-tuple-element.23), channel_id=1, source_target_pairs={{0,2},{1,3},{2,0},{3,1},{4,6},{5,7},{6,4},{7,5},{8,10},{9,11},{10,... | collective-permute-start | bytes 393224 | tf_op jit(solution)/shard_map/ppermute | solution.py:291
  16.2 18.3 %copy-start.4 = (bf16[128,256]{1,0:T(8,128)(2,1)S(1)}, bf16[128,256]{1,0:T(8,128)(2,1)}, u32[]{:S(2)}) copy-start(bf16[128,256]{1,0:T(8,128)(2,1)} %get-tuple-element.21.refs_2_) | copy-start | bytes 196612
  16.2 18.3 %copy-start.5 = (f32[4]{0:T(128)S(1)}, f32[4]{0:T(128)}, u32[]{:S(2)}) copy-start(f32[4]{0:T(128)} %refs_0_.1) | copy-start | bytes 52
  16.2 10.4 %collective-permute-start.8 = (bf16[64,1024]{1,0:T(8,128)(2,1)S(1)}, bf16[64,1024]{1,0:T(8,128)(2,1)S(1)}, u32[]{:S(2)}, u32[]{:S(2)}) collective-permute-start(bf16[64,1024]{1,0:T(8,128)(2,1)S(1)} %get-tuple-element.40), channel_id=1, source_target_pairs={{0,1},{1,0},{2,3},{3,2},{4,5},{5,4},{6,7},{7,6},{8,9},{9,8},{10,11... | collective-permute-start | bytes 393224 | tf_op jit(solution)/shard_map/ppermute | solution.py:291
  20.3 7.5 %collective-permute-start.4 = (bf16[256,384]{1,0:T(8,128)(2,1)S(1)}, bf16[256,384]{1,0:T(8,128)(2,1)S(1)}, u32[]{:S(2)}, u32[]{:S(2)}) collective-permute-start(bf16[256,384]{1,0:T(8,128)(2,1)S(1)} %collective-permute-done.3.refs_4_), channel_id=1, source_target_pairs={{0,4},{1,5},{2,6},{3,7},{4,0},{5,1},{6,2},{7,3},{8,12},{9,13},{10,... | collective-permute-start | bytes 589832 | tf_op jit(solution)/shard_map/ppermute | solution.py:291
  24.6 7.2 %collective-permute-start.6 = (bf16[256,384]{1,0:T(8,128)(2,1)S(1)}, bf16[256,384]{1,0:T(8,128)(2,1)S(1)}, u32[]{:S(2)}, u32[]{:S(2)}) collective-permute-start(bf16[256,384]{1,0:T(8,128)(2,1)S(1)} %collective-permute-done.5.refs_6_), channel_id=1, source_target_pairs={{0,4},{1,5},{2,6},{3,7},{4,0},{5,1},{6,2},{7,3},{8,12},{9,13},{10,... | collective-permute-start | bytes 589832 | tf_op jit(solution)/shard_map/ppermute | solution.py:291
  26.5 1.3 %collective-permute-start.9 = (bf16[64,1024]{1,0:T(8,128)(2,1)S(1)}, bf16[64,1024]{1,0:T(8,128)(2,1)S(1)}, u32[]{:S(2)}, u32[]{:S(2)}) collective-permute-start(bf16[64,1024]{1,0:T(8,128)(2,1)S(1)} %get-tuple-element.39), channel_id=1, source_target_pairs={{0,1},{1,0},{2,3},{3,2},{4,5},{5,4},{6,7},{7,6},{8,9},{9,8},{10,11... | collective-permute-start | bytes 393224 | tf_op jit(solution)/shard_map/ppermute | solution.py:291
  26.6 7.9 %collective-permute-start.2 = (bf16[128,256]{1,0:T(8,128)(2,1)S(1)}, bf16[128,256]{1,0:T(8,128)(2,1)S(1)}, u32[]{:S(2)}, u32[]{:S(2)}) collective-permute-start(bf16[128,256]{1,0:T(8,128)(2,1)S(1)} %constant_dynamic-slice_fusion.3), channel_id=1, source_target_pairs={{0,1},{1,0},{2,3},{3,2},{4,5},{5,4},{6,7},{7,6},{8,9},{9,8},{10,11... | collective-permute-start | bytes 196616 | tf_op jit(solution)/shard_map/ppermute | solution.py:291
  40.6 5.3 %collective-permute-start.13 = (f32[32,768]{1,0:T(8,128)S(1)}, f32[32,768]{1,0:T(8,128)S(1)}, u32[]{:S(2)}, u32[]{:S(2)}) collective-permute-start(f32[32,768]{1,0:T(8,128)S(1)} %get-tuple-element.30.pack), channel_id=1, source_target_pairs={{0,1},{1,0},{2,3},{3,2},{4,5},{5,4},{6,7},{7,6},{8,9},{9,8},{10,11... | collective-permute-start | bytes 294920 | tf_op jit(solution)/shard_map/ppermute | solution.py:291
  40.7 5.2 %collective-permute-start.14 = (f32[32,768]{1,0:T(8,128)S(1)}, f32[32,768]{1,0:T(8,128)S(1)}, u32[]{:S(2)}, u32[]{:S(2)}) collective-permute-start(f32[32,768]{1,0:T(8,128)S(1)} %get-tuple-element.30.pack), channel_id=1, source_target_pairs={{0,2},{1,3},{2,0},{3,1},{4,6},{5,7},{6,4},{7,5},{8,10},{9,11},{10,... | collective-permute-start | bytes 294920 | tf_op jit(solution)/shard_map/ppermute | solution.py:291
  43.6 12.1 %copy-start.6 = (bf16[128,1024]{1,0:T(8,128)(2,1)S(1)}, bf16[128,1024]{1,0:T(8,128)(2,1)}, u32[]{:S(2)}) copy-start(bf16[128,1024]{1,0:T(8,128)(2,1)} %tokens.1) | copy-start | bytes 786436
  43.6 12.1 %copy-start.8 = (f32[1,1024]{1,0:T(1,128)S(1)}, f32[1,1024]{1,0:T(1,128)}, u32[]{:S(2)}) copy-start(f32[1,1024]{1,0:T(1,128)} %get-tuple-element.35) | copy-start | bytes 12292
  43.6 6.1 %collective-permute-start.10 = (bf16[128,1024]{1,0:T(8,128)(2,1)S(1)}, bf16[128,1024]{1,0:T(8,128)(2,1)S(1)}, u32[]{:S(2)}, u32[]{:S(2)}) collective-permute-start(bf16[128,1024]{1,0:T(8,128)(2,1)S(1)} %get-tuple-element.32), channel_id=1, source_target_pairs={{0,1},{1,0},{2,3},{3,2},{4,5},{5,4},{6,7},{7,6},{8,9},{9,8},{10,11... | collective-permute-start | bytes 786440 | tf_op jit(solution)/shard_map/ppermute | solution.py:291
  43.9 3.4 %collective-permute-start.11 = (bf16[128,1024]{1,0:T(8,128)(2,1)S(1)}, bf16[128,1024]{1,0:T(8,128)(2,1)S(1)}, u32[]{:S(2)}, u32[]{:S(2)}) collective-permute-start(bf16[128,1024]{1,0:T(8,128)(2,1)S(1)} %get-tuple-element.34), channel_id=1, source_target_pairs={{0,1},{1,0},{2,3},{3,2},{4,5},{5,4},{6,7},{7,6},{8,9},{9,8},{10,11... | collective-permute-start | bytes 786440 | tf_op jit(solution)/shard_map/ppermute | solution.py:291
  45.9 1.3 %collective-permute-start.15 = (f32[32,768]{1,0:T(8,128)S(1)}, f32[32,768]{1,0:T(8,128)S(1)}, u32[]{:S(2)}, u32[]{:S(2)}) collective-permute-start(f32[32,768]{1,0:T(8,128)S(1)} %collective-permute-done.14), channel_id=1, source_target_pairs={{0,1},{1,0},{2,3},{3,2},{4,5},{5,4},{6,7},{7,6},{8,9},{9,8},{10,11... | collective-permute-start | bytes 294920 | tf_op jit(solution)/shard_map/ppermute | solution.py:291
  47.2 8.7 %copy-start.7 = (f32[16,3072]{1,0:T(8,128)}, f32[16,3072]{1,0:T(8,128)S(1)}, u32[]{:S(2)}) copy-start(f32[16,3072]{1,0:T(8,128)S(1)} %slice_dynamic-update-slice_fusion) | copy-start | bytes 589828
  47.3 8.4 %collective-permute-start.12 = (bf16[128,1024]{1,0:T(8,128)(2,1)S(1)}, bf16[128,1024]{1,0:T(8,128)(2,1)S(1)}, u32[]{:S(2)}, u32[]{:S(2)}) collective-permute-start(bf16[128,1024]{1,0:T(8,128)(2,1)S(1)} %add_convert_fusion), channel_id=1, source_target_pairs={{0,2},{1,3},{2,0},{3,1},{4,6},{5,7},{6,4},{7,5},{8,10},{9,11},{10,... | collective-permute-start | bytes 786440 | tf_op jit(solution)/shard_map/ppermute | solution.py:291

commit v3 on v2

v3 whole, which is shorter than its diff:
```python
import functools
import math

import jax
import jax.numpy as jnp
from jax import lax
from jax.experimental import pallas as pl
from jax.experimental.pallas import tpu as pltpu
from jax.sharding import PartitionSpec as P

HEAD = 64
EMB = 256
EPS = 1e-06
LOG2E = 1.4426950408889634
BF = jnp.bfloat16
F32 = jnp.float32
VMEM = 16 * 1024 * 1024
SMALL = pl.CostEstimate(flops=1, bytes_accessed=1, transcendentals=0)


def time_features(timestep):
    half_emb = EMB // 2
    frequency = jnp.exp(-math.log(10000.0) * jnp.arange(half_emb, dtype=F32) / half_emb)
    phases = timestep.astype(F32)[0] * frequency
    return jnp.stack([jnp.cos(phases), jnp.sin(phases)])


def contract(a, b, a_dim, b_dim):
    return lax.dot_general(a, b, (((a_dim,), (b_dim,)), ((), ())), preferred_element_type=F32)


def columns(x, size):
    if x.shape[1] == size:
        return x[...]
    return x[:, pl.ds(pl.multiple_of(lax.axis_index("rows") * size, 128), size)]


def qkv_kernel(x_from, w_from, *refs):
    down_t, up_in = refs[-6:-4]
    r, odd = lax.axis_index("rows"), lax.rem(lax.axis_index("dp"), 2)
    up = columns(up_in, refs[-2].shape[0])
    x_all, w_all, qkv_t, low_t = refs[-4:]
    at = 0
    for i, rows in x_from:
        x_all[pl.ds(at, rows), :] = refs[i][...]
        at += rows
    for i, to, j, other in w_from:
        rows, cols = refs[i].shape
        holder = r ^ j if other is None else r ^ (j + (odd ^ other))
        base = pl.multiple_of(holder * rows, 16)
        w_all[pl.ds(base, rows), pl.ds(to, cols)] = refs[i][...]
    seq = x_all.shape[0]
    step = math.gcd(512, seq)
    for s in range(0, seq, step):
        x = x_all[pl.ds(s, step), :]
        low = contract(x, down_t[...], 1, 1).astype(BF)
        low_t[:, pl.ds(s, step)] = low.T
        qkv = jnp.dot(x, w_all[...], preferred_element_type=F32)
        qkv = qkv + 0.5 * jnp.dot(low, up, preferred_element_type=F32)
        qkv_t[:, pl.ds(s, step)] = qkv.astype(BF).T


def gate(xs, rows, *deps):
    wanted = [(i, at) for i, x in enumerate(xs) for at in range(0, x.shape[0], rows[i])]

    def kernel(*refs):
        for (i, at), out in zip(wanted, refs[len(xs) + len(deps) :]):
            out[...] = refs[i][pl.ds(at, rows[i]), :]

    return pl.pallas_call(
        kernel,
        out_shape=[in_vmem((rows[i], xs[i].shape[1]), xs[i].dtype) for i, _ in wanted],
        in_specs=whole_vmem(len(xs) + len(deps)),
        out_specs=whole_vmem(len(wanted)),
        compiler_params=pltpu.CompilerParams(vmem_limit_bytes=VMEM),
        cost_estimate=SMALL,
        name="gate",
    )(*vmem(xs), *vmem(deps))


def in_vmem(shape, dtype):
    return pltpu.VMEM(shape, dtype)


def vmem(xs):
    return [pltpu.with_memory_space_constraint(x, pltpu.VMEM) for x in xs]


def hbm(xs):
    return [pltpu.with_memory_space_constraint(x, pltpu.HBM) for x in xs]


def whole_vmem(count):
    return [pl.BlockSpec(memory_space=pltpu.VMEM)] * count


def qkv_call(arrays, x_from, w_from, down_t, up, seq, cols):
    rank, width = down_t.shape
    return pl.pallas_call(
        functools.partial(qkv_kernel, x_from, w_from),
        out_shape=[
            in_vmem((seq, width), BF),
            in_vmem((width, cols), BF),
            in_vmem((cols, seq), BF),
            in_vmem((rank, seq), BF),
        ],
        in_specs=whole_vmem(len(arrays) + 2),
        out_specs=whole_vmem(4),
        compiler_params=pltpu.CompilerParams(vmem_limit_bytes=VMEM),
        cost_estimate=SMALL,
        name="qkv",
    )(*vmem(arrays), down_t, up)


def token_grads(low_grad_t, grad_t, w_all, down_t, at, rows):
    grad = grad_t[:, pl.ds(at, rows)].T
    part = contract(grad, w_all[...], 1, 1)
    return part + contract(low_grad_t[:, pl.ds(at, rows)].astype(BF), down_t[...], 0, 0)


def attention_kernel(heads, tok, c_from, first, outs, *refs):
    refs = list(refs)
    scale = refs.pop(0)
    cots = [refs.pop(0) for _ in c_from]
    qkv_t, low_t, w_all, down_t, up_in = (refs.pop(0) for _ in range(5))
    parts = [refs.pop(0) for _ in range(outs)]
    grad_t, pack, cot_t = refs

    cols, seq = qkv_t.shape
    up = columns(up_in, cols)
    step = math.gcd(512, seq)
    width = cot_t.shape[0]
    start = lax.rem(lax.axis_index("rows"), 2) * width
    for j, (i, choose) in enumerate(c_from):
        if not choose:
            block = cots[i][...]
        elif width % 128 == 0:
            block = cots[i][:, pl.ds(pl.multiple_of(start, 128), width)]
        else:
            block = jnp.where(start == 0, cots[i][:, pl.ds(0, width)], cots[i][:, pl.ds(width, width)])
        cot_t[:, pl.ds(j * tok, tok)] = block.T

    for h in range(heads):
        o = 3 * HEAD * h
        kf = qkv_t[pl.ds(o + HEAD, HEAD), :].astype(F32)
        k_inv = lax.rsqrt(jnp.sum(kf * kf, 0, keepdims=True) + EPS)
        k_unit = kf * k_inv
        k_low = k_unit.astype(BF)
        v = qkv_t[pl.ds(o + 2 * HEAD, HEAD), :]
        sc = scale[h]
        gk = gv = None
        for s in range(0, seq, step):
            qf = qkv_t[pl.ds(o, HEAD), pl.ds(s, step)].astype(F32)
            q_inv = lax.rsqrt(jnp.sum(qf * qf, 0, keepdims=True) + EPS)
            q_unit = qf * q_inv
            q_low = q_unit.astype(BF)
            g = cot_t[pl.ds(HEAD * h, HEAD), pl.ds(s, step)]
            e = jnp.exp2(contract(k_low, q_low, 0, 0) * (sc * LOG2E))
            attention = e * (1.0 / jnp.sum(e, 0, keepdims=True))
            grad_probs = contract(v, g, 0, 0)
            delta = jnp.sum(attention * grad_probs, 0, keepdims=True)
            grad_scores = (attention * (grad_probs - delta)).astype(BF)
            gv_s = contract(g, attention.astype(BF), 1, 1)
            gk_s = sc * contract(q_low, grad_scores, 1, 1)
            gq = sc * jnp.dot(k_low, grad_scores, preferred_element_type=F32)
            gq = q_inv * (gq - q_unit * jnp.sum(q_unit * gq, 0, keepdims=True))
            grad_t[pl.ds(o, HEAD), pl.ds(s, step)] = gq.astype(BF)
            gv = gv_s if gv is None else gv + gv_s
            gk = gk_s if gk is None else gk + gk_s
        gk = k_inv * (gk - k_unit * jnp.sum(k_unit * gk, 0, keepdims=True))
        grad_t[pl.ds(o + HEAD, HEAD), :] = gk.astype(BF)
        grad_t[pl.ds(o + 2 * HEAD, HEAD), :] = gv.astype(BF)

    rank = up.shape[0]
    pack[pl.ds(0, rank), pl.ds(0, cols)] = 0.5 * contract(low_t[...], grad_t[...], 1, 1)
    low_grad_t = pack.at[pl.ds(rank, rank), pl.ds(0, seq)]
    low_grad_t[...] = 0.5 * jnp.dot(up, grad_t[...], preferred_element_type=F32)
    for p in range(outs):
        part = token_grads(low_grad_t, grad_t, w_all, down_t, (first + p) * tok, tok)
        parts[p][...] = part.astype(parts[p].dtype)


def attention_call(scale, cots, c_from, qkv_t, low_t, w_all, down_t, up, tok, first, dtypes):
    cols, seq = qkv_t.shape
    rank, width = down_t.shape
    smem = pl.BlockSpec(memory_space=pltpu.SMEM)
    outs = len(dtypes)
    return pl.pallas_call(
        functools.partial(attention_kernel, cols // (3 * HEAD), tok, c_from, first, outs),
        out_shape=[in_vmem((tok, width), t) for t in dtypes]
        + [in_vmem((cols, seq), BF), in_vmem((2 * rank, max(cols, seq)), F32)],
        in_specs=[smem] + whole_vmem(len(cots) + 5),
        out_specs=whole_vmem(outs + 2),
        scratch_shapes=[pltpu.VMEM((cols // 3, seq), BF)],
        compiler_params=pltpu.CompilerParams(vmem_limit_bytes=VMEM),
        cost_estimate=SMALL,
        name="attention_grads",
    )(scale, *vmem(cots), qkv_t, low_t, w_all, down_t, up)


def other_half(x):
    rows, cols = x.shape
    half = cols // 2
    if half % 128:
        return lax.dynamic_slice(x, (0, (lax.axis_index("rows") ^ 1) % 2 * half), (rows, half))

    def kernel(x, out):
        core = lax.rem(lax.axis_index("rows") ^ 1, 2)
        out[...] = x[:, pl.ds(pl.multiple_of(core * half, 128), half)]

    return pl.pallas_call(
        kernel,
        out_shape=in_vmem((rows, half), x.dtype),
        in_specs=whole_vmem(1),
        out_specs=whole_vmem(1)[0],
        compiler_params=pltpu.CompilerParams(vmem_limit_bytes=VMEM),
        cost_estimate=SMALL,
        name="other_half",
    )(*vmem([x]))


def add(a, b):
    def kernel(a, b, out):
        out[...] = (a[...] + b[...].astype(F32)).astype(BF)

    return pl.pallas_call(
        kernel,
        out_shape=in_vmem(a.shape, BF),
        in_specs=whole_vmem(2),
        out_specs=whole_vmem(1)[0],
        compiler_params=pltpu.CompilerParams(vmem_limit_bytes=VMEM),
        cost_estimate=SMALL,
        name="add",
    )(*vmem([a, b]))


def own_kernel(deps, grad_t, pack, w_all, down_t, *refs):
    mine, rest = refs[deps], refs[deps + 1 :]
    tok = mine.shape[0]
    rank = down_t.shape[0]
    low_grad_t = pack.at[pl.ds(rank, rank), :]
    mine[...] = token_grads(low_grad_t, grad_t, w_all, down_t, 0, tok)
    part = token_grads(low_grad_t, grad_t, w_all, down_t, tok, tok).astype(BF)
    at = 0
    for out in rest:
        out[...] = part[at : at + out.shape[0]]
        at += out.shape[0]


def own_call(grad_t, pack, w_all, down_t, tok, blocks, deps):
    width = down_t.shape[1]
    return pl.pallas_call(
        functools.partial(own_kernel, len(deps)),
        out_shape=[in_vmem((tok, width), F32)] + [in_vmem((rows, width), BF) for rows in blocks],
        in_specs=whole_vmem(4 + len(deps)),
        out_specs=whole_vmem(1 + len(blocks)),
        compiler_params=pltpu.CompilerParams(vmem_limit_bytes=VMEM),
        cost_estimate=SMALL,
        name="own_grads",
    )(grad_t, pack, w_all, down_t, *vmem(deps))


def adapter_kernel(tok, *refs):
    packs, (x_all, down_grad_t, up_grad) = refs[:-3], refs[-3:]
    rank = down_grad_t.shape[0]
    r = lax.axis_index("rows")
    total = None
    for j, pack in enumerate(packs):
        blocks = [pack[pl.ds(rank, rank), pl.ds((q ^ j) * tok, tok)] for q in range(len(packs))]
        term = jnp.concatenate(blocks, axis=1)
        total = term if total is None else total + term
    down_grad_t[...] = jnp.dot(total.astype(BF), x_all[...], preferred_element_type=F32)
    cols = up_grad.shape[1] // len(packs)
    for j, pack in enumerate(packs):
        if cols % 128 == 0:
            up_grad[:, pl.ds(pl.multiple_of((r ^ j) * cols, 128), cols)] = pack[pl.ds(0, rank), pl.ds(0, cols)]


def adapter_call(packs, x_all, rank, all_cols, tok):
    down_grad_t, up_grad = pl.pallas_call(
        functools.partial(adapter_kernel, tok),
        out_shape=[
            jax.ShapeDtypeStruct((rank, x_all.shape[1]), F32),
            jax.ShapeDtypeStruct((rank, all_cols), F32),
        ],
        in_specs=whole_vmem(len(packs) + 1),
        out_specs=whole_vmem(2),
        compiler_params=pltpu.CompilerParams(vmem_limit_bytes=VMEM),
        cost_estimate=SMALL,
        name="adapter_grads",
    )(*vmem(packs), x_all)
    cols = all_cols // len(packs)
    if cols % 128:
        for j, pack in enumerate(packs):
            up_grad = lax.dynamic_update_slice(up_grad, pack[:rank, :cols], (0, (lax.axis_index("rows") ^ j) * cols))
    return down_grad_t, up_grad


def final_kernel(tokens, gain, inv_rms, mine, *refs):
    refs, out = refs[:-1], refs[-1]
    grad = mine[...]
    part = []
    for x in refs:
        part.append(x[...].astype(F32))
        if sum(p.shape[0] for p in part) == tokens.shape[0]:
            grad = grad + jnp.concatenate(part, axis=0)
            part = []
    x = tokens[...].astype(F32)
    inv = inv_rms[...]
    scaled = grad * gain[...]
    mean = jnp.mean(scaled * x, -1, keepdims=True)
    out[...] = (inv * (scaled - x * (inv * inv * mean))).astype(BF)


def final_call(tokens, gain, inv_rms, mine, terms):
    return pl.pallas_call(
        final_kernel,
        out_shape=jax.ShapeDtypeStruct(tokens.shape, BF),
        in_specs=whole_vmem(4 + len(terms)),
        out_specs=whole_vmem(1)[0],
        compiler_params=pltpu.CompilerParams(vmem_limit_bytes=VMEM),
        cost_estimate=SMALL,
        name="input_grads",
    )(tokens, gain, inv_rms, mine, *vmem(terms))


def prepare_kernel(chips, head_cols, sizes, features, gain_map, tokens, core_tokens, cot, *refs):
    count, outs = len(sizes), len(sizes) + len(chips)
    normed, core_normed, gain, inv_rms = refs[count : count + 4]
    cut = refs[count + 4 : count + 4 + outs]
    map_in, tokens_in, core_in, sems = refs[count + 4 + outs :]
    r = lax.axis_index("rows")
    copies = [(tokens, tokens_in), (core_tokens, core_in), (gain_map, map_in)]
    for x, size, out in zip(refs, sizes, cut):
        copies.append((x.at[:, pl.ds(pl.multiple_of(r * size, 128), size)] if size else x, out))
    for j, out in zip(chips, cut[count:]):
        chip = lax.div(r ^ j, 2) * (2 * head_cols)
        copies.append((cot.at[:, pl.ds(pl.multiple_of(chip, 128), 2 * head_cols)], out))
    copies = [pltpu.make_async_copy(a, b, sems.at[i]) for i, (a, b) in enumerate(copies)]
    for c in copies:
        c.start()
    half = features.shape[1]
    col = features[...].T
    for c in copies[:3]:
        c.wait()
    total = jnp.sum(col[:, :1] * map_in[:half, :], 0, keepdims=True)
    total = total + jnp.sum(col[:, 1:] * map_in[half:, :], 0, keepdims=True)
    gain[...] = 1.0 + total
    for x, out in ((tokens_in, normed), (core_in, core_normed)):
        x = x[...].astype(F32)
        inv = lax.rsqrt(jnp.mean(x * x, -1, keepdims=True) + EPS)
        if out is normed:
            inv_rms[...] = inv
        out[...] = (x * inv * gain[...]).astype(BF)
    for c in copies[3:]:
        c.wait()


def prepare_call(features, gain_map, tokens, core_tokens, cot, chips, head_cols, arrays):
    tok, width = tokens.shape
    shapes = [((tok, width), BF), ((tok, width), BF), ((1, width), F32), ((tok, 1), F32)]
    shapes += [((x.shape[0], size or x.shape[1]), BF) for x, size in arrays]
    shapes += [((tok, 2 * head_cols), BF)] * len(chips)
    copies = 3 + len(arrays) + len(chips)
    return pl.pallas_call(
        functools.partial(prepare_kernel, chips, head_cols, [size for _, size in arrays]),
        out_shape=[in_vmem(*shape) for shape in shapes],
        in_specs=whole_vmem(1) + [pl.BlockSpec(memory_space=pl.ANY)] * (4 + len(arrays)),
        out_specs=whole_vmem(len(shapes)),
        scratch_shapes=[
            pltpu.VMEM(gain_map.shape, F32),
            pltpu.VMEM((tok, width), BF),
            pltpu.VMEM((tok, width), BF),
            pltpu.SemaphoreType.DMA((copies,)),
        ],
        compiler_params=pltpu.CompilerParams(vmem_limit_bytes=VMEM),
        cost_estimate=SMALL,
        name="prepare",
    )(features, gain_map, tokens, core_tokens, cot, *[x for x, _ in arrays])


def per_device(
    mesh_shape,
    tokens,
    timestep,
    timestep_gain_map,
    query_key_value_weight,
    adapter_down_weight,
    adapter_up_weight,
    head_score_scale,
    heads_output_grad,
):
    dp, n = mesh_shape
    axes = ("dp", "rows")
    r, d = lax.axis_index("rows"), lax.axis_index("dp")

    def send(x, target):
        perm = []
        for a in range(dp):
            for b in range(n):
                a2, b2 = target(a, b)
                perm.append((a * n + b, a2 * n + b2))
        return lax.ppermute(x, axes, perm)

    def to_row(x, j):
        return send(x, lambda a, b: (a, b ^ j))

    tok, width = tokens.shape
    weight, cot_all = query_key_value_weight, heads_output_grad
    k_rows = weight.shape[0]
    cols = weight.shape[1] // n
    head_cols = cot_all.shape[1] // n
    chips = list(range(2, n, 2))

    cuts = 2 if cols % 256 == 0 else 1
    part_cols = cols // cuts
    odd = d % 2
    fetched = []
    for j in chips:
        for c in range(cuts):
            x = lax.dynamic_slice(weight, (0, (r ^ (j + odd)) * cols + c * part_cols), (k_rows, part_cols))
            fetched.append((send(x, lambda a, b, j=j: (a, b ^ (j + a % 2))), j, c))

    core_weight, core_tokens, core_cot = (to_row(x, 1) for x in (weight, tokens, cot_all))

    def mine(x, size):
        return (x, size) if size % 128 == 0 else (lax.dynamic_slice(x, (0, r * size), (x.shape[0], size)), 0)

    own_map, own_tokens, own_cot = hbm([timestep_gain_map, tokens, cot_all])
    normed, core_normed, gain, inv_rms, own_w, core_w, own_cot, core_cot, *chip_cot = prepare_call(
        time_features(timestep), own_map, own_tokens, core_tokens, own_cot, chips, head_cols,
        [mine(weight, cols), mine(core_weight, cols), mine(cot_all, head_cols), mine(core_cot, head_cols)],
    )
    arrays = [own_w, core_w, normed, core_normed]
    w_from, x_from = [(0, 0, 0, None), (1, 0, 1, None)], [(2, tok), (3, tok)]
    rows = tok // 2 if tok % 32 == 0 else tok
    count = tok // rows
    first = [i for i, (_, _, c) in enumerate(fetched) if c == 0]
    later = gate(
        [normed] + chip_cot + [fetched[i][0] for i in first], [rows] + [tok] * len(chips) + [k_rows] * len(first)
    )
    later_normed, chip_cot = later[:count], later[count : count + len(chips)]
    for i, x in zip(first, later[count + len(chips) :]):
        fetched[i] = (x, *fetched[i][1:])
    sharers = []
    for x, j, c in fetched:
        for other in range(2):
            w_from.append((len(arrays), c * part_cols, j, other))
            arrays.append(send(x, lambda a, b: (a ^ 1, b)) if other else x)
            if other and c == 0:
                sharers.append(arrays[-1])

    halves = [to_row(x, j) for j in chips for x in later_normed]
    later = list(gate(halves, [rows] * len(halves), *sharers))
    for i in range(0, len(halves), count):
        for x in halves[i : i + count] + [to_row(x, 1) for x in later[i : i + count]]:
            x_from.append((len(arrays), rows))
            arrays.append(x)

    cots, c_from = [own_cot, core_cot], [(0, False), (1, False)]
    for j, x in zip(chips, chip_cot):
        x = to_row(x, j)
        c_from += [(len(cots), True), (len(cots) + 1, False)]
        cots += [x, to_row(other_half(x), 1)]

    rank = adapter_up_weight.shape[0]
    down_t = adapter_down_weight.T
    up = adapter_up_weight
    if cols % 128:
        up = lax.dynamic_slice(up, (0, r * cols), (rank, cols))
    x_all, w_all, qkv_t, low_t = qkv_call(
        arrays, tuple(x_from), tuple(w_from), down_t, up, n * tok, cols
    )
    *others, grad_t, pack = attention_call(
        head_score_scale, cots, tuple(c_from), qkv_t, low_t, w_all, down_t, up, tok, 2, (F32, BF) * len(chips)
    )

    totals = [add(others[2 * i], to_row(others[2 * i + 1], 1)) for i in range(len(chips))]
    sums = [to_row(x, j) for x, j in zip(totals, chips)]
    packs = {0: pack, 1: to_row(pack, 1)}
    for j in chips:
        packs[j] = to_row(pack, j)
    blocks = (tok * 3 // 4, tok // 4) if tok % 64 == 0 else (tok,)
    mine, *core_part = own_call(grad_t, pack, w_all, down_t, tok, blocks, totals + [packs[j] for j in chips])
    core_part = [to_row(x, 1) for x in core_part]

    for j in chips:
        packs[j ^ 1] = to_row(packs[j], 1)
    down_grad_t, up_grad = adapter_call([packs[j] for j in range(n)], x_all, rank, n * cols, tok)

    input_grad = final_call(tokens, gain, inv_rms, mine, core_part + sums)
    return (input_grad, down_grad_t.T, up_grad)


def solution(mesh):
    in_specs = (
        P(("dp", "rows"), None),
        P("dp"),
        P(),
        P("rows", None),
        P(),
        P(),
        P("rows"),
        P(("dp", "rows"), None),
    )
    out_specs = (P(("dp", "rows"), None), P("dp", None), P("dp", None))
    shape = (mesh.shape["dp"], mesh.shape["rows"])
    return jax.shard_map(
        functools.partial(per_device, shape), mesh=mesh, in_specs=in_specs, out_specs=out_specs, check_vma=False
    )
```

time: 57.1 us -> 44.6 us (0.78)
  waiting for transfers between devices: 24.6 us -> 12.6 us
  other arithmetic: 2.78 us -> 0.06 us
  starting transfers between devices: 11.8 us -> 14.5 us
  local copies, waits for them, and re-layouts: 1.3 us -> 2.48 us
  matrix products: 0.89 us -> 0 us
    ppermute x16 -> x20, waiting for transfers between devices: 24.6 us -> 12.6 us  [send(): return lax.ppermute(x, axes, perm)]
    ppermute x16 -> x20, starting transfers between devices: 11.8 us -> 14.5 us  [send(): return lax.ppermute(x, axes, perm)]
    unnamed x18 -> x10, local copies, waits for them, and re-layouts: 0.05 us -> 1.42 us
    convert_element_type x2 -> x0, other arithmetic: 0.97 us -> none  [the longest x1 0.92 us: per_device(): return (input_grad.astype(BF), down_grad_t.T, up_grad)]
    pallas_call x1 -> x0, other arithmetic: 0.94 us -> none  [prepare_call(): pl.pallas_call(functools.partial(prepare_kernel, (tok, cols, head_cols, s...]
    dot_general x1 -> x0, matrix products: 0.89 us -> none  [per_device(): jnp.dot(low_grad_t.astype(BF), x_all, preferred_element_type=F32)]
    another operation x1, other arithmetic: 0.59 us -> 0.01 us  [time_features(): return jnp.stack([jnp.cos(phases), jnp.sin(phases)])]
    pallas_call x2 -> x8, Pallas kernels: 5.06 us -> 5.06 us  [the longest x1 1.71 us: prepare_call(): pl.pallas_call(functools.partial(prepare_kernel, chips, head_cols, [size...]
  transfers between devices with their start and end apart: 16 -> 20, of which waited for: 9 -> 9; matrix products, arithmetic and copies ran while one was open for 5% -> 3% of each run, Pallas kernels for 7% -> 14%
where the time goes in v3:
time: 44.6 us; the launch traced here: 44.4 us
  starting transfers between devices  14.5 us (33%)
  Pallas kernels  13.3 us (30%)
  waiting for transfers between devices  12.6 us (28%)
  local copies, waits for them, and re-layouts  2.48 us (6%)
  between operations  1.48 us (3%)
    ppermute x20, starting transfers between devices, send(): return lax.ppermute(x, axes, perm)  14.5 us
    ppermute x20, waiting for transfers between devices, send(): return lax.ppermute(x, axes, perm)  12.6 us
    pallas_call x1, Pallas kernels, attention_call(): pl.pallas_call(functools.partial(attention_kernel, cols // (3 * HEAD), to...  6.14 us
    pallas_call x1, Pallas kernels, qkv_call(): pl.pallas_call(functools.partial(qkv_kernel, x_from, w_from), out_shape=[...  2.09 us
    pallas_call x1, Pallas kernels, prepare_call(): pl.pallas_call(functools.partial(prepare_kernel, chips, head_cols, [size...  1.71 us
    unnamed x10, local copies, waits for them, and re-layouts  1.42 us
    pallas_call x1, Pallas kernels, own_call(): pl.pallas_call(functools.partial(own_kernel, len(deps)), out_shape=[in_vm...  1.32 us
    dynamic_slice x1, local copies, waits for them, and re-layouts, per_device(): lax.dynamic_slice(weight, (0, (r ^ j + odd) * cols + c * part_cols), (k_r...  1.06 us
  transfers between devices with their start and end apart: 20, of which 9 were waited for; matrix products, arithmetic and copies ran while one was open for 3% of the time, Pallas kernels for 14%

profile of v3, /device:TPU:0, one launch (start us, length us, event | category | flops | bytes accessed | tf_op | source)
XLA Modules:
  0.0 44.4 jit_solution(10943050882155622833)
XLA Ops:
  0.6 0.5 %collective-permute-start.1 = (bf16[256,3072]{1,0:T(8,128)(2,1)}, bf16[256,3072]{1,0:T(8,128)(2,1)S(1)}, u32[]{:S(2)}, u32[]{:S(2)}) collective-permute-start(bf16[256,3072]{1,0:T(8,128)(2,1)} %refs_0_.2), channel_id=1, source_target_pairs={{0,1},{1,0},{2,3},{3,2},{4,5},{5,4},{6,7},{7,6},{8,9},{9,8},{10,11... | collective-permute-start | bytes 4718600 | tf_op jit(solution)/shard_map/ppermute | solution.py:403
  1.1 0.1 collective-permute-start
  1.2 0.4 collective-permute-start.2
  1.7 1.1 %constant_dynamic-slice_fusion = (bf16[256,384]{1,0:T(8,128)(2,1)S(1)}, bf16[256,384]{1,0:T(8,128)(2,1)S(1)}) fusion(bf16[256,3072]{1,0:T(8,128)(2,1)} %refs_0_.2, s32[]{:T(128)S(6)} %select_n.15, s32[]{:T(128)S(6)} %select_n.14), kind=kLoop, calls=%fused_computation.1 | loop fusion | bytes 786440 | tf_op jit(solution)/shard_map/dynamic_slice | solution.py:421
  2.7 2.7 %collective-permute-start.3 = (bf16[256,384]{1,0:T(8,128)(2,1)S(1)}, bf16[256,384]{1,0:T(8,128)(2,1)S(1)}, u32[]{:S(2)}, u32[]{:S(2)}) collective-permute-start(bf16[256,384]{1,0:T(8,128)(2,1)S(1)} %get-tuple-element.60), channel_id=1, source_target_pairs={{0,2},{1,3},{2,0},{3,1},{4,7},{5,6},{6,5},{7,4},{8,10},{9,11},{10,... | collective-permute-start | bytes 589832 | tf_op jit(solution)/shard_map/ppermute | solution.py:403
  6.2 1.4 %copy-done = bf16[256,3072]{1,0:T(8,128)(2,1)S(1)} copy-done((bf16[256,3072]{1,0:T(8,128)(2,1)S(1)}, bf16[256,3072]{1,0:T(8,128)(2,1)}, u32[]{:S(2)}) %copy-start) | copy-done | bytes 1572888
  7.6 1.7 %prepare.1 = (bf16[128,1024]{1,0:T(8,128)(2,1)S(1)}, bf16[128,1024]{1,0:T(8,128)(2,1)S(1)}, f32[1,1024]{1,0:T(1,128)S(1)}, f32[128,1]{1,0:T(8,128)S(1)}, bf16[25...) custom-call(f32[2,128]{1,0:T(2,128)S(1)} %pad_maximum_fusion.feature, ...), custom_call_target="tpu_custom_call" | custom-call | flops 1 | bytes 1 | tf_op jit(solution)/shard_map/prepare/pallas_call | solution.py:365
  9.3 1.8 %collective-permute-done.3.refs_2_ = bf16[256,384]{1,0:T(8,128)(2,1)S(1)} collective-permute-done((bf16[256,384]{1,0:T(8,128)(2,1)S(1)}, bf16[256,384]{1,0:T(8,128)(2,1)S(1)}, u32[]{:S(2)}, u32[]{:S(2)}) %collective-permute-start.3) | collective-permute-done | bytes 196640 | tf_op jit(solution)/shard_map/ppermute | solution.py:403
  11.2 1.1 %collective-permute-start.6 = (bf16[256,384]{1,0:T(8,128)(2,1)S(1)}, bf16[256,384]{1,0:T(8,128)(2,1)S(1)}, u32[]{:S(2)}, u32[]{:S(2)}) collective-permute-start(bf16[256,384]{1,0:T(8,128)(2,1)S(1)} %get-tuple-element.41.refs_4_), channel_id=1, source_target_pairs={{0,4},{1,5},{2,6},{3,7},{4,0},{5,1},{6,2},{7,3},{8,12},{9,13},{10,... | collective-permute-start | bytes 589832 | tf_op jit(solution)/shard_map/ppermute | solution.py:403
  12.3 1.3 %collective-permute-start.10 = (bf16[64,1024]{1,0:T(8,128)(2,1)S(1)}, bf16[64,1024]{1,0:T(8,128)(2,1)S(1)}, u32[]{:S(2)}, u32[]{:S(2)}) collective-permute-start(bf16[64,1024]{1,0:T(8,128)(2,1)S(1)} %get-tuple-element.43), channel_id=1, source_target_pairs={{0,2},{1,3},{2,0},{3,1},{4,6},{5,7},{6,4},{7,5},{8,10},{9,11},{10,... | collective-permute-start | bytes 393224 | tf_op jit(solution)/shard_map/ppermute | solution.py:403
  13.6 0.7 %collective-permute-start.9 = (bf16[64,1024]{1,0:T(8,128)(2,1)S(1)}, bf16[64,1024]{1,0:T(8,128)(2,1)S(1)}, u32[]{:S(2)}, u32[]{:S(2)}) collective-permute-start(bf16[64,1024]{1,0:T(8,128)(2,1)S(1)} %get-tuple-element.42), channel_id=1, source_target_pairs={{0,2},{1,3},{2,0},{3,1},{4,6},{5,7},{6,4},{7,5},{8,10},{9,11},{10,... | collective-permute-start | bytes 393224 | tf_op jit(solution)/shard_map/ppermute | solution.py:403
  14.3 0.8 %collective-permute-done.7.refs_6_ = bf16[256,384]{1,0:T(8,128)(2,1)S(1)} collective-permute-done((bf16[256,384]{1,0:T(8,128)(2,1)S(1)}, bf16[256,384]{1,0:T(8,128)(2,1)S(1)}, u32[]{:S(2)}, u32[]{:S(2)}) %collective-permute-start.7) | collective-permute-done | bytes 196640 | tf_op jit(solution)/shard_map/ppermute | solution.py:403
  15.1 1.3 %collective-permute-start.8 = (bf16[256,384]{1,0:T(8,128)(2,1)S(1)}, bf16[256,384]{1,0:T(8,128)(2,1)S(1)}, u32[]{:S(2)}, u32[]{:S(2)}) collective-permute-start(bf16[256,384]{1,0:T(8,128)(2,1)S(1)} %collective-permute-done.7.refs_6_), channel_id=1, source_target_pairs={{0,4},{1,5},{2,6},{3,7},{4,0},{5,1},{6,2},{7,3},{8,12},{9,13},{10,... | collective-permute-start | bytes 589832 | tf_op jit(solution)/shard_map/ppermute | solution.py:403
  16.4 1.3 %collective-permute-start.4 = (bf16[128,512]{1,0:T(8,128)(2,1)S(1)}, bf16[128,512]{1,0:T(8,128)(2,1)S(1)}, u32[]{:S(2)}, u32[]{:S(2)}) collective-permute-start(bf16[128,512]{1,0:T(8,128)(2,1)S(1)} %get-tuple-element.37), channel_id=1, source_target_pairs={{0,2},{1,3},{2,0},{3,1},{4,6},{5,7},{6,4},{7,5},{8,10},{9,11},{10,... | collective-permute-start | bytes 393224 | tf_op jit(solution)/shard_map/ppermute | solution.py:403
  17.7 0.9 %collective-permute-done.10.refs_1_.refs_9_ = bf16[64,1024]{1,0:T(8,128)(2,1)S(1)} collective-permute-done((bf16[64,1024]{1,0:T(8,128)(2,1)S(1)}, bf16[64,1024]{1,0:T(8,128)(2,1)S(1)}, u32[]{:S(2)}, u32[]{:S(2)}) %collective-permute-start.10) | collective-permute-done | bytes 131104 | tf_op jit(solution)/shard_map/ppermute | solution.py:403
  18.6 2.8 %collective-permute-done.9.refs_0_.refs_8_ = bf16[64,1024]{1,0:T(8,128)(2,1)S(1)} collective-permute-done((bf16[64,1024]{1,0:T(8,128)(2,1)S(1)}, bf16[64,1024]{1,0:T(8,128)(2,1)S(1)}, u32[]{:S(2)}, u32[]{:S(2)}) %collective-permute-start.9) | collective-permute-done | bytes 131104 | tf_op jit(solution)/shard_map/ppermute | solution.py:403
  21.6 0.5 %collective-permute-start.12 = (bf16[64,1024]{1,0:T(8,128)(2,1)S(1)}, bf16[64,1024]{1,0:T(8,128)(2,1)S(1)}, u32[]{:S(2)}, u32[]{:S(2)}) collective-permute-start(bf16[64,1024]{1,0:T(8,128)(2,1)S(1)} %get-tuple-element.45), channel_id=1, source_target_pairs={{0,1},{1,0},{2,3},{3,2},{4,5},{5,4},{6,7},{7,6},{8,9},{9,8},{10,11... | collective-permute-start | bytes 393224 | tf_op jit(solution)/shard_map/ppermute | solution.py:403
  22.1 2.0 %collective-permute-done.4.x.refs_3_ = bf16[128,512]{1,0:T(8,128)(2,1)S(1)} collective-permute-done((bf16[128,512]{1,0:T(8,128)(2,1)S(1)}, bf16[128,512]{1,0:T(8,128)(2,1)S(1)}, u32[]{:S(2)}, u32[]{:S(2)}) %collective-permute-start.4) | collective-permute-done | bytes 131104 | tf_op jit(solution)/shard_map/ppermute | solution.py:403
  24.2 2.1 %qkv.1 = (bf16[512,1024]{1,0:T(8,128)(2,1)S(1)}, bf16[1024,768]{1,0:T(8,128)(2,1)S(1)}, bf16[768,512]{1,0:T(8,128)(2,1)S(1)}, bf16[16,512]{1,0:T(8,128)(2,1)S(1)}) custom-call(bf16[256,768]{1,0:T(8,128)(2,1)S(1)} %get-tuple-element.38.refs_0_, bf16[256,768]{1,0:T(8,128)(2,1)S(1)} %get-tuple-element.39.refs_1_, ...), custom_call_target="tpu_custom_call" | custom-call | flops 1 | bytes 1 | tf_op jit(solution)/shard_map/qkv/pallas_call | solution.py:99
  26.3 6.1 %attention_grads.1 = (f32[128,1024]{1,0:T(8,128)S(1)}, bf16[128,1024]{1,0:T(8,128)(2,1)S(1)}, bf16[768,512]{1,0:T(8,128)(2,1)S(1)}, f32[32,768]{1,0:T(8,128)S(1)}) custom-call(f32[4]{0:T(128)S(1)} %copy-done.4, bf16[128,256]{1,0:T(8,128)(2,1)S(1)} %get-tuple-element.33.refs_1_, bf16[128,256]{1,0:T(8,128)(2,1)S(1)} %get-tuple-element.34.refs_2_, ...), custom_call_target="tpu_custom_call" | custom-call | flops 1 | bytes 1 | tf_op jit(solution)/shard_map/attention_grads/pallas_call | solution.py:188
  32.4 0.5 %collective-permute-start.13 = (bf16[128,1024]{1,0:T(8,128)(2,1)S(1)}, bf16[128,1024]{1,0:T(8,128)(2,1)S(1)}, u32[]{:S(2)}, u32[]{:S(2)}) collective-permute-start(bf16[128,1024]{1,0:T(8,128)(2,1)S(1)} %get-tuple-element.52), channel_id=1, source_target_pairs={{0,1},{1,0},{2,3},{3,2},{4,5},{5,4},{6,7},{7,6},{8,9},{9,8},{10,11... | collective-permute-start | bytes 786440 | tf_op jit(solution)/shard_map/ppermute | solution.py:403
  33.0 1.5 %collective-permute-start.14 = (f32[32,768]{1,0:T(8,128)S(1)}, f32[32,768]{1,0:T(8,128)S(1)}, u32[]{:S(2)}, u32[]{:S(2)}) collective-permute-start(f32[32,768]{1,0:T(8,128)S(1)} %get-tuple-element.50.pack.refs_0_), channel_id=1, source_target_pairs={{0,2},{1,3},{2,0},{3,1},{4,6},{5,7},{6,4},{7,5},{8,10},{9,11},{10,... | collective-permute-start | bytes 294920 | tf_op jit(solution)/shard_map/ppermute | solution.py:403
  34.6 1.2 %collective-permute-start.17 = (bf16[128,1024]{1,0:T(8,128)(2,1)S(1)}, bf16[128,1024]{1,0:T(8,128)(2,1)S(1)}, u32[]{:S(2)}, u32[]{:S(2)}) collective-permute-start(bf16[128,1024]{1,0:T(8,128)(2,1)S(1)} %add.25.refs_0_), channel_id=1, source_target_pairs={{0,2},{1,3},{2,0},{3,1},{4,6},{5,7},{6,4},{7,5},{8,10},{9,11},{10,... | collective-permute-start | bytes 786440 | tf_op jit(solution)/shard_map/ppermute | solution.py:403
  35.8 2.5 %collective-permute-done.14.refs_1_.refs_2_ = f32[32,768]{1,0:T(8,128)S(1)} collective-permute-done((f32[32,768]{1,0:T(8,128)S(1)}, f32[32,768]{1,0:T(8,128)S(1)}, u32[]{:S(2)}, u32[]{:S(2)}) %collective-permute-start.14) | collective-permute-done | bytes 98336 | tf_op jit(solution)/shard_map/ppermute | solution.py:403
  38.3 1.3 %own_grads.1 = (f32[128,1024]{1,0:T(8,128)S(1)}, bf16[96,1024]{1,0:T(8,128)(2,1)S(1)}, bf16[32,1024]{1,0:T(8,128)(2,1)S(1)}) custom-call(bf16[768,512]{1,0:T(8,128)(2,1)S(1)} %get-tuple-element.49.grad_t, f32[32,768]{1,0:T(8,128)S(1)} %get-tuple-element.50.pack.refs_0_, bf16[1024,768]{1,0:T(8,128)(2,1)S(1)} %get-tuple-element.48.refs_7_.w_all, ...), custom_call_target="tpu_custom_call" | custom-call | flops 1 | bytes 1 | tf_op jit(solution)/shard_map/own_grads/pallas_call | solution.py:252
  39.7 0.5 %collective-permute-start.18 = (f32[32,768]{1,0:T(8,128)S(1)}, f32[32,768]{1,0:T(8,128)S(1)}, u32[]{:S(2)}, u32[]{:S(2)}) collective-permute-start(f32[32,768]{1,0:T(8,128)S(1)} %get-tuple-element.50.pack.refs_0_), channel_id=1, source_target_pairs={{0,1},{1,0},{2,3},{3,2},{4,5},{5,4},{6,7},{7,6},{8,9},{9,8},{10,11... | collective-permute-start | bytes 294920 | tf_op jit(solution)/shard_map/ppermute | solution.py:403
  40.3 0.4 collective-permute-start.16
  40.7 0.6 %collective-permute-done.18.refs_1_ = f32[32,768]{1,0:T(8,128)S(1)} collective-permute-done((f32[32,768]{1,0:T(8,128)S(1)}, f32[32,768]{1,0:T(8,128)S(1)}, u32[]{:S(2)}, u32[]{:S(2)}) %collective-permute-start.18) | collective-permute-done | bytes 98336 | tf_op jit(solution)/shard_map/ppermute | solution.py:403
  41.3 0.2 collective-permute-done.19.refs_3_
  41.5 0.9 %adapter_grads.1 = (f32[16,1024]{1,0:T(8,128)}, f32[16,3072]{1,0:T(8,128)}) custom-call(f32[32,768]{1,0:T(8,128)S(1)} %get-tuple-element.50.pack.refs_0_, f32[32,768]{1,0:T(8,128)S(1)} %collective-permute-done.18.refs_1_, f32[32,768]{1,0:T(8,128)S(1)} %collective-permute-done.14.refs_1_.refs_2_, f32[32,768]{1,0:T(8,128)S(1)} %collective-permute-done.19.refs_3_, ...), custom_call_target="tpu_custom_call" | custom-call | flops 1 | bytes 1 | tf_op jit(solution)/shard_map/adapter_grads/pallas_call | solution.py:280
  42.4 1.0 %collective-permute-done.17.refs_2_ = bf16[128,1024]{1,0:T(8,128)(2,1)S(1)} collective-permute-done((bf16[128,1024]{1,0:T(8,128)(2,1)S(1)}, bf16[128,1024]{1,0:T(8,128)(2,1)S(1)}, u32[]{:S(2)}, u32[]{:S(2)}) %collective-permute-start.17) | collective-permute-done | bytes 262176 | tf_op jit(solution)/shard_map/ppermute | solution.py:403
  43.4 1.0 %input_grads.1 = bf16[128,1024]{1,0:T(8,128)(2,1)} custom-call(bf16[128,1024]{1,0:T(8,128)(2,1)S(1)} %copy-done.1, f32[1,1024]{1,0:T(1,128)S(1)} %get-tuple-element.31.gain, f32[128,1]{1,0:T(8,128)S(1)} %get-tuple-element.32.inv_rms, f32[128,1024]{1,0:T(8,128)S(1)} %get-tuple-element.53.mine, bf16[96,1024]{1,0:T(8,128)(2,1)S(1)} %collective-permute-done.15.refs_0_, ...), custom_call_target="tpu_custom_call" | custom-call | flops 1 | bytes 1 | tf_op jit(solution)/shard_map/input_grads/pallas_call | solution.py:316
  (31 shorter events, 0.5 us)
Async XLA Ops:
  0.6 5.6 %collective-permute-start.1 = (bf16[256,3072]{1,0:T(8,128)(2,1)}, bf16[256,3072]{1,0:T(8,128)(2,1)S(1)}, u32[]{:S(2)}, u32[]{:S(2)}) collective-permute-start(bf16[256,3072]{1,0:T(8,128)(2,1)} %refs_0_.2), channel_id=1, source_target_pairs={{0,1},{1,0},{2,3},{3,2},{4,5},{5,4},{6,7},{7,6},{8,9},{9,8},{10,11... | collective-permute-start | bytes 4718600 | tf_op jit(solution)/shard_map/ppermute | solution.py:403
  1.1 5.0 %collective-permute-start = (bf16[128,1024]{1,0:T(8,128)(2,1)}, bf16[128,1024]{1,0:T(8,128)(2,1)S(1)}, u32[]{:S(2)}, u32[]{:S(2)}) collective-permute-start(bf16[128,1024]{1,0:T(8,128)(2,1)} %tokens.3), channel_id=1, source_target_pairs={{0,1},{1,0},{2,3},{3,2},{4,5},{5,4},{6,7},{7,6},{8,9},{9,8},{10,11... | collective-permute-start | bytes 786440 | tf_op jit(solution)/shard_map/ppermute | solution.py:403
  1.2 5.0 %collective-permute-start.2 = (bf16[128,1024]{1,0:T(8,128)(2,1)}, bf16[128,1024]{1,0:T(8,128)(2,1)S(1)}, u32[]{:S(2)}, u32[]{:S(2)}) collective-permute-start(bf16[128,1024]{1,0:T(8,128)(2,1)} %refs_2_.1), channel_id=1, source_target_pairs={{0,1},{1,0},{2,3},{3,2},{4,5},{5,4},{6,7},{7,6},{8,9},{9,8},{10,11... | collective-permute-start | bytes 786440 | tf_op jit(solution)/shard_map/ppermute | solution.py:403
  2.7 8.4 %collective-permute-start.3 = (bf16[256,384]{1,0:T(8,128)(2,1)S(1)}, bf16[256,384]{1,0:T(8,128)(2,1)S(1)}, u32[]{:S(2)}, u32[]{:S(2)}) collective-permute-start(bf16[256,384]{1,0:T(8,128)(2,1)S(1)} %get-tuple-element.60), channel_id=1, source_target_pairs={{0,2},{1,3},{2,0},{3,1},{4,7},{5,6},{6,5},{7,4},{8,10},{9,11},{10,... | collective-permute-start | bytes 589832 | tf_op jit(solution)/shard_map/ppermute | solution.py:403
  5.4 9.7 %collective-permute-start.7 = (bf16[256,384]{1,0:T(8,128)(2,1)S(1)}, bf16[256,384]{1,0:T(8,128)(2,1)S(1)}, u32[]{:S(2)}, u32[]{:S(2)}) collective-permute-start(bf16[256,384]{1,0:T(8,128)(2,1)S(1)} %get-tuple-element.59), channel_id=1, source_target_pairs={{0,2},{1,3},{2,0},{3,1},{4,7},{5,6},{6,5},{7,4},{8,10},{9,11},{10,... | collective-permute-start | bytes 589832 | tf_op jit(solution)/shard_map/ppermute | solution.py:403
  6.2 1.4 %copy-start = (bf16[256,3072]{1,0:T(8,128)(2,1)S(1)}, bf16[256,3072]{1,0:T(8,128)(2,1)}, u32[]{:S(2)}) copy-start(bf16[256,3072]{1,0:T(8,128)(2,1)} %refs_0_.2) | copy-start | bytes 4718596
  7.6 16.5 %copy-start.2 = (bf16[16,3072]{1,0:T(8,128)(2,1)S(1)}, bf16[16,3072]{1,0:T(8,128)(2,1)}, u32[]{:S(2)}) copy-start(bf16[16,3072]{1,0:T(8,128)(2,1)} %refs_9_.1) | copy-start | bytes 294916
  7.6 16.5 %copy-start.3 = (bf16[1024,16]{0,1:T(8,128)(2,1)S(1)}, bf16[1024,16]{0,1:T(8,128)(2,1)}, u32[]{:S(2)}) copy-start(bf16[1024,16]{0,1:T(8,128)(2,1)} %param.12) | copy-start | bytes 98308
  11.2 10.3 %collective-permute-start.6 = (bf16[256,384]{1,0:T(8,128)(2,1)S(1)}, bf16[256,384]{1,0:T(8,128)(2,1)S(1)}, u32[]{:S(2)}, u32[]{:S(2)}) collective-permute-start(bf16[256,384]{1,0:T(8,128)(2,1)S(1)} %get-tuple-element.41.refs_4_), channel_id=1, source_target_pairs={{0,4},{1,5},{2,6},{3,7},{4,0},{5,1},{6,2},{7,3},{8,12},{9,13},{10,... | collective-permute-start | bytes 589832 | tf_op jit(solution)/shard_map/ppermute | solution.py:403
  12.3 6.4 %collective-permute-start.10 = (bf16[64,1024]{1,0:T(8,128)(2,1)S(1)}, bf16[64,1024]{1,0:T(8,128)(2,1)S(1)}, u32[]{:S(2)}, u32[]{:S(2)}) collective-permute-start(bf16[64,1024]{1,0:T(8,128)(2,1)S(1)} %get-tuple-element.43), channel_id=1, source_target_pairs={{0,2},{1,3},{2,0},{3,1},{4,6},{5,7},{6,4},{7,5},{8,10},{9,11},{10,... | collective-permute-start | bytes 393224 | tf_op jit(solution)/shard_map/ppermute | solution.py:403
  13.6 7.8 %collective-permute-start.9 = (bf16[64,1024]{1,0:T(8,128)(2,1)S(1)}, bf16[64,1024]{1,0:T(8,128)(2,1)S(1)}, u32[]{:S(2)}, u32[]{:S(2)}) collective-permute-start(bf16[64,1024]{1,0:T(8,128)(2,1)S(1)} %get-tuple-element.42), channel_id=1, source_target_pairs={{0,2},{1,3},{2,0},{3,1},{4,6},{5,7},{6,4},{7,5},{8,10},{9,11},{10,... | collective-permute-start | bytes 393224 | tf_op jit(solution)/shard_map/ppermute | solution.py:403
  15.1 9.0 %collective-permute-start.8 = (bf16[256,384]{1,0:T(8,128)(2,1)S(1)}, bf16[256,384]{1,0:T(8,128)(2,1)S(1)}, u32[]{:S(2)}, u32[]{:S(2)}) collective-permute-start(bf16[256,384]{1,0:T(8,128)(2,1)S(1)} %collective-permute-done.7.refs_6_), channel_id=1, source_target_pairs={{0,4},{1,5},{2,6},{3,7},{4,0},{5,1},{6,2},{7,3},{8,12},{9,13},{10,... | collective-permute-start | bytes 589832 | tf_op jit(solution)/shard_map/ppermute | solution.py:403
  16.4 7.7 %collective-permute-start.4 = (bf16[128,512]{1,0:T(8,128)(2,1)S(1)}, bf16[128,512]{1,0:T(8,128)(2,1)S(1)}, u32[]{:S(2)}, u32[]{:S(2)}) collective-permute-start(bf16[128,512]{1,0:T(8,128)(2,1)S(1)} %get-tuple-element.37), channel_id=1, source_target_pairs={{0,2},{1,3},{2,0},{3,1},{4,6},{5,7},{6,4},{7,5},{8,10},{9,11},{10,... | collective-permute-start | bytes 393224 | tf_op jit(solution)/shard_map/ppermute | solution.py:403
  21.5 4.8 %copy-start.4 = (f32[4]{0:T(128)S(1)}, f32[4]{0:T(128)}, u32[]{:S(2)}) copy-start(f32[4]{0:T(128)} %refs_0_.3) | copy-start | bytes 52
  21.5 2.6 %collective-permute-start.11 = (bf16[64,1024]{1,0:T(8,128)(2,1)S(1)}, bf16[64,1024]{1,0:T(8,128)(2,1)S(1)}, u32[]{:S(2)}, u32[]{:S(2)}) collective-permute-start(bf16[64,1024]{1,0:T(8,128)(2,1)S(1)} %get-tuple-element.44), channel_id=1, source_target_pairs={{0,1},{1,0},{2,3},{3,2},{4,5},{5,4},{6,7},{7,6},{8,9},{9,8},{10,11... | collective-permute-start | bytes 393224 | tf_op jit(solution)/shard_map/ppermute | solution.py:403
  21.6 2.6 %collective-permute-start.12 = (bf16[64,1024]{1,0:T(8,128)(2,1)S(1)}, bf16[64,1024]{1,0:T(8,128)(2,1)S(1)}, u32[]{:S(2)}, u32[]{:S(2)}) collective-permute-start(bf16[64,1024]{1,0:T(8,128)(2,1)S(1)} %get-tuple-element.45), channel_id=1, source_target_pairs={{0,1},{1,0},{2,3},{3,2},{4,5},{5,4},{6,7},{7,6},{8,9},{9,8},{10,11... | collective-permute-start | bytes 393224 | tf_op jit(solution)/shard_map/ppermute | solution.py:403
  24.1 2.2 %collective-permute-start.5 = (bf16[128,256]{1,0:T(8,128)(2,1)S(1)}, bf16[128,256]{1,0:T(8,128)(2,1)S(1)}, u32[]{:S(2)}, u32[]{:S(2)}) collective-permute-start(bf16[128,256]{1,0:T(8,128)(2,1)S(1)} %other_half.1), channel_id=1, source_target_pairs={{0,1},{1,0},{2,3},{3,2},{4,5},{5,4},{6,7},{7,6},{8,9},{9,8},{10,11... | collective-permute-start | bytes 196616 | tf_op jit(solution)/shard_map/ppermute | solution.py:403
  32.4 2.1 %collective-permute-start.13 = (bf16[128,1024]{1,0:T(8,128)(2,1)S(1)}, bf16[128,1024]{1,0:T(8,128)(2,1)S(1)}, u32[]{:S(2)}, u32[]{:S(2)}) collective-permute-start(bf16[128,1024]{1,0:T(8,128)(2,1)S(1)} %get-tuple-element.52), channel_id=1, source_target_pairs={{0,1},{1,0},{2,3},{3,2},{4,5},{5,4},{6,7},{7,6},{8,9},{9,8},{10,11... | collective-permute-start | bytes 786440 | tf_op jit(solution)/shard_map/ppermute | solution.py:403
  33.0 5.3 %collective-permute-start.14 = (f32[32,768]{1,0:T(8,128)S(1)}, f32[32,768]{1,0:T(8,128)S(1)}, u32[]{:S(2)}, u32[]{:S(2)}) collective-permute-start(f32[32,768]{1,0:T(8,128)S(1)} %get-tuple-element.50.pack.refs_0_), channel_id=1, source_target_pairs={{0,2},{1,3},{2,0},{3,1},{4,6},{5,7},{6,4},{7,5},{8,10},{9,11},{10,... | collective-permute-start | bytes 294920 | tf_op jit(solution)/shard_map/ppermute | solution.py:403
  34.6 8.8 %collective-permute-start.17 = (bf16[128,1024]{1,0:T(8,128)(2,1)S(1)}, bf16[128,1024]{1,0:T(8,128)(2,1)S(1)}, u32[]{:S(2)}, u32[]{:S(2)}) collective-permute-start(bf16[128,1024]{1,0:T(8,128)(2,1)S(1)} %add.25.refs_0_), channel_id=1, source_target_pairs={{0,2},{1,3},{2,0},{3,1},{4,6},{5,7},{6,4},{7,5},{8,10},{9,11},{10,... | collective-permute-start | bytes 786440 | tf_op jit(solution)/shard_map/ppermute | solution.py:403
  38.3 5.1 %copy-start.1 = (bf16[128,1024]{1,0:T(8,128)(2,1)S(1)}, bf16[128,1024]{1,0:T(8,128)(2,1)}, u32[]{:S(2)}) copy-start(bf16[128,1024]{1,0:T(8,128)(2,1)} %tokens.3) | copy-start | bytes 786436
  39.6 2.8 %collective-permute-start.15 = (bf16[96,1024]{1,0:T(8,128)(2,1)S(1)}, bf16[96,1024]{1,0:T(8,128)(2,1)S(1)}, u32[]{:S(2)}, u32[]{:S(2)}) collective-permute-start(bf16[96,1024]{1,0:T(8,128)(2,1)S(1)} %get-tuple-element.54), channel_id=1, source_target_pairs={{0,1},{1,0},{2,3},{3,2},{4,5},{5,4},{6,7},{7,6},{8,9},{9,8},{10,11... | collective-permute-start | bytes 589832 | tf_op jit(solution)/shard_map/ppermute | solution.py:403
  39.7 1.6 %collective-permute-start.18 = (f32[32,768]{1,0:T(8,128)S(1)}, f32[32,768]{1,0:T(8,128)S(1)}, u32[]{:S(2)}, u32[]{:S(2)}) collective-permute-start(f32[32,768]{1,0:T(8,128)S(1)} %get-tuple-element.50.pack.refs_0_), channel_id=1, source_target_pairs={{0,1},{1,0},{2,3},{3,2},{4,5},{5,4},{6,7},{7,6},{8,9},{9,8},{10,11... | collective-permute-start | bytes 294920 | tf_op jit(solution)/shard_map/ppermute | solution.py:403
  40.2 1.3 %collective-permute-start.19 = (f32[32,768]{1,0:T(8,128)S(1)}, f32[32,768]{1,0:T(8,128)S(1)}, u32[]{:S(2)}, u32[]{:S(2)}) collective-permute-start(f32[32,768]{1,0:T(8,128)S(1)} %collective-permute-done.14.refs_1_.refs_2_), channel_id=1, source_target_pairs={{0,1},{1,0},{2,3},{3,2},{4,5},{5,4},{6,7},{7,6},{8,9},{9,8},{10,11... | collective-permute-start | bytes 294920 | tf_op jit(solution)/shard_map/ppermute | solution.py:403
  40.3 2.1 %collective-permute-start.16 = (bf16[32,1024]{1,0:T(8,128)(2,1)S(1)}, bf16[32,1024]{1,0:T(8,128)(2,1)S(1)}, u32[]{:S(2)}, u32[]{:S(2)}) collective-permute-start(bf16[32,1024]{1,0:T(8,128)(2,1)S(1)} %get-tuple-element.55), channel_id=1, source_target_pairs={{0,1},{1,0},{2,3},{3,2},{4,5},{5,4},{6,7},{7,6},{8,9},{9,8},{10,11... | collective-permute-start | bytes 196616 | tf_op jit(solution)/shard_map/ppermute | solution.py:403

commit v4 on v3

--- a/solution.py
+++ b/solution.py
@@ -115,7 +115,7 @@
 def token_grads(low_grad_t, grad_t, w_all, down_t, at, rows):
     grad = grad_t[:, pl.ds(at, rows)].T
     part = contract(grad, w_all[...], 1, 1)
-    return part + contract(low_grad_t[:, pl.ds(at, rows)].astype(BF), down_t[...], 0, 0)
+    return part + contract(low_grad_t[:, pl.ds(at, rows)], down_t[...], 0, 0)
 
 
 def attention_kernel(heads, tok, c_from, first, outs, *refs):
@@ -156,25 +156,27 @@
             q_low = q_unit.astype(BF)
             g = cot_t[pl.ds(HEAD * h, HEAD), pl.ds(s, step)]
             e = jnp.exp2(contract(k_low, q_low, 0, 0) * (sc * LOG2E))
-            attention = e * (1.0 / jnp.sum(e, 0, keepdims=True))
+            share = 1.0 / jnp.sum(e, 0, keepdims=True)
             grad_probs = contract(v, g, 0, 0)
-            delta = jnp.sum(attention * grad_probs, 0, keepdims=True)
+            delta = jnp.sum(e * grad_probs, 0, keepdims=True) * share
+            attention = e * share
             grad_scores = (attention * (grad_probs - delta)).astype(BF)
-            gv_s = contract(g, attention.astype(BF), 1, 1)
-            gk_s = sc * contract(q_low, grad_scores, 1, 1)
+            gv_s = jnp.dot(attention.astype(BF), g.T, preferred_element_type=F32)
+            gk_s = jnp.dot(grad_scores, q_low.T, preferred_element_type=F32)
             gq = sc * jnp.dot(k_low, grad_scores, preferred_element_type=F32)
             gq = q_inv * (gq - q_unit * jnp.sum(q_unit * gq, 0, keepdims=True))
             grad_t[pl.ds(o, HEAD), pl.ds(s, step)] = gq.astype(BF)
             gv = gv_s if gv is None else gv + gv_s
             gk = gk_s if gk is None else gk + gk_s
+        gk = sc * gk.T
         gk = k_inv * (gk - k_unit * jnp.sum(k_unit * gk, 0, keepdims=True))
         grad_t[pl.ds(o + HEAD, HEAD), :] = gk.astype(BF)
-        grad_t[pl.ds(o + 2 * HEAD, HEAD), :] = gv.astype(BF)
+        grad_t[pl.ds(o + 2 * HEAD, HEAD), :] = gv.astype(BF).T
 
     rank = up.shape[0]
-    pack[pl.ds(0, rank), pl.ds(0, cols)] = 0.5 * contract(low_t[...], grad_t[...], 1, 1)
+    pack[pl.ds(0, rank), pl.ds(0, cols)] = (0.5 * contract(low_t[...], grad_t[...], 1, 1)).astype(BF)
     low_grad_t = pack.at[pl.ds(rank, rank), pl.ds(0, seq)]
-    low_grad_t[...] = 0.5 * jnp.dot(up, grad_t[...], preferred_element_type=F32)
+    low_grad_t[...] = (0.5 * jnp.dot(up, grad_t[...], preferred_element_type=F32)).astype(BF)
     for p in range(outs):
         part = token_grads(low_grad_t, grad_t, w_all, down_t, (first + p) * tok, tok)
         parts[p][...] = part.astype(parts[p].dtype)
@@ -188,7 +190,7 @@
     return pl.pallas_call(
         functools.partial(attention_kernel, cols // (3 * HEAD), tok, c_from, first, outs),
         out_shape=[in_vmem((tok, width), t) for t in dtypes]
-        + [in_vmem((cols, seq), BF), in_vmem((2 * rank, max(cols, seq)), F32)],
+        + [in_vmem((cols, seq), BF), in_vmem((2 * rank, max(cols, seq)), BF)],
         in_specs=[smem] + whole_vmem(len(cots) + 5),
         out_specs=whole_vmem(outs + 2),
         scratch_shapes=[pltpu.VMEM((cols // 3, seq), BF)],
@@ -267,13 +269,13 @@
     total = None
     for j, pack in enumerate(packs):
         blocks = [pack[pl.ds(rank, rank), pl.ds((q ^ j) * tok, tok)] for q in range(len(packs))]
-        term = jnp.concatenate(blocks, axis=1)
+        term = jnp.concatenate(blocks, axis=1).astype(F32)
         total = term if total is None else total + term
     down_grad_t[...] = jnp.dot(total.astype(BF), x_all[...], preferred_element_type=F32)
     cols = up_grad.shape[1] // len(packs)
     for j, pack in enumerate(packs):
         if cols % 128 == 0:
-            up_grad[:, pl.ds(pl.multiple_of((r ^ j) * cols, 128), cols)] = pack[pl.ds(0, rank), pl.ds(0, cols)]
+            up_grad[:, pl.ds(pl.multiple_of((r ^ j) * cols, 128), cols)] = pack[pl.ds(0, rank), pl.ds(0, cols)].astype(F32)
 
 
 def adapter_call(packs, x_all, rank, all_cols, tok):
@@ -292,7 +294,7 @@
     cols = all_cols // len(packs)
     if cols % 128:
         for j, pack in enumerate(packs):
-            up_grad = lax.dynamic_update_slice(up_grad, pack[:rank, :cols], (0, (lax.axis_index("rows") ^ j) * cols))
+            up_grad = lax.dynamic_update_slice(up_grad, pack[:rank, :cols].astype(F32), (0, (lax.axis_index("rows") ^ j) * cols))
     return down_grad_t, up_grad
 
 
@@ -480,7 +482,7 @@
     packs = {0: pack, 1: to_row(pack, 1)}
     for j in chips:
         packs[j] = to_row(pack, j)
-    blocks = (tok * 3 // 4, tok // 4) if tok % 64 == 0 else (tok,)
+    blocks = (tok * 7 // 8, tok // 8) if tok % 128 == 0 else (tok,)
     mine, *core_part = own_call(grad_t, pack, w_all, down_t, tok, blocks, totals + [packs[j] for j in chips])
     core_part = [to_row(x, 1) for x in core_part]
 

time: 44.6 us -> 43.6 us (0.978)
  Pallas kernels: 13.3 us -> 12.8 us
  waiting for transfers between devices: 12.6 us -> 12.1 us
    ppermute x20, waiting for transfers between devices: 12.6 us -> 12.1 us  [send(): return lax.ppermute(x, axes, perm)]
    pallas_call x1, Pallas kernels: 6.14 us -> 5.68 us  [attention_call(): pl.pallas_call(functools.partial(attention_kernel, cols // (3 * HEAD), to...]
where the time goes in v4:
time: 43.6 us; the launch traced here: 43.4 us
  starting transfers between devices  14.4 us (33%)
  Pallas kernels  12.8 us (29%)
  waiting for transfers between devices  12.1 us (28%)
  local copies, waits for them, and re-layouts  2.48 us (6%)
  between operations  1.48 us (3%)
    ppermute x20, starting transfers between devices, send(): return lax.ppermute(x, axes, perm)  14.4 us
    ppermute x20, waiting for transfers between devices, send(): return lax.ppermute(x, axes, perm)  12.1 us
    pallas_call x1, Pallas kernels, attention_call(): pl.pallas_call(functools.partial(attention_kernel, cols // (3 * HEAD), to...  5.68 us
    pallas_call x1, Pallas kernels, qkv_call(): pl.pallas_call(functools.partial(qkv_kernel, x_from, w_from), out_shape=[...  2.09 us
    pallas_call x1, Pallas kernels, prepare_call(): pl.pallas_call(functools.partial(prepare_kernel, chips, head_cols, [size...  1.71 us
    unnamed x10, local copies, waits for them, and re-layouts  1.42 us
    pallas_call x1, Pallas kernels, own_call(): pl.pallas_call(functools.partial(own_kernel, len(deps)), out_shape=[in_vm...  1.32 us
    dynamic_slice x1, local copies, waits for them, and re-layouts, per_device(): lax.dynamic_slice(weight, (0, (r ^ j + odd) * cols + c * part_cols), (k_r...  1.06 us
  transfers between devices with their start and end apart: 20, of which 9 were waited for; matrix products, arithmetic and copies ran while one was open for 3% of the time, Pallas kernels for 14%

profile of v4, /device:TPU:0, one launch (start us, length us, event | category | flops | bytes accessed | tf_op | source)
XLA Modules:
  0.0 43.4 jit_solution(1391104614762476556)
XLA Ops:
  0.6 0.5 %collective-permute-start.1 = (bf16[256,3072]{1,0:T(8,128)(2,1)}, bf16[256,3072]{1,0:T(8,128)(2,1)S(1)}, u32[]{:S(2)}, u32[]{:S(2)}) collective-permute-start(bf16[256,3072]{1,0:T(8,128)(2,1)} %refs_0_.2), channel_id=1, source_target_pairs={{0,1},{1,0},{2,3},{3,2},{4,5},{5,4},{6,7},{7,6},{8,9},{9,8},{10,11... | collective-permute-start | bytes 4718600 | tf_op jit(solution)/shard_map/ppermute | solution.py:405
  1.1 0.1 collective-permute-start
  1.2 0.4 collective-permute-start.2
  1.7 1.1 %constant_dynamic-slice_fusion = (bf16[256,384]{1,0:T(8,128)(2,1)S(1)}, bf16[256,384]{1,0:T(8,128)(2,1)S(1)}) fusion(bf16[256,3072]{1,0:T(8,128)(2,1)} %refs_0_.2, s32[]{:T(128)S(6)} %select_n.15, s32[]{:T(128)S(6)} %select_n.14), kind=kLoop, calls=%fused_computation.1 | loop fusion | bytes 786440 | tf_op jit(solution)/shard_map/dynamic_slice | solution.py:423
  2.7 2.7 %collective-permute-start.3 = (bf16[256,384]{1,0:T(8,128)(2,1)S(1)}, bf16[256,384]{1,0:T(8,128)(2,1)S(1)}, u32[]{:S(2)}, u32[]{:S(2)}) collective-permute-start(bf16[256,384]{1,0:T(8,128)(2,1)S(1)} %get-tuple-element.60), channel_id=1, source_target_pairs={{0,2},{1,3},{2,0},{3,1},{4,7},{5,6},{6,5},{7,4},{8,10},{9,11},{10,... | collective-permute-start | bytes 589832 | tf_op jit(solution)/shard_map/ppermute | solution.py:405
  6.2 1.4 %copy-done = bf16[256,3072]{1,0:T(8,128)(2,1)S(1)} copy-done((bf16[256,3072]{1,0:T(8,128)(2,1)S(1)}, bf16[256,3072]{1,0:T(8,128)(2,1)}, u32[]{:S(2)}) %copy-start) | copy-done | bytes 1572888
  7.6 1.7 %prepare.1 = (bf16[128,1024]{1,0:T(8,128)(2,1)S(1)}, bf16[128,1024]{1,0:T(8,128)(2,1)S(1)}, f32[1,1024]{1,0:T(1,128)S(1)}, f32[128,1]{1,0:T(8,128)S(1)}, bf16[25...) custom-call(f32[2,128]{1,0:T(2,128)S(1)} %pad_maximum_fusion.feature, ...), custom_call_target="tpu_custom_call" | custom-call | flops 1 | bytes 1 | tf_op jit(solution)/shard_map/prepare/pallas_call | solution.py:367
  9.3 1.8 %collective-permute-done.3.refs_2_ = bf16[256,384]{1,0:T(8,128)(2,1)S(1)} collective-permute-done((bf16[256,384]{1,0:T(8,128)(2,1)S(1)}, bf16[256,384]{1,0:T(8,128)(2,1)S(1)}, u32[]{:S(2)}, u32[]{:S(2)}) %collective-permute-start.3) | collective-permute-done | bytes 196640 | tf_op jit(solution)/shard_map/ppermute | solution.py:405
  11.2 1.1 %collective-permute-start.6 = (bf16[256,384]{1,0:T(8,128)(2,1)S(1)}, bf16[256,384]{1,0:T(8,128)(2,1)S(1)}, u32[]{:S(2)}, u32[]{:S(2)}) collective-permute-start(bf16[256,384]{1,0:T(8,128)(2,1)S(1)} %get-tuple-element.41.refs_4_), channel_id=1, source_target_pairs={{0,4},{1,5},{2,6},{3,7},{4,0},{5,1},{6,2},{7,3},{8,12},{9,13},{10,... | collective-permute-start | bytes 589832 | tf_op jit(solution)/shard_map/ppermute | solution.py:405
  12.3 1.3 %collective-permute-start.10 = (bf16[64,1024]{1,0:T(8,128)(2,1)S(1)}, bf16[64,1024]{1,0:T(8,128)(2,1)S(1)}, u32[]{:S(2)}, u32[]{:S(2)}) collective-permute-start(bf16[64,1024]{1,0:T(8,128)(2,1)S(1)} %get-tuple-element.43), channel_id=1, source_target_pairs={{0,2},{1,3},{2,0},{3,1},{4,6},{5,7},{6,4},{7,5},{8,10},{9,11},{10,... | collective-permute-start | bytes 393224 | tf_op jit(solution)/shard_map/ppermute | solution.py:405
  13.6 0.7 %collective-permute-start.9 = (bf16[64,1024]{1,0:T(8,128)(2,1)S(1)}, bf16[64,1024]{1,0:T(8,128)(2,1)S(1)}, u32[]{:S(2)}, u32[]{:S(2)}) collective-permute-start(bf16[64,1024]{1,0:T(8,128)(2,1)S(1)} %get-tuple-element.42), channel_id=1, source_target_pairs={{0,2},{1,3},{2,0},{3,1},{4,6},{5,7},{6,4},{7,5},{8,10},{9,11},{10,... | collective-permute-start | bytes 393224 | tf_op jit(solution)/shard_map/ppermute | solution.py:405
  14.3 0.8 %collective-permute-done.7.refs_6_ = bf16[256,384]{1,0:T(8,128)(2,1)S(1)} collective-permute-done((bf16[256,384]{1,0:T(8,128)(2,1)S(1)}, bf16[256,384]{1,0:T(8,128)(2,1)S(1)}, u32[]{:S(2)}, u32[]{:S(2)}) %collective-permute-start.7) | collective-permute-done | bytes 196640 | tf_op jit(solution)/shard_map/ppermute | solution.py:405
  15.1 1.3 %collective-permute-start.8 = (bf16[256,384]{1,0:T(8,128)(2,1)S(1)}, bf16[256,384]{1,0:T(8,128)(2,1)S(1)}, u32[]{:S(2)}, u32[]{:S(2)}) collective-permute-start(bf16[256,384]{1,0:T(8,128)(2,1)S(1)} %collective-permute-done.7.refs_6_), channel_id=1, source_target_pairs={{0,4},{1,5},{2,6},{3,7},{4,0},{5,1},{6,2},{7,3},{8,12},{9,13},{10,... | collective-permute-start | bytes 589832 | tf_op jit(solution)/shard_map/ppermute | solution.py:405
  16.4 1.3 %collective-permute-start.4 = (bf16[128,512]{1,0:T(8,128)(2,1)S(1)}, bf16[128,512]{1,0:T(8,128)(2,1)S(1)}, u32[]{:S(2)}, u32[]{:S(2)}) collective-permute-start(bf16[128,512]{1,0:T(8,128)(2,1)S(1)} %get-tuple-element.37), channel_id=1, source_target_pairs={{0,2},{1,3},{2,0},{3,1},{4,6},{5,7},{6,4},{7,5},{8,10},{9,11},{10,... | collective-permute-start | bytes 393224 | tf_op jit(solution)/shard_map/ppermute | solution.py:405
  17.7 0.9 %collective-permute-done.10.refs_1_.refs_9_ = bf16[64,1024]{1,0:T(8,128)(2,1)S(1)} collective-permute-done((bf16[64,1024]{1,0:T(8,128)(2,1)S(1)}, bf16[64,1024]{1,0:T(8,128)(2,1)S(1)}, u32[]{:S(2)}, u32[]{:S(2)}) %collective-permute-start.10) | collective-permute-done | bytes 131104 | tf_op jit(solution)/shard_map/ppermute | solution.py:405
  18.6 2.8 %collective-permute-done.9.refs_0_.refs_8_ = bf16[64,1024]{1,0:T(8,128)(2,1)S(1)} collective-permute-done((bf16[64,1024]{1,0:T(8,128)(2,1)S(1)}, bf16[64,1024]{1,0:T(8,128)(2,1)S(1)}, u32[]{:S(2)}, u32[]{:S(2)}) %collective-permute-start.9) | collective-permute-done | bytes 131104 | tf_op jit(solution)/shard_map/ppermute | solution.py:405
  21.6 0.5 %collective-permute-start.12 = (bf16[64,1024]{1,0:T(8,128)(2,1)S(1)}, bf16[64,1024]{1,0:T(8,128)(2,1)S(1)}, u32[]{:S(2)}, u32[]{:S(2)}) collective-permute-start(bf16[64,1024]{1,0:T(8,128)(2,1)S(1)} %get-tuple-element.45), channel_id=1, source_target_pairs={{0,1},{1,0},{2,3},{3,2},{4,5},{5,4},{6,7},{7,6},{8,9},{9,8},{10,11... | collective-permute-start | bytes 393224 | tf_op jit(solution)/shard_map/ppermute | solution.py:405
  22.1 2.0 %collective-permute-done.4.x.refs_3_ = bf16[128,512]{1,0:T(8,128)(2,1)S(1)} collective-permute-done((bf16[128,512]{1,0:T(8,128)(2,1)S(1)}, bf16[128,512]{1,0:T(8,128)(2,1)S(1)}, u32[]{:S(2)}, u32[]{:S(2)}) %collective-permute-start.4) | collective-permute-done | bytes 131104 | tf_op jit(solution)/shard_map/ppermute | solution.py:405
  24.2 2.1 %qkv.1 = (bf16[512,1024]{1,0:T(8,128)(2,1)S(1)}, bf16[1024,768]{1,0:T(8,128)(2,1)S(1)}, bf16[768,512]{1,0:T(8,128)(2,1)S(1)}, bf16[16,512]{1,0:T(8,128)(2,1)S(1)}) custom-call(bf16[256,768]{1,0:T(8,128)(2,1)S(1)} %get-tuple-element.38.refs_0_, bf16[256,768]{1,0:T(8,128)(2,1)S(1)} %get-tuple-element.39.refs_1_, ...), custom_call_target="tpu_custom_call" | custom-call | flops 1 | bytes 1 | tf_op jit(solution)/shard_map/qkv/pallas_call | solution.py:99
  26.3 5.7 %attention_grads.1 = (f32[128,1024]{1,0:T(8,128)S(1)}, bf16[128,1024]{1,0:T(8,128)(2,1)S(1)}, bf16[768,512]{1,0:T(8,128)(2,1)S(1)}, bf16[32,768]{1,0:T(8,128)(2,1)S(1)}) custom-call(f32[4]{0:T(128)S(1)} %copy-done.4, bf16[128,256]{1,0:T(8,128)(2,1)S(1)} %get-tuple-element.33.refs_1_, bf16[128,256]{1,0:T(8,128)(2,1)S(1)} %get-tuple-element.34.refs_2_, ...), custom_call_target="tpu_custom_call" | custom-call | flops 1 | bytes 1 | tf_op jit(solution)/shard_map/attention_grads/pallas_call | solution.py:190
  32.0 0.5 %collective-permute-start.13 = (bf16[128,1024]{1,0:T(8,128)(2,1)S(1)}, bf16[128,1024]{1,0:T(8,128)(2,1)S(1)}, u32[]{:S(2)}, u32[]{:S(2)}) collective-permute-start(bf16[128,1024]{1,0:T(8,128)(2,1)S(1)} %get-tuple-element.52), channel_id=1, source_target_pairs={{0,1},{1,0},{2,3},{3,2},{4,5},{5,4},{6,7},{7,6},{8,9},{9,8},{10,11... | collective-permute-start | bytes 786440 | tf_op jit(solution)/shard_map/ppermute | solution.py:405
  32.5 1.5 %collective-permute-start.14 = (bf16[32,768]{1,0:T(8,128)(2,1)S(1)}, bf16[32,768]{1,0:T(8,128)(2,1)S(1)}, u32[]{:S(2)}, u32[]{:S(2)}) collective-permute-start(bf16[32,768]{1,0:T(8,128)(2,1)S(1)} %get-tuple-element.50.pack.refs_0_), channel_id=1, source_target_pairs={{0,2},{1,3},{2,0},{3,1},{4,6},{5,7},{6,4},{7,5},{8,10},{9,11},{10,... | collective-permute-start | bytes 147464 | tf_op jit(solution)/shard_map/ppermute | solution.py:405
  34.1 1.2 %collective-permute-start.17 = (bf16[128,1024]{1,0:T(8,128)(2,1)S(1)}, bf16[128,1024]{1,0:T(8,128)(2,1)S(1)}, u32[]{:S(2)}, u32[]{:S(2)}) collective-permute-start(bf16[128,1024]{1,0:T(8,128)(2,1)S(1)} %add.25.refs_0_), channel_id=1, source_target_pairs={{0,2},{1,3},{2,0},{3,1},{4,6},{5,7},{6,4},{7,5},{8,10},{9,11},{10,... | collective-permute-start | bytes 786440 | tf_op jit(solution)/shard_map/ppermute | solution.py:405
  35.3 1.3 %collective-permute-done.14.refs_1_.refs_2_ = bf16[32,768]{1,0:T(8,128)(2,1)S(1)} collective-permute-done((bf16[32,768]{1,0:T(8,128)(2,1)S(1)}, bf16[32,768]{1,0:T(8,128)(2,1)S(1)}, u32[]{:S(2)}, u32[]{:S(2)}) %collective-permute-start.14) | collective-permute-done | bytes 49184 | tf_op jit(solution)/shard_map/ppermute | solution.py:405
  36.6 1.3 %own_grads.1 = (f32[128,1024]{1,0:T(8,128)S(1)}, bf16[112,1024]{1,0:T(8,128)(2,1)S(1)}, bf16[16,1024]{1,0:T(8,128)(2,1)S(1)}) custom-call(bf16[768,512]{1,0:T(8,128)(2,1)S(1)} %get-tuple-element.49.grad_t, bf16[32,768]{1,0:T(8,128)(2,1)S(1)} %get-tuple-element.50.pack.refs_0_, bf16[1024,768]{1,0:T(8,128)(2,1)S(1)} %get-tuple-element.48.refs_7_.w_all, ...), custom_call_target="tpu_custom_call" | custom-call | flops 1 | bytes 1 | tf_op jit(solution)/shard_map/own_grads/pallas_call | solution.py:254
  38.0 0.5 %collective-permute-start.18 = (bf16[32,768]{1,0:T(8,128)(2,1)S(1)}, bf16[32,768]{1,0:T(8,128)(2,1)S(1)}, u32[]{:S(2)}, u32[]{:S(2)}) collective-permute-start(bf16[32,768]{1,0:T(8,128)(2,1)S(1)} %get-tuple-element.50.pack.refs_0_), channel_id=1, source_target_pairs={{0,1},{1,0},{2,3},{3,2},{4,5},{5,4},{6,7},{7,6},{8,9},{9,8},{10,11... | collective-permute-start | bytes 147464 | tf_op jit(solution)/shard_map/ppermute | solution.py:405
  38.6 0.4 collective-permute-start.16
  39.0 0.5 %collective-permute-done.18.refs_1_ = bf16[32,768]{1,0:T(8,128)(2,1)S(1)} collective-permute-done((bf16[32,768]{1,0:T(8,128)(2,1)S(1)}, bf16[32,768]{1,0:T(8,128)(2,1)S(1)}, u32[]{:S(2)}, u32[]{:S(2)}) %collective-permute-start.18) | collective-permute-done | bytes 49184 | tf_op jit(solution)/shard_map/ppermute | solution.py:405
  39.5 0.2 collective-permute-done.19.refs_3_
  39.7 0.9 %adapter_grads.1 = (f32[16,1024]{1,0:T(8,128)}, f32[16,3072]{1,0:T(8,128)}) custom-call(bf16[32,768]{1,0:T(8,128)(2,1)S(1)} %get-tuple-element.50.pack.refs_0_, bf16[32,768]{1,0:T(8,128)(2,1)S(1)} %collective-permute-done.18.refs_1_, bf16[32,768]{1,0:T(8,128)(2,1)S(1)} %collective-permute-done.14.refs_1_.refs_2_, ...), custom_call_target="tpu_custom_call" | custom-call | flops 1 | bytes 1 | tf_op jit(solution)/shard_map/adapter_grads/pallas_call | solution.py:282
  40.6 1.8 %collective-permute-done.17.refs_2_ = bf16[128,1024]{1,0:T(8,128)(2,1)S(1)} collective-permute-done((bf16[128,1024]{1,0:T(8,128)(2,1)S(1)}, bf16[128,1024]{1,0:T(8,128)(2,1)S(1)}, u32[]{:S(2)}, u32[]{:S(2)}) %collective-permute-start.17) | collective-permute-done | bytes 262176 | tf_op jit(solution)/shard_map/ppermute | solution.py:405
  42.4 1.0 %input_grads.1 = bf16[128,1024]{1,0:T(8,128)(2,1)} custom-call(bf16[128,1024]{1,0:T(8,128)(2,1)S(1)} %copy-done.1, f32[1,1024]{1,0:T(1,128)S(1)} %get-tuple-element.31.gain, f32[128,1]{1,0:T(8,128)S(1)} %get-tuple-element.32.inv_rms, f32[128,1024]{1,0:T(8,128)S(1)} %get-tuple-element.53.mine, bf16[112,1024]{1,0:T(8,128)(2,1)S(1)} %collective-permute-done.15.refs_0_, ...), custom_call_target="tpu_custom_call" | custom-call | flops 1 | bytes 1 | tf_op jit(solution)/shard_map/input_grads/pallas_call | solution.py:318
  (31 shorter events, 0.5 us)
Async XLA Ops:
  0.6 5.6 %collective-permute-start.1 = (bf16[256,3072]{1,0:T(8,128)(2,1)}, bf16[256,3072]{1,0:T(8,128)(2,1)S(1)}, u32[]{:S(2)}, u32[]{:S(2)}) collective-permute-start(bf16[256,3072]{1,0:T(8,128)(2,1)} %refs_0_.2), channel_id=1, source_target_pairs={{0,1},{1,0},{2,3},{3,2},{4,5},{5,4},{6,7},{7,6},{8,9},{9,8},{10,11... | collective-permute-start | bytes 4718600 | tf_op jit(solution)/shard_map/ppermute | solution.py:405
  1.1 5.0 %collective-permute-start = (bf16[128,1024]{1,0:T(8,128)(2,1)}, bf16[128,1024]{1,0:T(8,128)(2,1)S(1)}, u32[]{:S(2)}, u32[]{:S(2)}) collective-permute-start(bf16[128,1024]{1,0:T(8,128)(2,1)} %tokens.3), channel_id=1, source_target_pairs={{0,1},{1,0},{2,3},{3,2},{4,5},{5,4},{6,7},{7,6},{8,9},{9,8},{10,11... | collective-permute-start | bytes 786440 | tf_op jit(solution)/shard_map/ppermute | solution.py:405
  1.2 5.0 %collective-permute-start.2 = (bf16[128,1024]{1,0:T(8,128)(2,1)}, bf16[128,1024]{1,0:T(8,128)(2,1)S(1)}, u32[]{:S(2)}, u32[]{:S(2)}) collective-permute-start(bf16[128,1024]{1,0:T(8,128)(2,1)} %refs_2_.1), channel_id=1, source_target_pairs={{0,1},{1,0},{2,3},{3,2},{4,5},{5,4},{6,7},{7,6},{8,9},{9,8},{10,11... | collective-permute-start | bytes 786440 | tf_op jit(solution)/shard_map/ppermute | solution.py:405
  2.7 8.4 %collective-permute-start.3 = (bf16[256,384]{1,0:T(8,128)(2,1)S(1)}, bf16[256,384]{1,0:T(8,128)(2,1)S(1)}, u32[]{:S(2)}, u32[]{:S(2)}) collective-permute-start(bf16[256,384]{1,0:T(8,128)(2,1)S(1)} %get-tuple-element.60), channel_id=1, source_target_pairs={{0,2},{1,3},{2,0},{3,1},{4,7},{5,6},{6,5},{7,4},{8,10},{9,11},{10,... | collective-permute-start | bytes 589832 | tf_op jit(solution)/shard_map/ppermute | solution.py:405
  5.4 9.7 %collective-permute-start.7 = (bf16[256,384]{1,0:T(8,128)(2,1)S(1)}, bf16[256,384]{1,0:T(8,128)(2,1)S(1)}, u32[]{:S(2)}, u32[]{:S(2)}) collective-permute-start(bf16[256,384]{1,0:T(8,128)(2,1)S(1)} %get-tuple-element.59), channel_id=1, source_target_pairs={{0,2},{1,3},{2,0},{3,1},{4,7},{5,6},{6,5},{7,4},{8,10},{9,11},{10,... | collective-permute-start | bytes 589832 | tf_op jit(solution)/shard_map/ppermute | solution.py:405
  6.2 1.4 %copy-start = (bf16[256,3072]{1,0:T(8,128)(2,1)S(1)}, bf16[256,3072]{1,0:T(8,128)(2,1)}, u32[]{:S(2)}) copy-start(bf16[256,3072]{1,0:T(8,128)(2,1)} %refs_0_.2) | copy-start | bytes 4718596
  7.6 16.5 %copy-start.2 = (bf16[16,3072]{1,0:T(8,128)(2,1)S(1)}, bf16[16,3072]{1,0:T(8,128)(2,1)}, u32[]{:S(2)}) copy-start(bf16[16,3072]{1,0:T(8,128)(2,1)} %refs_9_.1) | copy-start | bytes 294916
  7.6 16.5 %copy-start.3 = (bf16[1024,16]{0,1:T(8,128)(2,1)S(1)}, bf16[1024,16]{0,1:T(8,128)(2,1)}, u32[]{:S(2)}) copy-start(bf16[1024,16]{0,1:T(8,128)(2,1)} %param.12) | copy-start | bytes 98308
  11.2 10.3 %collective-permute-start.6 = (bf16[256,384]{1,0:T(8,128)(2,1)S(1)}, bf16[256,384]{1,0:T(8,128)(2,1)S(1)}, u32[]{:S(2)}, u32[]{:S(2)}) collective-permute-start(bf16[256,384]{1,0:T(8,128)(2,1)S(1)} %get-tuple-element.41.refs_4_), channel_id=1, source_target_pairs={{0,4},{1,5},{2,6},{3,7},{4,0},{5,1},{6,2},{7,3},{8,12},{9,13},{10,... | collective-permute-start | bytes 589832 | tf_op jit(solution)/shard_map/ppermute | solution.py:405
  12.3 6.4 %collective-permute-start.10 = (bf16[64,1024]{1,0:T(8,128)(2,1)S(1)}, bf16[64,1024]{1,0:T(8,128)(2,1)S(1)}, u32[]{:S(2)}, u32[]{:S(2)}) collective-permute-start(bf16[64,1024]{1,0:T(8,128)(2,1)S(1)} %get-tuple-element.43), channel_id=1, source_target_pairs={{0,2},{1,3},{2,0},{3,1},{4,6},{5,7},{6,4},{7,5},{8,10},{9,11},{10,... | collective-permute-start | bytes 393224 | tf_op jit(solution)/shard_map/ppermute | solution.py:405
  13.6 7.8 %collective-permute-start.9 = (bf16[64,1024]{1,0:T(8,128)(2,1)S(1)}, bf16[64,1024]{1,0:T(8,128)(2,1)S(1)}, u32[]{:S(2)}, u32[]{:S(2)}) collective-permute-start(bf16[64,1024]{1,0:T(8,128)(2,1)S(1)} %get-tuple-element.42), channel_id=1, source_target_pairs={{0,2},{1,3},{2,0},{3,1},{4,6},{5,7},{6,4},{7,5},{8,10},{9,11},{10,... | collective-permute-start | bytes 393224 | tf_op jit(solution)/shard_map/ppermute | solution.py:405
  15.1 9.0 %collective-permute-start.8 = (bf16[256,384]{1,0:T(8,128)(2,1)S(1)}, bf16[256,384]{1,0:T(8,128)(2,1)S(1)}, u32[]{:S(2)}, u32[]{:S(2)}) collective-permute-start(bf16[256,384]{1,0:T(8,128)(2,1)S(1)} %collective-permute-done.7.refs_6_), channel_id=1, source_target_pairs={{0,4},{1,5},{2,6},{3,7},{4,0},{5,1},{6,2},{7,3},{8,12},{9,13},{10,... | collective-permute-start | bytes 589832 | tf_op jit(solution)/shard_map/ppermute | solution.py:405
  16.4 7.7 %collective-permute-start.4 = (bf16[128,512]{1,0:T(8,128)(2,1)S(1)}, bf16[128,512]{1,0:T(8,128)(2,1)S(1)}, u32[]{:S(2)}, u32[]{:S(2)}) collective-permute-start(bf16[128,512]{1,0:T(8,128)(2,1)S(1)} %get-tuple-element.37), channel_id=1, source_target_pairs={{0,2},{1,3},{2,0},{3,1},{4,6},{5,7},{6,4},{7,5},{8,10},{9,11},{10,... | collective-permute-start | bytes 393224 | tf_op jit(solution)/shard_map/ppermute | solution.py:405
  21.5 4.8 %copy-start.4 = (f32[4]{0:T(128)S(1)}, f32[4]{0:T(128)}, u32[]{:S(2)}) copy-start(f32[4]{0:T(128)} %refs_0_.3) | copy-start | bytes 52
  21.5 2.6 %collective-permute-start.11 = (bf16[64,1024]{1,0:T(8,128)(2,1)S(1)}, bf16[64,1024]{1,0:T(8,128)(2,1)S(1)}, u32[]{:S(2)}, u32[]{:S(2)}) collective-permute-start(bf16[64,1024]{1,0:T(8,128)(2,1)S(1)} %get-tuple-element.44), channel_id=1, source_target_pairs={{0,1},{1,0},{2,3},{3,2},{4,5},{5,4},{6,7},{7,6},{8,9},{9,8},{10,11... | collective-permute-start | bytes 393224 | tf_op jit(solution)/shard_map/ppermute | solution.py:405
  21.6 2.6 %collective-permute-start.12 = (bf16[64,1024]{1,0:T(8,128)(2,1)S(1)}, bf16[64,1024]{1,0:T(8,128)(2,1)S(1)}, u32[]{:S(2)}, u32[]{:S(2)}) collective-permute-start(bf16[64,1024]{1,0:T(8,128)(2,1)S(1)} %get-tuple-element.45), channel_id=1, source_target_pairs={{0,1},{1,0},{2,3},{3,2},{4,5},{5,4},{6,7},{7,6},{8,9},{9,8},{10,11... | collective-permute-start | bytes 393224 | tf_op jit(solution)/shard_map/ppermute | solution.py:405
  24.1 2.2 %collective-permute-start.5 = (bf16[128,256]{1,0:T(8,128)(2,1)S(1)}, bf16[128,256]{1,0:T(8,128)(2,1)S(1)}, u32[]{:S(2)}, u32[]{:S(2)}) collective-permute-start(bf16[128,256]{1,0:T(8,128)(2,1)S(1)} %other_half.1), channel_id=1, source_target_pairs={{0,1},{1,0},{2,3},{3,2},{4,5},{5,4},{6,7},{7,6},{8,9},{9,8},{10,11... | collective-permute-start | bytes 196616 | tf_op jit(solution)/shard_map/ppermute | solution.py:405
  32.0 2.0 %collective-permute-start.13 = (bf16[128,1024]{1,0:T(8,128)(2,1)S(1)}, bf16[128,1024]{1,0:T(8,128)(2,1)S(1)}, u32[]{:S(2)}, u32[]{:S(2)}) collective-permute-start(bf16[128,1024]{1,0:T(8,128)(2,1)S(1)} %get-tuple-element.52), channel_id=1, source_target_pairs={{0,1},{1,0},{2,3},{3,2},{4,5},{5,4},{6,7},{7,6},{8,9},{9,8},{10,11... | collective-permute-start | bytes 786440 | tf_op jit(solution)/shard_map/ppermute | solution.py:405
  32.5 4.1 %collective-permute-start.14 = (bf16[32,768]{1,0:T(8,128)(2,1)S(1)}, bf16[32,768]{1,0:T(8,128)(2,1)S(1)}, u32[]{:S(2)}, u32[]{:S(2)}) collective-permute-start(bf16[32,768]{1,0:T(8,128)(2,1)S(1)} %get-tuple-element.50.pack.refs_0_), channel_id=1, source_target_pairs={{0,2},{1,3},{2,0},{3,1},{4,6},{5,7},{6,4},{7,5},{8,10},{9,11},{10,... | collective-permute-start | bytes 147464 | tf_op jit(solution)/shard_map/ppermute | solution.py:405
  34.1 8.3 %collective-permute-start.17 = (bf16[128,1024]{1,0:T(8,128)(2,1)S(1)}, bf16[128,1024]{1,0:T(8,128)(2,1)S(1)}, u32[]{:S(2)}, u32[]{:S(2)}) collective-permute-start(bf16[128,1024]{1,0:T(8,128)(2,1)S(1)} %add.25.refs_0_), channel_id=1, source_target_pairs={{0,2},{1,3},{2,0},{3,1},{4,6},{5,7},{6,4},{7,5},{8,10},{9,11},{10,... | collective-permute-start | bytes 786440 | tf_op jit(solution)/shard_map/ppermute | solution.py:405
  36.6 5.8 %copy-start.1 = (bf16[128,1024]{1,0:T(8,128)(2,1)S(1)}, bf16[128,1024]{1,0:T(8,128)(2,1)}, u32[]{:S(2)}) copy-start(bf16[128,1024]{1,0:T(8,128)(2,1)} %tokens.3) | copy-start | bytes 786436
  37.9 2.7 %collective-permute-start.15 = (bf16[112,1024]{1,0:T(8,128)(2,1)S(1)}, bf16[112,1024]{1,0:T(8,128)(2,1)S(1)}, u32[]{:S(2)}, u32[]{:S(2)}) collective-permute-start(bf16[112,1024]{1,0:T(8,128)(2,1)S(1)} %get-tuple-element.54), channel_id=1, source_target_pairs={{0,1},{1,0},{2,3},{3,2},{4,5},{5,4},{6,7},{7,6},{8,9},{9,8},{10,11... | collective-permute-start | bytes 688136 | tf_op jit(solution)/shard_map/ppermute | solution.py:405
  38.0 1.5 %collective-permute-start.18 = (bf16[32,768]{1,0:T(8,128)(2,1)S(1)}, bf16[32,768]{1,0:T(8,128)(2,1)S(1)}, u32[]{:S(2)}, u32[]{:S(2)}) collective-permute-start(bf16[32,768]{1,0:T(8,128)(2,1)S(1)} %get-tuple-element.50.pack.refs_0_), channel_id=1, source_target_pairs={{0,1},{1,0},{2,3},{3,2},{4,5},{5,4},{6,7},{7,6},{8,9},{9,8},{10,11... | collective-permute-start | bytes 147464 | tf_op jit(solution)/shard_map/ppermute | solution.py:405
  38.5 1.2 %collective-permute-start.19 = (bf16[32,768]{1,0:T(8,128)(2,1)S(1)}, bf16[32,768]{1,0:T(8,128)(2,1)S(1)}, u32[]{:S(2)}, u32[]{:S(2)}) collective-permute-start(bf16[32,768]{1,0:T(8,128)(2,1)S(1)} %collective-permute-done.14.refs_1_.refs_2_), channel_id=1, source_target_pairs={{0,1},{1,0},{2,3},{3,2},{4,5},{5,4},{6,7},{7,6},{8,9},{9,8},{10,11... | collective-permute-start | bytes 147464 | tf_op jit(solution)/shard_map/ppermute | solution.py:405
  38.6 2.0 %collective-permute-start.16 = (bf16[16,1024]{1,0:T(8,128)(2,1)S(1)}, bf16[16,1024]{1,0:T(8,128)(2,1)S(1)}, u32[]{:S(2)}, u32[]{:S(2)}) collective-permute-start(bf16[16,1024]{1,0:T(8,128)(2,1)S(1)} %get-tuple-element.55), channel_id=1, source_target_pairs={{0,1},{1,0},{2,3},{3,2},{4,5},{5,4},{6,7},{7,6},{8,9},{9,8},{10,11... | collective-permute-start | bytes 98312 | tf_op jit(solution)/shard_map/ppermute | solution.py:405

commit v5 on v4

--- a/solution.py
+++ b/solution.py
@@ -33,6 +33,17 @@
     if x.shape[1] == size:
         return x[...]
     return x[:, pl.ds(pl.multiple_of(lax.axis_index("rows") * size, 128), size)]
+
+
+def multiply(x_all, w_all, down_t, up, put):
+    seq = x_all.shape[0]
+    step = math.gcd(512, seq) if seq > 512 else seq
+    for s in range(0, seq, step):
+        x = x_all[pl.ds(s, step), :]
+        low = contract(x, down_t[...], 1, 1).astype(BF)
+        qkv = jnp.dot(x, w_all[...], preferred_element_type=F32)
+        qkv = qkv + 0.5 * jnp.dot(low, up, preferred_element_type=F32)
+        put(s, step, qkv.astype(BF).T, low.T)
 
 
 def qkv_kernel(x_from, w_from, *refs):
@@ -49,27 +60,81 @@
         holder = r ^ j if other is None else r ^ (j + (odd ^ other))
         base = pl.multiple_of(holder * rows, 16)
         w_all[pl.ds(base, rows), pl.ds(to, cols)] = refs[i][...]
-    seq = x_all.shape[0]
-    step = math.gcd(512, seq)
-    for s in range(0, seq, step):
-        x = x_all[pl.ds(s, step), :]
-        low = contract(x, down_t[...], 1, 1).astype(BF)
-        low_t[:, pl.ds(s, step)] = low.T
-        qkv = jnp.dot(x, w_all[...], preferred_element_type=F32)
-        qkv = qkv + 0.5 * jnp.dot(low, up, preferred_element_type=F32)
-        qkv_t[:, pl.ds(s, step)] = qkv.astype(BF).T
-
-
-def gate(xs, rows, *deps):
-    wanted = [(i, at) for i, x in enumerate(xs) for at in range(0, x.shape[0], rows[i])]
+
+    def put(start, rows, qkv, low):
+        qkv_t[:, pl.ds(start, rows)] = qkv
+        low_t[:, pl.ds(start, rows)] = low
+
+    multiply(x_all, w_all, down_t, up, put)
+
+
+def qkv_call(arrays, x_from, w_from, down_t, up, seq, cols):
+    rank, width = down_t.shape
+    return pl.pallas_call(
+        functools.partial(qkv_kernel, x_from, w_from),
+        out_shape=[
+            in_vmem((seq, width), BF),
+            in_vmem((width, cols), BF),
+            in_vmem((cols, seq), BF),
+            in_vmem((rank, seq), BF),
+        ],
+        in_specs=whole_vmem(len(arrays) + 2),
+        out_specs=whole_vmem(4),
+        compiler_params=pltpu.CompilerParams(vmem_limit_bytes=VMEM),
+        cost_estimate=SMALL,
+        name="qkv",
+    )(*vmem(arrays), down_t, up)
+
+
+def last_qkv_kernel(tok, places, last_places, *refs):
+    w_all, first_qkv, first_low, down_t, up_in, x_all, qkv_t, low_t = refs[-8:]
+    at = 0
+    for x in refs[:-8]:
+        rows = x.shape[0]
+        x_all[pl.ds(at, rows), :] = x[...]
+        at += rows
+    for i, place in enumerate(places):
+        qkv_t[:, pl.ds(place * tok, tok)] = first_qkv[:, pl.ds(i * tok, tok)]
+        low_t[:, pl.ds(place * tok, tok)] = first_low[:, pl.ds(i * tok, tok)]
+
+    def put(start, rows, qkv, low):
+        for at in range(start, start + rows, tok):
+            place = last_places[at // tok] * tok
+            qkv_t[:, pl.ds(place, tok)] = qkv[:, at - start : at - start + tok]
+            low_t[:, pl.ds(place, tok)] = low[:, at - start : at - start + tok]
+
+    multiply(x_all, w_all, down_t, columns(up_in, qkv_t.shape[0]), put)
+
+
+def last_qkv_call(tok, places, last_places, xs, w_all, first_qkv, first_low, down_t, up):
+    rank, width = down_t.shape
+    cols = w_all.shape[1]
+    seq = (len(places) + len(last_places)) * tok
+    return pl.pallas_call(
+        functools.partial(last_qkv_kernel, tok, places, last_places),
+        out_shape=[
+            in_vmem((len(last_places) * tok, width), BF),
+            in_vmem((cols, seq), BF),
+            in_vmem((rank, seq), BF),
+        ],
+        in_specs=whole_vmem(len(xs) + 5),
+        out_specs=whole_vmem(3),
+        compiler_params=pltpu.CompilerParams(vmem_limit_bytes=VMEM),
+        cost_estimate=SMALL,
+        name="last_qkv",
+    )(*vmem(xs), *vmem([w_all, first_qkv, first_low]), down_t, up)
+
+
+def gate(xs, blocks, *deps):
+    wanted = [(i, sum(sizes[:k]), rows) for i, sizes in enumerate(blocks) for k, rows in enumerate(sizes)]
 
     def kernel(*refs):
-        for (i, at), out in zip(wanted, refs[len(xs) + len(deps) :]):
-            out[...] = refs[i][pl.ds(at, rows[i]), :]
+        for (i, at, rows), out in zip(wanted, refs[len(xs) + len(deps) :]):
+            out[...] = refs[i][pl.ds(at, rows), :]
 
     return pl.pallas_call(
         kernel,
-        out_shape=[in_vmem((rows[i], xs[i].shape[1]), xs[i].dtype) for i, _ in wanted],
+        out_shape=[in_vmem((rows, xs[i].shape[1]), xs[i].dtype) for i, _, rows in wanted],
         in_specs=whole_vmem(len(xs) + len(deps)),
         out_specs=whole_vmem(len(wanted)),
         compiler_params=pltpu.CompilerParams(vmem_limit_bytes=VMEM),
@@ -177,9 +242,12 @@
     pack[pl.ds(0, rank), pl.ds(0, cols)] = (0.5 * contract(low_t[...], grad_t[...], 1, 1)).astype(BF)
     low_grad_t = pack.at[pl.ds(rank, rank), pl.ds(0, seq)]
     low_grad_t[...] = (0.5 * jnp.dot(up, grad_t[...], preferred_element_type=F32)).astype(BF)
-    for p in range(outs):
-        part = token_grads(low_grad_t, grad_t, w_all, down_t, (first + p) * tok, tok)
-        parts[p][...] = part.astype(parts[p].dtype)
+    for p in range(0, outs, 4):
+        count = min(4, outs - p)
+        part = token_grads(low_grad_t, grad_t, w_all, down_t, (first + p) * tok, count * tok)
+        for i in range(count):
+            out = parts[p + i]
+            out[...] = part[i * tok : (i + 1) * tok].astype(out.dtype)
 
 
 def attention_call(scale, cots, c_from, qkv_t, low_t, w_all, down_t, up, tok, first, dtypes):
@@ -200,25 +268,25 @@
     )(scale, *vmem(cots), qkv_t, low_t, w_all, down_t, up)
 
 
-def other_half(x):
+def other_half(x, dep):
     rows, cols = x.shape
     half = cols // 2
     if half % 128:
         return lax.dynamic_slice(x, (0, (lax.axis_index("rows") ^ 1) % 2 * half), (rows, half))
 
-    def kernel(x, out):
+    def kernel(x, dep, out):
         core = lax.rem(lax.axis_index("rows") ^ 1, 2)
         out[...] = x[:, pl.ds(pl.multiple_of(core * half, 128), half)]
 
     return pl.pallas_call(
         kernel,
         out_shape=in_vmem((rows, half), x.dtype),
-        in_specs=whole_vmem(1),
+        in_specs=whole_vmem(2),
         out_specs=whole_vmem(1)[0],
         compiler_params=pltpu.CompilerParams(vmem_limit_bytes=VMEM),
         cost_estimate=SMALL,
         name="other_half",
-    )(*vmem([x]))
+    )(*vmem([x, dep]))
 
 
 def add(a, b):
@@ -241,8 +309,9 @@
     tok = mine.shape[0]
     rank = down_t.shape[0]
     low_grad_t = pack.at[pl.ds(rank, rank), :]
-    mine[...] = token_grads(low_grad_t, grad_t, w_all, down_t, 0, tok)
-    part = token_grads(low_grad_t, grad_t, w_all, down_t, tok, tok).astype(BF)
+    part = token_grads(low_grad_t, grad_t, w_all, down_t, 0, 2 * tok)
+    mine[...] = part[:tok]
+    part = part[tok:].astype(BF)
     at = 0
     for out in rest:
         out[...] = part[at : at + out.shape[0]]
@@ -262,8 +331,8 @@
     )(grad_t, pack, w_all, down_t, *vmem(deps))
 
 
-def adapter_kernel(tok, *refs):
-    packs, (x_all, down_grad_t, up_grad) = refs[:-3], refs[-3:]
+def adapter_kernel(tok, places, *refs):
+    packs, (first_x, last_x, down_grad_t, up_grad) = refs[:-4], refs[-4:]
     rank = down_grad_t.shape[0]
     r = lax.axis_index("rows")
     total = None
@@ -271,26 +340,32 @@
         blocks = [pack[pl.ds(rank, rank), pl.ds((q ^ j) * tok, tok)] for q in range(len(packs))]
         term = jnp.concatenate(blocks, axis=1).astype(F32)
         total = term if total is None else total + term
-    down_grad_t[...] = jnp.dot(total.astype(BF), x_all[...], preferred_element_type=F32)
+    total = total.astype(BF)
+    grad = None
+    for x, held in zip((first_x, last_x), places):
+        part = jnp.concatenate([total[:, p * tok : (p + 1) * tok] for p in held], axis=1)
+        term = jnp.dot(part, x[...], preferred_element_type=F32)
+        grad = term if grad is None else grad + term
+    down_grad_t[...] = grad
     cols = up_grad.shape[1] // len(packs)
     for j, pack in enumerate(packs):
         if cols % 128 == 0:
             up_grad[:, pl.ds(pl.multiple_of((r ^ j) * cols, 128), cols)] = pack[pl.ds(0, rank), pl.ds(0, cols)].astype(F32)
 
 
-def adapter_call(packs, x_all, rank, all_cols, tok):
+def adapter_call(packs, first_x, last_x, places, rank, all_cols, tok):
     down_grad_t, up_grad = pl.pallas_call(
-        functools.partial(adapter_kernel, tok),
+        functools.partial(adapter_kernel, tok, places),
         out_shape=[
-            jax.ShapeDtypeStruct((rank, x_all.shape[1]), F32),
+            jax.ShapeDtypeStruct((rank, first_x.shape[1]), F32),
             jax.ShapeDtypeStruct((rank, all_cols), F32),
         ],
-        in_specs=whole_vmem(len(packs) + 1),
+        in_specs=whole_vmem(len(packs) + 2),
         out_specs=whole_vmem(2),
         compiler_params=pltpu.CompilerParams(vmem_limit_bytes=VMEM),
         cost_estimate=SMALL,
         name="adapter_grads",
-    )(*vmem(packs), x_all)
+    )(*vmem(packs), *vmem([first_x, last_x]))
     cols = all_cols // len(packs)
     if cols % 128:
         for j, pack in enumerate(packs):
@@ -426,6 +501,8 @@
     core_weight, core_tokens, core_cot = (to_row(x, 1) for x in (weight, tokens, cot_all))
 
     def mine(x, size):
+        if size % 128 == 0 and x is weight:
+            return hbm([x])[0], size
         return (x, size) if size % 128 == 0 else (lax.dynamic_slice(x, (0, r * size), (x.shape[0], size)), 0)
 
     own_map, own_tokens, own_cot = hbm([timestep_gain_map, tokens, cot_all])
@@ -435,14 +512,13 @@
     )
     arrays = [own_w, core_w, normed, core_normed]
     w_from, x_from = [(0, 0, 0, None), (1, 0, 1, None)], [(2, tok), (3, tok)]
-    rows = tok // 2 if tok % 32 == 0 else tok
-    count = tok // rows
+    rows = (tok * 5 // 8, tok * 3 // 8) if tok % 128 == 0 else (tok,)
     first = [i for i, (_, _, c) in enumerate(fetched) if c == 0]
     later = gate(
-        [normed] + chip_cot + [fetched[i][0] for i in first], [rows] + [tok] * len(chips) + [k_rows] * len(first)
-    )
-    later_normed, chip_cot = later[:count], later[count : count + len(chips)]
-    for i, x in zip(first, later[count + len(chips) :]):
+        [normed] + chip_cot + [fetched[i][0] for i in first], [rows] + [(tok,)] * len(chips) + [(k_rows,)] * len(first)
+    )
+    later_normed, chip_cot = later[: len(rows)], later[len(rows) : len(rows) + len(chips)]
+    for i, x in zip(first, later[len(rows) + len(chips) :]):
         fetched[i] = (x, *fetched[i][1:])
     sharers = []
     for x, j, c in fetched:
@@ -452,27 +528,31 @@
             if other and c == 0:
                 sharers.append(arrays[-1])
 
-    halves = [to_row(x, j) for j in chips for x in later_normed]
-    later = list(gate(halves, [rows] * len(halves), *sharers))
-    for i in range(0, len(halves), count):
-        for x in halves[i : i + count] + [to_row(x, 1) for x in later[i : i + count]]:
-            x_from.append((len(arrays), rows))
-            arrays.append(x)
-
-    cots, c_from = [own_cot, core_cot], [(0, False), (1, False)]
-    for j, x in zip(chips, chip_cot):
-        x = to_row(x, j)
-        c_from += [(len(cots), True), (len(cots) + 1, False)]
-        cots += [x, to_row(other_half(x), 1)]
+    chip_normed = [to_row(x, j) for j in chips for x in later_normed]
+    later = list(gate(chip_normed, [(x.shape[0],) for x in chip_normed], *sharers))
+    for x in chip_normed:
+        x_from.append((len(arrays), x.shape[0]))
+        arrays.append(x)
 
     rank = adapter_up_weight.shape[0]
     down_t = adapter_down_weight.T
     up = adapter_up_weight
     if cols % 128:
         up = lax.dynamic_slice(up, (0, r * cols), (rank, cols))
-    x_all, w_all, qkv_t, low_t = qkv_call(
-        arrays, tuple(x_from), tuple(w_from), down_t, up, n * tok, cols
-    )
+    places, last_places = (0, 1, *chips), tuple(j + 1 for j in chips)
+    first_x, w_all, first_qkv, first_low = qkv_call(
+        arrays, tuple(x_from), tuple(w_from), down_t, up, len(places) * tok, cols
+    )
+    last_x, qkv_t, low_t = last_qkv_call(
+        tok, places, last_places, [to_row(x, 1) for x in later], w_all, first_qkv, first_low, down_t, up
+    )
+
+    cots, c_from = [own_cot, core_cot], [(0, False), (1, False)]
+    for j, x in zip(chips, chip_cot):
+        x = to_row(x, j)
+        c_from += [(len(cots), True), (len(cots) + 1, False)]
+        cots += [x, to_row(other_half(x, first_low), 1)]
+
     *others, grad_t, pack = attention_call(
         head_score_scale, cots, tuple(c_from), qkv_t, low_t, w_all, down_t, up, tok, 2, (F32, BF) * len(chips)
     )
@@ -488,7 +568,9 @@
 
     for j in chips:
         packs[j ^ 1] = to_row(packs[j], 1)
-    down_grad_t, up_grad = adapter_call([packs[j] for j in range(n)], x_all, rank, n * cols, tok)
+    down_grad_t, up_grad = adapter_call(
+        [packs[j] for j in range(n)], first_x, last_x, (places, last_places), rank, n * cols, tok
+    )
 
     input_grad = final_call(tokens, gain, inv_rms, mine, core_part + sums)
     return (input_grad, down_grad_t.T, up_grad)

time: 43.6 us -> 42.3 us (0.970)
  local copies, waits for them, and re-layouts: 2.48 us -> 1.09 us
  waiting for transfers between devices: 12.1 us -> 13.3 us
  Pallas kernels: 12.8 us -> 11.8 us
    unnamed x10 -> x8, local copies, waits for them, and re-layouts: 1.42 us -> 0.02 us
    ppermute x20, waiting for transfers between devices: 12.1 us -> 13.3 us  [send(): return lax.ppermute(x, axes, perm)]
    pallas_call x3 -> x4, Pallas kernels: 0.95 us -> 1.7 us  [the longest x1 0.88 us: adapter_call(): pl.pallas_call(functools.partial(adapter_kernel, tok, places), out_shape=...]
    pallas_call x1, Pallas kernels: 5.68 us -> 4.97 us  [attention_call(): pl.pallas_call(functools.partial(attention_kernel, cols // (3 * HEAD), to...]
    pallas_call x1, Pallas kernels: 1.32 us -> 0.73 us  [own_call(): pl.pallas_call(functools.partial(own_kernel, len(deps)), out_shape=[in_vm...]
where the time goes in v5:
time: 42.3 us; the launch traced here: 42.1 us
  starting transfers between devices  14.3 us (34%)
  waiting for transfers between devices  13.3 us (31%)
  Pallas kernels  11.8 us (28%)
  between operations  1.46 us (3%)
  local copies, waits for them, and re-layouts  1.09 us (3%)
    ppermute x20, starting transfers between devices, send(): return lax.ppermute(x, axes, perm)  14.3 us
    ppermute x20, waiting for transfers between devices, send(): return lax.ppermute(x, axes, perm)  13.3 us
    pallas_call x1, Pallas kernels, attention_call(): pl.pallas_call(functools.partial(attention_kernel, cols // (3 * HEAD), to...  4.97 us
    pallas_call x1, Pallas kernels, prepare_call(): pl.pallas_call(functools.partial(prepare_kernel, chips, head_cols, [size...  1.7 us
    pallas_call x1, Pallas kernels, qkv_call(): pl.pallas_call(functools.partial(qkv_kernel, x_from, w_from), out_shape=[...  1.66 us
    dynamic_slice x1, local copies, waits for them, and re-layouts, per_device(): lax.dynamic_slice(weight, (0, (r ^ j + odd) * cols + c * part_cols), (k_r...  1.06 us
    pallas_call x1, Pallas kernels, final_call(): pl.pallas_call(final_kernel, out_shape=jax.ShapeDtypeStruct(tokens.shape,...  1.02 us
    pallas_call x1, Pallas kernels, adapter_call(): pl.pallas_call(functools.partial(adapter_kernel, tok, places), out_shape=...  0.88 us
  transfers between devices with their start and end apart: 20, of which 9 were waited for; matrix products, arithmetic and copies ran while one was open for 3% of the time, Pallas kernels for 14%

profile of v5, /device:TPU:0, one launch (start us, length us, event | category | flops | bytes accessed | tf_op | source)
XLA Modules:
  0.0 42.1 jit_solution(7716444852193774101)
XLA Ops:
  0.6 0.5 %collective-permute-start.1 = (bf16[256,3072]{1,0:T(8,128)(2,1)}, bf16[256,3072]{1,0:T(8,128)(2,1)S(1)}, u32[]{:S(2)}, u32[]{:S(2)}) collective-permute-start(bf16[256,3072]{1,0:T(8,128)(2,1)} %refs_0_.2), channel_id=1, source_target_pairs={{0,1},{1,0},{2,3},{3,2},{4,5},{5,4},{6,7},{7,6},{8,9},{9,8},{10,11... | collective-permute-start | bytes 4718600 | tf_op jit(solution)/shard_map/ppermute | solution.py:480
  1.1 0.1 collective-permute-start
  1.2 0.4 %collective-permute-start.2 = (bf16[128,1024]{1,0:T(8,128)(2,1)}, bf16[128,1024]{1,0:T(8,128)(2,1)S(1)}, u32[]{:S(2)}, u32[]{:S(2)}) collective-permute-start(bf16[128,1024]{1,0:T(8,128)(2,1)} %refs_2_.1), channel_id=1, source_target_pairs={{0,1},{1,0},{2,3},{3,2},{4,5},{5,4},{6,7},{7,6},{8,9},{9,8},{10,11... | collective-permute-start | bytes 786440 | tf_op jit(solution)/shard_map/ppermute | solution.py:480
  1.7 1.1 %constant_dynamic-slice_fusion = (bf16[256,384]{1,0:T(8,128)(2,1)S(1)}, bf16[256,384]{1,0:T(8,128)(2,1)S(1)}) fusion(bf16[256,3072]{1,0:T(8,128)(2,1)} %refs_0_.2, s32[]{:T(128)S(6)} %select_n.15, s32[]{:T(128)S(6)} %select_n.14), kind=kLoop, calls=%fused_computation.1 | loop fusion | bytes 786440 | tf_op jit(solution)/shard_map/dynamic_slice | solution.py:498
  2.7 2.7 %collective-permute-start.3 = (bf16[256,384]{1,0:T(8,128)(2,1)S(1)}, bf16[256,384]{1,0:T(8,128)(2,1)S(1)}, u32[]{:S(2)}, u32[]{:S(2)}) collective-permute-start(bf16[256,384]{1,0:T(8,128)(2,1)S(1)} %get-tuple-element.66), channel_id=1, source_target_pairs={{0,2},{1,3},{2,0},{3,1},{4,7},{5,6},{6,5},{7,4},{8,10},{9,11},{10,... | collective-permute-start | bytes 589832 | tf_op jit(solution)/shard_map/ppermute | solution.py:480
  6.2 1.7 %prepare.1 = (bf16[128,1024]{1,0:T(8,128)(2,1)S(1)}, bf16[128,1024]{1,0:T(8,128)(2,1)S(1)}, f32[1,1024]{1,0:T(1,128)S(1)}, f32[128,1]{1,0:T(8,128)S(1)}, bf16[25...) custom-call(f32[2,128]{1,0:T(2,128)S(1)} %pad_maximum_fusion.feature, ...), custom_call_target="tpu_custom_call" | custom-call | flops 1 | bytes 1 | tf_op jit(solution)/shard_map/prepare/pallas_call | solution.py:442
  7.9 3.2 %collective-permute-done.3.refs_2_ = bf16[256,384]{1,0:T(8,128)(2,1)S(1)} collective-permute-done((bf16[256,384]{1,0:T(8,128)(2,1)S(1)}, bf16[256,384]{1,0:T(8,128)(2,1)S(1)}, u32[]{:S(2)}, u32[]{:S(2)}) %collective-permute-start.3) | collective-permute-done | bytes 196640 | tf_op jit(solution)/shard_map/ppermute | solution.py:480
  11.2 1.1 %collective-permute-start.5 = (bf16[256,384]{1,0:T(8,128)(2,1)S(1)}, bf16[256,384]{1,0:T(8,128)(2,1)S(1)}, u32[]{:S(2)}, u32[]{:S(2)}) collective-permute-start(bf16[256,384]{1,0:T(8,128)(2,1)S(1)} %get-tuple-element.44.refs_4_), channel_id=1, source_target_pairs={{0,4},{1,5},{2,6},{3,7},{4,0},{5,1},{6,2},{7,3},{8,12},{9,13},{10,... | collective-permute-start | bytes 589832 | tf_op jit(solution)/shard_map/ppermute | solution.py:480
  12.3 1.3 %collective-permute-start.8 = (bf16[80,1024]{1,0:T(8,128)(2,1)S(1)}, bf16[80,1024]{1,0:T(8,128)(2,1)S(1)}, u32[]{:S(2)}, u32[]{:S(2)}) collective-permute-start(bf16[80,1024]{1,0:T(8,128)(2,1)S(1)} %get-tuple-element.45), channel_id=1, source_target_pairs={{0,2},{1,3},{2,0},{3,1},{4,6},{5,7},{6,4},{7,5},{8,10},{9,11},{10,... | collective-permute-start | bytes 491528 | tf_op jit(solution)/shard_map/ppermute | solution.py:480
  13.6 1.5 %collective-permute-done.6.refs_6_ = bf16[256,384]{1,0:T(8,128)(2,1)S(1)} collective-permute-done((bf16[256,384]{1,0:T(8,128)(2,1)S(1)}, bf16[256,384]{1,0:T(8,128)(2,1)S(1)}, u32[]{:S(2)}, u32[]{:S(2)}) %collective-permute-start.6) | collective-permute-done | bytes 196640 | tf_op jit(solution)/shard_map/ppermute | solution.py:480
  15.1 1.3 %collective-permute-start.7 = (bf16[256,384]{1,0:T(8,128)(2,1)S(1)}, bf16[256,384]{1,0:T(8,128)(2,1)S(1)}, u32[]{:S(2)}, u32[]{:S(2)}) collective-permute-start(bf16[256,384]{1,0:T(8,128)(2,1)S(1)} %collective-permute-done.6.refs_6_), channel_id=1, source_target_pairs={{0,4},{1,5},{2,6},{3,7},{4,0},{5,1},{6,2},{7,3},{8,12},{9,13},{10,... | collective-permute-start | bytes 589832 | tf_op jit(solution)/shard_map/ppermute | solution.py:480
  16.4 1.3 %collective-permute-start.9 = (bf16[48,1024]{1,0:T(8,128)(2,1)S(1)}, bf16[48,1024]{1,0:T(8,128)(2,1)S(1)}, u32[]{:S(2)}, u32[]{:S(2)}) collective-permute-start(bf16[48,1024]{1,0:T(8,128)(2,1)S(1)} %get-tuple-element.46), channel_id=1, source_target_pairs={{0,2},{1,3},{2,0},{3,1},{4,6},{5,7},{6,4},{7,5},{8,10},{9,11},{10,... | collective-permute-start | bytes 294920 | tf_op jit(solution)/shard_map/ppermute | solution.py:480
  17.7 0.7 %collective-permute-start.4 = (bf16[128,512]{1,0:T(8,128)(2,1)S(1)}, bf16[128,512]{1,0:T(8,128)(2,1)S(1)}, u32[]{:S(2)}, u32[]{:S(2)}) collective-permute-start(bf16[128,512]{1,0:T(8,128)(2,1)S(1)} %get-tuple-element.40), channel_id=1, source_target_pairs={{0,2},{1,3},{2,0},{3,1},{4,6},{5,7},{6,4},{7,5},{8,10},{9,11},{10,... | collective-permute-start | bytes 393224 | tf_op jit(solution)/shard_map/ppermute | solution.py:480
  18.4 3.6 %collective-permute-done.9.refs_9_.refs_1_ = bf16[48,1024]{1,0:T(8,128)(2,1)S(1)} collective-permute-done((bf16[48,1024]{1,0:T(8,128)(2,1)S(1)}, bf16[48,1024]{1,0:T(8,128)(2,1)S(1)}, u32[]{:S(2)}, u32[]{:S(2)}) %collective-permute-start.9) | collective-permute-done | bytes 98336 | tf_op jit(solution)/shard_map/ppermute | solution.py:480
  22.2 0.5 %collective-permute-start.12 = (bf16[48,1024]{1,0:T(8,128)(2,1)S(1)}, bf16[48,1024]{1,0:T(8,128)(2,1)S(1)}, u32[]{:S(2)}, u32[]{:S(2)}) collective-permute-start(bf16[48,1024]{1,0:T(8,128)(2,1)S(1)} %get-tuple-element.49), channel_id=1, source_target_pairs={{0,1},{1,0},{2,3},{3,2},{4,5},{5,4},{6,7},{7,6},{8,9},{9,8},{10,11... | collective-permute-start | bytes 294920 | tf_op jit(solution)/shard_map/ppermute | solution.py:480
  22.7 1.7 %qkv.1 = (bf16[384,1024]{1,0:T(8,128)(2,1)S(1)}, bf16[1024,768]{1,0:T(8,128)(2,1)S(1)}, bf16[768,384]{1,0:T(8,128)(2,1)S(1)}, bf16[16,384]{1,0:T(8,128)(2,1)S(1)}) custom-call(bf16[256,768]{1,0:T(8,128)(2,1)S(1)} %get-tuple-element.41.refs_0_, bf16[256,768]{1,0:T(8,128)(2,1)S(1)} %get-tuple-element.42.refs_1_, ...), custom_call_target="tpu_custom_call" | custom-call | flops 1 | bytes 1 | tf_op jit(solution)/shard_map/qkv/pallas_call | solution.py:164
  24.3 0.3 collective-permute-done.4.x.refs_3_
  24.7 0.8 %last_qkv.1 = (bf16[128,1024]{1,0:T(8,128)(2,1)S(1)}, bf16[768,512]{1,0:T(8,128)(2,1)S(1)}, bf16[16,512]{1,0:T(8,128)(2,1)S(1)}) custom-call(bf16[80,1024]{1,0:T(8,128)(2,1)S(1)} %collective-permute-done.11.refs_0_, bf16[48,1024]{1,0:T(8,128)(2,1)S(1)} %collective-permute-done.12.refs_1_, bf16[1024,768]{1,0:T(8,128)(2,1)S(1)} %get-tuple-element.50.refs_2_.refs_7_.w_all, ...), custom_call_target="tpu_custom_call" | custom-call | flops 1 | bytes 1 | tf_op jit(solution)/shard_map/last_qkv/pallas_call | solution.py:113
  25.5 0.5 %collective-permute-done.10.refs_4_ = bf16[128,256]{1,0:T(8,128)(2,1)S(1)} collective-permute-done((bf16[128,256]{1,0:T(8,128)(2,1)S(1)}, bf16[128,256]{1,0:T(8,128)(2,1)S(1)}, u32[]{:S(2)}, u32[]{:S(2)}) %collective-permute-start.10) | collective-permute-done | bytes 65568 | tf_op jit(solution)/shard_map/ppermute | solution.py:480
  25.9 5.0 %attention_grads.1 = (f32[128,1024]{1,0:T(8,128)S(1)}, bf16[128,1024]{1,0:T(8,128)(2,1)S(1)}, bf16[768,512]{1,0:T(8,128)(2,1)S(1)}, bf16[32,768]{1,0:T(8,128)(2,1)S(1)}) custom-call(f32[4]{0:T(128)S(1)} %copy-done.3, bf16[128,256]{1,0:T(8,128)(2,1)S(1)} %get-tuple-element.36.refs_1_, bf16[128,256]{1,0:T(8,128)(2,1)S(1)} %get-tuple-element.37.refs_2_, ...), custom_call_target="tpu_custom_call" | custom-call | flops 1 | bytes 1 | tf_op jit(solution)/shard_map/attention_grads/pallas_call | solution.py:258
  30.9 0.2 collective-permute-start.13
  31.1 1.5 %collective-permute-start.14 = (bf16[32,768]{1,0:T(8,128)(2,1)S(1)}, bf16[32,768]{1,0:T(8,128)(2,1)S(1)}, u32[]{:S(2)}, u32[]{:S(2)}) collective-permute-start(bf16[32,768]{1,0:T(8,128)(2,1)S(1)} %get-tuple-element.55.pack.refs_0_), channel_id=1, source_target_pairs={{0,2},{1,3},{2,0},{3,1},{4,6},{5,7},{6,4},{7,5},{8,10},{9,11},{10,... | collective-permute-start | bytes 147464 | tf_op jit(solution)/shard_map/ppermute | solution.py:480
  32.7 1.4 %collective-permute-start.17 = (bf16[128,1024]{1,0:T(8,128)(2,1)S(1)}, bf16[128,1024]{1,0:T(8,128)(2,1)S(1)}, u32[]{:S(2)}, u32[]{:S(2)}) collective-permute-start(bf16[128,1024]{1,0:T(8,128)(2,1)S(1)} %add.25.refs_0_), channel_id=1, source_target_pairs={{0,2},{1,3},{2,0},{3,1},{4,6},{5,7},{6,4},{7,5},{8,10},{9,11},{10,... | collective-permute-start | bytes 786440 | tf_op jit(solution)/shard_map/ppermute | solution.py:480
  34.2 1.1 %collective-permute-done.14.refs_1_.refs_2_ = bf16[32,768]{1,0:T(8,128)(2,1)S(1)} collective-permute-done((bf16[32,768]{1,0:T(8,128)(2,1)S(1)}, bf16[32,768]{1,0:T(8,128)(2,1)S(1)}, u32[]{:S(2)}, u32[]{:S(2)}) %collective-permute-start.14) | collective-permute-done | bytes 49184 | tf_op jit(solution)/shard_map/ppermute | solution.py:480
  35.2 0.7 %own_grads.1 = (f32[128,1024]{1,0:T(8,128)S(1)}, bf16[112,1024]{1,0:T(8,128)(2,1)S(1)}, bf16[16,1024]{1,0:T(8,128)(2,1)S(1)}) custom-call(bf16[768,512]{1,0:T(8,128)(2,1)S(1)} %get-tuple-element.54.grad_t, bf16[32,768]{1,0:T(8,128)(2,1)S(1)} %get-tuple-element.55.pack.refs_0_, bf16[1024,768]{1,0:T(8,128)(2,1)S(1)} %get-tuple-element.50.refs_2_.refs_7_.w_all, ...), custom_call_target="tpu_custom_call" | custom-call | flops 1 | bytes 1 | tf_op jit(solution)/shard_map/own_grads/pallas_call | solution.py:323
  36.1 0.5 %collective-permute-start.18 = (bf16[32,768]{1,0:T(8,128)(2,1)S(1)}, bf16[32,768]{1,0:T(8,128)(2,1)S(1)}, u32[]{:S(2)}, u32[]{:S(2)}) collective-permute-start(bf16[32,768]{1,0:T(8,128)(2,1)S(1)} %get-tuple-element.55.pack.refs_0_), channel_id=1, source_target_pairs={{0,1},{1,0},{2,3},{3,2},{4,5},{5,4},{6,7},{7,6},{8,9},{9,8},{10,11... | collective-permute-start | bytes 147464 | tf_op jit(solution)/shard_map/ppermute | solution.py:480
  36.6 0.4 %collective-permute-start.16 = (bf16[16,1024]{1,0:T(8,128)(2,1)S(1)}, bf16[16,1024]{1,0:T(8,128)(2,1)S(1)}, u32[]{:S(2)}, u32[]{:S(2)}) collective-permute-start(bf16[16,1024]{1,0:T(8,128)(2,1)S(1)} %get-tuple-element.60), channel_id=1, source_target_pairs={{0,1},{1,0},{2,3},{3,2},{4,5},{5,4},{6,7},{7,6},{8,9},{9,8},{10,11... | collective-permute-start | bytes 98312 | tf_op jit(solution)/shard_map/ppermute | solution.py:480
  37.1 0.5 %collective-permute-done.18.refs_1_ = bf16[32,768]{1,0:T(8,128)(2,1)S(1)} collective-permute-done((bf16[32,768]{1,0:T(8,128)(2,1)S(1)}, bf16[32,768]{1,0:T(8,128)(2,1)S(1)}, u32[]{:S(2)}, u32[]{:S(2)}) %collective-permute-start.18) | collective-permute-done | bytes 49184 | tf_op jit(solution)/shard_map/ppermute | solution.py:480
  37.6 0.2 collective-permute-done.19.refs_3_
  37.8 0.9 %adapter_grads.1 = (f32[16,1024]{1,0:T(8,128)}, f32[16,3072]{1,0:T(8,128)}) custom-call(bf16[32,768]{1,0:T(8,128)(2,1)S(1)} %get-tuple-element.55.pack.refs_0_, bf16[32,768]{1,0:T(8,128)(2,1)S(1)} %collective-permute-done.18.refs_1_, bf16[32,768]{1,0:T(8,128)(2,1)S(1)} %collective-permute-done.14.refs_1_.refs_2_, ...), custom_call_target="tpu_custom_call" | custom-call | flops 1 | bytes 1 | tf_op jit(solution)/shard_map/adapter_grads/pallas_call | solution.py:357
  38.7 2.4 %collective-permute-done.17.refs_2_ = bf16[128,1024]{1,0:T(8,128)(2,1)S(1)} collective-permute-done((bf16[128,1024]{1,0:T(8,128)(2,1)S(1)}, bf16[128,1024]{1,0:T(8,128)(2,1)S(1)}, u32[]{:S(2)}, u32[]{:S(2)}) %collective-permute-start.17) | collective-permute-done | bytes 262176 | tf_op jit(solution)/shard_map/ppermute | solution.py:480
  41.1 1.0 %input_grads.1 = bf16[128,1024]{1,0:T(8,128)(2,1)} custom-call(bf16[128,1024]{1,0:T(8,128)(2,1)S(1)} %copy-done, f32[1,1024]{1,0:T(1,128)S(1)} %get-tuple-element.34.gain, f32[128,1]{1,0:T(8,128)S(1)} %get-tuple-element.35.inv_rms, f32[128,1024]{1,0:T(8,128)S(1)} %get-tuple-element.58.mine, bf16[112,1024]{1,0:T(8,128)(2,1)S(1)} %collective-permute-done.15.refs_0_, ...), custom_call_target="tpu_custom_call" | custom-call | flops 1 | bytes 1 | tf_op jit(solution)/shard_map/input_grads/pallas_call | solution.py:393
  (30 shorter events, 0.5 us)
Async XLA Ops:
  0.6 5.6 %collective-permute-start.1 = (bf16[256,3072]{1,0:T(8,128)(2,1)}, bf16[256,3072]{1,0:T(8,128)(2,1)S(1)}, u32[]{:S(2)}, u32[]{:S(2)}) collective-permute-start(bf16[256,3072]{1,0:T(8,128)(2,1)} %refs_0_.2), channel_id=1, source_target_pairs={{0,1},{1,0},{2,3},{3,2},{4,5},{5,4},{6,7},{7,6},{8,9},{9,8},{10,11... | collective-permute-start | bytes 4718600 | tf_op jit(solution)/shard_map/ppermute | solution.py:480
  1.1 5.1 %collective-permute-start = (bf16[128,1024]{1,0:T(8,128)(2,1)}, bf16[128,1024]{1,0:T(8,128)(2,1)S(1)}, u32[]{:S(2)}, u32[]{:S(2)}) collective-permute-start(bf16[128,1024]{1,0:T(8,128)(2,1)} %tokens.3), channel_id=1, source_target_pairs={{0,1},{1,0},{2,3},{3,2},{4,5},{5,4},{6,7},{7,6},{8,9},{9,8},{10,11... | collective-permute-start | bytes 786440 | tf_op jit(solution)/shard_map/ppermute | solution.py:480
  1.2 5.0 %collective-permute-start.2 = (bf16[128,1024]{1,0:T(8,128)(2,1)}, bf16[128,1024]{1,0:T(8,128)(2,1)S(1)}, u32[]{:S(2)}, u32[]{:S(2)}) collective-permute-start(bf16[128,1024]{1,0:T(8,128)(2,1)} %refs_2_.1), channel_id=1, source_target_pairs={{0,1},{1,0},{2,3},{3,2},{4,5},{5,4},{6,7},{7,6},{8,9},{9,8},{10,11... | collective-permute-start | bytes 786440 | tf_op jit(solution)/shard_map/ppermute | solution.py:480
  2.7 8.4 %collective-permute-start.3 = (bf16[256,384]{1,0:T(8,128)(2,1)S(1)}, bf16[256,384]{1,0:T(8,128)(2,1)S(1)}, u32[]{:S(2)}, u32[]{:S(2)}) collective-permute-start(bf16[256,384]{1,0:T(8,128)(2,1)S(1)} %get-tuple-element.66), channel_id=1, source_target_pairs={{0,2},{1,3},{2,0},{3,1},{4,7},{5,6},{6,5},{7,4},{8,10},{9,11},{10,... | collective-permute-start | bytes 589832 | tf_op jit(solution)/shard_map/ppermute | solution.py:480
  5.4 9.7 %collective-permute-start.6 = (bf16[256,384]{1,0:T(8,128)(2,1)S(1)}, bf16[256,384]{1,0:T(8,128)(2,1)S(1)}, u32[]{:S(2)}, u32[]{:S(2)}) collective-permute-start(bf16[256,384]{1,0:T(8,128)(2,1)S(1)} %get-tuple-element.65), channel_id=1, source_target_pairs={{0,2},{1,3},{2,0},{3,1},{4,7},{5,6},{6,5},{7,4},{8,10},{9,11},{10,... | collective-permute-start | bytes 589832 | tf_op jit(solution)/shard_map/ppermute | solution.py:480
  6.2 16.5 %copy-start.1 = (bf16[16,3072]{1,0:T(8,128)(2,1)S(1)}, bf16[16,3072]{1,0:T(8,128)(2,1)}, u32[]{:S(2)}) copy-start(bf16[16,3072]{1,0:T(8,128)(2,1)} %refs_9_.1) | copy-start | bytes 294916
  6.2 16.5 %copy-start.2 = (bf16[1024,16]{0,1:T(8,128)(2,1)S(1)}, bf16[1024,16]{0,1:T(8,128)(2,1)}, u32[]{:S(2)}) copy-start(bf16[1024,16]{0,1:T(8,128)(2,1)} %param.12) | copy-start | bytes 98308
  11.2 10.9 %collective-permute-start.5 = (bf16[256,384]{1,0:T(8,128)(2,1)S(1)}, bf16[256,384]{1,0:T(8,128)(2,1)S(1)}, u32[]{:S(2)}, u32[]{:S(2)}) collective-permute-start(bf16[256,384]{1,0:T(8,128)(2,1)S(1)} %get-tuple-element.44.refs_4_), channel_id=1, source_target_pairs={{0,4},{1,5},{2,6},{3,7},{4,0},{5,1},{6,2},{7,3},{8,12},{9,13},{10,... | collective-permute-start | bytes 589832 | tf_op jit(solution)/shard_map/ppermute | solution.py:480
  12.3 9.8 %collective-permute-start.8 = (bf16[80,1024]{1,0:T(8,128)(2,1)S(1)}, bf16[80,1024]{1,0:T(8,128)(2,1)S(1)}, u32[]{:S(2)}, u32[]{:S(2)}) collective-permute-start(bf16[80,1024]{1,0:T(8,128)(2,1)S(1)} %get-tuple-element.45), channel_id=1, source_target_pairs={{0,2},{1,3},{2,0},{3,1},{4,6},{5,7},{6,4},{7,5},{8,10},{9,11},{10,... | collective-permute-start | bytes 491528 | tf_op jit(solution)/shard_map/ppermute | solution.py:480
  15.1 7.6 %collective-permute-start.7 = (bf16[256,384]{1,0:T(8,128)(2,1)S(1)}, bf16[256,384]{1,0:T(8,128)(2,1)S(1)}, u32[]{:S(2)}, u32[]{:S(2)}) collective-permute-start(bf16[256,384]{1,0:T(8,128)(2,1)S(1)} %collective-permute-done.6.refs_6_), channel_id=1, source_target_pairs={{0,4},{1,5},{2,6},{3,7},{4,0},{5,1},{6,2},{7,3},{8,12},{9,13},{10,... | collective-permute-start | bytes 589832 | tf_op jit(solution)/shard_map/ppermute | solution.py:480
  16.4 5.7 %collective-permute-start.9 = (bf16[48,1024]{1,0:T(8,128)(2,1)S(1)}, bf16[48,1024]{1,0:T(8,128)(2,1)S(1)}, u32[]{:S(2)}, u32[]{:S(2)}) collective-permute-start(bf16[48,1024]{1,0:T(8,128)(2,1)S(1)} %get-tuple-element.46), channel_id=1, source_target_pairs={{0,2},{1,3},{2,0},{3,1},{4,6},{5,7},{6,4},{7,5},{8,10},{9,11},{10,... | collective-permute-start | bytes 294920 | tf_op jit(solution)/shard_map/ppermute | solution.py:480
  17.7 7.0 %collective-permute-start.4 = (bf16[128,512]{1,0:T(8,128)(2,1)S(1)}, bf16[128,512]{1,0:T(8,128)(2,1)S(1)}, u32[]{:S(2)}, u32[]{:S(2)}) collective-permute-start(bf16[128,512]{1,0:T(8,128)(2,1)S(1)} %get-tuple-element.40), channel_id=1, source_target_pairs={{0,2},{1,3},{2,0},{3,1},{4,6},{5,7},{6,4},{7,5},{8,10},{9,11},{10,... | collective-permute-start | bytes 393224 | tf_op jit(solution)/shard_map/ppermute | solution.py:480
  22.1 2.6 %collective-permute-start.11 = (bf16[80,1024]{1,0:T(8,128)(2,1)S(1)}, bf16[80,1024]{1,0:T(8,128)(2,1)S(1)}, u32[]{:S(2)}, u32[]{:S(2)}) collective-permute-start(bf16[80,1024]{1,0:T(8,128)(2,1)S(1)} %get-tuple-element.48), channel_id=1, source_target_pairs={{0,1},{1,0},{2,3},{3,2},{4,5},{5,4},{6,7},{7,6},{8,9},{9,8},{10,11... | collective-permute-start | bytes 491528 | tf_op jit(solution)/shard_map/ppermute | solution.py:480
  22.2 2.5 %collective-permute-start.12 = (bf16[48,1024]{1,0:T(8,128)(2,1)S(1)}, bf16[48,1024]{1,0:T(8,128)(2,1)S(1)}, u32[]{:S(2)}, u32[]{:S(2)}) collective-permute-start(bf16[48,1024]{1,0:T(8,128)(2,1)S(1)} %get-tuple-element.49), channel_id=1, source_target_pairs={{0,1},{1,0},{2,3},{3,2},{4,5},{5,4},{6,7},{7,6},{8,9},{9,8},{10,11... | collective-permute-start | bytes 294920 | tf_op jit(solution)/shard_map/ppermute | solution.py:480
  24.3 1.6 %copy-start.3 = (f32[4]{0:T(128)S(1)}, f32[4]{0:T(128)}, u32[]{:S(2)}) copy-start(f32[4]{0:T(128)} %refs_0_.3) | copy-start | bytes 52
  24.7 1.3 %collective-permute-start.10 = (bf16[128,256]{1,0:T(8,128)(2,1)S(1)}, bf16[128,256]{1,0:T(8,128)(2,1)S(1)}, u32[]{:S(2)}, u32[]{:S(2)}) collective-permute-start(bf16[128,256]{1,0:T(8,128)(2,1)S(1)} %other_half.1), channel_id=1, source_target_pairs={{0,1},{1,0},{2,3},{3,2},{4,5},{5,4},{6,7},{7,6},{8,9},{9,8},{10,11... | collective-permute-start | bytes 196616 | tf_op jit(solution)/shard_map/ppermute | solution.py:480
  30.9 1.7 %collective-permute-start.13 = (bf16[128,1024]{1,0:T(8,128)(2,1)S(1)}, bf16[128,1024]{1,0:T(8,128)(2,1)S(1)}, u32[]{:S(2)}, u32[]{:S(2)}) collective-permute-start(bf16[128,1024]{1,0:T(8,128)(2,1)S(1)} %get-tuple-element.57), channel_id=1, source_target_pairs={{0,1},{1,0},{2,3},{3,2},{4,5},{5,4},{6,7},{7,6},{8,9},{9,8},{10,11... | collective-permute-start | bytes 786440 | tf_op jit(solution)/shard_map/ppermute | solution.py:480
  31.1 4.1 %collective-permute-start.14 = (bf16[32,768]{1,0:T(8,128)(2,1)S(1)}, bf16[32,768]{1,0:T(8,128)(2,1)S(1)}, u32[]{:S(2)}, u32[]{:S(2)}) collective-permute-start(bf16[32,768]{1,0:T(8,128)(2,1)S(1)} %get-tuple-element.55.pack.refs_0_), channel_id=1, source_target_pairs={{0,2},{1,3},{2,0},{3,1},{4,6},{5,7},{6,4},{7,5},{8,10},{9,11},{10,... | collective-permute-start | bytes 147464 | tf_op jit(solution)/shard_map/ppermute | solution.py:480
  32.7 8.3 %collective-permute-start.17 = (bf16[128,1024]{1,0:T(8,128)(2,1)S(1)}, bf16[128,1024]{1,0:T(8,128)(2,1)S(1)}, u32[]{:S(2)}, u32[]{:S(2)}) collective-permute-start(bf16[128,1024]{1,0:T(8,128)(2,1)S(1)} %add.25.refs_0_), channel_id=1, source_target_pairs={{0,2},{1,3},{2,0},{3,1},{4,6},{5,7},{6,4},{7,5},{8,10},{9,11},{10,... | collective-permute-start | bytes 786440 | tf_op jit(solution)/shard_map/ppermute | solution.py:480
  35.2 5.8 %copy-start = (bf16[128,1024]{1,0:T(8,128)(2,1)S(1)}, bf16[128,1024]{1,0:T(8,128)(2,1)}, u32[]{:S(2)}) copy-start(bf16[128,1024]{1,0:T(8,128)(2,1)} %tokens.3) | copy-start | bytes 786436
  36.0 2.7 %collective-permute-start.15 = (bf16[112,1024]{1,0:T(8,128)(2,1)S(1)}, bf16[112,1024]{1,0:T(8,128)(2,1)S(1)}, u32[]{:S(2)}, u32[]{:S(2)}) collective-permute-start(bf16[112,1024]{1,0:T(8,128)(2,1)S(1)} %get-tuple-element.59), channel_id=1, source_target_pairs={{0,1},{1,0},{2,3},{3,2},{4,5},{5,4},{6,7},{7,6},{8,9},{9,8},{10,11... | collective-permute-start | bytes 688136 | tf_op jit(solution)/shard_map/ppermute | solution.py:480
  36.1 1.5 %collective-permute-start.18 = (bf16[32,768]{1,0:T(8,128)(2,1)S(1)}, bf16[32,768]{1,0:T(8,128)(2,1)S(1)}, u32[]{:S(2)}, u32[]{:S(2)}) collective-permute-start(bf16[32,768]{1,0:T(8,128)(2,1)S(1)} %get-tuple-element.55.pack.refs_0_), channel_id=1, source_target_pairs={{0,1},{1,0},{2,3},{3,2},{4,5},{5,4},{6,7},{7,6},{8,9},{9,8},{10,11... | collective-permute-start | bytes 147464 | tf_op jit(solution)/shard_map/ppermute | solution.py:480
  36.6 1.2 %collective-permute-start.19 = (bf16[32,768]{1,0:T(8,128)(2,1)S(1)}, bf16[32,768]{1,0:T(8,128)(2,1)S(1)}, u32[]{:S(2)}, u32[]{:S(2)}) collective-permute-start(bf16[32,768]{1,0:T(8,128)(2,1)S(1)} %collective-permute-done.14.refs_1_.refs_2_), channel_id=1, source_target_pairs={{0,1},{1,0},{2,3},{3,2},{4,5},{5,4},{6,7},{7,6},{8,9},{9,8},{10,11... | collective-permute-start | bytes 147464 | tf_op jit(solution)/shard_map/ppermute | solution.py:480
  36.6 2.0 %collective-permute-start.16 = (bf16[16,1024]{1,0:T(8,128)(2,1)S(1)}, bf16[16,1024]{1,0:T(8,128)(2,1)S(1)}, u32[]{:S(2)}, u32[]{:S(2)}) collective-permute-start(bf16[16,1024]{1,0:T(8,128)(2,1)S(1)} %get-tuple-element.60), channel_id=1, source_target_pairs={{0,1},{1,0},{2,3},{3,2},{4,5},{5,4},{6,7},{7,6},{8,9},{9,8},{10,11... | collective-permute-start | bytes 98312 | tf_op jit(solution)/shard_map/ppermute | solution.py:480

commit v6 on v5

--- a/solution.py
+++ b/solution.py
@@ -126,21 +126,30 @@
 
 
 def gate(xs, blocks, *deps):
+    xs = [x if isinstance(x, list) else [x] for x in xs]
+    flat = [(i, x) for i, parts in enumerate(xs) for x in parts]
     wanted = [(i, sum(sizes[:k]), rows) for i, sizes in enumerate(blocks) for k, rows in enumerate(sizes)]
 
     def kernel(*refs):
-        for (i, at, rows), out in zip(wanted, refs[len(xs) + len(deps) :]):
-            out[...] = refs[i][pl.ds(at, rows), :]
+        outs = refs[len(flat) + len(deps) :]
+        for (i, at, rows), out in zip(wanted, outs):
+            start = 0
+            for (owner, _), x in zip(flat, refs):
+                if owner == i:
+                    low, high = max(at, start), min(at + rows, start + x.shape[0])
+                    if low < high:
+                        out[pl.ds(low - at, high - low), :] = x[pl.ds(low - start, high - low), :]
+                    start += x.shape[0]
 
     return pl.pallas_call(
         kernel,
-        out_shape=[in_vmem((rows, xs[i].shape[1]), xs[i].dtype) for i, _, rows in wanted],
-        in_specs=whole_vmem(len(xs) + len(deps)),
+        out_shape=[in_vmem((rows, xs[i][0].shape[1]), xs[i][0].dtype) for i, _, rows in wanted],
+        in_specs=whole_vmem(len(flat) + len(deps)),
         out_specs=whole_vmem(len(wanted)),
         compiler_params=pltpu.CompilerParams(vmem_limit_bytes=VMEM),
         cost_estimate=SMALL,
         name="gate",
-    )(*vmem(xs), *vmem(deps))
+    )(*vmem([x for _, x in flat]), *vmem(deps))
 
 
 def in_vmem(shape, dtype):
@@ -239,8 +248,8 @@
         grad_t[pl.ds(o + 2 * HEAD, HEAD), :] = gv.astype(BF).T
 
     rank = up.shape[0]
-    pack[pl.ds(0, rank), pl.ds(0, cols)] = (0.5 * contract(low_t[...], grad_t[...], 1, 1)).astype(BF)
-    low_grad_t = pack.at[pl.ds(rank, rank), pl.ds(0, seq)]
+    pack[:, pl.ds(seq, cols)] = (0.5 * contract(low_t[...], grad_t[...], 1, 1)).astype(BF)
+    low_grad_t = pack.at[:, pl.ds(0, seq)]
     low_grad_t[...] = (0.5 * jnp.dot(up, grad_t[...], preferred_element_type=F32)).astype(BF)
     for p in range(0, outs, 4):
         count = min(4, outs - p)
@@ -258,7 +267,7 @@
     return pl.pallas_call(
         functools.partial(attention_kernel, cols // (3 * HEAD), tok, c_from, first, outs),
         out_shape=[in_vmem((tok, width), t) for t in dtypes]
-        + [in_vmem((cols, seq), BF), in_vmem((2 * rank, max(cols, seq)), BF)],
+        + [in_vmem((cols, seq), BF), in_vmem((rank, seq + cols), BF)],
         in_specs=[smem] + whole_vmem(len(cots) + 5),
         out_specs=whole_vmem(outs + 2),
         scratch_shapes=[pltpu.VMEM((cols // 3, seq), BF)],
@@ -307,9 +316,7 @@
 def own_kernel(deps, grad_t, pack, w_all, down_t, *refs):
     mine, rest = refs[deps], refs[deps + 1 :]
     tok = mine.shape[0]
-    rank = down_t.shape[0]
-    low_grad_t = pack.at[pl.ds(rank, rank), :]
-    part = token_grads(low_grad_t, grad_t, w_all, down_t, 0, 2 * tok)
+    part = token_grads(pack, grad_t, w_all, down_t, 0, 2 * tok)
     mine[...] = part[:tok]
     part = part[tok:].astype(BF)
     at = 0
@@ -333,11 +340,10 @@
 
 def adapter_kernel(tok, places, *refs):
     packs, (first_x, last_x, down_grad_t, up_grad) = refs[:-4], refs[-4:]
-    rank = down_grad_t.shape[0]
     r = lax.axis_index("rows")
     total = None
     for j, pack in enumerate(packs):
-        blocks = [pack[pl.ds(rank, rank), pl.ds((q ^ j) * tok, tok)] for q in range(len(packs))]
+        blocks = [pack[:, pl.ds((q ^ j) * tok, tok)] for q in range(len(packs))]
         term = jnp.concatenate(blocks, axis=1).astype(F32)
         total = term if total is None else total + term
     total = total.astype(BF)
@@ -350,7 +356,7 @@
     cols = up_grad.shape[1] // len(packs)
     for j, pack in enumerate(packs):
         if cols % 128 == 0:
-            up_grad[:, pl.ds(pl.multiple_of((r ^ j) * cols, 128), cols)] = pack[pl.ds(0, rank), pl.ds(0, cols)].astype(F32)
+            up_grad[:, pl.ds(pl.multiple_of((r ^ j) * cols, 128), cols)] = pack[:, pl.ds(len(packs) * tok, cols)].astype(F32)
 
 
 def adapter_call(packs, first_x, last_x, places, rank, all_cols, tok):
@@ -369,36 +375,67 @@
     cols = all_cols // len(packs)
     if cols % 128:
         for j, pack in enumerate(packs):
-            up_grad = lax.dynamic_update_slice(up_grad, pack[:rank, :cols].astype(F32), (0, (lax.axis_index("rows") ^ j) * cols))
+            up_grad = lax.dynamic_update_slice(up_grad, pack[:, len(packs) * tok :].astype(F32), (0, (lax.axis_index("rows") ^ j) * cols))
     return down_grad_t, up_grad
 
 
-def final_kernel(tokens, gain, inv_rms, mine, *refs):
-    refs, out = refs[:-1], refs[-1]
-    grad = mine[...]
-    part = []
-    for x in refs:
-        part.append(x[...].astype(F32))
-        if sum(p.shape[0] for p in part) == tokens.shape[0]:
-            grad = grad + jnp.concatenate(part, axis=0)
-            part = []
+def scale_kernel(tokens, gain, inv_rms, mine, *refs):
+    blocks, (total, token_gain, scale, slope) = refs[:-4], refs[-4:]
+    at = 0
+    for block in blocks:
+        rows = pl.ds(at, block.shape[0])
+        total[rows, :] = mine[rows, :] + block[...].astype(F32)
+        at += block.shape[0]
     x = tokens[...].astype(F32)
     inv = inv_rms[...]
-    scaled = grad * gain[...]
-    mean = jnp.mean(scaled * x, -1, keepdims=True)
-    out[...] = (inv * (scaled - x * (inv * inv * mean))).astype(BF)
-
-
-def final_call(tokens, gain, inv_rms, mine, terms):
+    token_gain[...] = x * gain[...]
+    scale[...] = inv * gain[...]
+    slope[...] = x * (inv * inv * inv * (1.0 / x.shape[1]))
+
+
+def scale_call(tokens, gain, inv_rms, mine, blocks):
+    return pl.pallas_call(
+        scale_kernel,
+        out_shape=[in_vmem(tokens.shape, F32)] * 4,
+        in_specs=whole_vmem(4 + len(blocks)),
+        out_specs=whole_vmem(4),
+        compiler_params=pltpu.CompilerParams(vmem_limit_bytes=VMEM),
+        cost_estimate=SMALL,
+        name="scale",
+    )(tokens, gain, inv_rms, mine, *vmem(blocks))
+
+
+def final_kernel(total, token_gain, scale, slope, *refs):
+    terms, (out, made, sems) = refs[:-3], refs[-3:]
+    count = sems.shape[0]
+    rows = made.shape[0] // count
+    copies = []
+    for i in range(count):
+        block = pl.ds(i * rows, rows)
+        grad = total[block, :]
+        for x in terms:
+            grad = grad + x[block, :].astype(F32)
+        moment = jnp.sum(grad * token_gain[block, :], -1, keepdims=True)
+        made[block, :] = (grad * scale[block, :] - slope[block, :] * moment).astype(BF)
+        copies.append(pltpu.make_async_copy(made.at[block], out.at[block], sems.at[i]))
+        copies[-1].start()
+    for c in copies:
+        c.wait()
+
+
+def final_call(held, terms):
+    shape = held[0].shape
+    count = 4 if shape[0] % 64 == 0 else 1
     return pl.pallas_call(
         final_kernel,
-        out_shape=jax.ShapeDtypeStruct(tokens.shape, BF),
+        out_shape=jax.ShapeDtypeStruct(shape, BF),
         in_specs=whole_vmem(4 + len(terms)),
-        out_specs=whole_vmem(1)[0],
+        out_specs=pl.BlockSpec(memory_space=pltpu.HBM),
+        scratch_shapes=[pltpu.VMEM(shape, BF), pltpu.SemaphoreType.DMA((count,))],
         compiler_params=pltpu.CompilerParams(vmem_limit_bytes=VMEM),
         cost_estimate=SMALL,
         name="input_grads",
-    )(tokens, gain, inv_rms, mine, *vmem(terms))
+    )(*vmem(held), *vmem(terms))
 
 
 def prepare_kernel(chips, head_cols, sizes, features, gain_map, tokens, core_tokens, cot, *refs):
@@ -512,7 +549,8 @@
     )
     arrays = [own_w, core_w, normed, core_normed]
     w_from, x_from = [(0, 0, 0, None), (1, 0, 1, None)], [(2, tok), (3, tok)]
-    rows = (tok * 5 // 8, tok * 3 // 8) if tok % 128 == 0 else (tok,)
+    rows = (tok // 2, tok // 2) if tok % 128 == 0 else (tok,)
+    relay_rows = (tok * 5 // 8, tok * 3 // 8) if tok % 128 == 0 else (tok,)
     first = [i for i, (_, _, c) in enumerate(fetched) if c == 0]
     later = gate(
         [normed] + chip_cot + [fetched[i][0] for i in first], [rows] + [(tok,)] * len(chips) + [(k_rows,)] * len(first)
@@ -528,9 +566,9 @@
             if other and c == 0:
                 sharers.append(arrays[-1])
 
-    chip_normed = [to_row(x, j) for j in chips for x in later_normed]
-    later = list(gate(chip_normed, [(x.shape[0],) for x in chip_normed], *sharers))
-    for x in chip_normed:
+    chip_normed = [[to_row(x, j) for x in later_normed] for j in chips]
+    later = list(gate(chip_normed, [relay_rows] * len(chips), *sharers))
+    for x in sum(chip_normed, []):
         x_from.append((len(arrays), x.shape[0]))
         arrays.append(x)
 
@@ -572,7 +610,7 @@
         [packs[j] for j in range(n)], first_x, last_x, (places, last_places), rank, n * cols, tok
     )
 
-    input_grad = final_call(tokens, gain, inv_rms, mine, core_part + sums)
+    input_grad = final_call(scale_call(tokens, gain, inv_rms, mine, core_part), sums)
     return (input_grad, down_grad_t.T, up_grad)
 
 

time: 42.3 us -> 41.8 us (0.988)
  waiting for transfers between devices: 13.3 us -> 12.8 us
    ppermute x20, waiting for transfers between devices: 13.3 us -> 12.8 us  [send(): return lax.ppermute(x, axes, perm)]
    pallas_call x3 -> x4, Pallas kernels: 1.08 us -> 1.09 us  [the longest x1 0.84 us: final_call(): pl.pallas_call(final_kernel, out_shape=jax.ShapeDtypeStruct(shape, BF), i...]
  transfers between devices with their start and end apart: 20 -> 20, of which waited for: 9 -> 10; matrix products, arithmetic and copies ran while one was open for 3% -> 3% of each run, Pallas kernels for 14% -> 15%
where the time goes in v6:
time: 41.8 us; the launch traced here: 41.6 us
  starting transfers between devices  14.4 us (34%)
  waiting for transfers between devices  12.8 us (31%)
  Pallas kernels  11.8 us (28%)
  between operations  1.48 us (4%)
  local copies, waits for them, and re-layouts  1.09 us (3%)
    ppermute x20, starting transfers between devices, send(): return lax.ppermute(x, axes, perm)  14.4 us
    ppermute x20, waiting for transfers between devices, send(): return lax.ppermute(x, axes, perm)  12.8 us
    pallas_call x1, Pallas kernels, attention_call(): pl.pallas_call(functools.partial(attention_kernel, cols // (3 * HEAD), to...  4.96 us
    pallas_call x1, Pallas kernels, prepare_call(): pl.pallas_call(functools.partial(prepare_kernel, chips, head_cols, [size...  1.7 us
    pallas_call x1, Pallas kernels, qkv_call(): pl.pallas_call(functools.partial(qkv_kernel, x_from, w_from), out_shape=[...  1.66 us
    dynamic_slice x1, local copies, waits for them, and re-layouts, per_device(): lax.dynamic_slice(weight, (0, (r ^ j + odd) * cols + c * part_cols), (k_r...  1.06 us
    pallas_call x1, Pallas kernels, adapter_call(): pl.pallas_call(functools.partial(adapter_kernel, tok, places), out_shape=...  0.89 us
  transfers between devices with their start and end apart: 20, of which 10 were waited for; matrix products, arithmetic and copies ran while one was open for 3% of the time, Pallas kernels for 15%

profile of v6, /device:TPU:0, one launch (start us, length us, event | category | flops | bytes accessed | tf_op | source)
XLA Modules:
  0.0 41.6 jit_solution(18327443071077223446)
XLA Ops:
  0.6 0.5 %collective-permute-start.1 = (bf16[256,3072]{1,0:T(8,128)(2,1)}, bf16[256,3072]{1,0:T(8,128)(2,1)S(1)}, u32[]{:S(2)}, u32[]{:S(2)}) collective-permute-start(bf16[256,3072]{1,0:T(8,128)(2,1)} %refs_0_.2), channel_id=1, source_target_pairs={{0,1},{1,0},{2,3},{3,2},{4,5},{5,4},{6,7},{7,6},{8,9},{9,8},{10,11... | collective-permute-start | bytes 4718600 | tf_op jit(solution)/shard_map/ppermute | solution.py:517
  1.2 0.4 %collective-permute-start.2 = (bf16[128,1024]{1,0:T(8,128)(2,1)}, bf16[128,1024]{1,0:T(8,128)(2,1)S(1)}, u32[]{:S(2)}, u32[]{:S(2)}) collective-permute-start(bf16[128,1024]{1,0:T(8,128)(2,1)} %refs_2_.1), channel_id=1, source_target_pairs={{0,1},{1,0},{2,3},{3,2},{4,5},{5,4},{6,7},{7,6},{8,9},{9,8},{10,11... | collective-permute-start | bytes 786440 | tf_op jit(solution)/shard_map/ppermute | solution.py:517
  1.7 1.1 %constant_dynamic-slice_fusion = (bf16[256,384]{1,0:T(8,128)(2,1)S(1)}, bf16[256,384]{1,0:T(8,128)(2,1)S(1)}) fusion(bf16[256,3072]{1,0:T(8,128)(2,1)} %refs_0_.2, s32[]{:T(128)S(6)} %select_n.15, s32[]{:T(128)S(6)} %select_n.14), kind=kLoop, calls=%fused_computation.1 | loop fusion | bytes 786440 | tf_op jit(solution)/shard_map/dynamic_slice | solution.py:535
  2.7 2.7 %collective-permute-start.3 = (bf16[256,384]{1,0:T(8,128)(2,1)S(1)}, bf16[256,384]{1,0:T(8,128)(2,1)S(1)}, u32[]{:S(2)}, u32[]{:S(2)}) collective-permute-start(bf16[256,384]{1,0:T(8,128)(2,1)S(1)} %get-tuple-element.74), channel_id=1, source_target_pairs={{0,2},{1,3},{2,0},{3,1},{4,7},{5,6},{6,5},{7,4},{8,10},{9,11},{10,... | collective-permute-start | bytes 589832 | tf_op jit(solution)/shard_map/ppermute | solution.py:517
  6.2 1.7 %prepare.1 = (bf16[128,1024]{1,0:T(8,128)(2,1)S(1)}, bf16[128,1024]{1,0:T(8,128)(2,1)S(1)}, f32[1,1024]{1,0:T(1,128)S(1)}, f32[128,1]{1,0:T(8,128)S(1)}, bf16[25...) custom-call(f32[2,128]{1,0:T(2,128)S(1)} %pad_maximum_fusion.feature, ...), custom_call_target="tpu_custom_call" | custom-call | flops 1 | bytes 1 | tf_op jit(solution)/shard_map/prepare/pallas_call | solution.py:479
  7.9 3.2 %collective-permute-done.3.refs_2_ = bf16[256,384]{1,0:T(8,128)(2,1)S(1)} collective-permute-done((bf16[256,384]{1,0:T(8,128)(2,1)S(1)}, bf16[256,384]{1,0:T(8,128)(2,1)S(1)}, u32[]{:S(2)}, u32[]{:S(2)}) %collective-permute-start.3) | collective-permute-done | bytes 196640 | tf_op jit(solution)/shard_map/ppermute | solution.py:517
  11.2 1.1 %collective-permute-start.5 = (bf16[256,384]{1,0:T(8,128)(2,1)S(1)}, bf16[256,384]{1,0:T(8,128)(2,1)S(1)}, u32[]{:S(2)}, u32[]{:S(2)}) collective-permute-start(bf16[256,384]{1,0:T(8,128)(2,1)S(1)} %get-tuple-element.48.refs_4_), channel_id=1, source_target_pairs={{0,4},{1,5},{2,6},{3,7},{4,0},{5,1},{6,2},{7,3},{8,12},{9,13},{10,... | collective-permute-start | bytes 589832 | tf_op jit(solution)/shard_map/ppermute | solution.py:517
  12.3 1.3 %collective-permute-start.8 = (bf16[64,1024]{1,0:T(8,128)(2,1)S(1)}, bf16[64,1024]{1,0:T(8,128)(2,1)S(1)}, u32[]{:S(2)}, u32[]{:S(2)}) collective-permute-start(bf16[64,1024]{1,0:T(8,128)(2,1)S(1)} %get-tuple-element.49), channel_id=1, source_target_pairs={{0,2},{1,3},{2,0},{3,1},{4,6},{5,7},{6,4},{7,5},{8,10},{9,11},{10,... | collective-permute-start | bytes 393224 | tf_op jit(solution)/shard_map/ppermute | solution.py:517
  13.6 0.7 %collective-permute-start.9 = (bf16[64,1024]{1,0:T(8,128)(2,1)S(1)}, bf16[64,1024]{1,0:T(8,128)(2,1)S(1)}, u32[]{:S(2)}, u32[]{:S(2)}) collective-permute-start(bf16[64,1024]{1,0:T(8,128)(2,1)S(1)} %get-tuple-element.50), channel_id=1, source_target_pairs={{0,2},{1,3},{2,0},{3,1},{4,6},{5,7},{6,4},{7,5},{8,10},{9,11},{10,... | collective-permute-start | bytes 393224 | tf_op jit(solution)/shard_map/ppermute | solution.py:517
  14.3 0.8 %collective-permute-done.6.refs_6_ = bf16[256,384]{1,0:T(8,128)(2,1)S(1)} collective-permute-done((bf16[256,384]{1,0:T(8,128)(2,1)S(1)}, bf16[256,384]{1,0:T(8,128)(2,1)S(1)}, u32[]{:S(2)}, u32[]{:S(2)}) %collective-permute-start.6) | collective-permute-done | bytes 196640 | tf_op jit(solution)/shard_map/ppermute | solution.py:517
  15.1 1.3 %collective-permute-start.7 = (bf16[256,384]{1,0:T(8,128)(2,1)S(1)}, bf16[256,384]{1,0:T(8,128)(2,1)S(1)}, u32[]{:S(2)}, u32[]{:S(2)}) collective-permute-start(bf16[256,384]{1,0:T(8,128)(2,1)S(1)} %collective-permute-done.6.refs_6_), channel_id=1, source_target_pairs={{0,4},{1,5},{2,6},{3,7},{4,0},{5,1},{6,2},{7,3},{8,12},{9,13},{10,... | collective-permute-start | bytes 589832 | tf_op jit(solution)/shard_map/ppermute | solution.py:517
  16.4 1.3 %collective-permute-start.4 = (bf16[128,512]{1,0:T(8,128)(2,1)S(1)}, bf16[128,512]{1,0:T(8,128)(2,1)S(1)}, u32[]{:S(2)}, u32[]{:S(2)}) collective-permute-start(bf16[128,512]{1,0:T(8,128)(2,1)S(1)} %get-tuple-element.44), channel_id=1, source_target_pairs={{0,2},{1,3},{2,0},{3,1},{4,6},{5,7},{6,4},{7,5},{8,10},{9,11},{10,... | collective-permute-start | bytes 393224 | tf_op jit(solution)/shard_map/ppermute | solution.py:517
  17.7 0.9 %collective-permute-done.8.refs_8_.refs_0_ = bf16[64,1024]{1,0:T(8,128)(2,1)S(1)} collective-permute-done((bf16[64,1024]{1,0:T(8,128)(2,1)S(1)}, bf16[64,1024]{1,0:T(8,128)(2,1)S(1)}, u32[]{:S(2)}, u32[]{:S(2)}) %collective-permute-start.8) | collective-permute-done | bytes 131104 | tf_op jit(solution)/shard_map/ppermute | solution.py:517
  18.6 2.8 %collective-permute-done.9.refs_9_.refs_1_ = bf16[64,1024]{1,0:T(8,128)(2,1)S(1)} collective-permute-done((bf16[64,1024]{1,0:T(8,128)(2,1)S(1)}, bf16[64,1024]{1,0:T(8,128)(2,1)S(1)}, u32[]{:S(2)}, u32[]{:S(2)}) %collective-permute-start.9) | collective-permute-done | bytes 131104 | tf_op jit(solution)/shard_map/ppermute | solution.py:517
  21.6 0.5 %collective-permute-start.12 = (bf16[48,1024]{1,0:T(8,128)(2,1)S(1)}, bf16[48,1024]{1,0:T(8,128)(2,1)S(1)}, u32[]{:S(2)}, u32[]{:S(2)}) collective-permute-start(bf16[48,1024]{1,0:T(8,128)(2,1)S(1)} %get-tuple-element.53), channel_id=1, source_target_pairs={{0,1},{1,0},{2,3},{3,2},{4,5},{5,4},{6,7},{7,6},{8,9},{9,8},{10,11... | collective-permute-start | bytes 294920 | tf_op jit(solution)/shard_map/ppermute | solution.py:517
  22.1 0.6 %collective-permute-done.7.refs_7_ = bf16[256,384]{1,0:T(8,128)(2,1)S(1)} collective-permute-done((bf16[256,384]{1,0:T(8,128)(2,1)S(1)}, bf16[256,384]{1,0:T(8,128)(2,1)S(1)}, u32[]{:S(2)}, u32[]{:S(2)}) %collective-permute-start.7) | collective-permute-done | bytes 196640 | tf_op jit(solution)/shard_map/ppermute | solution.py:517
  22.6 1.7 %qkv.1 = (bf16[384,1024]{1,0:T(8,128)(2,1)S(1)}, bf16[1024,768]{1,0:T(8,128)(2,1)S(1)}, bf16[768,384]{1,0:T(8,128)(2,1)S(1)}, bf16[16,384]{1,0:T(8,128)(2,1)S(1)}) custom-call(bf16[256,768]{1,0:T(8,128)(2,1)S(1)} %get-tuple-element.45.refs_0_, bf16[256,768]{1,0:T(8,128)(2,1)S(1)} %get-tuple-element.46.refs_1_, ...), custom_call_target="tpu_custom_call" | custom-call | flops 1 | bytes 1 | tf_op jit(solution)/shard_map/qkv/pallas_call | solution.py:173
  24.5 0.8 %last_qkv.1 = (bf16[128,1024]{1,0:T(8,128)(2,1)S(1)}, bf16[768,512]{1,0:T(8,128)(2,1)S(1)}, bf16[16,512]{1,0:T(8,128)(2,1)S(1)}) custom-call(bf16[80,1024]{1,0:T(8,128)(2,1)S(1)} %collective-permute-done.11.refs_0_, bf16[48,1024]{1,0:T(8,128)(2,1)S(1)} %collective-permute-done.12.refs_1_, bf16[1024,768]{1,0:T(8,128)(2,1)S(1)} %get-tuple-element.54.refs_2_.refs_7_.w_all, ...), custom_call_target="tpu_custom_call" | custom-call | flops 1 | bytes 1 | tf_op jit(solution)/shard_map/last_qkv/pallas_call | solution.py:113
  25.2 0.5 %collective-permute-done.10.refs_4_ = bf16[128,256]{1,0:T(8,128)(2,1)S(1)} collective-permute-done((bf16[128,256]{1,0:T(8,128)(2,1)S(1)}, bf16[128,256]{1,0:T(8,128)(2,1)S(1)}, u32[]{:S(2)}, u32[]{:S(2)}) %collective-permute-start.10) | collective-permute-done | bytes 65568 | tf_op jit(solution)/shard_map/ppermute | solution.py:517
  25.7 5.0 %attention_grads.1 = (f32[128,1024]{1,0:T(8,128)S(1)}, bf16[128,1024]{1,0:T(8,128)(2,1)S(1)}, bf16[768,512]{1,0:T(8,128)(2,1)S(1)}, bf16[16,1280]{1,0:T(8,128)(2,1)S(1)}) custom-call(f32[4]{0:T(128)S(1)} %copy-done.3, bf16[128,256]{1,0:T(8,128)(2,1)S(1)} %get-tuple-element.40.refs_1_, bf16[128,256]{1,0:T(8,128)(2,1)S(1)} %get-tuple-element.41.refs_2_, ...), custom_call_target="tpu_custom_call" | custom-call | flops 1 | bytes 1 | tf_op jit(solution)/shard_map/attention_grads/pallas_call | solution.py:267
  30.6 0.2 collective-permute-start.13
  30.9 1.5 %collective-permute-start.14 = (bf16[16,1280]{1,0:T(8,128)(2,1)S(1)}, bf16[16,1280]{1,0:T(8,128)(2,1)S(1)}, u32[]{:S(2)}, u32[]{:S(2)}) collective-permute-start(bf16[16,1280]{1,0:T(8,128)(2,1)S(1)} %get-tuple-element.59.pack.refs_0_), channel_id=1, source_target_pairs={{0,2},{1,3},{2,0},{3,1},{4,6},{5,7},{6,4},{7,5},{8,10},{9,11},{10,... | collective-permute-start | bytes 122888 | tf_op jit(solution)/shard_map/ppermute | solution.py:517
  32.4 1.4 %collective-permute-start.17 = (bf16[128,1024]{1,0:T(8,128)(2,1)S(1)}, bf16[128,1024]{1,0:T(8,128)(2,1)S(1)}, u32[]{:S(2)}, u32[]{:S(2)}) collective-permute-start(bf16[128,1024]{1,0:T(8,128)(2,1)S(1)} %add.25.refs_0_), channel_id=1, source_target_pairs={{0,2},{1,3},{2,0},{3,1},{4,6},{5,7},{6,4},{7,5},{8,10},{9,11},{10,... | collective-permute-start | bytes 786440 | tf_op jit(solution)/shard_map/ppermute | solution.py:517
  33.9 1.0 %collective-permute-done.14.refs_1_.refs_2_ = bf16[16,1280]{1,0:T(8,128)(2,1)S(1)} collective-permute-done((bf16[16,1280]{1,0:T(8,128)(2,1)S(1)}, bf16[16,1280]{1,0:T(8,128)(2,1)S(1)}, u32[]{:S(2)}, u32[]{:S(2)}) %collective-permute-start.14) | collective-permute-done | bytes 40992 | tf_op jit(solution)/shard_map/ppermute | solution.py:517
  34.9 0.7 %own_grads.1 = (f32[128,1024]{1,0:T(8,128)S(1)}, bf16[112,1024]{1,0:T(8,128)(2,1)S(1)}, bf16[16,1024]{1,0:T(8,128)(2,1)S(1)}) custom-call(bf16[768,512]{1,0:T(8,128)(2,1)S(1)} %get-tuple-element.58.grad_t, bf16[16,1280]{1,0:T(8,128)(2,1)S(1)} %get-tuple-element.59.pack.refs_0_, bf16[1024,768]{1,0:T(8,128)(2,1)S(1)} %get-tuple-element.54.refs_2_.refs_7_.w_all, ...), custom_call_target="tpu_custom_call" | custom-call | flops 1 | bytes 1 | tf_op jit(solution)/shard_map/own_grads/pallas_call | solution.py:330
  35.7 0.5 %collective-permute-start.18 = (bf16[16,1280]{1,0:T(8,128)(2,1)S(1)}, bf16[16,1280]{1,0:T(8,128)(2,1)S(1)}, u32[]{:S(2)}, u32[]{:S(2)}) collective-permute-start(bf16[16,1280]{1,0:T(8,128)(2,1)S(1)} %get-tuple-element.59.pack.refs_0_), channel_id=1, source_target_pairs={{0,1},{1,0},{2,3},{3,2},{4,5},{5,4},{6,7},{7,6},{8,9},{9,8},{10,11... | collective-permute-start | bytes 122888 | tf_op jit(solution)/shard_map/ppermute | solution.py:517
  36.3 0.4 %collective-permute-start.16 = (bf16[16,1024]{1,0:T(8,128)(2,1)S(1)}, bf16[16,1024]{1,0:T(8,128)(2,1)S(1)}, u32[]{:S(2)}, u32[]{:S(2)}) collective-permute-start(bf16[16,1024]{1,0:T(8,128)(2,1)S(1)} %get-tuple-element.64), channel_id=1, source_target_pairs={{0,1},{1,0},{2,3},{3,2},{4,5},{5,4},{6,7},{7,6},{8,9},{9,8},{10,11... | collective-permute-start | bytes 98312 | tf_op jit(solution)/shard_map/ppermute | solution.py:517
  36.7 0.5 %collective-permute-done.18.refs_1_ = bf16[16,1280]{1,0:T(8,128)(2,1)S(1)} collective-permute-done((bf16[16,1280]{1,0:T(8,128)(2,1)S(1)}, bf16[16,1280]{1,0:T(8,128)(2,1)S(1)}, u32[]{:S(2)}, u32[]{:S(2)}) %collective-permute-start.18) | collective-permute-done | bytes 40992 | tf_op jit(solution)/shard_map/ppermute | solution.py:517
  37.4 0.9 %adapter_grads.1 = (f32[16,1024]{1,0:T(8,128)}, f32[16,3072]{1,0:T(8,128)}) custom-call(bf16[16,1280]{1,0:T(8,128)(2,1)S(1)} %get-tuple-element.59.pack.refs_0_, bf16[16,1280]{1,0:T(8,128)(2,1)S(1)} %collective-permute-done.18.refs_1_, bf16[16,1280]{1,0:T(8,128)(2,1)S(1)} %collective-permute-done.14.refs_1_.refs_2_, ...), custom_call_target="tpu_custom_call" | custom-call | flops 1 | bytes 1 | tf_op jit(solution)/shard_map/adapter_grads/pallas_call | solution.py:363
  38.3 0.2 scale.1
  38.5 2.3 %collective-permute-done.17.refs_0_ = bf16[128,1024]{1,0:T(8,128)(2,1)S(1)} collective-permute-done((bf16[128,1024]{1,0:T(8,128)(2,1)S(1)}, bf16[128,1024]{1,0:T(8,128)(2,1)S(1)}, u32[]{:S(2)}, u32[]{:S(2)}) %collective-permute-start.17) | collective-permute-done | bytes 262176 | tf_op jit(solution)/shard_map/ppermute | solution.py:517
  40.8 0.8 %input_grads.1 = bf16[128,1024]{1,0:T(8,128)(2,1)} custom-call(f32[128,1024]{1,0:T(8,128)S(1)} %get-tuple-element.65.total, f32[128,1024]{1,0:T(8,128)S(1)} %get-tuple-element.66.token_gain, f32[128,1024]{1,0:T(8,128)S(1)} %get-tuple-element.67.scale, f32[128,1024]{1,0:T(8,128)S(1)} %get-tuple-element.68.slope, ...), custom_call_target="tpu_custom_call" | custom-call | flops 1 | bytes 1 | tf_op jit(solution)/shard_map/input_grads/pallas_call | solution.py:429
  (31 shorter events, 0.9 us)
Async XLA Ops:
  0.6 5.6 %collective-permute-start.1 = (bf16[256,3072]{1,0:T(8,128)(2,1)}, bf16[256,3072]{1,0:T(8,128)(2,1)S(1)}, u32[]{:S(2)}, u32[]{:S(2)}) collective-permute-start(bf16[256,3072]{1,0:T(8,128)(2,1)} %refs_0_.2), channel_id=1, source_target_pairs={{0,1},{1,0},{2,3},{3,2},{4,5},{5,4},{6,7},{7,6},{8,9},{9,8},{10,11... | collective-permute-start | bytes 4718600 | tf_op jit(solution)/shard_map/ppermute | solution.py:517
  1.1 5.1 %collective-permute-start = (bf16[128,1024]{1,0:T(8,128)(2,1)}, bf16[128,1024]{1,0:T(8,128)(2,1)S(1)}, u32[]{:S(2)}, u32[]{:S(2)}) collective-permute-start(bf16[128,1024]{1,0:T(8,128)(2,1)} %tokens.3), channel_id=1, source_target_pairs={{0,1},{1,0},{2,3},{3,2},{4,5},{5,4},{6,7},{7,6},{8,9},{9,8},{10,11... | collective-permute-start | bytes 786440 | tf_op jit(solution)/shard_map/ppermute | solution.py:517
  1.2 5.0 %collective-permute-start.2 = (bf16[128,1024]{1,0:T(8,128)(2,1)}, bf16[128,1024]{1,0:T(8,128)(2,1)S(1)}, u32[]{:S(2)}, u32[]{:S(2)}) collective-permute-start(bf16[128,1024]{1,0:T(8,128)(2,1)} %refs_2_.1), channel_id=1, source_target_pairs={{0,1},{1,0},{2,3},{3,2},{4,5},{5,4},{6,7},{7,6},{8,9},{9,8},{10,11... | collective-permute-start | bytes 786440 | tf_op jit(solution)/shard_map/ppermute | solution.py:517
  2.7 8.4 %collective-permute-start.3 = (bf16[256,384]{1,0:T(8,128)(2,1)S(1)}, bf16[256,384]{1,0:T(8,128)(2,1)S(1)}, u32[]{:S(2)}, u32[]{:S(2)}) collective-permute-start(bf16[256,384]{1,0:T(8,128)(2,1)S(1)} %get-tuple-element.74), channel_id=1, source_target_pairs={{0,2},{1,3},{2,0},{3,1},{4,7},{5,6},{6,5},{7,4},{8,10},{9,11},{10,... | collective-permute-start | bytes 589832 | tf_op jit(solution)/shard_map/ppermute | solution.py:517
  5.4 9.7 %collective-permute-start.6 = (bf16[256,384]{1,0:T(8,128)(2,1)S(1)}, bf16[256,384]{1,0:T(8,128)(2,1)S(1)}, u32[]{:S(2)}, u32[]{:S(2)}) collective-permute-start(bf16[256,384]{1,0:T(8,128)(2,1)S(1)} %get-tuple-element.73), channel_id=1, source_target_pairs={{0,2},{1,3},{2,0},{3,1},{4,7},{5,6},{6,5},{7,4},{8,10},{9,11},{10,... | collective-permute-start | bytes 589832 | tf_op jit(solution)/shard_map/ppermute | solution.py:517
  6.2 16.4 %copy-start.1 = (bf16[16,3072]{1,0:T(8,128)(2,1)S(1)}, bf16[16,3072]{1,0:T(8,128)(2,1)}, u32[]{:S(2)}) copy-start(bf16[16,3072]{1,0:T(8,128)(2,1)} %refs_9_.1) | copy-start | bytes 294916
  6.2 16.4 %copy-start.2 = (bf16[1024,16]{0,1:T(8,128)(2,1)S(1)}, bf16[1024,16]{0,1:T(8,128)(2,1)}, u32[]{:S(2)}) copy-start(bf16[1024,16]{0,1:T(8,128)(2,1)} %param.12) | copy-start | bytes 98308
  11.2 10.3 %collective-permute-start.5 = (bf16[256,384]{1,0:T(8,128)(2,1)S(1)}, bf16[256,384]{1,0:T(8,128)(2,1)S(1)}, u32[]{:S(2)}, u32[]{:S(2)}) collective-permute-start(bf16[256,384]{1,0:T(8,128)(2,1)S(1)} %get-tuple-element.48.refs_4_), channel_id=1, source_target_pairs={{0,4},{1,5},{2,6},{3,7},{4,0},{5,1},{6,2},{7,3},{8,12},{9,13},{10,... | collective-permute-start | bytes 589832 | tf_op jit(solution)/shard_map/ppermute | solution.py:517
  12.3 6.4 %collective-permute-start.8 = (bf16[64,1024]{1,0:T(8,128)(2,1)S(1)}, bf16[64,1024]{1,0:T(8,128)(2,1)S(1)}, u32[]{:S(2)}, u32[]{:S(2)}) collective-permute-start(bf16[64,1024]{1,0:T(8,128)(2,1)S(1)} %get-tuple-element.49), channel_id=1, source_target_pairs={{0,2},{1,3},{2,0},{3,1},{4,6},{5,7},{6,4},{7,5},{8,10},{9,11},{10,... | collective-permute-start | bytes 393224 | tf_op jit(solution)/shard_map/ppermute | solution.py:517
  13.6 7.8 %collective-permute-start.9 = (bf16[64,1024]{1,0:T(8,128)(2,1)S(1)}, bf16[64,1024]{1,0:T(8,128)(2,1)S(1)}, u32[]{:S(2)}, u32[]{:S(2)}) collective-permute-start(bf16[64,1024]{1,0:T(8,128)(2,1)S(1)} %get-tuple-element.50), channel_id=1, source_target_pairs={{0,2},{1,3},{2,0},{3,1},{4,6},{5,7},{6,4},{7,5},{8,10},{9,11},{10,... | collective-permute-start | bytes 393224 | tf_op jit(solution)/shard_map/ppermute | solution.py:517
  15.1 7.5 %collective-permute-start.7 = (bf16[256,384]{1,0:T(8,128)(2,1)S(1)}, bf16[256,384]{1,0:T(8,128)(2,1)S(1)}, u32[]{:S(2)}, u32[]{:S(2)}) collective-permute-start(bf16[256,384]{1,0:T(8,128)(2,1)S(1)} %collective-permute-done.6.refs_6_), channel_id=1, source_target_pairs={{0,4},{1,5},{2,6},{3,7},{4,0},{5,1},{6,2},{7,3},{8,12},{9,13},{10,... | collective-permute-start | bytes 589832 | tf_op jit(solution)/shard_map/ppermute | solution.py:517
  16.4 7.9 %collective-permute-start.4 = (bf16[128,512]{1,0:T(8,128)(2,1)S(1)}, bf16[128,512]{1,0:T(8,128)(2,1)S(1)}, u32[]{:S(2)}, u32[]{:S(2)}) collective-permute-start(bf16[128,512]{1,0:T(8,128)(2,1)S(1)} %get-tuple-element.44), channel_id=1, source_target_pairs={{0,2},{1,3},{2,0},{3,1},{4,6},{5,7},{6,4},{7,5},{8,10},{9,11},{10,... | collective-permute-start | bytes 393224 | tf_op jit(solution)/shard_map/ppermute | solution.py:517
  21.5 3.0 %collective-permute-start.11 = (bf16[80,1024]{1,0:T(8,128)(2,1)S(1)}, bf16[80,1024]{1,0:T(8,128)(2,1)S(1)}, u32[]{:S(2)}, u32[]{:S(2)}) collective-permute-start(bf16[80,1024]{1,0:T(8,128)(2,1)S(1)} %get-tuple-element.52), channel_id=1, source_target_pairs={{0,1},{1,0},{2,3},{3,2},{4,5},{5,4},{6,7},{7,6},{8,9},{9,8},{10,11... | collective-permute-start | bytes 491528 | tf_op jit(solution)/shard_map/ppermute | solution.py:517
  21.6 2.9 %collective-permute-start.12 = (bf16[48,1024]{1,0:T(8,128)(2,1)S(1)}, bf16[48,1024]{1,0:T(8,128)(2,1)S(1)}, u32[]{:S(2)}, u32[]{:S(2)}) collective-permute-start(bf16[48,1024]{1,0:T(8,128)(2,1)S(1)} %get-tuple-element.53), channel_id=1, source_target_pairs={{0,1},{1,0},{2,3},{3,2},{4,5},{5,4},{6,7},{7,6},{8,9},{9,8},{10,11... | collective-permute-start | bytes 294920 | tf_op jit(solution)/shard_map/ppermute | solution.py:517
  24.3 1.4 %copy-start.3 = (f32[4]{0:T(128)S(1)}, f32[4]{0:T(128)}, u32[]{:S(2)}) copy-start(f32[4]{0:T(128)} %refs_0_.3) | copy-start | bytes 52
  24.4 1.3 %collective-permute-start.10 = (bf16[128,256]{1,0:T(8,128)(2,1)S(1)}, bf16[128,256]{1,0:T(8,128)(2,1)S(1)}, u32[]{:S(2)}, u32[]{:S(2)}) collective-permute-start(bf16[128,256]{1,0:T(8,128)(2,1)S(1)} %other_half.1), channel_id=1, source_target_pairs={{0,1},{1,0},{2,3},{3,2},{4,5},{5,4},{6,7},{7,6},{8,9},{9,8},{10,11... | collective-permute-start | bytes 196616 | tf_op jit(solution)/shard_map/ppermute | solution.py:517
  30.6 1.7 %collective-permute-start.13 = (bf16[128,1024]{1,0:T(8,128)(2,1)S(1)}, bf16[128,1024]{1,0:T(8,128)(2,1)S(1)}, u32[]{:S(2)}, u32[]{:S(2)}) collective-permute-start(bf16[128,1024]{1,0:T(8,128)(2,1)S(1)} %get-tuple-element.61), channel_id=1, source_target_pairs={{0,1},{1,0},{2,3},{3,2},{4,5},{5,4},{6,7},{7,6},{8,9},{9,8},{10,11... | collective-permute-start | bytes 786440 | tf_op jit(solution)/shard_map/ppermute | solution.py:517
  30.9 4.0 %collective-permute-start.14 = (bf16[16,1280]{1,0:T(8,128)(2,1)S(1)}, bf16[16,1280]{1,0:T(8,128)(2,1)S(1)}, u32[]{:S(2)}, u32[]{:S(2)}) collective-permute-start(bf16[16,1280]{1,0:T(8,128)(2,1)S(1)} %get-tuple-element.59.pack.refs_0_), channel_id=1, source_target_pairs={{0,2},{1,3},{2,0},{3,1},{4,6},{5,7},{6,4},{7,5},{8,10},{9,11},{10,... | collective-permute-start | bytes 122888 | tf_op jit(solution)/shard_map/ppermute | solution.py:517
  32.4 8.3 %collective-permute-start.17 = (bf16[128,1024]{1,0:T(8,128)(2,1)S(1)}, bf16[128,1024]{1,0:T(8,128)(2,1)S(1)}, u32[]{:S(2)}, u32[]{:S(2)}) collective-permute-start(bf16[128,1024]{1,0:T(8,128)(2,1)S(1)} %add.25.refs_0_), channel_id=1, source_target_pairs={{0,2},{1,3},{2,0},{3,1},{4,6},{5,7},{6,4},{7,5},{8,10},{9,11},{10,... | collective-permute-start | bytes 786440 | tf_op jit(solution)/shard_map/ppermute | solution.py:517
  34.9 3.4 %copy-start = (bf16[128,1024]{1,0:T(8,128)(2,1)S(1)}, bf16[128,1024]{1,0:T(8,128)(2,1)}, u32[]{:S(2)}) copy-start(bf16[128,1024]{1,0:T(8,128)(2,1)} %tokens.3) | copy-start | bytes 786436
  35.6 2.7 %collective-permute-start.15 = (bf16[112,1024]{1,0:T(8,128)(2,1)S(1)}, bf16[112,1024]{1,0:T(8,128)(2,1)S(1)}, u32[]{:S(2)}, u32[]{:S(2)}) collective-permute-start(bf16[112,1024]{1,0:T(8,128)(2,1)S(1)} %get-tuple-element.63), channel_id=1, source_target_pairs={{0,1},{1,0},{2,3},{3,2},{4,5},{5,4},{6,7},{7,6},{8,9},{9,8},{10,11... | collective-permute-start | bytes 688136 | tf_op jit(solution)/shard_map/ppermute | solution.py:517
  35.7 1.5 %collective-permute-start.18 = (bf16[16,1280]{1,0:T(8,128)(2,1)S(1)}, bf16[16,1280]{1,0:T(8,128)(2,1)S(1)}, u32[]{:S(2)}, u32[]{:S(2)}) collective-permute-start(bf16[16,1280]{1,0:T(8,128)(2,1)S(1)} %get-tuple-element.59.pack.refs_0_), channel_id=1, source_target_pairs={{0,1},{1,0},{2,3},{3,2},{4,5},{5,4},{6,7},{7,6},{8,9},{9,8},{10,11... | collective-permute-start | bytes 122888 | tf_op jit(solution)/shard_map/ppermute | solution.py:517
  36.2 1.2 %collective-permute-start.19 = (bf16[16,1280]{1,0:T(8,128)(2,1)S(1)}, bf16[16,1280]{1,0:T(8,128)(2,1)S(1)}, u32[]{:S(2)}, u32[]{:S(2)}) collective-permute-start(bf16[16,1280]{1,0:T(8,128)(2,1)S(1)} %collective-permute-done.14.refs_1_.refs_2_), channel_id=1, source_target_pairs={{0,1},{1,0},{2,3},{3,2},{4,5},{5,4},{6,7},{7,6},{8,9},{9,8},{10,11... | collective-permute-start | bytes 122888 | tf_op jit(solution)/shard_map/ppermute | solution.py:517
  36.3 2.0 %collective-permute-start.16 = (bf16[16,1024]{1,0:T(8,128)(2,1)S(1)}, bf16[16,1024]{1,0:T(8,128)(2,1)S(1)}, u32[]{:S(2)}, u32[]{:S(2)}) collective-permute-start(bf16[16,1024]{1,0:T(8,128)(2,1)S(1)} %get-tuple-element.64), channel_id=1, source_target_pairs={{0,1},{1,0},{2,3},{3,2},{4,5},{5,4},{6,7},{7,6},{8,9},{9,8},{10,11... | collective-permute-start | bytes 98312 | tf_op jit(solution)/shard_map/ppermute | solution.py:517

commit v7 on v6

--- a/solution.py
+++ b/solution.py
@@ -46,19 +46,25 @@
         put(s, step, qkv.astype(BF).T, low.T)
 
 
-def qkv_kernel(x_from, w_from, *refs):
+def qkv_kernel(n, x_from, w_from, *refs):
     down_t, up_in = refs[-6:-4]
-    r, odd = lax.axis_index("rows"), lax.rem(lax.axis_index("dp"), 2)
+    r, d = lax.axis_index("rows"), lax.axis_index("dp")
     up = columns(up_in, refs[-2].shape[0])
     x_all, w_all, qkv_t, low_t = refs[-4:]
     at = 0
     for i, rows in x_from:
         x_all[pl.ds(at, rows), :] = refs[i][...]
         at += rows
-    for i, to, j, other in w_from:
+    for i, to, j, group, other, row in w_from:
         rows, cols = refs[i].shape
-        holder = r ^ j if other is None else r ^ (j + (odd ^ other))
-        base = pl.multiple_of(holder * rows, 16)
+        holder, part = r ^ j, 0
+        if group == 2:
+            holder = r ^ (j + (lax.rem(lax.div(d, 2), 2) ^ other))
+        elif group == 4:
+            share = lax.rem(d, 4) ^ other
+            holder, part = r ^ (j + lax.rem(share, 2)), lax.div(share, 2)
+        held_rows = w_all.shape[0] // n
+        base = pl.multiple_of(holder * held_rows + part * (held_rows // 2) + row, 16)
         w_all[pl.ds(base, rows), pl.ds(to, cols)] = refs[i][...]
 
     def put(start, rows, qkv, low):
@@ -68,10 +74,10 @@
     multiply(x_all, w_all, down_t, up, put)
 
 
-def qkv_call(arrays, x_from, w_from, down_t, up, seq, cols):
+def qkv_call(n, arrays, x_from, w_from, down_t, up, seq, cols):
     rank, width = down_t.shape
     return pl.pallas_call(
-        functools.partial(qkv_kernel, x_from, w_from),
+        functools.partial(qkv_kernel, n, x_from, w_from),
         out_shape=[
             in_vmem((seq, width), BF),
             in_vmem((width, cols), BF),
@@ -168,10 +174,10 @@
     return [pl.BlockSpec(memory_space=pltpu.VMEM)] * count
 
 
-def qkv_call(arrays, x_from, w_from, down_t, up, seq, cols):
+def qkv_call(n, arrays, x_from, w_from, down_t, up, seq, cols):
     rank, width = down_t.shape
     return pl.pallas_call(
-        functools.partial(qkv_kernel, x_from, w_from),
+        functools.partial(qkv_kernel, n, x_from, w_from),
         out_shape=[
             in_vmem((seq, width), BF),
             in_vmem((width, cols), BF),
@@ -195,7 +201,7 @@
 def attention_kernel(heads, tok, c_from, first, outs, *refs):
     refs = list(refs)
     scale = refs.pop(0)
-    cots = [refs.pop(0) for _ in c_from]
+    cots = [[refs.pop(0) for _ in range(count)] for count, _ in c_from]
     qkv_t, low_t, w_all, down_t, up_in = (refs.pop(0) for _ in range(5))
     parts = [refs.pop(0) for _ in range(outs)]
     grad_t, pack, cot_t = refs
@@ -205,13 +211,13 @@
     step = math.gcd(512, seq)
     width = cot_t.shape[0]
     start = lax.rem(lax.axis_index("rows"), 2) * width
-    for j, (i, choose) in enumerate(c_from):
+    for j, (blocks, (_, choose)) in enumerate(zip(cots, c_from)):
         if not choose:
-            block = cots[i][...]
+            block = jnp.concatenate([x[...] for x in blocks], axis=0)
         elif width % 128 == 0:
-            block = cots[i][:, pl.ds(pl.multiple_of(start, 128), width)]
+            block = blocks[0][:, pl.ds(pl.multiple_of(start, 128), width)]
         else:
-            block = jnp.where(start == 0, cots[i][:, pl.ds(0, width)], cots[i][:, pl.ds(width, width)])
+            block = jnp.where(start == 0, blocks[0][:, pl.ds(0, width)], blocks[0][:, pl.ds(width, width)])
         cot_t[:, pl.ds(j * tok, tok)] = block.T
 
     for h in range(heads):
@@ -277,21 +283,23 @@
     )(scale, *vmem(cots), qkv_t, low_t, w_all, down_t, up)
 
 
-def other_half(x, dep):
-    rows, cols = x.shape
-    half = cols // 2
+def other_half(x, blocks, dep):
+    half = x.shape[1] // 2
+    starts = [sum(blocks[:i]) for i in range(len(blocks))]
     if half % 128:
-        return lax.dynamic_slice(x, (0, (lax.axis_index("rows") ^ 1) % 2 * half), (rows, half))
-
-    def kernel(x, dep, out):
+        col = (lax.axis_index("rows") ^ 1) % 2 * half
+        return [lax.dynamic_slice(x, (at, col), (rows, half)) for at, rows in zip(starts, blocks)]
+
+    def kernel(x, dep, *outs):
         core = lax.rem(lax.axis_index("rows") ^ 1, 2)
-        out[...] = x[:, pl.ds(pl.multiple_of(core * half, 128), half)]
+        for at, rows, out in zip(starts, blocks, outs):
+            out[...] = x[pl.ds(at, rows), pl.ds(pl.multiple_of(core * half, 128), half)]
 
     return pl.pallas_call(
         kernel,
-        out_shape=in_vmem((rows, half), x.dtype),
+        out_shape=[in_vmem((rows, half), x.dtype) for rows in blocks],
         in_specs=whole_vmem(2),
-        out_specs=whole_vmem(1)[0],
+        out_specs=whole_vmem(len(blocks)),
         compiler_params=pltpu.CompilerParams(vmem_limit_bytes=VMEM),
         cost_estimate=SMALL,
         name="other_half",
@@ -526,14 +534,16 @@
     head_cols = cot_all.shape[1] // n
     chips = list(range(2, n, 2))
 
-    cuts = 2 if cols % 256 == 0 else 1
-    part_cols = cols // cuts
-    odd = d % 2
-    fetched = []
+    pair_cols = cols // 2 if cols % 256 == 0 else cols
+    half = k_rows // 2
+    pair, quad = [], []
     for j in chips:
-        for c in range(cuts):
-            x = lax.dynamic_slice(weight, (0, (r ^ (j + odd)) * cols + c * part_cols), (k_rows, part_cols))
-            fetched.append((send(x, lambda a, b, j=j: (a, b ^ (j + a % 2))), j, c))
+        if pair_cols < cols:
+            start = (d % 4 // 2 * half, (r ^ (j + d % 2)) * cols + pair_cols)
+            x = lax.dynamic_slice(weight, start, (half, cols - pair_cols))
+            quad.append(send(x, lambda a, b, j=j: (a, b ^ (j + a % 2))))
+        x = lax.dynamic_slice(weight, (0, (r ^ (j + d // 2 % 2)) * cols), (k_rows, pair_cols))
+        pair.append(send(x, lambda a, b, j=j: (a, b ^ (j + a // 2 % 2))))
 
     core_weight, core_tokens, core_cot = (to_row(x, 1) for x in (weight, tokens, cot_all))
 
@@ -548,27 +558,30 @@
         [mine(weight, cols), mine(core_weight, cols), mine(cot_all, head_cols), mine(core_cot, head_cols)],
     )
     arrays = [own_w, core_w, normed, core_normed]
-    w_from, x_from = [(0, 0, 0, None), (1, 0, 1, None)], [(2, tok), (3, tok)]
-    rows = (tok // 2, tok // 2) if tok % 128 == 0 else (tok,)
+    w_from, x_from = [(0, 0, 0, 1, 0, 0), (1, 0, 1, 1, 0, 0)], [(2, tok), (3, tok)]
+    def exchange(x, other):
+        return send(x, lambda a, b: (a ^ other, b))
+
+    early = []
+    for j, x in zip(chips, quad):
+        held = [x, exchange(x, 1), exchange(x, 2)]
+        for other, x in enumerate(held):
+            w_from.append((len(arrays), pair_cols, j, 4, other, 0))
+            arrays.append(x)
+        early.append(held[1])
+        cut = (half * 7 // 8, half // 8)
+        for at, x in zip((0, cut[0]), gate([held[2]], [cut])):
+            early.append(exchange(x, 1))
+            w_from.append((len(arrays), pair_cols, j, 4, 3, at))
+            arrays.append(early[-1])
+    for j, x in zip(chips, pair):
+        w_from += [(len(arrays), 0, j, 2, 0, 0), (len(arrays) + 1, 0, j, 2, 1, 0)]
+        arrays += [x, exchange(x, 2)]
+
     relay_rows = (tok * 5 // 8, tok * 3 // 8) if tok % 128 == 0 else (tok,)
-    first = [i for i, (_, _, c) in enumerate(fetched) if c == 0]
-    later = gate(
-        [normed] + chip_cot + [fetched[i][0] for i in first], [rows] + [(tok,)] * len(chips) + [(k_rows,)] * len(first)
-    )
-    later_normed, chip_cot = later[: len(rows)], later[len(rows) : len(rows) + len(chips)]
-    for i, x in zip(first, later[len(rows) + len(chips) :]):
-        fetched[i] = (x, *fetched[i][1:])
-    sharers = []
-    for x, j, c in fetched:
-        for other in range(2):
-            w_from.append((len(arrays), c * part_cols, j, other))
-            arrays.append(send(x, lambda a, b: (a ^ 1, b)) if other else x)
-            if other and c == 0:
-                sharers.append(arrays[-1])
-
-    chip_normed = [[to_row(x, j) for x in later_normed] for j in chips]
-    later = list(gate(chip_normed, [relay_rows] * len(chips), *sharers))
-    for x in sum(chip_normed, []):
+    chip_normed = [to_row(normed, j) for j in chips]
+    later = list(gate(chip_normed, [relay_rows] * len(chips), *early))
+    for x in chip_normed:
         x_from.append((len(arrays), x.shape[0]))
         arrays.append(x)
 
@@ -579,17 +592,18 @@
         up = lax.dynamic_slice(up, (0, r * cols), (rank, cols))
     places, last_places = (0, 1, *chips), tuple(j + 1 for j in chips)
     first_x, w_all, first_qkv, first_low = qkv_call(
-        arrays, tuple(x_from), tuple(w_from), down_t, up, len(places) * tok, cols
+        n, arrays, tuple(x_from), tuple(w_from), down_t, up, len(places) * tok, cols
     )
     last_x, qkv_t, low_t = last_qkv_call(
         tok, places, last_places, [to_row(x, 1) for x in later], w_all, first_qkv, first_low, down_t, up
     )
 
-    cots, c_from = [own_cot, core_cot], [(0, False), (1, False)]
+    cots, c_from = [own_cot, core_cot], [(1, False), (1, False)]
+    blocks = (tok * 7 // 8, tok // 8) if tok % 128 == 0 else (tok,)
     for j, x in zip(chips, chip_cot):
         x = to_row(x, j)
-        c_from += [(len(cots), True), (len(cots) + 1, False)]
-        cots += [x, to_row(other_half(x, first_low), 1)]
+        c_from += [(1, True), (len(blocks), False)]
+        cots += [x] + [to_row(y, 1) for y in other_half(x, blocks, first_low)]
 
     *others, grad_t, pack = attention_call(
         head_score_scale, cots, tuple(c_from), qkv_t, low_t, w_all, down_t, up, tok, 2, (F32, BF) * len(chips)

time: 41.8 us -> 41.3 us (0.988)
  waiting for transfers between devices: 12.8 us -> 8.39 us
  starting transfers between devices: 14.4 us -> 17.5 us
  local copies, waits for them, and re-layouts: 1.09 us -> 1.87 us
    ppermute x20 -> x23, waiting for transfers between devices: 12.8 us -> 8.39 us  [send(): return lax.ppermute(x, axes, perm)]
    ppermute x20 -> x23, starting transfers between devices: 14.4 us -> 17.5 us  [send(): return lax.ppermute(x, axes, perm)]
    dynamic_slice x1 -> x2, local copies, waits for them, and re-layouts: 1.06 us -> 1.85 us  [the longest x1 0.95 us: per_device(): lax.dynamic_slice(weight, (0, (r ^ j + d // 2 % 2) * cols), (k_rows, pair...]
  transfers between devices with their start and end apart: 20 -> 23, of which waited for: 10 -> 8; matrix products, arithmetic and copies ran while one was open for 3% -> 5% of each run, Pallas kernels for 15% -> 15%
where the time goes in v7:
time: 41.3 us; the launch traced here: 41.1 us
  starting transfers between devices  17.5 us (42%)
  Pallas kernels  11.8 us (29%)
  waiting for transfers between devices  8.39 us (20%)
  local copies, waits for them, and re-layouts  1.87 us (5%)
  between operations  1.46 us (4%)
    ppermute x23, starting transfers between devices, send(): return lax.ppermute(x, axes, perm)  17.5 us
    ppermute x23, waiting for transfers between devices, send(): return lax.ppermute(x, axes, perm)  8.39 us
    pallas_call x1, Pallas kernels, attention_call(): pl.pallas_call(functools.partial(attention_kernel, cols // (3 * HEAD), to...  4.96 us
    pallas_call x1, Pallas kernels, prepare_call(): pl.pallas_call(functools.partial(prepare_kernel, chips, head_cols, [size...  1.7 us
    pallas_call x1, Pallas kernels, qkv_call(): pl.pallas_call(functools.partial(qkv_kernel, n, x_from, w_from), out_shap...  1.67 us
    dynamic_slice x1, local copies, waits for them, and re-layouts, per_device(): lax.dynamic_slice(weight, (0, (r ^ j + d // 2 % 2) * cols), (k_rows, pair...  0.95 us
    dynamic_slice x1, local copies, waits for them, and re-layouts, per_device(): x = lax.dynamic_slice(weight, start, (half, cols - pair_cols))  0.9 us
    pallas_call x1, Pallas kernels, adapter_call(): pl.pallas_call(functools.partial(adapter_kernel, tok, places), out_shape=...  0.89 us
  transfers between devices with their start and end apart: 23, of which 8 were waited for; matrix products, arithmetic and copies ran while one was open for 5% of the time, Pallas kernels for 15%

profile of v7, /device:TPU:0, one launch (start us, length us, event | category | flops | bytes accessed | tf_op | source)
XLA Modules:
  0.0 41.1 jit_solution(9852104800625248570)
XLA Ops:
  0.6 0.5 %collective-permute-start.1 = (bf16[256,3072]{1,0:T(8,128)(2,1)}, bf16[256,3072]{1,0:T(8,128)(2,1)S(1)}, u32[]{:S(2)}, u32[]{:S(2)}) collective-permute-start(bf16[256,3072]{1,0:T(8,128)(2,1)} %refs_0_.2), channel_id=1, source_target_pairs={{0,1},{1,0},{2,3},{3,2},{4,5},{5,4},{6,7},{7,6},{8,9},{9,8},{10,11... | collective-permute-start | bytes 4718600 | tf_op jit(solution)/shard_map/ppermute | solution.py:525
  1.2 0.4 %collective-permute-start.2 = (bf16[128,1024]{1,0:T(8,128)(2,1)}, bf16[128,1024]{1,0:T(8,128)(2,1)S(1)}, u32[]{:S(2)}, u32[]{:S(2)}) collective-permute-start(bf16[128,1024]{1,0:T(8,128)(2,1)} %refs_2_.1), channel_id=1, source_target_pairs={{0,1},{1,0},{2,3},{3,2},{4,5},{5,4},{6,7},{7,6},{8,9},{9,8},{10,11... | collective-permute-start | bytes 786440 | tf_op jit(solution)/shard_map/ppermute | solution.py:525
  1.7 0.9 %dynamic_slice.6 = bf16[128,384]{1,0:T(8,128)(2,1)S(1)} dynamic-slice(bf16[256,3072]{1,0:T(8,128)(2,1)} %refs_0_.2, s32[]{:T(128)S(6)} %select_n.33, s32[]{:T(128)S(6)} %select_n.35), dynamic_slice_sizes={128,384} | dynamic-slice | bytes 196612 | tf_op jit(solution)/shard_map/dynamic_slice | solution.py:543
  2.6 2.7 %collective-permute-start.4 = (bf16[128,384]{1,0:T(8,128)(2,1)S(1)}, bf16[128,384]{1,0:T(8,128)(2,1)S(1)}, u32[]{:S(2)}, u32[]{:S(2)}) collective-permute-start(bf16[128,384]{1,0:T(8,128)(2,1)S(1)} %dynamic_slice.6), channel_id=1, source_target_pairs={{0,2},{1,3},{2,0},{3,1},{4,7},{5,6},{6,5},{7,4},{8,10},{9,11},{10,... | collective-permute-start | bytes 294920 | tf_op jit(solution)/shard_map/ppermute | solution.py:525
  5.2 0.9 %constant_dynamic-slice_fusion = bf16[256,384]{1,0:T(8,128)(2,1)S(1)} fusion(bf16[256,3072]{1,0:T(8,128)(2,1)} %refs_0_.2, s32[]{:T(128)S(6)} %select_n.38), kind=kLoop, calls=%fused_computation.2 | loop fusion | bytes 393220 | tf_op jit(solution)/shard_map/dynamic_slice | solution.py:545
  7.1 1.7 %prepare.1 = (bf16[128,1024]{1,0:T(8,128)(2,1)S(1)}, bf16[128,1024]{1,0:T(8,128)(2,1)S(1)}, f32[1,1024]{1,0:T(1,128)S(1)}, f32[128,1]{1,0:T(8,128)S(1)}, bf16[25...) custom-call(f32[2,128]{1,0:T(2,128)S(1)} %pad_maximum_fusion.feature, ...), custom_call_target="tpu_custom_call" | custom-call | flops 1 | bytes 1 | tf_op jit(solution)/shard_map/prepare/pallas_call | solution.py:487
  8.8 2.0 %collective-permute-start.11 = (bf16[128,1024]{1,0:T(8,128)(2,1)S(1)}, bf16[128,1024]{1,0:T(8,128)(2,1)S(1)}, u32[]{:S(2)}, u32[]{:S(2)}) collective-permute-start(bf16[128,1024]{1,0:T(8,128)(2,1)S(1)} %get-tuple-element.45.refs_2_), channel_id=1, source_target_pairs={{0,2},{1,3},{2,0},{3,1},{4,6},{5,7},{6,4},{7,5},{8,10},{9,11},{10,... | collective-permute-start | bytes 786440 | tf_op jit(solution)/shard_map/ppermute | solution.py:525
  10.8 1.3 %collective-permute-start.6 = (bf16[128,384]{1,0:T(8,128)(2,1)S(1)}, bf16[128,384]{1,0:T(8,128)(2,1)S(1)}, u32[]{:S(2)}, u32[]{:S(2)}) collective-permute-start(bf16[128,384]{1,0:T(8,128)(2,1)S(1)} %collective-permute-done.4.refs_4_), channel_id=1, source_target_pairs={{0,8},{1,9},{2,10},{3,11},{4,12},{5,13},{6,14},{7,15},{8,0},{9,1},... | collective-permute-start | bytes 294920 | tf_op jit(solution)/shard_map/ppermute | solution.py:525
  12.2 1.4 %collective-permute-start.5 = (bf16[128,384]{1,0:T(8,128)(2,1)S(1)}, bf16[128,384]{1,0:T(8,128)(2,1)S(1)}, u32[]{:S(2)}, u32[]{:S(2)}) collective-permute-start(bf16[128,384]{1,0:T(8,128)(2,1)S(1)} %collective-permute-done.4.refs_4_), channel_id=1, source_target_pairs={{0,4},{1,5},{2,6},{3,7},{4,0},{5,1},{6,2},{7,3},{8,12},{9,13},{10,... | collective-permute-start | bytes 294920 | tf_op jit(solution)/shard_map/ppermute | solution.py:525
  13.6 0.4 collective-permute-done.9.refs_9_
  14.0 0.7 %collective-permute-start.10 = (bf16[256,384]{1,0:T(8,128)(2,1)S(1)}, bf16[256,384]{1,0:T(8,128)(2,1)S(1)}, u32[]{:S(2)}, u32[]{:S(2)}) collective-permute-start(bf16[256,384]{1,0:T(8,128)(2,1)S(1)} %collective-permute-done.9.refs_9_), channel_id=1, source_target_pairs={{0,8},{1,9},{2,10},{3,11},{4,12},{5,13},{6,14},{7,15},{8,0},{9,1},... | collective-permute-start | bytes 589832 | tf_op jit(solution)/shard_map/ppermute | solution.py:525
  14.7 0.8 %collective-permute-done.6.refs_0_.refs_6_ = bf16[128,384]{1,0:T(8,128)(2,1)S(1)} collective-permute-done((bf16[128,384]{1,0:T(8,128)(2,1)S(1)}, bf16[128,384]{1,0:T(8,128)(2,1)S(1)}, u32[]{:S(2)}, u32[]{:S(2)}) %collective-permute-start.6) | collective-permute-done | bytes 98336 | tf_op jit(solution)/shard_map/ppermute | solution.py:525
  15.5 1.6 %collective-permute-start.7 = (bf16[112,384]{1,0:T(8,128)(2,1)S(1)}, bf16[112,384]{1,0:T(8,128)(2,1)S(1)}, u32[]{:S(2)}, u32[]{:S(2)}) collective-permute-start(bf16[112,384]{1,0:T(8,128)(2,1)S(1)} %get-tuple-element.47), channel_id=1, source_target_pairs={{0,4},{1,5},{2,6},{3,7},{4,0},{5,1},{6,2},{7,3},{8,12},{9,13},{10,... | collective-permute-start | bytes 258056 | tf_op jit(solution)/shard_map/ppermute | solution.py:525
  17.1 0.5 %collective-permute-start.3 = (bf16[128,512]{1,0:T(8,128)(2,1)S(1)}, bf16[128,512]{1,0:T(8,128)(2,1)S(1)}, u32[]{:S(2)}, u32[]{:S(2)}) collective-permute-start(bf16[128,512]{1,0:T(8,128)(2,1)S(1)} %get-tuple-element.42), channel_id=1, source_target_pairs={{0,2},{1,3},{2,0},{3,1},{4,6},{5,7},{6,4},{7,5},{8,10},{9,11},{10,... | collective-permute-start | bytes 393224 | tf_op jit(solution)/shard_map/ppermute | solution.py:525
  17.6 0.7 %collective-permute-start.8 = (bf16[16,384]{1,0:T(8,128)(2,1)S(1)}, bf16[16,384]{1,0:T(8,128)(2,1)S(1)}, u32[]{:S(2)}, u32[]{:S(2)}) collective-permute-start(bf16[16,384]{1,0:T(8,128)(2,1)S(1)} %get-tuple-element.48), channel_id=1, source_target_pairs={{0,4},{1,5},{2,6},{3,7},{4,0},{5,1},{6,2},{7,3},{8,12},{9,13},{10,... | collective-permute-start | bytes 36872 | tf_op jit(solution)/shard_map/ppermute | solution.py:525
  18.2 3.0 %collective-permute-done.8.refs_8_.refs_3_ = bf16[16,384]{1,0:T(8,128)(2,1)S(1)} collective-permute-done((bf16[16,384]{1,0:T(8,128)(2,1)S(1)}, bf16[16,384]{1,0:T(8,128)(2,1)S(1)}, u32[]{:S(2)}, u32[]{:S(2)}) %collective-permute-start.8) | collective-permute-done | bytes 12320 | tf_op jit(solution)/shard_map/ppermute | solution.py:525
  21.4 0.5 %collective-permute-start.15 = (bf16[48,1024]{1,0:T(8,128)(2,1)S(1)}, bf16[48,1024]{1,0:T(8,128)(2,1)S(1)}, u32[]{:S(2)}, u32[]{:S(2)}) collective-permute-start(bf16[48,1024]{1,0:T(8,128)(2,1)S(1)} %get-tuple-element.53), channel_id=1, source_target_pairs={{0,1},{1,0},{2,3},{3,2},{4,5},{5,4},{6,7},{7,6},{8,9},{9,8},{10,11... | collective-permute-start | bytes 294920 | tf_op jit(solution)/shard_map/ppermute | solution.py:525
  21.9 1.7 %qkv.1 = (bf16[384,1024]{1,0:T(8,128)(2,1)S(1)}, bf16[1024,768]{1,0:T(8,128)(2,1)S(1)}, bf16[768,384]{1,0:T(8,128)(2,1)S(1)}, bf16[16,384]{1,0:T(8,128)(2,1)S(1)}) custom-call(bf16[256,768]{1,0:T(8,128)(2,1)S(1)} %get-tuple-element.43.refs_0_, bf16[256,768]{1,0:T(8,128)(2,1)S(1)} %get-tuple-element.44.refs_1_, ...), custom_call_target="tpu_custom_call" | custom-call | flops 1 | bytes 1 | tf_op jit(solution)/shard_map/qkv/pallas_call | solution.py:179
  23.7 0.4 %collective-permute-start.13 = (bf16[16,256]{1,0:T(8,128)(2,1)S(1)}, bf16[16,256]{1,0:T(8,128)(2,1)S(1)}, u32[]{:S(2)}, u32[]{:S(2)}) collective-permute-start(bf16[16,256]{1,0:T(8,128)(2,1)S(1)} %get-tuple-element.51), channel_id=1, source_target_pairs={{0,1},{1,0},{2,3},{3,2},{4,5},{5,4},{6,7},{7,6},{8,9},{9,8},{10,11... | collective-permute-start | bytes 24584 | tf_op jit(solution)/shard_map/ppermute | solution.py:525
  24.2 0.8 %last_qkv.1 = (bf16[128,1024]{1,0:T(8,128)(2,1)S(1)}, bf16[768,512]{1,0:T(8,128)(2,1)S(1)}, bf16[16,512]{1,0:T(8,128)(2,1)S(1)}) custom-call(bf16[80,1024]{1,0:T(8,128)(2,1)S(1)} %collective-permute-done.14.refs_0_, bf16[48,1024]{1,0:T(8,128)(2,1)S(1)} %collective-permute-done.15.refs_1_, bf16[1024,768]{1,0:T(8,128)(2,1)S(1)} %get-tuple-element.54.refs_2_.refs_8_.w_all, ...), custom_call_target="tpu_custom_call" | custom-call | flops 1 | bytes 1 | tf_op jit(solution)/shard_map/last_qkv/pallas_call | solution.py:119
  25.0 5.0 %attention_grads.1 = (f32[128,1024]{1,0:T(8,128)S(1)}, bf16[128,1024]{1,0:T(8,128)(2,1)S(1)}, bf16[768,512]{1,0:T(8,128)(2,1)S(1)}, bf16[16,1280]{1,0:T(8,128)(2,1)S(1)}) custom-call(f32[4]{0:T(128)S(1)} %copy-done.3, bf16[128,256]{1,0:T(8,128)(2,1)S(1)} %get-tuple-element.40.refs_1_, bf16[128,256]{1,0:T(8,128)(2,1)S(1)} %get-tuple-element.41.refs_2_, ...), custom_call_target="tpu_custom_call" | custom-call | flops 1 | bytes 1 | tf_op jit(solution)/shard_map/attention_grads/pallas_call | solution.py:273
  30.0 0.4 %collective-permute-start.16 = (bf16[128,1024]{1,0:T(8,128)(2,1)S(1)}, bf16[128,1024]{1,0:T(8,128)(2,1)S(1)}, u32[]{:S(2)}, u32[]{:S(2)}) collective-permute-start(bf16[128,1024]{1,0:T(8,128)(2,1)S(1)} %get-tuple-element.61), channel_id=1, source_target_pairs={{0,1},{1,0},{2,3},{3,2},{4,5},{5,4},{6,7},{7,6},{8,9},{9,8},{10,11... | collective-permute-start | bytes 786440 | tf_op jit(solution)/shard_map/ppermute | solution.py:525
  30.4 1.5 %collective-permute-start.17 = (bf16[16,1280]{1,0:T(8,128)(2,1)S(1)}, bf16[16,1280]{1,0:T(8,128)(2,1)S(1)}, u32[]{:S(2)}, u32[]{:S(2)}) collective-permute-start(bf16[16,1280]{1,0:T(8,128)(2,1)S(1)} %get-tuple-element.59.pack.refs_0_), channel_id=1, source_target_pairs={{0,2},{1,3},{2,0},{3,1},{4,6},{5,7},{6,4},{7,5},{8,10},{9,11},{10,... | collective-permute-start | bytes 122888 | tf_op jit(solution)/shard_map/ppermute | solution.py:525
  32.0 1.3 %collective-permute-start.20 = (bf16[128,1024]{1,0:T(8,128)(2,1)S(1)}, bf16[128,1024]{1,0:T(8,128)(2,1)S(1)}, u32[]{:S(2)}, u32[]{:S(2)}) collective-permute-start(bf16[128,1024]{1,0:T(8,128)(2,1)S(1)} %add.42.refs_0_), channel_id=1, source_target_pairs={{0,2},{1,3},{2,0},{3,1},{4,6},{5,7},{6,4},{7,5},{8,10},{9,11},{10,... | collective-permute-start | bytes 786440 | tf_op jit(solution)/shard_map/ppermute | solution.py:525
  33.2 1.2 %collective-permute-done.17.refs_1_.refs_2_ = bf16[16,1280]{1,0:T(8,128)(2,1)S(1)} collective-permute-done((bf16[16,1280]{1,0:T(8,128)(2,1)S(1)}, bf16[16,1280]{1,0:T(8,128)(2,1)S(1)}, u32[]{:S(2)}, u32[]{:S(2)}) %collective-permute-start.17) | collective-permute-done | bytes 40992 | tf_op jit(solution)/shard_map/ppermute | solution.py:525
  34.4 0.7 %own_grads.1 = (f32[128,1024]{1,0:T(8,128)S(1)}, bf16[112,1024]{1,0:T(8,128)(2,1)S(1)}, bf16[16,1024]{1,0:T(8,128)(2,1)S(1)}) custom-call(bf16[768,512]{1,0:T(8,128)(2,1)S(1)} %get-tuple-element.58.grad_t, bf16[16,1280]{1,0:T(8,128)(2,1)S(1)} %get-tuple-element.59.pack.refs_0_, bf16[1024,768]{1,0:T(8,128)(2,1)S(1)} %get-tuple-element.54.refs_2_.refs_8_.w_all, ...), custom_call_target="tpu_custom_call" | custom-call | flops 1 | bytes 1 | tf_op jit(solution)/shard_map/own_grads/pallas_call | solution.py:338
  35.2 0.5 %collective-permute-start.21 = (bf16[16,1280]{1,0:T(8,128)(2,1)S(1)}, bf16[16,1280]{1,0:T(8,128)(2,1)S(1)}, u32[]{:S(2)}, u32[]{:S(2)}) collective-permute-start(bf16[16,1280]{1,0:T(8,128)(2,1)S(1)} %get-tuple-element.59.pack.refs_0_), channel_id=1, source_target_pairs={{0,1},{1,0},{2,3},{3,2},{4,5},{5,4},{6,7},{7,6},{8,9},{9,8},{10,11... | collective-permute-start | bytes 122888 | tf_op jit(solution)/shard_map/ppermute | solution.py:525
  35.8 0.4 %collective-permute-start.19 = (bf16[16,1024]{1,0:T(8,128)(2,1)S(1)}, bf16[16,1024]{1,0:T(8,128)(2,1)S(1)}, u32[]{:S(2)}, u32[]{:S(2)}) collective-permute-start(bf16[16,1024]{1,0:T(8,128)(2,1)S(1)} %get-tuple-element.64), channel_id=1, source_target_pairs={{0,1},{1,0},{2,3},{3,2},{4,5},{5,4},{6,7},{7,6},{8,9},{9,8},{10,11... | collective-permute-start | bytes 98312 | tf_op jit(solution)/shard_map/ppermute | solution.py:525
  36.2 0.5 %collective-permute-done.21.refs_1_ = bf16[16,1280]{1,0:T(8,128)(2,1)S(1)} collective-permute-done((bf16[16,1280]{1,0:T(8,128)(2,1)S(1)}, bf16[16,1280]{1,0:T(8,128)(2,1)S(1)}, u32[]{:S(2)}, u32[]{:S(2)}) %collective-permute-start.21) | collective-permute-done | bytes 40992 | tf_op jit(solution)/shard_map/ppermute | solution.py:525
  36.9 0.9 %adapter_grads.1 = (f32[16,1024]{1,0:T(8,128)}, f32[16,3072]{1,0:T(8,128)}) custom-call(bf16[16,1280]{1,0:T(8,128)(2,1)S(1)} %get-tuple-element.59.pack.refs_0_, bf16[16,1280]{1,0:T(8,128)(2,1)S(1)} %collective-permute-done.21.refs_1_, bf16[16,1280]{1,0:T(8,128)(2,1)S(1)} %collective-permute-done.17.refs_1_.refs_2_, ...), custom_call_target="tpu_custom_call" | custom-call | flops 1 | bytes 1 | tf_op jit(solution)/shard_map/adapter_grads/pallas_call | solution.py:371
  38.0 2.2 %collective-permute-done.20.refs_0_ = bf16[128,1024]{1,0:T(8,128)(2,1)S(1)} collective-permute-done((bf16[128,1024]{1,0:T(8,128)(2,1)S(1)}, bf16[128,1024]{1,0:T(8,128)(2,1)S(1)}, u32[]{:S(2)}, u32[]{:S(2)}) %collective-permute-start.20) | collective-permute-done | bytes 262176 | tf_op jit(solution)/shard_map/ppermute | solution.py:525
  40.3 0.8 %input_grads.1 = bf16[128,1024]{1,0:T(8,128)(2,1)} custom-call(f32[128,1024]{1,0:T(8,128)S(1)} %get-tuple-element.65.total, f32[128,1024]{1,0:T(8,128)S(1)} %get-tuple-element.66.token_gain, f32[128,1024]{1,0:T(8,128)S(1)} %get-tuple-element.67.scale, f32[128,1024]{1,0:T(8,128)S(1)} %get-tuple-element.68.slope, ...), custom_call_target="tpu_custom_call" | custom-call | flops 1 | bytes 1 | tf_op jit(solution)/shard_map/input_grads/pallas_call | solution.py:437
  (38 shorter events, 1.2 us)
Async XLA Ops:
  0.6 6.4 %collective-permute-start.1 = (bf16[256,3072]{1,0:T(8,128)(2,1)}, bf16[256,3072]{1,0:T(8,128)(2,1)S(1)}, u32[]{:S(2)}, u32[]{:S(2)}) collective-permute-start(bf16[256,3072]{1,0:T(8,128)(2,1)} %refs_0_.2), channel_id=1, source_target_pairs={{0,1},{1,0},{2,3},{3,2},{4,5},{5,4},{6,7},{7,6},{8,9},{9,8},{10,11... | collective-permute-start | bytes 4718600 | tf_op jit(solution)/shard_map/ppermute | solution.py:525
  1.1 5.9 %collective-permute-start = (bf16[128,1024]{1,0:T(8,128)(2,1)}, bf16[128,1024]{1,0:T(8,128)(2,1)S(1)}, u32[]{:S(2)}, u32[]{:S(2)}) collective-permute-start(bf16[128,1024]{1,0:T(8,128)(2,1)} %tokens.3), channel_id=1, source_target_pairs={{0,1},{1,0},{2,3},{3,2},{4,5},{5,4},{6,7},{7,6},{8,9},{9,8},{10,11... | collective-permute-start | bytes 786440 | tf_op jit(solution)/shard_map/ppermute | solution.py:525
  1.2 5.8 %collective-permute-start.2 = (bf16[128,1024]{1,0:T(8,128)(2,1)}, bf16[128,1024]{1,0:T(8,128)(2,1)S(1)}, u32[]{:S(2)}, u32[]{:S(2)}) collective-permute-start(bf16[128,1024]{1,0:T(8,128)(2,1)} %refs_2_.1), channel_id=1, source_target_pairs={{0,1},{1,0},{2,3},{3,2},{4,5},{5,4},{6,7},{7,6},{8,9},{9,8},{10,11... | collective-permute-start | bytes 786440 | tf_op jit(solution)/shard_map/ppermute | solution.py:525
  2.6 8.3 %collective-permute-start.4 = (bf16[128,384]{1,0:T(8,128)(2,1)S(1)}, bf16[128,384]{1,0:T(8,128)(2,1)S(1)}, u32[]{:S(2)}, u32[]{:S(2)}) collective-permute-start(bf16[128,384]{1,0:T(8,128)(2,1)S(1)} %dynamic_slice.6), channel_id=1, source_target_pairs={{0,2},{1,3},{2,0},{3,1},{4,7},{5,6},{6,5},{7,4},{8,10},{9,11},{10,... | collective-permute-start | bytes 294920 | tf_op jit(solution)/shard_map/ppermute | solution.py:525
  6.2 7.8 %collective-permute-start.9 = (bf16[256,384]{1,0:T(8,128)(2,1)S(1)}, bf16[256,384]{1,0:T(8,128)(2,1)S(1)}, u32[]{:S(2)}, u32[]{:S(2)}) collective-permute-start(bf16[256,384]{1,0:T(8,128)(2,1)S(1)} %constant_dynamic-slice_fusion), channel_id=1, source_target_pairs={{0,2},{1,3},{2,0},{3,1},{4,6},{5,7},{6,4},{7,5},{8,11},{9,10},{10,... | collective-permute-start | bytes 589832 | tf_op jit(solution)/shard_map/ppermute | solution.py:525
  7.0 14.9 %copy-start.1 = (bf16[16,3072]{1,0:T(8,128)(2,1)S(1)}, bf16[16,3072]{1,0:T(8,128)(2,1)}, u32[]{:S(2)}) copy-start(bf16[16,3072]{1,0:T(8,128)(2,1)} %refs_10_.1) | copy-start | bytes 294916
  7.0 14.8 %copy-start.2 = (bf16[1024,16]{0,1:T(8,128)(2,1)S(1)}, bf16[1024,16]{0,1:T(8,128)(2,1)}, u32[]{:S(2)}) copy-start(bf16[1024,16]{0,1:T(8,128)(2,1)} %param.12) | copy-start | bytes 98308
  8.8 12.5 %collective-permute-start.11 = (bf16[128,1024]{1,0:T(8,128)(2,1)S(1)}, bf16[128,1024]{1,0:T(8,128)(2,1)S(1)}, u32[]{:S(2)}, u32[]{:S(2)}) collective-permute-start(bf16[128,1024]{1,0:T(8,128)(2,1)S(1)} %get-tuple-element.45.refs_2_), channel_id=1, source_target_pairs={{0,2},{1,3},{2,0},{3,1},{4,6},{5,7},{6,4},{7,5},{8,10},{9,11},{10,... | collective-permute-start | bytes 786440 | tf_op jit(solution)/shard_map/ppermute | solution.py:525
  10.8 4.6 %collective-permute-start.6 = (bf16[128,384]{1,0:T(8,128)(2,1)S(1)}, bf16[128,384]{1,0:T(8,128)(2,1)S(1)}, u32[]{:S(2)}, u32[]{:S(2)}) collective-permute-start(bf16[128,384]{1,0:T(8,128)(2,1)S(1)} %collective-permute-done.4.refs_4_), channel_id=1, source_target_pairs={{0,8},{1,9},{2,10},{3,11},{4,12},{5,13},{6,14},{7,15},{8,0},{9,1},... | collective-permute-start | bytes 294920 | tf_op jit(solution)/shard_map/ppermute | solution.py:525
  12.2 5.4 %collective-permute-start.5 = (bf16[128,384]{1,0:T(8,128)(2,1)S(1)}, bf16[128,384]{1,0:T(8,128)(2,1)S(1)}, u32[]{:S(2)}, u32[]{:S(2)}) collective-permute-start(bf16[128,384]{1,0:T(8,128)(2,1)S(1)} %collective-permute-done.4.refs_4_), channel_id=1, source_target_pairs={{0,4},{1,5},{2,6},{3,7},{4,0},{5,1},{6,2},{7,3},{8,12},{9,13},{10,... | collective-permute-start | bytes 294920 | tf_op jit(solution)/shard_map/ppermute | solution.py:525
  14.0 7.9 %collective-permute-start.10 = (bf16[256,384]{1,0:T(8,128)(2,1)S(1)}, bf16[256,384]{1,0:T(8,128)(2,1)S(1)}, u32[]{:S(2)}, u32[]{:S(2)}) collective-permute-start(bf16[256,384]{1,0:T(8,128)(2,1)S(1)} %collective-permute-done.9.refs_9_), channel_id=1, source_target_pairs={{0,8},{1,9},{2,10},{3,11},{4,12},{5,13},{6,14},{7,15},{8,0},{9,1},... | collective-permute-start | bytes 589832 | tf_op jit(solution)/shard_map/ppermute | solution.py:525
  15.5 5.8 %collective-permute-start.7 = (bf16[112,384]{1,0:T(8,128)(2,1)S(1)}, bf16[112,384]{1,0:T(8,128)(2,1)S(1)}, u32[]{:S(2)}, u32[]{:S(2)}) collective-permute-start(bf16[112,384]{1,0:T(8,128)(2,1)S(1)} %get-tuple-element.47), channel_id=1, source_target_pairs={{0,4},{1,5},{2,6},{3,7},{4,0},{5,1},{6,2},{7,3},{8,12},{9,13},{10,... | collective-permute-start | bytes 258056 | tf_op jit(solution)/shard_map/ppermute | solution.py:525
  17.1 6.5 %collective-permute-start.3 = (bf16[128,512]{1,0:T(8,128)(2,1)S(1)}, bf16[128,512]{1,0:T(8,128)(2,1)S(1)}, u32[]{:S(2)}, u32[]{:S(2)}) collective-permute-start(bf16[128,512]{1,0:T(8,128)(2,1)S(1)} %get-tuple-element.42), channel_id=1, source_target_pairs={{0,2},{1,3},{2,0},{3,1},{4,6},{5,7},{6,4},{7,5},{8,10},{9,11},{10,... | collective-permute-start | bytes 393224 | tf_op jit(solution)/shard_map/ppermute | solution.py:525
  17.6 3.7 %collective-permute-start.8 = (bf16[16,384]{1,0:T(8,128)(2,1)S(1)}, bf16[16,384]{1,0:T(8,128)(2,1)S(1)}, u32[]{:S(2)}, u32[]{:S(2)}) collective-permute-start(bf16[16,384]{1,0:T(8,128)(2,1)S(1)} %get-tuple-element.48), channel_id=1, source_target_pairs={{0,4},{1,5},{2,6},{3,7},{4,0},{5,1},{6,2},{7,3},{8,12},{9,13},{10,... | collective-permute-start | bytes 36872 | tf_op jit(solution)/shard_map/ppermute | solution.py:525
  21.3 2.9 %collective-permute-start.14 = (bf16[80,1024]{1,0:T(8,128)(2,1)S(1)}, bf16[80,1024]{1,0:T(8,128)(2,1)S(1)}, u32[]{:S(2)}, u32[]{:S(2)}) collective-permute-start(bf16[80,1024]{1,0:T(8,128)(2,1)S(1)} %get-tuple-element.52), channel_id=1, source_target_pairs={{0,1},{1,0},{2,3},{3,2},{4,5},{5,4},{6,7},{7,6},{8,9},{9,8},{10,11... | collective-permute-start | bytes 491528 | tf_op jit(solution)/shard_map/ppermute | solution.py:525
  21.4 2.8 %collective-permute-start.15 = (bf16[48,1024]{1,0:T(8,128)(2,1)S(1)}, bf16[48,1024]{1,0:T(8,128)(2,1)S(1)}, u32[]{:S(2)}, u32[]{:S(2)}) collective-permute-start(bf16[48,1024]{1,0:T(8,128)(2,1)S(1)} %get-tuple-element.53), channel_id=1, source_target_pairs={{0,1},{1,0},{2,3},{3,2},{4,5},{5,4},{6,7},{7,6},{8,9},{9,8},{10,11... | collective-permute-start | bytes 294920 | tf_op jit(solution)/shard_map/ppermute | solution.py:525
  23.6 1.5 %copy-start.3 = (f32[4]{0:T(128)S(1)}, f32[4]{0:T(128)}, u32[]{:S(2)}) copy-start(f32[4]{0:T(128)} %refs_0_.3) | copy-start | bytes 52
  23.6 1.4 %collective-permute-start.12 = (bf16[112,256]{1,0:T(8,128)(2,1)S(1)}, bf16[112,256]{1,0:T(8,128)(2,1)S(1)}, u32[]{:S(2)}, u32[]{:S(2)}) collective-permute-start(bf16[112,256]{1,0:T(8,128)(2,1)S(1)} %get-tuple-element.50), channel_id=1, source_target_pairs={{0,1},{1,0},{2,3},{3,2},{4,5},{5,4},{6,7},{7,6},{8,9},{9,8},{10,11... | collective-permute-start | bytes 172040 | tf_op jit(solution)/shard_map/ppermute | solution.py:525
  23.7 1.3 %collective-permute-start.13 = (bf16[16,256]{1,0:T(8,128)(2,1)S(1)}, bf16[16,256]{1,0:T(8,128)(2,1)S(1)}, u32[]{:S(2)}, u32[]{:S(2)}) collective-permute-start(bf16[16,256]{1,0:T(8,128)(2,1)S(1)} %get-tuple-element.51), channel_id=1, source_target_pairs={{0,1},{1,0},{2,3},{3,2},{4,5},{5,4},{6,7},{7,6},{8,9},{9,8},{10,11... | collective-permute-start | bytes 24584 | tf_op jit(solution)/shard_map/ppermute | solution.py:525
  30.0 1.9 %collective-permute-start.16 = (bf16[128,1024]{1,0:T(8,128)(2,1)S(1)}, bf16[128,1024]{1,0:T(8,128)(2,1)S(1)}, u32[]{:S(2)}, u32[]{:S(2)}) collective-permute-start(bf16[128,1024]{1,0:T(8,128)(2,1)S(1)} %get-tuple-element.61), channel_id=1, source_target_pairs={{0,1},{1,0},{2,3},{3,2},{4,5},{5,4},{6,7},{7,6},{8,9},{9,8},{10,11... | collective-permute-start | bytes 786440 | tf_op jit(solution)/shard_map/ppermute | solution.py:525
  30.4 4.0 %collective-permute-start.17 = (bf16[16,1280]{1,0:T(8,128)(2,1)S(1)}, bf16[16,1280]{1,0:T(8,128)(2,1)S(1)}, u32[]{:S(2)}, u32[]{:S(2)}) collective-permute-start(bf16[16,1280]{1,0:T(8,128)(2,1)S(1)} %get-tuple-element.59.pack.refs_0_), channel_id=1, source_target_pairs={{0,2},{1,3},{2,0},{3,1},{4,6},{5,7},{6,4},{7,5},{8,10},{9,11},{10,... | collective-permute-start | bytes 122888 | tf_op jit(solution)/shard_map/ppermute | solution.py:525
  32.0 8.3 %collective-permute-start.20 = (bf16[128,1024]{1,0:T(8,128)(2,1)S(1)}, bf16[128,1024]{1,0:T(8,128)(2,1)S(1)}, u32[]{:S(2)}, u32[]{:S(2)}) collective-permute-start(bf16[128,1024]{1,0:T(8,128)(2,1)S(1)} %add.42.refs_0_), channel_id=1, source_target_pairs={{0,2},{1,3},{2,0},{3,1},{4,6},{5,7},{6,4},{7,5},{8,10},{9,11},{10,... | collective-permute-start | bytes 786440 | tf_op jit(solution)/shard_map/ppermute | solution.py:525
  34.4 3.4 %copy-start = (bf16[128,1024]{1,0:T(8,128)(2,1)S(1)}, bf16[128,1024]{1,0:T(8,128)(2,1)}, u32[]{:S(2)}) copy-start(bf16[128,1024]{1,0:T(8,128)(2,1)} %tokens.3) | copy-start | bytes 786436
  35.1 2.7 %collective-permute-start.18 = (bf16[112,1024]{1,0:T(8,128)(2,1)S(1)}, bf16[112,1024]{1,0:T(8,128)(2,1)S(1)}, u32[]{:S(2)}, u32[]{:S(2)}) collective-permute-start(bf16[112,1024]{1,0:T(8,128)(2,1)S(1)} %get-tuple-element.63), channel_id=1, source_target_pairs={{0,1},{1,0},{2,3},{3,2},{4,5},{5,4},{6,7},{7,6},{8,9},{9,8},{10,11... | collective-permute-start | bytes 688136 | tf_op jit(solution)/shard_map/ppermute | solution.py:525
  35.2 1.5 %collective-permute-start.21 = (bf16[16,1280]{1,0:T(8,128)(2,1)S(1)}, bf16[16,1280]{1,0:T(8,128)(2,1)S(1)}, u32[]{:S(2)}, u32[]{:S(2)}) collective-permute-start(bf16[16,1280]{1,0:T(8,128)(2,1)S(1)} %get-tuple-element.59.pack.refs_0_), channel_id=1, source_target_pairs={{0,1},{1,0},{2,3},{3,2},{4,5},{5,4},{6,7},{7,6},{8,9},{9,8},{10,11... | collective-permute-start | bytes 122888 | tf_op jit(solution)/shard_map/ppermute | solution.py:525
  35.7 1.2 %collective-permute-start.22 = (bf16[16,1280]{1,0:T(8,128)(2,1)S(1)}, bf16[16,1280]{1,0:T(8,128)(2,1)S(1)}, u32[]{:S(2)}, u32[]{:S(2)}) collective-permute-start(bf16[16,1280]{1,0:T(8,128)(2,1)S(1)} %collective-permute-done.17.refs_1_.refs_2_), channel_id=1, source_target_pairs={{0,1},{1,0},{2,3},{3,2},{4,5},{5,4},{6,7},{7,6},{8,9},{9,8},{10,11... | collective-permute-start | bytes 122888 | tf_op jit(solution)/shard_map/ppermute | solution.py:525
  35.8 2.0 %collective-permute-start.19 = (bf16[16,1024]{1,0:T(8,128)(2,1)S(1)}, bf16[16,1024]{1,0:T(8,128)(2,1)S(1)}, u32[]{:S(2)}, u32[]{:S(2)}) collective-permute-start(bf16[16,1024]{1,0:T(8,128)(2,1)S(1)} %get-tuple-element.64), channel_id=1, source_target_pairs={{0,1},{1,0},{2,3},{3,2},{4,5},{5,4},{6,7},{7,6},{8,9},{9,8},{10,11... | collective-permute-start | bytes 98312 | tf_op jit(solution)/shard_map/ppermute | solution.py:525

commit v8 on v7

--- a/solution.py
+++ b/solution.py
@@ -569,7 +569,7 @@
             w_from.append((len(arrays), pair_cols, j, 4, other, 0))
             arrays.append(x)
         early.append(held[1])
-        cut = (half * 7 // 8, half // 8)
+        cut = (half * 3 // 4, half // 4)
         for at, x in zip((0, cut[0]), gate([held[2]], [cut])):
             early.append(exchange(x, 1))
             w_from.append((len(arrays), pair_cols, j, 4, 3, at))
@@ -599,7 +599,7 @@
     )
 
     cots, c_from = [own_cot, core_cot], [(1, False), (1, False)]
-    blocks = (tok * 7 // 8, tok // 8) if tok % 128 == 0 else (tok,)
+    blocks = (tok * 3 // 4, tok // 4) if tok % 64 == 0 else (tok,)
     for j, x in zip(chips, chip_cot):
         x = to_row(x, j)
         c_from += [(1, True), (len(blocks), False)]

time: 41.3 us -> 41 us (level)
  starting transfers between devices: 17.5 us -> 15.7 us
  waiting for transfers between devices: 8.39 us -> 9.8 us
    ppermute x23, starting transfers between devices: 17.5 us -> 15.7 us  [send(): return lax.ppermute(x, axes, perm)]
    ppermute x23, waiting for transfers between devices: 8.39 us -> 9.8 us  [send(): return lax.ppermute(x, axes, perm)]
  transfers between devices with their start and end apart: 23 -> 23, of which waited for: 8 -> 9; matrix products, arithmetic and copies ran while one was open for 5% -> 5% of each run, Pallas kernels for 15% -> 15%
where the time goes in v8:
time: 41 us; the launch traced here: 40.7 us
  starting transfers between devices  15.7 us (38%)
  Pallas kernels  11.8 us (29%)
  waiting for transfers between devices  9.8 us (24%)
  local copies, waits for them, and re-layouts  1.87 us (5%)
  between operations  1.46 us (4%)
    ppermute x23, starting transfers between devices, send(): return lax.ppermute(x, axes, perm)  15.7 us
    ppermute x23, waiting for transfers between devices, send(): return lax.ppermute(x, axes, perm)  9.8 us
    pallas_call x1, Pallas kernels, attention_call(): pl.pallas_call(functools.partial(attention_kernel, cols // (3 * HEAD), to...  4.98 us
    pallas_call x1, Pallas kernels, prepare_call(): pl.pallas_call(functools.partial(prepare_kernel, chips, head_cols, [size...  1.7 us
    pallas_call x1, Pallas kernels, qkv_call(): pl.pallas_call(functools.partial(qkv_kernel, n, x_from, w_from), out_shap...  1.67 us
    dynamic_slice x1, local copies, waits for them, and re-layouts, per_device(): lax.dynamic_slice(weight, (0, (r ^ j + d // 2 % 2) * cols), (k_rows, pair...  0.95 us
    dynamic_slice x1, local copies, waits for them, and re-layouts, per_device(): x = lax.dynamic_slice(weight, start, (half, cols - pair_cols))  0.9 us
    pallas_call x1, Pallas kernels, adapter_call(): pl.pallas_call(functools.partial(adapter_kernel, tok, places), out_shape=...  0.89 us
  transfers between devices with their start and end apart: 23, of which 9 were waited for; matrix products, arithmetic and copies ran while one was open for 5% of the time, Pallas kernels for 15%

profile of v8, /device:TPU:0, one launch (start us, length us, event | category | flops | bytes accessed | tf_op | source)
XLA Modules:
  0.0 40.7 jit_solution(7492299111475482804)
XLA Ops:
  0.6 0.5 %collective-permute-start.1 = (bf16[256,3072]{1,0:T(8,128)(2,1)}, bf16[256,3072]{1,0:T(8,128)(2,1)S(1)}, u32[]{:S(2)}, u32[]{:S(2)}) collective-permute-start(bf16[256,3072]{1,0:T(8,128)(2,1)} %refs_0_.2), channel_id=1, source_target_pairs={{0,1},{1,0},{2,3},{3,2},{4,5},{5,4},{6,7},{7,6},{8,9},{9,8},{10,11... | collective-permute-start | bytes 4718600 | tf_op jit(solution)/shard_map/ppermute | solution.py:525
  1.2 0.4 %collective-permute-start.2 = (bf16[128,1024]{1,0:T(8,128)(2,1)}, bf16[128,1024]{1,0:T(8,128)(2,1)S(1)}, u32[]{:S(2)}, u32[]{:S(2)}) collective-permute-start(bf16[128,1024]{1,0:T(8,128)(2,1)} %refs_2_.1), channel_id=1, source_target_pairs={{0,1},{1,0},{2,3},{3,2},{4,5},{5,4},{6,7},{7,6},{8,9},{9,8},{10,11... | collective-permute-start | bytes 786440 | tf_op jit(solution)/shard_map/ppermute | solution.py:525
  1.7 0.9 %dynamic_slice.6 = bf16[128,384]{1,0:T(8,128)(2,1)S(1)} dynamic-slice(bf16[256,3072]{1,0:T(8,128)(2,1)} %refs_0_.2, s32[]{:T(128)S(6)} %select_n.33, s32[]{:T(128)S(6)} %select_n.35), dynamic_slice_sizes={128,384} | dynamic-slice | bytes 196612 | tf_op jit(solution)/shard_map/dynamic_slice | solution.py:543
  2.6 2.7 %collective-permute-start.4 = (bf16[128,384]{1,0:T(8,128)(2,1)S(1)}, bf16[128,384]{1,0:T(8,128)(2,1)S(1)}, u32[]{:S(2)}, u32[]{:S(2)}) collective-permute-start(bf16[128,384]{1,0:T(8,128)(2,1)S(1)} %dynamic_slice.6), channel_id=1, source_target_pairs={{0,2},{1,3},{2,0},{3,1},{4,7},{5,6},{6,5},{7,4},{8,10},{9,11},{10,... | collective-permute-start | bytes 294920 | tf_op jit(solution)/shard_map/ppermute | solution.py:525
  5.2 0.9 %constant_dynamic-slice_fusion = bf16[256,384]{1,0:T(8,128)(2,1)S(1)} fusion(bf16[256,3072]{1,0:T(8,128)(2,1)} %refs_0_.2, s32[]{:T(128)S(6)} %select_n.38), kind=kLoop, calls=%fused_computation.2 | loop fusion | bytes 393220 | tf_op jit(solution)/shard_map/dynamic_slice | solution.py:545
  7.1 1.7 %prepare.1 = (bf16[128,1024]{1,0:T(8,128)(2,1)S(1)}, bf16[128,1024]{1,0:T(8,128)(2,1)S(1)}, f32[1,1024]{1,0:T(1,128)S(1)}, f32[128,1]{1,0:T(8,128)S(1)}, bf16[25...) custom-call(f32[2,128]{1,0:T(2,128)S(1)} %pad_maximum_fusion.feature, ...), custom_call_target="tpu_custom_call" | custom-call | flops 1 | bytes 1 | tf_op jit(solution)/shard_map/prepare/pallas_call | solution.py:487
  8.8 2.0 %collective-permute-start.11 = (bf16[128,1024]{1,0:T(8,128)(2,1)S(1)}, bf16[128,1024]{1,0:T(8,128)(2,1)S(1)}, u32[]{:S(2)}, u32[]{:S(2)}) collective-permute-start(bf16[128,1024]{1,0:T(8,128)(2,1)S(1)} %get-tuple-element.45.refs_2_), channel_id=1, source_target_pairs={{0,2},{1,3},{2,0},{3,1},{4,6},{5,7},{6,4},{7,5},{8,10},{9,11},{10,... | collective-permute-start | bytes 786440 | tf_op jit(solution)/shard_map/ppermute | solution.py:525
  10.8 1.3 %collective-permute-start.6 = (bf16[128,384]{1,0:T(8,128)(2,1)S(1)}, bf16[128,384]{1,0:T(8,128)(2,1)S(1)}, u32[]{:S(2)}, u32[]{:S(2)}) collective-permute-start(bf16[128,384]{1,0:T(8,128)(2,1)S(1)} %collective-permute-done.4.refs_4_), channel_id=1, source_target_pairs={{0,8},{1,9},{2,10},{3,11},{4,12},{5,13},{6,14},{7,15},{8,0},{9,1},... | collective-permute-start | bytes 294920 | tf_op jit(solution)/shard_map/ppermute | solution.py:525
  12.2 1.4 %collective-permute-start.5 = (bf16[128,384]{1,0:T(8,128)(2,1)S(1)}, bf16[128,384]{1,0:T(8,128)(2,1)S(1)}, u32[]{:S(2)}, u32[]{:S(2)}) collective-permute-start(bf16[128,384]{1,0:T(8,128)(2,1)S(1)} %collective-permute-done.4.refs_4_), channel_id=1, source_target_pairs={{0,4},{1,5},{2,6},{3,7},{4,0},{5,1},{6,2},{7,3},{8,12},{9,13},{10,... | collective-permute-start | bytes 294920 | tf_op jit(solution)/shard_map/ppermute | solution.py:525
  13.6 0.4 collective-permute-done.9.refs_9_
  14.0 0.7 %collective-permute-start.10 = (bf16[256,384]{1,0:T(8,128)(2,1)S(1)}, bf16[256,384]{1,0:T(8,128)(2,1)S(1)}, u32[]{:S(2)}, u32[]{:S(2)}) collective-permute-start(bf16[256,384]{1,0:T(8,128)(2,1)S(1)} %collective-permute-done.9.refs_9_), channel_id=1, source_target_pairs={{0,8},{1,9},{2,10},{3,11},{4,12},{5,13},{6,14},{7,15},{8,0},{9,1},... | collective-permute-start | bytes 589832 | tf_op jit(solution)/shard_map/ppermute | solution.py:525
  14.7 0.8 %collective-permute-done.6.refs_0_.refs_6_ = bf16[128,384]{1,0:T(8,128)(2,1)S(1)} collective-permute-done((bf16[128,384]{1,0:T(8,128)(2,1)S(1)}, bf16[128,384]{1,0:T(8,128)(2,1)S(1)}, u32[]{:S(2)}, u32[]{:S(2)}) %collective-permute-start.6) | collective-permute-done | bytes 98336 | tf_op jit(solution)/shard_map/ppermute | solution.py:525
  15.5 1.6 %collective-permute-start.7 = (bf16[96,384]{1,0:T(8,128)(2,1)S(1)}, bf16[96,384]{1,0:T(8,128)(2,1)S(1)}, u32[]{:S(2)}, u32[]{:S(2)}) collective-permute-start(bf16[96,384]{1,0:T(8,128)(2,1)S(1)} %get-tuple-element.47), channel_id=1, source_target_pairs={{0,4},{1,5},{2,6},{3,7},{4,0},{5,1},{6,2},{7,3},{8,12},{9,13},{10,... | collective-permute-start | bytes 221192 | tf_op jit(solution)/shard_map/ppermute | solution.py:525
  17.1 0.5 %collective-permute-start.8 = (bf16[32,384]{1,0:T(8,128)(2,1)S(1)}, bf16[32,384]{1,0:T(8,128)(2,1)S(1)}, u32[]{:S(2)}, u32[]{:S(2)}) collective-permute-start(bf16[32,384]{1,0:T(8,128)(2,1)S(1)} %get-tuple-element.48), channel_id=1, source_target_pairs={{0,4},{1,5},{2,6},{3,7},{4,0},{5,1},{6,2},{7,3},{8,12},{9,13},{10,... | collective-permute-start | bytes 73736 | tf_op jit(solution)/shard_map/ppermute | solution.py:525
  17.8 3.1 %collective-permute-done.8.refs_8_.refs_3_ = bf16[32,384]{1,0:T(8,128)(2,1)S(1)} collective-permute-done((bf16[32,384]{1,0:T(8,128)(2,1)S(1)}, bf16[32,384]{1,0:T(8,128)(2,1)S(1)}, u32[]{:S(2)}, u32[]{:S(2)}) %collective-permute-start.8) | collective-permute-done | bytes 24608 | tf_op jit(solution)/shard_map/ppermute | solution.py:525
  21.0 0.5 %collective-permute-start.15 = (bf16[48,1024]{1,0:T(8,128)(2,1)S(1)}, bf16[48,1024]{1,0:T(8,128)(2,1)S(1)}, u32[]{:S(2)}, u32[]{:S(2)}) collective-permute-start(bf16[48,1024]{1,0:T(8,128)(2,1)S(1)} %get-tuple-element.53), channel_id=1, source_target_pairs={{0,1},{1,0},{2,3},{3,2},{4,5},{5,4},{6,7},{7,6},{8,9},{9,8},{10,11... | collective-permute-start | bytes 294920 | tf_op jit(solution)/shard_map/ppermute | solution.py:525
  21.5 1.7 %qkv.1 = (bf16[384,1024]{1,0:T(8,128)(2,1)S(1)}, bf16[1024,768]{1,0:T(8,128)(2,1)S(1)}, bf16[768,384]{1,0:T(8,128)(2,1)S(1)}, bf16[16,384]{1,0:T(8,128)(2,1)S(1)}) custom-call(bf16[256,768]{1,0:T(8,128)(2,1)S(1)} %get-tuple-element.43.refs_0_, bf16[256,768]{1,0:T(8,128)(2,1)S(1)} %get-tuple-element.44.refs_1_, ...), custom_call_target="tpu_custom_call" | custom-call | flops 1 | bytes 1 | tf_op jit(solution)/shard_map/qkv/pallas_call | solution.py:179
  23.4 0.4 %collective-permute-start.13 = (bf16[32,256]{1,0:T(8,128)(2,1)S(1)}, bf16[32,256]{1,0:T(8,128)(2,1)S(1)}, u32[]{:S(2)}, u32[]{:S(2)}) collective-permute-start(bf16[32,256]{1,0:T(8,128)(2,1)S(1)} %get-tuple-element.51), channel_id=1, source_target_pairs={{0,1},{1,0},{2,3},{3,2},{4,5},{5,4},{6,7},{7,6},{8,9},{9,8},{10,11... | collective-permute-start | bytes 49160 | tf_op jit(solution)/shard_map/ppermute | solution.py:525
  23.8 0.8 %last_qkv.1 = (bf16[128,1024]{1,0:T(8,128)(2,1)S(1)}, bf16[768,512]{1,0:T(8,128)(2,1)S(1)}, bf16[16,512]{1,0:T(8,128)(2,1)S(1)}) custom-call(bf16[80,1024]{1,0:T(8,128)(2,1)S(1)} %collective-permute-done.14.refs_0_, bf16[48,1024]{1,0:T(8,128)(2,1)S(1)} %collective-permute-done.15.refs_1_, bf16[1024,768]{1,0:T(8,128)(2,1)S(1)} %get-tuple-element.54.refs_2_.refs_8_.w_all, ...), custom_call_target="tpu_custom_call" | custom-call | flops 1 | bytes 1 | tf_op jit(solution)/shard_map/last_qkv/pallas_call | solution.py:119
  24.6 5.0 %attention_grads.1 = (f32[128,1024]{1,0:T(8,128)S(1)}, bf16[128,1024]{1,0:T(8,128)(2,1)S(1)}, bf16[768,512]{1,0:T(8,128)(2,1)S(1)}, bf16[16,1280]{1,0:T(8,128)(2,1)S(1)}) custom-call(f32[4]{0:T(128)S(1)} %copy-done.3, bf16[128,256]{1,0:T(8,128)(2,1)S(1)} %get-tuple-element.40.refs_1_, bf16[128,256]{1,0:T(8,128)(2,1)S(1)} %get-tuple-element.41.refs_2_, ...), custom_call_target="tpu_custom_call" | custom-call | flops 1 | bytes 1 | tf_op jit(solution)/shard_map/attention_grads/pallas_call | solution.py:273
  29.6 0.4 collective-permute-start.16
  30.0 0.5 %collective-permute-start.17 = (bf16[16,1280]{1,0:T(8,128)(2,1)S(1)}, bf16[16,1280]{1,0:T(8,128)(2,1)S(1)}, u32[]{:S(2)}, u32[]{:S(2)}) collective-permute-start(bf16[16,1280]{1,0:T(8,128)(2,1)S(1)} %get-tuple-element.59.pack.refs_0_), channel_id=1, source_target_pairs={{0,2},{1,3},{2,0},{3,1},{4,6},{5,7},{6,4},{7,5},{8,10},{9,11},{10,... | collective-permute-start | bytes 122888 | tf_op jit(solution)/shard_map/ppermute | solution.py:525
  30.5 0.7 %collective-permute-done.16.b = bf16[128,1024]{1,0:T(8,128)(2,1)S(1)} collective-permute-done((bf16[128,1024]{1,0:T(8,128)(2,1)S(1)}, bf16[128,1024]{1,0:T(8,128)(2,1)S(1)}, u32[]{:S(2)}, u32[]{:S(2)}) %collective-permute-start.16) | collective-permute-done | bytes 262176 | tf_op jit(solution)/shard_map/ppermute | solution.py:525
  31.3 0.9 %collective-permute-start.20 = (bf16[128,1024]{1,0:T(8,128)(2,1)S(1)}, bf16[128,1024]{1,0:T(8,128)(2,1)S(1)}, u32[]{:S(2)}, u32[]{:S(2)}) collective-permute-start(bf16[128,1024]{1,0:T(8,128)(2,1)S(1)} %add.42.refs_0_), channel_id=1, source_target_pairs={{0,2},{1,3},{2,0},{3,1},{4,6},{5,7},{6,4},{7,5},{8,10},{9,11},{10,... | collective-permute-start | bytes 786440 | tf_op jit(solution)/shard_map/ppermute | solution.py:525
  32.2 1.9 %collective-permute-done.17.refs_1_.refs_2_ = bf16[16,1280]{1,0:T(8,128)(2,1)S(1)} collective-permute-done((bf16[16,1280]{1,0:T(8,128)(2,1)S(1)}, bf16[16,1280]{1,0:T(8,128)(2,1)S(1)}, u32[]{:S(2)}, u32[]{:S(2)}) %collective-permute-start.17) | collective-permute-done | bytes 40992 | tf_op jit(solution)/shard_map/ppermute | solution.py:525
  34.0 0.7 %own_grads.1 = (f32[128,1024]{1,0:T(8,128)S(1)}, bf16[112,1024]{1,0:T(8,128)(2,1)S(1)}, bf16[16,1024]{1,0:T(8,128)(2,1)S(1)}) custom-call(bf16[768,512]{1,0:T(8,128)(2,1)S(1)} %get-tuple-element.58.grad_t, bf16[16,1280]{1,0:T(8,128)(2,1)S(1)} %get-tuple-element.59.pack.refs_0_, bf16[1024,768]{1,0:T(8,128)(2,1)S(1)} %get-tuple-element.54.refs_2_.refs_8_.w_all, ...), custom_call_target="tpu_custom_call" | custom-call | flops 1 | bytes 1 | tf_op jit(solution)/shard_map/own_grads/pallas_call | solution.py:338
  34.9 0.5 %collective-permute-start.21 = (bf16[16,1280]{1,0:T(8,128)(2,1)S(1)}, bf16[16,1280]{1,0:T(8,128)(2,1)S(1)}, u32[]{:S(2)}, u32[]{:S(2)}) collective-permute-start(bf16[16,1280]{1,0:T(8,128)(2,1)S(1)} %get-tuple-element.59.pack.refs_0_), channel_id=1, source_target_pairs={{0,1},{1,0},{2,3},{3,2},{4,5},{5,4},{6,7},{7,6},{8,9},{9,8},{10,11... | collective-permute-start | bytes 122888 | tf_op jit(solution)/shard_map/ppermute | solution.py:525
  35.4 0.4 %collective-permute-start.19 = (bf16[16,1024]{1,0:T(8,128)(2,1)S(1)}, bf16[16,1024]{1,0:T(8,128)(2,1)S(1)}, u32[]{:S(2)}, u32[]{:S(2)}) collective-permute-start(bf16[16,1024]{1,0:T(8,128)(2,1)S(1)} %get-tuple-element.64), channel_id=1, source_target_pairs={{0,1},{1,0},{2,3},{3,2},{4,5},{5,4},{6,7},{7,6},{8,9},{9,8},{10,11... | collective-permute-start | bytes 98312 | tf_op jit(solution)/shard_map/ppermute | solution.py:525
  35.9 0.5 %collective-permute-done.21.refs_1_ = bf16[16,1280]{1,0:T(8,128)(2,1)S(1)} collective-permute-done((bf16[16,1280]{1,0:T(8,128)(2,1)S(1)}, bf16[16,1280]{1,0:T(8,128)(2,1)S(1)}, u32[]{:S(2)}, u32[]{:S(2)}) %collective-permute-start.21) | collective-permute-done | bytes 40992 | tf_op jit(solution)/shard_map/ppermute | solution.py:525
  36.6 0.9 %adapter_grads.1 = (f32[16,1024]{1,0:T(8,128)}, f32[16,3072]{1,0:T(8,128)}) custom-call(bf16[16,1280]{1,0:T(8,128)(2,1)S(1)} %get-tuple-element.59.pack.refs_0_, bf16[16,1280]{1,0:T(8,128)(2,1)S(1)} %collective-permute-done.21.refs_1_, bf16[16,1280]{1,0:T(8,128)(2,1)S(1)} %collective-permute-done.17.refs_1_.refs_2_, ...), custom_call_target="tpu_custom_call" | custom-call | flops 1 | bytes 1 | tf_op jit(solution)/shard_map/adapter_grads/pallas_call | solution.py:371
  37.7 2.2 %collective-permute-done.20.refs_0_ = bf16[128,1024]{1,0:T(8,128)(2,1)S(1)} collective-permute-done((bf16[128,1024]{1,0:T(8,128)(2,1)S(1)}, bf16[128,1024]{1,0:T(8,128)(2,1)S(1)}, u32[]{:S(2)}, u32[]{:S(2)}) %collective-permute-start.20) | collective-permute-done | bytes 262176 | tf_op jit(solution)/shard_map/ppermute | solution.py:525
  39.9 0.8 %input_grads.1 = bf16[128,1024]{1,0:T(8,128)(2,1)} custom-call(f32[128,1024]{1,0:T(8,128)S(1)} %get-tuple-element.65.total, f32[128,1024]{1,0:T(8,128)S(1)} %get-tuple-element.66.token_gain, f32[128,1024]{1,0:T(8,128)S(1)} %get-tuple-element.67.scale, f32[128,1024]{1,0:T(8,128)S(1)} %get-tuple-element.68.slope, ...), custom_call_target="tpu_custom_call" | custom-call | flops 1 | bytes 1 | tf_op jit(solution)/shard_map/input_grads/pallas_call | solution.py:437
  (38 shorter events, 1.5 us)
Async XLA Ops:
  0.6 6.4 %collective-permute-start.1 = (bf16[256,3072]{1,0:T(8,128)(2,1)}, bf16[256,3072]{1,0:T(8,128)(2,1)S(1)}, u32[]{:S(2)}, u32[]{:S(2)}) collective-permute-start(bf16[256,3072]{1,0:T(8,128)(2,1)} %refs_0_.2), channel_id=1, source_target_pairs={{0,1},{1,0},{2,3},{3,2},{4,5},{5,4},{6,7},{7,6},{8,9},{9,8},{10,11... | collective-permute-start | bytes 4718600 | tf_op jit(solution)/shard_map/ppermute | solution.py:525
  1.1 5.9 %collective-permute-start = (bf16[128,1024]{1,0:T(8,128)(2,1)}, bf16[128,1024]{1,0:T(8,128)(2,1)S(1)}, u32[]{:S(2)}, u32[]{:S(2)}) collective-permute-start(bf16[128,1024]{1,0:T(8,128)(2,1)} %tokens.3), channel_id=1, source_target_pairs={{0,1},{1,0},{2,3},{3,2},{4,5},{5,4},{6,7},{7,6},{8,9},{9,8},{10,11... | collective-permute-start | bytes 786440 | tf_op jit(solution)/shard_map/ppermute | solution.py:525
  1.2 5.8 %collective-permute-start.2 = (bf16[128,1024]{1,0:T(8,128)(2,1)}, bf16[128,1024]{1,0:T(8,128)(2,1)S(1)}, u32[]{:S(2)}, u32[]{:S(2)}) collective-permute-start(bf16[128,1024]{1,0:T(8,128)(2,1)} %refs_2_.1), channel_id=1, source_target_pairs={{0,1},{1,0},{2,3},{3,2},{4,5},{5,4},{6,7},{7,6},{8,9},{9,8},{10,11... | collective-permute-start | bytes 786440 | tf_op jit(solution)/shard_map/ppermute | solution.py:525
  2.6 8.3 %collective-permute-start.4 = (bf16[128,384]{1,0:T(8,128)(2,1)S(1)}, bf16[128,384]{1,0:T(8,128)(2,1)S(1)}, u32[]{:S(2)}, u32[]{:S(2)}) collective-permute-start(bf16[128,384]{1,0:T(8,128)(2,1)S(1)} %dynamic_slice.6), channel_id=1, source_target_pairs={{0,2},{1,3},{2,0},{3,1},{4,7},{5,6},{6,5},{7,4},{8,10},{9,11},{10,... | collective-permute-start | bytes 294920 | tf_op jit(solution)/shard_map/ppermute | solution.py:525
  6.2 7.8 %collective-permute-start.9 = (bf16[256,384]{1,0:T(8,128)(2,1)S(1)}, bf16[256,384]{1,0:T(8,128)(2,1)S(1)}, u32[]{:S(2)}, u32[]{:S(2)}) collective-permute-start(bf16[256,384]{1,0:T(8,128)(2,1)S(1)} %constant_dynamic-slice_fusion), channel_id=1, source_target_pairs={{0,2},{1,3},{2,0},{3,1},{4,6},{5,7},{6,4},{7,5},{8,11},{9,10},{10,... | collective-permute-start | bytes 589832 | tf_op jit(solution)/shard_map/ppermute | solution.py:525
  7.0 14.5 %copy-start.1 = (bf16[16,3072]{1,0:T(8,128)(2,1)S(1)}, bf16[16,3072]{1,0:T(8,128)(2,1)}, u32[]{:S(2)}) copy-start(bf16[16,3072]{1,0:T(8,128)(2,1)} %refs_10_.1) | copy-start | bytes 294916
  7.0 14.5 %copy-start.2 = (bf16[1024,16]{0,1:T(8,128)(2,1)S(1)}, bf16[1024,16]{0,1:T(8,128)(2,1)}, u32[]{:S(2)}) copy-start(bf16[1024,16]{0,1:T(8,128)(2,1)} %param.12) | copy-start | bytes 98308
  8.8 12.1 %collective-permute-start.11 = (bf16[128,1024]{1,0:T(8,128)(2,1)S(1)}, bf16[128,1024]{1,0:T(8,128)(2,1)S(1)}, u32[]{:S(2)}, u32[]{:S(2)}) collective-permute-start(bf16[128,1024]{1,0:T(8,128)(2,1)S(1)} %get-tuple-element.45.refs_2_), channel_id=1, source_target_pairs={{0,2},{1,3},{2,0},{3,1},{4,6},{5,7},{6,4},{7,5},{8,10},{9,11},{10,... | collective-permute-start | bytes 786440 | tf_op jit(solution)/shard_map/ppermute | solution.py:525
  10.8 4.6 %collective-permute-start.6 = (bf16[128,384]{1,0:T(8,128)(2,1)S(1)}, bf16[128,384]{1,0:T(8,128)(2,1)S(1)}, u32[]{:S(2)}, u32[]{:S(2)}) collective-permute-start(bf16[128,384]{1,0:T(8,128)(2,1)S(1)} %collective-permute-done.4.refs_4_), channel_id=1, source_target_pairs={{0,8},{1,9},{2,10},{3,11},{4,12},{5,13},{6,14},{7,15},{8,0},{9,1},... | collective-permute-start | bytes 294920 | tf_op jit(solution)/shard_map/ppermute | solution.py:525
  12.2 5.4 %collective-permute-start.5 = (bf16[128,384]{1,0:T(8,128)(2,1)S(1)}, bf16[128,384]{1,0:T(8,128)(2,1)S(1)}, u32[]{:S(2)}, u32[]{:S(2)}) collective-permute-start(bf16[128,384]{1,0:T(8,128)(2,1)S(1)} %collective-permute-done.4.refs_4_), channel_id=1, source_target_pairs={{0,4},{1,5},{2,6},{3,7},{4,0},{5,1},{6,2},{7,3},{8,12},{9,13},{10,... | collective-permute-start | bytes 294920 | tf_op jit(solution)/shard_map/ppermute | solution.py:525
  14.0 7.5 %collective-permute-start.10 = (bf16[256,384]{1,0:T(8,128)(2,1)S(1)}, bf16[256,384]{1,0:T(8,128)(2,1)S(1)}, u32[]{:S(2)}, u32[]{:S(2)}) collective-permute-start(bf16[256,384]{1,0:T(8,128)(2,1)S(1)} %collective-permute-done.9.refs_9_), channel_id=1, source_target_pairs={{0,8},{1,9},{2,10},{3,11},{4,12},{5,13},{6,14},{7,15},{8,0},{9,1},... | collective-permute-start | bytes 589832 | tf_op jit(solution)/shard_map/ppermute | solution.py:525
  15.5 5.4 %collective-permute-start.7 = (bf16[96,384]{1,0:T(8,128)(2,1)S(1)}, bf16[96,384]{1,0:T(8,128)(2,1)S(1)}, u32[]{:S(2)}, u32[]{:S(2)}) collective-permute-start(bf16[96,384]{1,0:T(8,128)(2,1)S(1)} %get-tuple-element.47), channel_id=1, source_target_pairs={{0,4},{1,5},{2,6},{3,7},{4,0},{5,1},{6,2},{7,3},{8,12},{9,13},{10,... | collective-permute-start | bytes 221192 | tf_op jit(solution)/shard_map/ppermute | solution.py:525
  17.1 3.8 %collective-permute-start.8 = (bf16[32,384]{1,0:T(8,128)(2,1)S(1)}, bf16[32,384]{1,0:T(8,128)(2,1)S(1)}, u32[]{:S(2)}, u32[]{:S(2)}) collective-permute-start(bf16[32,384]{1,0:T(8,128)(2,1)S(1)} %get-tuple-element.48), channel_id=1, source_target_pairs={{0,4},{1,5},{2,6},{3,7},{4,0},{5,1},{6,2},{7,3},{8,12},{9,13},{10,... | collective-permute-start | bytes 73736 | tf_op jit(solution)/shard_map/ppermute | solution.py:525
  17.5 5.6 %collective-permute-start.3 = (bf16[128,512]{1,0:T(8,128)(2,1)S(1)}, bf16[128,512]{1,0:T(8,128)(2,1)S(1)}, u32[]{:S(2)}, u32[]{:S(2)}) collective-permute-start(bf16[128,512]{1,0:T(8,128)(2,1)S(1)} %get-tuple-element.42), channel_id=1, source_target_pairs={{0,2},{1,3},{2,0},{3,1},{4,6},{5,7},{6,4},{7,5},{8,10},{9,11},{10,... | collective-permute-start | bytes 393224 | tf_op jit(solution)/shard_map/ppermute | solution.py:525
  20.9 2.9 %collective-permute-start.14 = (bf16[80,1024]{1,0:T(8,128)(2,1)S(1)}, bf16[80,1024]{1,0:T(8,128)(2,1)S(1)}, u32[]{:S(2)}, u32[]{:S(2)}) collective-permute-start(bf16[80,1024]{1,0:T(8,128)(2,1)S(1)} %get-tuple-element.52), channel_id=1, source_target_pairs={{0,1},{1,0},{2,3},{3,2},{4,5},{5,4},{6,7},{7,6},{8,9},{9,8},{10,11... | collective-permute-start | bytes 491528 | tf_op jit(solution)/shard_map/ppermute | solution.py:525
  21.0 2.8 %collective-permute-start.15 = (bf16[48,1024]{1,0:T(8,128)(2,1)S(1)}, bf16[48,1024]{1,0:T(8,128)(2,1)S(1)}, u32[]{:S(2)}, u32[]{:S(2)}) collective-permute-start(bf16[48,1024]{1,0:T(8,128)(2,1)S(1)} %get-tuple-element.53), channel_id=1, source_target_pairs={{0,1},{1,0},{2,3},{3,2},{4,5},{5,4},{6,7},{7,6},{8,9},{9,8},{10,11... | collective-permute-start | bytes 294920 | tf_op jit(solution)/shard_map/ppermute | solution.py:525
  23.2 1.5 %copy-start.3 = (f32[4]{0:T(128)S(1)}, f32[4]{0:T(128)}, u32[]{:S(2)}) copy-start(f32[4]{0:T(128)} %refs_0_.3) | copy-start | bytes 52
  23.2 1.4 %collective-permute-start.12 = (bf16[96,256]{1,0:T(8,128)(2,1)S(1)}, bf16[96,256]{1,0:T(8,128)(2,1)S(1)}, u32[]{:S(2)}, u32[]{:S(2)}) collective-permute-start(bf16[96,256]{1,0:T(8,128)(2,1)S(1)} %get-tuple-element.50), channel_id=1, source_target_pairs={{0,1},{1,0},{2,3},{3,2},{4,5},{5,4},{6,7},{7,6},{8,9},{9,8},{10,11... | collective-permute-start | bytes 147464 | tf_op jit(solution)/shard_map/ppermute | solution.py:525
  23.4 1.3 %collective-permute-start.13 = (bf16[32,256]{1,0:T(8,128)(2,1)S(1)}, bf16[32,256]{1,0:T(8,128)(2,1)S(1)}, u32[]{:S(2)}, u32[]{:S(2)}) collective-permute-start(bf16[32,256]{1,0:T(8,128)(2,1)S(1)} %get-tuple-element.51), channel_id=1, source_target_pairs={{0,1},{1,0},{2,3},{3,2},{4,5},{5,4},{6,7},{7,6},{8,9},{9,8},{10,11... | collective-permute-start | bytes 49160 | tf_op jit(solution)/shard_map/ppermute | solution.py:525
  29.6 1.6 %collective-permute-start.16 = (bf16[128,1024]{1,0:T(8,128)(2,1)S(1)}, bf16[128,1024]{1,0:T(8,128)(2,1)S(1)}, u32[]{:S(2)}, u32[]{:S(2)}) collective-permute-start(bf16[128,1024]{1,0:T(8,128)(2,1)S(1)} %get-tuple-element.61), channel_id=1, source_target_pairs={{0,1},{1,0},{2,3},{3,2},{4,5},{5,4},{6,7},{7,6},{8,9},{9,8},{10,11... | collective-permute-start | bytes 786440 | tf_op jit(solution)/shard_map/ppermute | solution.py:525
  30.0 4.0 %collective-permute-start.17 = (bf16[16,1280]{1,0:T(8,128)(2,1)S(1)}, bf16[16,1280]{1,0:T(8,128)(2,1)S(1)}, u32[]{:S(2)}, u32[]{:S(2)}) collective-permute-start(bf16[16,1280]{1,0:T(8,128)(2,1)S(1)} %get-tuple-element.59.pack.refs_0_), channel_id=1, source_target_pairs={{0,2},{1,3},{2,0},{3,1},{4,6},{5,7},{6,4},{7,5},{8,10},{9,11},{10,... | collective-permute-start | bytes 122888 | tf_op jit(solution)/shard_map/ppermute | solution.py:525
  31.3 8.6 %collective-permute-start.20 = (bf16[128,1024]{1,0:T(8,128)(2,1)S(1)}, bf16[128,1024]{1,0:T(8,128)(2,1)S(1)}, u32[]{:S(2)}, u32[]{:S(2)}) collective-permute-start(bf16[128,1024]{1,0:T(8,128)(2,1)S(1)} %add.42.refs_0_), channel_id=1, source_target_pairs={{0,2},{1,3},{2,0},{3,1},{4,6},{5,7},{6,4},{7,5},{8,10},{9,11},{10,... | collective-permute-start | bytes 786440 | tf_op jit(solution)/shard_map/ppermute | solution.py:525
  34.0 3.4 %copy-start = (bf16[128,1024]{1,0:T(8,128)(2,1)S(1)}, bf16[128,1024]{1,0:T(8,128)(2,1)}, u32[]{:S(2)}) copy-start(bf16[128,1024]{1,0:T(8,128)(2,1)} %tokens.3) | copy-start | bytes 786436
  34.8 2.7 %collective-permute-start.18 = (bf16[112,1024]{1,0:T(8,128)(2,1)S(1)}, bf16[112,1024]{1,0:T(8,128)(2,1)S(1)}, u32[]{:S(2)}, u32[]{:S(2)}) collective-permute-start(bf16[112,1024]{1,0:T(8,128)(2,1)S(1)} %get-tuple-element.63), channel_id=1, source_target_pairs={{0,1},{1,0},{2,3},{3,2},{4,5},{5,4},{6,7},{7,6},{8,9},{9,8},{10,11... | collective-permute-start | bytes 688136 | tf_op jit(solution)/shard_map/ppermute | solution.py:525
  34.9 1.5 %collective-permute-start.21 = (bf16[16,1280]{1,0:T(8,128)(2,1)S(1)}, bf16[16,1280]{1,0:T(8,128)(2,1)S(1)}, u32[]{:S(2)}, u32[]{:S(2)}) collective-permute-start(bf16[16,1280]{1,0:T(8,128)(2,1)S(1)} %get-tuple-element.59.pack.refs_0_), channel_id=1, source_target_pairs={{0,1},{1,0},{2,3},{3,2},{4,5},{5,4},{6,7},{7,6},{8,9},{9,8},{10,11... | collective-permute-start | bytes 122888 | tf_op jit(solution)/shard_map/ppermute | solution.py:525
  35.3 1.2 %collective-permute-start.22 = (bf16[16,1280]{1,0:T(8,128)(2,1)S(1)}, bf16[16,1280]{1,0:T(8,128)(2,1)S(1)}, u32[]{:S(2)}, u32[]{:S(2)}) collective-permute-start(bf16[16,1280]{1,0:T(8,128)(2,1)S(1)} %collective-permute-done.17.refs_1_.refs_2_), channel_id=1, source_target_pairs={{0,1},{1,0},{2,3},{3,2},{4,5},{5,4},{6,7},{7,6},{8,9},{9,8},{10,11... | collective-permute-start | bytes 122888 | tf_op jit(solution)/shard_map/ppermute | solution.py:525
  35.4 2.0 %collective-permute-start.19 = (bf16[16,1024]{1,0:T(8,128)(2,1)S(1)}, bf16[16,1024]{1,0:T(8,128)(2,1)S(1)}, u32[]{:S(2)}, u32[]{:S(2)}) collective-permute-start(bf16[16,1024]{1,0:T(8,128)(2,1)S(1)} %get-tuple-element.64), channel_id=1, source_target_pairs={{0,1},{1,0},{2,3},{3,2},{4,5},{5,4},{6,7},{7,6},{8,9},{9,8},{10,11... | collective-permute-start | bytes 98312 | tf_op jit(solution)/shard_map/ppermute | solution.py:525

commit v9 on v8

--- a/solution.py
+++ b/solution.py
@@ -446,6 +446,40 @@
     )(*vmem(held), *vmem(terms))
 
 
+def shares_kernel(chips, pair_cols, weight, *refs):
+    r, d = lax.axis_index("rows"), lax.axis_index("dp")
+    outs, sems = refs[:-1], refs[-1]
+    cols = pair_cols + outs[0].shape[1]
+    copies = []
+    for i, j in enumerate(chips):
+        half = outs[2 * i].shape[0]
+        row = pl.multiple_of(lax.div(lax.rem(d, 4), 2) * half, 16)
+        col = pl.multiple_of((r ^ (j + lax.rem(d, 2))) * cols + pair_cols, 128)
+        copies.append((weight.at[pl.ds(row, half), pl.ds(col, cols - pair_cols)], outs[2 * i]))
+        col = pl.multiple_of((r ^ (j + lax.rem(lax.div(d, 2), 2))) * cols, 128)
+        copies.append((weight.at[:, pl.ds(col, pair_cols)], outs[2 * i + 1]))
+    copies = [pltpu.make_async_copy(a, b, sems.at[i]) for i, (a, b) in enumerate(copies)]
+    for c in copies:
+        c.start()
+    for c in copies:
+        c.wait()
+
+
+def shares_call(weight, chips, cols, pair_cols):
+    rows = weight.shape[0]
+    count = 2 * len(chips)
+    return pl.pallas_call(
+        functools.partial(shares_kernel, chips, pair_cols),
+        out_shape=[in_vmem((rows // 2, cols - pair_cols), BF), in_vmem((rows, pair_cols), BF)] * len(chips),
+        in_specs=[pl.BlockSpec(memory_space=pltpu.HBM)],
+        out_specs=whole_vmem(count),
+        scratch_shapes=[pltpu.SemaphoreType.DMA((count,))],
+        compiler_params=pltpu.CompilerParams(vmem_limit_bytes=VMEM),
+        cost_estimate=SMALL,
+        name="shares",
+    )(*hbm([weight]))
+
+
 def prepare_kernel(chips, head_cols, sizes, features, gain_map, tokens, core_tokens, cot, *refs):
     count, outs = len(sizes), len(sizes) + len(chips)
     normed, core_normed, gain, inv_rms = refs[count : count + 4]
@@ -537,13 +571,13 @@
     pair_cols = cols // 2 if cols % 256 == 0 else cols
     half = k_rows // 2
     pair, quad = [], []
-    for j in chips:
-        if pair_cols < cols:
-            start = (d % 4 // 2 * half, (r ^ (j + d % 2)) * cols + pair_cols)
-            x = lax.dynamic_slice(weight, start, (half, cols - pair_cols))
-            quad.append(send(x, lambda a, b, j=j: (a, b ^ (j + a % 2))))
-        x = lax.dynamic_slice(weight, (0, (r ^ (j + d // 2 % 2)) * cols), (k_rows, pair_cols))
-        pair.append(send(x, lambda a, b, j=j: (a, b ^ (j + a // 2 % 2))))
+    if pair_cols < cols:
+        pieces = shares_call(weight, chips, cols, pair_cols)
+        quad, pair = list(pieces[0::2]), list(pieces[1::2])
+    else:
+        pair = [lax.dynamic_slice(weight, (0, (r ^ (j + d // 2 % 2)) * cols), (k_rows, cols)) for j in chips]
+    quad = [send(x, lambda a, b, j=j: (a, b ^ (j + a % 2))) for x, j in zip(quad, chips)]
+    pair = [send(x, lambda a, b, j=j: (a, b ^ (j + a // 2 % 2))) for x, j in zip(pair, chips)]
 
     core_weight, core_tokens, core_cot = (to_row(x, 1) for x in (weight, tokens, cot_all))
 

time: 41 us -> 40 us (0.976)
  starting transfers between devices: 15.7 us -> 18.5 us
  waiting for transfers between devices: 9.8 us -> 7 us
  local copies, waits for them, and re-layouts: 1.87 us -> 0.02 us
  Pallas kernels: 11.8 us -> 12.8 us
    ppermute x23, waiting for transfers between devices: 9.8 us -> 7 us  [send(): return lax.ppermute(x, axes, perm)]
    ppermute x23, starting transfers between devices: 15.7 us -> 18.5 us  [send(): return lax.ppermute(x, axes, perm)]
    dynamic_slice x2 -> x0, local copies, waits for them, and re-layouts: 1.85 us -> none  [the longest x1 0.95 us: per_device(): lax.dynamic_slice(weight, (0, (r ^ j + d // 2 % 2) * cols), (k_rows, pair...]
    pallas_call x0 -> x1, Pallas kernels: none -> 0.99 us  [shares_call(): pl.pallas_call(functools.partial(shares_kernel, chips, pair_cols), out_sh...]
  transfers between devices with their start and end apart: 23 -> 23, of which waited for: 9 -> 8; matrix products, arithmetic and copies ran while one was open for 5% -> 0% of each run, Pallas kernels for 15% -> 18%
where the time goes in v9:
time: 40 us; the launch traced here: 39.8 us
  starting transfers between devices  18.5 us (46%)
  Pallas kernels  12.8 us (32%)
  waiting for transfers between devices  7 us (18%)
  between operations  1.47 us (4%)
    ppermute x23, starting transfers between devices, send(): return lax.ppermute(x, axes, perm)  18.5 us
    ppermute x23, waiting for transfers between devices, send(): return lax.ppermute(x, axes, perm)  7 us
    pallas_call x1, Pallas kernels, attention_call(): pl.pallas_call(functools.partial(attention_kernel, cols // (3 * HEAD), to...  4.96 us
    pallas_call x1, Pallas kernels, prepare_call(): pl.pallas_call(functools.partial(prepare_kernel, chips, head_cols, [size...  1.7 us
    pallas_call x1, Pallas kernels, qkv_call(): pl.pallas_call(functools.partial(qkv_kernel, n, x_from, w_from), out_shap...  1.67 us
    pallas_call x1, Pallas kernels, shares_call(): pl.pallas_call(functools.partial(shares_kernel, chips, pair_cols), out_sh...  0.99 us
    pallas_call x1, Pallas kernels, adapter_call(): pl.pallas_call(functools.partial(adapter_kernel, tok, places), out_shape=...  0.89 us
    pallas_call x1, Pallas kernels, final_call(): pl.pallas_call(final_kernel, out_shape=jax.ShapeDtypeStruct(shape, BF), i...  0.84 us
  transfers between devices with their start and end apart: 23, of which 8 were waited for; matrix products, arithmetic and copies ran while one was open for 0% of the time, Pallas kernels for 18%

profile of v9, /device:TPU:0, one launch (start us, length us, event | category | flops | bytes accessed | tf_op | source)
XLA Modules:
  0.0 39.8 jit_solution(1517935589396854682)
XLA Ops:
  0.6 0.5 %collective-permute-start.1 = (bf16[256,3072]{1,0:T(8,128)(2,1)}, bf16[256,3072]{1,0:T(8,128)(2,1)S(1)}, u32[]{:S(2)}, u32[]{:S(2)}) collective-permute-start(bf16[256,3072]{1,0:T(8,128)(2,1)} %weight.1), channel_id=1, source_target_pairs={{0,1},{1,0},{2,3},{3,2},{4,5},{5,4},{6,7},{7,6},{8,9},{9,8},{10,11... | collective-permute-start | bytes 4718600 | tf_op jit(solution)/shard_map/ppermute | solution.py:559
  1.2 0.4 %collective-permute-start.2 = (bf16[128,1024]{1,0:T(8,128)(2,1)}, bf16[128,1024]{1,0:T(8,128)(2,1)S(1)}, u32[]{:S(2)}, u32[]{:S(2)}) collective-permute-start(bf16[128,1024]{1,0:T(8,128)(2,1)} %refs_2_.1), channel_id=1, source_target_pairs={{0,1},{1,0},{2,3},{3,2},{4,5},{5,4},{6,7},{7,6},{8,9},{9,8},{10,11... | collective-permute-start | bytes 786440 | tf_op jit(solution)/shard_map/ppermute | solution.py:559
  1.7 1.0 %shares.1 = (bf16[128,384]{1,0:T(8,128)(2,1)S(1)}, bf16[256,384]{1,0:T(8,128)(2,1)S(1)}) custom-call(bf16[256,3072]{1,0:T(8,128)(2,1)} %weight.1), custom_call_target="tpu_custom_call" | custom-call | flops 1 | bytes 1 | tf_op jit(solution)/shard_map/shares/pallas_call | solution.py:471
  2.7 2.7 %collective-permute-start.4 = (bf16[128,384]{1,0:T(8,128)(2,1)S(1)}, bf16[128,384]{1,0:T(8,128)(2,1)S(1)}, u32[]{:S(2)}, u32[]{:S(2)}) collective-permute-start(bf16[128,384]{1,0:T(8,128)(2,1)S(1)} %get-tuple-element.49), channel_id=1, source_target_pairs={{0,2},{1,3},{2,0},{3,1},{4,7},{5,6},{6,5},{7,4},{8,10},{9,11},{10,... | collective-permute-start | bytes 294920 | tf_op jit(solution)/shard_map/ppermute | solution.py:559
  6.2 1.7 %prepare.1 = (bf16[128,1024]{1,0:T(8,128)(2,1)S(1)}, bf16[128,1024]{1,0:T(8,128)(2,1)S(1)}, f32[1,1024]{1,0:T(1,128)S(1)}, f32[128,1]{1,0:T(8,128)S(1)}, bf16[25...) custom-call(f32[2,128]{1,0:T(2,128)S(1)} %pad_maximum_fusion.feature, ...), custom_call_target="tpu_custom_call" | custom-call | flops 1 | bytes 1 | tf_op jit(solution)/shard_map/prepare/pallas_call | solution.py:521
  7.9 2.0 %collective-permute-start.11 = (bf16[128,1024]{1,0:T(8,128)(2,1)S(1)}, bf16[128,1024]{1,0:T(8,128)(2,1)S(1)}, u32[]{:S(2)}, u32[]{:S(2)}) collective-permute-start(bf16[128,1024]{1,0:T(8,128)(2,1)S(1)} %get-tuple-element.47.refs_2_), channel_id=1, source_target_pairs={{0,2},{1,3},{2,0},{3,1},{4,6},{5,7},{6,4},{7,5},{8,10},{9,11},{10,... | collective-permute-start | bytes 786440 | tf_op jit(solution)/shard_map/ppermute | solution.py:559
  9.9 1.5 %collective-permute-start.6 = (bf16[128,384]{1,0:T(8,128)(2,1)S(1)}, bf16[128,384]{1,0:T(8,128)(2,1)S(1)}, u32[]{:S(2)}, u32[]{:S(2)}) collective-permute-start(bf16[128,384]{1,0:T(8,128)(2,1)S(1)} %collective-permute-done.4.refs_4_), channel_id=1, source_target_pairs={{0,8},{1,9},{2,10},{3,11},{4,12},{5,13},{6,14},{7,15},{8,0},{9,1},... | collective-permute-start | bytes 294920 | tf_op jit(solution)/shard_map/ppermute | solution.py:559
  11.4 1.5 %collective-permute-start.5 = (bf16[128,384]{1,0:T(8,128)(2,1)S(1)}, bf16[128,384]{1,0:T(8,128)(2,1)S(1)}, u32[]{:S(2)}, u32[]{:S(2)}) collective-permute-start(bf16[128,384]{1,0:T(8,128)(2,1)S(1)} %collective-permute-done.4.refs_4_), channel_id=1, source_target_pairs={{0,4},{1,5},{2,6},{3,7},{4,0},{5,1},{6,2},{7,3},{8,12},{9,13},{10,... | collective-permute-start | bytes 294920 | tf_op jit(solution)/shard_map/ppermute | solution.py:559
  12.9 0.3 collective-permute-done.9.refs_9_
  13.2 1.1 %collective-permute-start.10 = (bf16[256,384]{1,0:T(8,128)(2,1)S(1)}, bf16[256,384]{1,0:T(8,128)(2,1)S(1)}, u32[]{:S(2)}, u32[]{:S(2)}) collective-permute-start(bf16[256,384]{1,0:T(8,128)(2,1)S(1)} %collective-permute-done.9.refs_9_), channel_id=1, source_target_pairs={{0,8},{1,9},{2,10},{3,11},{4,12},{5,13},{6,14},{7,15},{8,0},{9,1},... | collective-permute-start | bytes 589832 | tf_op jit(solution)/shard_map/ppermute | solution.py:559
  14.3 0.2 collective-permute-done.6.refs_0_.refs_6_
  14.5 1.6 %collective-permute-start.7 = (bf16[96,384]{1,0:T(8,128)(2,1)S(1)}, bf16[96,384]{1,0:T(8,128)(2,1)S(1)}, u32[]{:S(2)}, u32[]{:S(2)}) collective-permute-start(bf16[96,384]{1,0:T(8,128)(2,1)S(1)} %get-tuple-element.50), channel_id=1, source_target_pairs={{0,4},{1,5},{2,6},{3,7},{4,0},{5,1},{6,2},{7,3},{8,12},{9,13},{10,... | collective-permute-start | bytes 221192 | tf_op jit(solution)/shard_map/ppermute | solution.py:559
  16.1 0.5 %collective-permute-start.8 = (bf16[32,384]{1,0:T(8,128)(2,1)S(1)}, bf16[32,384]{1,0:T(8,128)(2,1)S(1)}, u32[]{:S(2)}, u32[]{:S(2)}) collective-permute-start(bf16[32,384]{1,0:T(8,128)(2,1)S(1)} %get-tuple-element.51), channel_id=1, source_target_pairs={{0,4},{1,5},{2,6},{3,7},{4,0},{5,1},{6,2},{7,3},{8,12},{9,13},{10,... | collective-permute-start | bytes 73736 | tf_op jit(solution)/shard_map/ppermute | solution.py:559
  16.6 1.3 %collective-permute-start.3 = (bf16[128,512]{1,0:T(8,128)(2,1)S(1)}, bf16[128,512]{1,0:T(8,128)(2,1)S(1)}, u32[]{:S(2)}, u32[]{:S(2)}) collective-permute-start(bf16[128,512]{1,0:T(8,128)(2,1)S(1)} %get-tuple-element.44), channel_id=1, source_target_pairs={{0,2},{1,3},{2,0},{3,1},{4,6},{5,7},{6,4},{7,5},{8,10},{9,11},{10,... | collective-permute-start | bytes 393224 | tf_op jit(solution)/shard_map/ppermute | solution.py:559
  17.9 2.1 %collective-permute-done.8.refs_8_.refs_3_ = bf16[32,384]{1,0:T(8,128)(2,1)S(1)} collective-permute-done((bf16[32,384]{1,0:T(8,128)(2,1)S(1)}, bf16[32,384]{1,0:T(8,128)(2,1)S(1)}, u32[]{:S(2)}, u32[]{:S(2)}) %collective-permute-start.8) | collective-permute-done | bytes 24608 | tf_op jit(solution)/shard_map/ppermute | solution.py:559
  20.1 0.5 %collective-permute-start.15 = (bf16[48,1024]{1,0:T(8,128)(2,1)S(1)}, bf16[48,1024]{1,0:T(8,128)(2,1)S(1)}, u32[]{:S(2)}, u32[]{:S(2)}) collective-permute-start(bf16[48,1024]{1,0:T(8,128)(2,1)S(1)} %get-tuple-element.57), channel_id=1, source_target_pairs={{0,1},{1,0},{2,3},{3,2},{4,5},{5,4},{6,7},{7,6},{8,9},{9,8},{10,11... | collective-permute-start | bytes 294920 | tf_op jit(solution)/shard_map/ppermute | solution.py:559
  20.6 1.7 %qkv.1 = (bf16[384,1024]{1,0:T(8,128)(2,1)S(1)}, bf16[1024,768]{1,0:T(8,128)(2,1)S(1)}, bf16[768,384]{1,0:T(8,128)(2,1)S(1)}, bf16[16,384]{1,0:T(8,128)(2,1)S(1)}) custom-call(bf16[256,768]{1,0:T(8,128)(2,1)S(1)} %get-tuple-element.45.refs_0_, bf16[256,768]{1,0:T(8,128)(2,1)S(1)} %get-tuple-element.46.refs_1_, ...), custom_call_target="tpu_custom_call" | custom-call | flops 1 | bytes 1 | tf_op jit(solution)/shard_map/qkv/pallas_call | solution.py:179
  22.4 0.4 %collective-permute-start.13 = (bf16[32,256]{1,0:T(8,128)(2,1)S(1)}, bf16[32,256]{1,0:T(8,128)(2,1)S(1)}, u32[]{:S(2)}, u32[]{:S(2)}) collective-permute-start(bf16[32,256]{1,0:T(8,128)(2,1)S(1)} %get-tuple-element.55), channel_id=1, source_target_pairs={{0,1},{1,0},{2,3},{3,2},{4,5},{5,4},{6,7},{7,6},{8,9},{9,8},{10,11... | collective-permute-start | bytes 49160 | tf_op jit(solution)/shard_map/ppermute | solution.py:559
  22.9 0.8 %last_qkv.1 = (bf16[128,1024]{1,0:T(8,128)(2,1)S(1)}, bf16[768,512]{1,0:T(8,128)(2,1)S(1)}, bf16[16,512]{1,0:T(8,128)(2,1)S(1)}) custom-call(bf16[80,1024]{1,0:T(8,128)(2,1)S(1)} %collective-permute-done.14.refs_0_, bf16[48,1024]{1,0:T(8,128)(2,1)S(1)} %collective-permute-done.15.refs_1_, bf16[1024,768]{1,0:T(8,128)(2,1)S(1)} %get-tuple-element.58.refs_2_.refs_8_.w_all, ...), custom_call_target="tpu_custom_call" | custom-call | flops 1 | bytes 1 | tf_op jit(solution)/shard_map/last_qkv/pallas_call | solution.py:119
  23.7 5.0 %attention_grads.1 = (f32[128,1024]{1,0:T(8,128)S(1)}, bf16[128,1024]{1,0:T(8,128)(2,1)S(1)}, bf16[768,512]{1,0:T(8,128)(2,1)S(1)}, bf16[16,1280]{1,0:T(8,128)(2,1)S(1)}) custom-call(f32[4]{0:T(128)S(1)} %copy-done.3, bf16[128,256]{1,0:T(8,128)(2,1)S(1)} %get-tuple-element.42.refs_1_, bf16[128,256]{1,0:T(8,128)(2,1)S(1)} %get-tuple-element.43.refs_2_, ...), custom_call_target="tpu_custom_call" | custom-call | flops 1 | bytes 1 | tf_op jit(solution)/shard_map/attention_grads/pallas_call | solution.py:273
  28.7 0.4 %collective-permute-start.16 = (bf16[128,1024]{1,0:T(8,128)(2,1)S(1)}, bf16[128,1024]{1,0:T(8,128)(2,1)S(1)}, u32[]{:S(2)}, u32[]{:S(2)}) collective-permute-start(bf16[128,1024]{1,0:T(8,128)(2,1)S(1)} %get-tuple-element.65), channel_id=1, source_target_pairs={{0,1},{1,0},{2,3},{3,2},{4,5},{5,4},{6,7},{7,6},{8,9},{9,8},{10,11... | collective-permute-start | bytes 786440 | tf_op jit(solution)/shard_map/ppermute | solution.py:559
  29.1 1.4 %collective-permute-start.17 = (bf16[16,1280]{1,0:T(8,128)(2,1)S(1)}, bf16[16,1280]{1,0:T(8,128)(2,1)S(1)}, u32[]{:S(2)}, u32[]{:S(2)}) collective-permute-start(bf16[16,1280]{1,0:T(8,128)(2,1)S(1)} %get-tuple-element.63.pack.refs_0_), channel_id=1, source_target_pairs={{0,2},{1,3},{2,0},{3,1},{4,6},{5,7},{6,4},{7,5},{8,10},{9,11},{10,... | collective-permute-start | bytes 122888 | tf_op jit(solution)/shard_map/ppermute | solution.py:559
  30.5 1.3 %collective-permute-start.20 = (bf16[128,1024]{1,0:T(8,128)(2,1)S(1)}, bf16[128,1024]{1,0:T(8,128)(2,1)S(1)}, u32[]{:S(2)}, u32[]{:S(2)}) collective-permute-start(bf16[128,1024]{1,0:T(8,128)(2,1)S(1)} %add.1.refs_0_), channel_id=1, source_target_pairs={{0,2},{1,3},{2,0},{3,1},{4,6},{5,7},{6,4},{7,5},{8,10},{9,11},{10,... | collective-permute-start | bytes 786440 | tf_op jit(solution)/shard_map/ppermute | solution.py:559
  31.8 1.3 %collective-permute-done.17.refs_1_.refs_2_ = bf16[16,1280]{1,0:T(8,128)(2,1)S(1)} collective-permute-done((bf16[16,1280]{1,0:T(8,128)(2,1)S(1)}, bf16[16,1280]{1,0:T(8,128)(2,1)S(1)}, u32[]{:S(2)}, u32[]{:S(2)}) %collective-permute-start.17) | collective-permute-done | bytes 40992 | tf_op jit(solution)/shard_map/ppermute | solution.py:559
  33.1 0.7 %own_grads.1 = (f32[128,1024]{1,0:T(8,128)S(1)}, bf16[112,1024]{1,0:T(8,128)(2,1)S(1)}, bf16[16,1024]{1,0:T(8,128)(2,1)S(1)}) custom-call(bf16[768,512]{1,0:T(8,128)(2,1)S(1)} %get-tuple-element.62.grad_t, bf16[16,1280]{1,0:T(8,128)(2,1)S(1)} %get-tuple-element.63.pack.refs_0_, bf16[1024,768]{1,0:T(8,128)(2,1)S(1)} %get-tuple-element.58.refs_2_.refs_8_.w_all, ...), custom_call_target="tpu_custom_call" | custom-call | flops 1 | bytes 1 | tf_op jit(solution)/shard_map/own_grads/pallas_call | solution.py:338
  33.9 0.5 %collective-permute-start.21 = (bf16[16,1280]{1,0:T(8,128)(2,1)S(1)}, bf16[16,1280]{1,0:T(8,128)(2,1)S(1)}, u32[]{:S(2)}, u32[]{:S(2)}) collective-permute-start(bf16[16,1280]{1,0:T(8,128)(2,1)S(1)} %get-tuple-element.63.pack.refs_0_), channel_id=1, source_target_pairs={{0,1},{1,0},{2,3},{3,2},{4,5},{5,4},{6,7},{7,6},{8,9},{9,8},{10,11... | collective-permute-start | bytes 122888 | tf_op jit(solution)/shard_map/ppermute | solution.py:559
  34.5 0.4 %collective-permute-start.19 = (bf16[16,1024]{1,0:T(8,128)(2,1)S(1)}, bf16[16,1024]{1,0:T(8,128)(2,1)S(1)}, u32[]{:S(2)}, u32[]{:S(2)}) collective-permute-start(bf16[16,1024]{1,0:T(8,128)(2,1)S(1)} %get-tuple-element.68), channel_id=1, source_target_pairs={{0,1},{1,0},{2,3},{3,2},{4,5},{5,4},{6,7},{7,6},{8,9},{9,8},{10,11... | collective-permute-start | bytes 98312 | tf_op jit(solution)/shard_map/ppermute | solution.py:559
  34.9 0.5 %collective-permute-done.21.refs_1_ = bf16[16,1280]{1,0:T(8,128)(2,1)S(1)} collective-permute-done((bf16[16,1280]{1,0:T(8,128)(2,1)S(1)}, bf16[16,1280]{1,0:T(8,128)(2,1)S(1)}, u32[]{:S(2)}, u32[]{:S(2)}) %collective-permute-start.21) | collective-permute-done | bytes 40992 | tf_op jit(solution)/shard_map/ppermute | solution.py:559
  35.6 0.9 %adapter_grads.1 = (f32[16,1024]{1,0:T(8,128)}, f32[16,3072]{1,0:T(8,128)}) custom-call(bf16[16,1280]{1,0:T(8,128)(2,1)S(1)} %get-tuple-element.63.pack.refs_0_, bf16[16,1280]{1,0:T(8,128)(2,1)S(1)} %collective-permute-done.21.refs_1_, bf16[16,1280]{1,0:T(8,128)(2,1)S(1)} %collective-permute-done.17.refs_1_.refs_2_, ...), custom_call_target="tpu_custom_call" | custom-call | flops 1 | bytes 1 | tf_op jit(solution)/shard_map/adapter_grads/pallas_call | solution.py:371
  36.5 0.2 scale.1
  36.7 2.2 %collective-permute-done.20.refs_0_ = bf16[128,1024]{1,0:T(8,128)(2,1)S(1)} collective-permute-done((bf16[128,1024]{1,0:T(8,128)(2,1)S(1)}, bf16[128,1024]{1,0:T(8,128)(2,1)S(1)}, u32[]{:S(2)}, u32[]{:S(2)}) %collective-permute-start.20) | collective-permute-done | bytes 262176 | tf_op jit(solution)/shard_map/ppermute | solution.py:559
  39.0 0.8 %input_grads.1 = bf16[128,1024]{1,0:T(8,128)(2,1)} custom-call(f32[128,1024]{1,0:T(8,128)S(1)} %get-tuple-element.69.total, f32[128,1024]{1,0:T(8,128)S(1)} %get-tuple-element.70.token_gain, f32[128,1024]{1,0:T(8,128)S(1)} %get-tuple-element.71.scale, f32[128,1024]{1,0:T(8,128)S(1)} %get-tuple-element.72.slope, ...), custom_call_target="tpu_custom_call" | custom-call | flops 1 | bytes 1 | tf_op jit(solution)/shard_map/input_grads/pallas_call | solution.py:437
  (37 shorter events, 1.0 us)
Async XLA Ops:
  0.6 5.5 %collective-permute-start.1 = (bf16[256,3072]{1,0:T(8,128)(2,1)}, bf16[256,3072]{1,0:T(8,128)(2,1)S(1)}, u32[]{:S(2)}, u32[]{:S(2)}) collective-permute-start(bf16[256,3072]{1,0:T(8,128)(2,1)} %weight.1), channel_id=1, source_target_pairs={{0,1},{1,0},{2,3},{3,2},{4,5},{5,4},{6,7},{7,6},{8,9},{9,8},{10,11... | collective-permute-start | bytes 4718600 | tf_op jit(solution)/shard_map/ppermute | solution.py:559
  1.1 5.0 %collective-permute-start = (bf16[128,1024]{1,0:T(8,128)(2,1)}, bf16[128,1024]{1,0:T(8,128)(2,1)S(1)}, u32[]{:S(2)}, u32[]{:S(2)}) collective-permute-start(bf16[128,1024]{1,0:T(8,128)(2,1)} %tokens.3), channel_id=1, source_target_pairs={{0,1},{1,0},{2,3},{3,2},{4,5},{5,4},{6,7},{7,6},{8,9},{9,8},{10,11... | collective-permute-start | bytes 786440 | tf_op jit(solution)/shard_map/ppermute | solution.py:559
  1.2 4.9 %collective-permute-start.2 = (bf16[128,1024]{1,0:T(8,128)(2,1)}, bf16[128,1024]{1,0:T(8,128)(2,1)S(1)}, u32[]{:S(2)}, u32[]{:S(2)}) collective-permute-start(bf16[128,1024]{1,0:T(8,128)(2,1)} %refs_2_.1), channel_id=1, source_target_pairs={{0,1},{1,0},{2,3},{3,2},{4,5},{5,4},{6,7},{7,6},{8,9},{9,8},{10,11... | collective-permute-start | bytes 786440 | tf_op jit(solution)/shard_map/ppermute | solution.py:559
  2.7 7.2 %collective-permute-start.4 = (bf16[128,384]{1,0:T(8,128)(2,1)S(1)}, bf16[128,384]{1,0:T(8,128)(2,1)S(1)}, u32[]{:S(2)}, u32[]{:S(2)}) collective-permute-start(bf16[128,384]{1,0:T(8,128)(2,1)S(1)} %get-tuple-element.49), channel_id=1, source_target_pairs={{0,2},{1,3},{2,0},{3,1},{4,7},{5,6},{6,5},{7,4},{8,10},{9,11},{10,... | collective-permute-start | bytes 294920 | tf_op jit(solution)/shard_map/ppermute | solution.py:559
  5.3 7.9 %collective-permute-start.9 = (bf16[256,384]{1,0:T(8,128)(2,1)S(1)}, bf16[256,384]{1,0:T(8,128)(2,1)S(1)}, u32[]{:S(2)}, u32[]{:S(2)}) collective-permute-start(bf16[256,384]{1,0:T(8,128)(2,1)S(1)} %get-tuple-element.52), channel_id=1, source_target_pairs={{0,2},{1,3},{2,0},{3,1},{4,6},{5,7},{6,4},{7,5},{8,11},{9,10},{10,... | collective-permute-start | bytes 589832 | tf_op jit(solution)/shard_map/ppermute | solution.py:559
  6.1 14.5 %copy-start.1 = (bf16[16,3072]{1,0:T(8,128)(2,1)S(1)}, bf16[16,3072]{1,0:T(8,128)(2,1)}, u32[]{:S(2)}) copy-start(bf16[16,3072]{1,0:T(8,128)(2,1)} %refs_10_.1) | copy-start | bytes 294916
  6.1 14.4 %copy-start.2 = (bf16[1024,16]{0,1:T(8,128)(2,1)S(1)}, bf16[1024,16]{0,1:T(8,128)(2,1)}, u32[]{:S(2)}) copy-start(bf16[1024,16]{0,1:T(8,128)(2,1)} %param.12) | copy-start | bytes 98308
  7.9 12.1 %collective-permute-start.11 = (bf16[128,1024]{1,0:T(8,128)(2,1)S(1)}, bf16[128,1024]{1,0:T(8,128)(2,1)S(1)}, u32[]{:S(2)}, u32[]{:S(2)}) collective-permute-start(bf16[128,1024]{1,0:T(8,128)(2,1)S(1)} %get-tuple-element.47.refs_2_), channel_id=1, source_target_pairs={{0,2},{1,3},{2,0},{3,1},{4,6},{5,7},{6,4},{7,5},{8,10},{9,11},{10,... | collective-permute-start | bytes 786440 | tf_op jit(solution)/shard_map/ppermute | solution.py:559
  9.9 4.6 %collective-permute-start.6 = (bf16[128,384]{1,0:T(8,128)(2,1)S(1)}, bf16[128,384]{1,0:T(8,128)(2,1)S(1)}, u32[]{:S(2)}, u32[]{:S(2)}) collective-permute-start(bf16[128,384]{1,0:T(8,128)(2,1)S(1)} %collective-permute-done.4.refs_4_), channel_id=1, source_target_pairs={{0,8},{1,9},{2,10},{3,11},{4,12},{5,13},{6,14},{7,15},{8,0},{9,1},... | collective-permute-start | bytes 294920 | tf_op jit(solution)/shard_map/ppermute | solution.py:559
  11.4 5.2 %collective-permute-start.5 = (bf16[128,384]{1,0:T(8,128)(2,1)S(1)}, bf16[128,384]{1,0:T(8,128)(2,1)S(1)}, u32[]{:S(2)}, u32[]{:S(2)}) collective-permute-start(bf16[128,384]{1,0:T(8,128)(2,1)S(1)} %collective-permute-done.4.refs_4_), channel_id=1, source_target_pairs={{0,4},{1,5},{2,6},{3,7},{4,0},{5,1},{6,2},{7,3},{8,12},{9,13},{10,... | collective-permute-start | bytes 294920 | tf_op jit(solution)/shard_map/ppermute | solution.py:559
  13.2 7.4 %collective-permute-start.10 = (bf16[256,384]{1,0:T(8,128)(2,1)S(1)}, bf16[256,384]{1,0:T(8,128)(2,1)S(1)}, u32[]{:S(2)}, u32[]{:S(2)}) collective-permute-start(bf16[256,384]{1,0:T(8,128)(2,1)S(1)} %collective-permute-done.9.refs_9_), channel_id=1, source_target_pairs={{0,8},{1,9},{2,10},{3,11},{4,12},{5,13},{6,14},{7,15},{8,0},{9,1},... | collective-permute-start | bytes 589832 | tf_op jit(solution)/shard_map/ppermute | solution.py:559
  14.5 5.4 %collective-permute-start.7 = (bf16[96,384]{1,0:T(8,128)(2,1)S(1)}, bf16[96,384]{1,0:T(8,128)(2,1)S(1)}, u32[]{:S(2)}, u32[]{:S(2)}) collective-permute-start(bf16[96,384]{1,0:T(8,128)(2,1)S(1)} %get-tuple-element.50), channel_id=1, source_target_pairs={{0,4},{1,5},{2,6},{3,7},{4,0},{5,1},{6,2},{7,3},{8,12},{9,13},{10,... | collective-permute-start | bytes 221192 | tf_op jit(solution)/shard_map/ppermute | solution.py:559
  16.1 3.8 %collective-permute-start.8 = (bf16[32,384]{1,0:T(8,128)(2,1)S(1)}, bf16[32,384]{1,0:T(8,128)(2,1)S(1)}, u32[]{:S(2)}, u32[]{:S(2)}) collective-permute-start(bf16[32,384]{1,0:T(8,128)(2,1)S(1)} %get-tuple-element.51), channel_id=1, source_target_pairs={{0,4},{1,5},{2,6},{3,7},{4,0},{5,1},{6,2},{7,3},{8,12},{9,13},{10,... | collective-permute-start | bytes 73736 | tf_op jit(solution)/shard_map/ppermute | solution.py:559
  16.6 5.6 %collective-permute-start.3 = (bf16[128,512]{1,0:T(8,128)(2,1)S(1)}, bf16[128,512]{1,0:T(8,128)(2,1)S(1)}, u32[]{:S(2)}, u32[]{:S(2)}) collective-permute-start(bf16[128,512]{1,0:T(8,128)(2,1)S(1)} %get-tuple-element.44), channel_id=1, source_target_pairs={{0,2},{1,3},{2,0},{3,1},{4,6},{5,7},{6,4},{7,5},{8,10},{9,11},{10,... | collective-permute-start | bytes 393224 | tf_op jit(solution)/shard_map/ppermute | solution.py:559
  20.0 2.9 %collective-permute-start.14 = (bf16[80,1024]{1,0:T(8,128)(2,1)S(1)}, bf16[80,1024]{1,0:T(8,128)(2,1)S(1)}, u32[]{:S(2)}, u32[]{:S(2)}) collective-permute-start(bf16[80,1024]{1,0:T(8,128)(2,1)S(1)} %get-tuple-element.56), channel_id=1, source_target_pairs={{0,1},{1,0},{2,3},{3,2},{4,5},{5,4},{6,7},{7,6},{8,9},{9,8},{10,11... | collective-permute-start | bytes 491528 | tf_op jit(solution)/shard_map/ppermute | solution.py:559
  20.1 2.8 %collective-permute-start.15 = (bf16[48,1024]{1,0:T(8,128)(2,1)S(1)}, bf16[48,1024]{1,0:T(8,128)(2,1)S(1)}, u32[]{:S(2)}, u32[]{:S(2)}) collective-permute-start(bf16[48,1024]{1,0:T(8,128)(2,1)S(1)} %get-tuple-element.57), channel_id=1, source_target_pairs={{0,1},{1,0},{2,3},{3,2},{4,5},{5,4},{6,7},{7,6},{8,9},{9,8},{10,11... | collective-permute-start | bytes 294920 | tf_op jit(solution)/shard_map/ppermute | solution.py:559
  22.3 1.5 %copy-start.3 = (f32[4]{0:T(128)S(1)}, f32[4]{0:T(128)}, u32[]{:S(2)}) copy-start(f32[4]{0:T(128)} %refs_0_.3) | copy-start | bytes 52
  22.3 1.4 %collective-permute-start.12 = (bf16[96,256]{1,0:T(8,128)(2,1)S(1)}, bf16[96,256]{1,0:T(8,128)(2,1)S(1)}, u32[]{:S(2)}, u32[]{:S(2)}) collective-permute-start(bf16[96,256]{1,0:T(8,128)(2,1)S(1)} %get-tuple-element.54), channel_id=1, source_target_pairs={{0,1},{1,0},{2,3},{3,2},{4,5},{5,4},{6,7},{7,6},{8,9},{9,8},{10,11... | collective-permute-start | bytes 147464 | tf_op jit(solution)/shard_map/ppermute | solution.py:559
  22.4 1.3 %collective-permute-start.13 = (bf16[32,256]{1,0:T(8,128)(2,1)S(1)}, bf16[32,256]{1,0:T(8,128)(2,1)S(1)}, u32[]{:S(2)}, u32[]{:S(2)}) collective-permute-start(bf16[32,256]{1,0:T(8,128)(2,1)S(1)} %get-tuple-element.55), channel_id=1, source_target_pairs={{0,1},{1,0},{2,3},{3,2},{4,5},{5,4},{6,7},{7,6},{8,9},{9,8},{10,11... | collective-permute-start | bytes 49160 | tf_op jit(solution)/shard_map/ppermute | solution.py:559
  28.7 1.8 %collective-permute-start.16 = (bf16[128,1024]{1,0:T(8,128)(2,1)S(1)}, bf16[128,1024]{1,0:T(8,128)(2,1)S(1)}, u32[]{:S(2)}, u32[]{:S(2)}) collective-permute-start(bf16[128,1024]{1,0:T(8,128)(2,1)S(1)} %get-tuple-element.65), channel_id=1, source_target_pairs={{0,1},{1,0},{2,3},{3,2},{4,5},{5,4},{6,7},{7,6},{8,9},{9,8},{10,11... | collective-permute-start | bytes 786440 | tf_op jit(solution)/shard_map/ppermute | solution.py:559
  29.1 4.0 %collective-permute-start.17 = (bf16[16,1280]{1,0:T(8,128)(2,1)S(1)}, bf16[16,1280]{1,0:T(8,128)(2,1)S(1)}, u32[]{:S(2)}, u32[]{:S(2)}) collective-permute-start(bf16[16,1280]{1,0:T(8,128)(2,1)S(1)} %get-tuple-element.63.pack.refs_0_), channel_id=1, source_target_pairs={{0,2},{1,3},{2,0},{3,1},{4,6},{5,7},{6,4},{7,5},{8,10},{9,11},{10,... | collective-permute-start | bytes 122888 | tf_op jit(solution)/shard_map/ppermute | solution.py:559
  30.5 8.5 %collective-permute-start.20 = (bf16[128,1024]{1,0:T(8,128)(2,1)S(1)}, bf16[128,1024]{1,0:T(8,128)(2,1)S(1)}, u32[]{:S(2)}, u32[]{:S(2)}) collective-permute-start(bf16[128,1024]{1,0:T(8,128)(2,1)S(1)} %add.1.refs_0_), channel_id=1, source_target_pairs={{0,2},{1,3},{2,0},{3,1},{4,6},{5,7},{6,4},{7,5},{8,10},{9,11},{10,... | collective-permute-start | bytes 786440 | tf_op jit(solution)/shard_map/ppermute | solution.py:559
  33.1 3.4 %copy-start = (bf16[128,1024]{1,0:T(8,128)(2,1)S(1)}, bf16[128,1024]{1,0:T(8,128)(2,1)}, u32[]{:S(2)}) copy-start(bf16[128,1024]{1,0:T(8,128)(2,1)} %tokens.3) | copy-start | bytes 786436
  33.8 2.7 %collective-permute-start.18 = (bf16[112,1024]{1,0:T(8,128)(2,1)S(1)}, bf16[112,1024]{1,0:T(8,128)(2,1)S(1)}, u32[]{:S(2)}, u32[]{:S(2)}) collective-permute-start(bf16[112,1024]{1,0:T(8,128)(2,1)S(1)} %get-tuple-element.67), channel_id=1, source_target_pairs={{0,1},{1,0},{2,3},{3,2},{4,5},{5,4},{6,7},{7,6},{8,9},{9,8},{10,11... | collective-permute-start | bytes 688136 | tf_op jit(solution)/shard_map/ppermute | solution.py:559
  33.9 1.5 %collective-permute-start.21 = (bf16[16,1280]{1,0:T(8,128)(2,1)S(1)}, bf16[16,1280]{1,0:T(8,128)(2,1)S(1)}, u32[]{:S(2)}, u32[]{:S(2)}) collective-permute-start(bf16[16,1280]{1,0:T(8,128)(2,1)S(1)} %get-tuple-element.63.pack.refs_0_), channel_id=1, source_target_pairs={{0,1},{1,0},{2,3},{3,2},{4,5},{5,4},{6,7},{7,6},{8,9},{9,8},{10,11... | collective-permute-start | bytes 122888 | tf_op jit(solution)/shard_map/ppermute | solution.py:559
  34.4 1.2 %collective-permute-start.22 = (bf16[16,1280]{1,0:T(8,128)(2,1)S(1)}, bf16[16,1280]{1,0:T(8,128)(2,1)S(1)}, u32[]{:S(2)}, u32[]{:S(2)}) collective-permute-start(bf16[16,1280]{1,0:T(8,128)(2,1)S(1)} %collective-permute-done.17.refs_1_.refs_2_), channel_id=1, source_target_pairs={{0,1},{1,0},{2,3},{3,2},{4,5},{5,4},{6,7},{7,6},{8,9},{9,8},{10,11... | collective-permute-start | bytes 122888 | tf_op jit(solution)/shard_map/ppermute | solution.py:559
  34.5 2.0 %collective-permute-start.19 = (bf16[16,1024]{1,0:T(8,128)(2,1)S(1)}, bf16[16,1024]{1,0:T(8,128)(2,1)S(1)}, u32[]{:S(2)}, u32[]{:S(2)}) collective-permute-start(bf16[16,1024]{1,0:T(8,128)(2,1)S(1)} %get-tuple-element.68), channel_id=1, source_target_pairs={{0,1},{1,0},{2,3},{3,2},{4,5},{5,4},{6,7},{7,6},{8,9},{9,8},{10,11... | collective-permute-start | bytes 98312 | tf_op jit(solution)/shard_map/ppermute | solution.py:559

commit v10 on v9

--- a/solution.py
+++ b/solution.py
@@ -193,9 +193,8 @@
 
 
 def token_grads(low_grad_t, grad_t, w_all, down_t, at, rows):
-    grad = grad_t[:, pl.ds(at, rows)].T
-    part = contract(grad, w_all[...], 1, 1)
-    return part + contract(low_grad_t[:, pl.ds(at, rows)], down_t[...], 0, 0)
+    low = contract(low_grad_t[:, pl.ds(at, rows)], down_t[...], 0, 0)
+    return low + contract(grad_t[:, pl.ds(at, rows)], w_all[...], 0, 1)
 
 
 def attention_kernel(heads, tok, c_from, first, outs, *refs):

time: 40 us -> 39.6 us (0.990)
  Pallas kernels: 12.8 us -> 12.4 us
where the time goes in v10:
time: 39.6 us; the launch traced here: 39.4 us
  starting transfers between devices  18.5 us (47%)
  Pallas kernels  12.4 us (31%)
  waiting for transfers between devices  6.99 us (18%)
  between operations  1.47 us (4%)
    ppermute x23, starting transfers between devices, send(): return lax.ppermute(x, axes, perm)  18.5 us
    ppermute x23, waiting for transfers between devices, send(): return lax.ppermute(x, axes, perm)  6.99 us
    pallas_call x1, Pallas kernels, attention_call(): pl.pallas_call(functools.partial(attention_kernel, cols // (3 * HEAD), to...  4.58 us
    pallas_call x1, Pallas kernels, prepare_call(): pl.pallas_call(functools.partial(prepare_kernel, chips, head_cols, [size...  1.7 us
    pallas_call x1, Pallas kernels, qkv_call(): pl.pallas_call(functools.partial(qkv_kernel, n, x_from, w_from), out_shap...  1.67 us
    pallas_call x1, Pallas kernels, shares_call(): pl.pallas_call(functools.partial(shares_kernel, chips, pair_cols), out_sh...  0.99 us
    pallas_call x1, Pallas kernels, adapter_call(): pl.pallas_call(functools.partial(adapter_kernel, tok, places), out_shape=...  0.89 us
    pallas_call x1, Pallas kernels, final_call(): pl.pallas_call(final_kernel, out_shape=jax.ShapeDtypeStruct(shape, BF), i...  0.84 us
  transfers between devices with their start and end apart: 23, of which 8 were waited for; matrix products, arithmetic and copies ran while one was open for 0% of the time, Pallas kernels for 18%

profile of v10, /device:TPU:0, one launch (start us, length us, event | category | flops | bytes accessed | tf_op | source)
XLA Modules:
  0.0 39.4 jit_solution(6069164517960497135)
XLA Ops:
  0.6 0.5 %collective-permute-start.1 = (bf16[256,3072]{1,0:T(8,128)(2,1)}, bf16[256,3072]{1,0:T(8,128)(2,1)S(1)}, u32[]{:S(2)}, u32[]{:S(2)}) collective-permute-start(bf16[256,3072]{1,0:T(8,128)(2,1)} %weight.1), channel_id=1, source_target_pairs={{0,1},{1,0},{2,3},{3,2},{4,5},{5,4},{6,7},{7,6},{8,9},{9,8},{10,11... | collective-permute-start | bytes 4718600 | tf_op jit(solution)/shard_map/ppermute | solution.py:558
  1.2 0.4 %collective-permute-start.2 = (bf16[128,1024]{1,0:T(8,128)(2,1)}, bf16[128,1024]{1,0:T(8,128)(2,1)S(1)}, u32[]{:S(2)}, u32[]{:S(2)}) collective-permute-start(bf16[128,1024]{1,0:T(8,128)(2,1)} %refs_2_.1), channel_id=1, source_target_pairs={{0,1},{1,0},{2,3},{3,2},{4,5},{5,4},{6,7},{7,6},{8,9},{9,8},{10,11... | collective-permute-start | bytes 786440 | tf_op jit(solution)/shard_map/ppermute | solution.py:558
  1.7 1.0 %shares.1 = (bf16[128,384]{1,0:T(8,128)(2,1)S(1)}, bf16[256,384]{1,0:T(8,128)(2,1)S(1)}) custom-call(bf16[256,3072]{1,0:T(8,128)(2,1)} %weight.1), custom_call_target="tpu_custom_call" | custom-call | flops 1 | bytes 1 | tf_op jit(solution)/shard_map/shares/pallas_call | solution.py:470
  2.7 2.7 %collective-permute-start.4 = (bf16[128,384]{1,0:T(8,128)(2,1)S(1)}, bf16[128,384]{1,0:T(8,128)(2,1)S(1)}, u32[]{:S(2)}, u32[]{:S(2)}) collective-permute-start(bf16[128,384]{1,0:T(8,128)(2,1)S(1)} %get-tuple-element.49), channel_id=1, source_target_pairs={{0,2},{1,3},{2,0},{3,1},{4,7},{5,6},{6,5},{7,4},{8,10},{9,11},{10,... | collective-permute-start | bytes 294920 | tf_op jit(solution)/shard_map/ppermute | solution.py:558
  6.2 1.7 %prepare.1 = (bf16[128,1024]{1,0:T(8,128)(2,1)S(1)}, bf16[128,1024]{1,0:T(8,128)(2,1)S(1)}, f32[1,1024]{1,0:T(1,128)S(1)}, f32[128,1]{1,0:T(8,128)S(1)}, bf16[25...) custom-call(f32[2,128]{1,0:T(2,128)S(1)} %pad_maximum_fusion.feature, ...), custom_call_target="tpu_custom_call" | custom-call | flops 1 | bytes 1 | tf_op jit(solution)/shard_map/prepare/pallas_call | solution.py:520
  7.9 2.0 %collective-permute-start.11 = (bf16[128,1024]{1,0:T(8,128)(2,1)S(1)}, bf16[128,1024]{1,0:T(8,128)(2,1)S(1)}, u32[]{:S(2)}, u32[]{:S(2)}) collective-permute-start(bf16[128,1024]{1,0:T(8,128)(2,1)S(1)} %get-tuple-element.47.refs_2_), channel_id=1, source_target_pairs={{0,2},{1,3},{2,0},{3,1},{4,6},{5,7},{6,4},{7,5},{8,10},{9,11},{10,... | collective-permute-start | bytes 786440 | tf_op jit(solution)/shard_map/ppermute | solution.py:558
  9.9 1.5 %collective-permute-start.6 = (bf16[128,384]{1,0:T(8,128)(2,1)S(1)}, bf16[128,384]{1,0:T(8,128)(2,1)S(1)}, u32[]{:S(2)}, u32[]{:S(2)}) collective-permute-start(bf16[128,384]{1,0:T(8,128)(2,1)S(1)} %collective-permute-done.4.refs_4_), channel_id=1, source_target_pairs={{0,8},{1,9},{2,10},{3,11},{4,12},{5,13},{6,14},{7,15},{8,0},{9,1},... | collective-permute-start | bytes 294920 | tf_op jit(solution)/shard_map/ppermute | solution.py:558
  11.4 1.5 %collective-permute-start.5 = (bf16[128,384]{1,0:T(8,128)(2,1)S(1)}, bf16[128,384]{1,0:T(8,128)(2,1)S(1)}, u32[]{:S(2)}, u32[]{:S(2)}) collective-permute-start(bf16[128,384]{1,0:T(8,128)(2,1)S(1)} %collective-permute-done.4.refs_4_), channel_id=1, source_target_pairs={{0,4},{1,5},{2,6},{3,7},{4,0},{5,1},{6,2},{7,3},{8,12},{9,13},{10,... | collective-permute-start | bytes 294920 | tf_op jit(solution)/shard_map/ppermute | solution.py:558
  12.9 0.3 collective-permute-done.9.refs_9_
  13.2 1.1 %collective-permute-start.10 = (bf16[256,384]{1,0:T(8,128)(2,1)S(1)}, bf16[256,384]{1,0:T(8,128)(2,1)S(1)}, u32[]{:S(2)}, u32[]{:S(2)}) collective-permute-start(bf16[256,384]{1,0:T(8,128)(2,1)S(1)} %collective-permute-done.9.refs_9_), channel_id=1, source_target_pairs={{0,8},{1,9},{2,10},{3,11},{4,12},{5,13},{6,14},{7,15},{8,0},{9,1},... | collective-permute-start | bytes 589832 | tf_op jit(solution)/shard_map/ppermute | solution.py:558
  14.3 0.2 collective-permute-done.6.refs_0_.refs_6_
  14.5 1.6 %collective-permute-start.7 = (bf16[96,384]{1,0:T(8,128)(2,1)S(1)}, bf16[96,384]{1,0:T(8,128)(2,1)S(1)}, u32[]{:S(2)}, u32[]{:S(2)}) collective-permute-start(bf16[96,384]{1,0:T(8,128)(2,1)S(1)} %get-tuple-element.50), channel_id=1, source_target_pairs={{0,4},{1,5},{2,6},{3,7},{4,0},{5,1},{6,2},{7,3},{8,12},{9,13},{10,... | collective-permute-start | bytes 221192 | tf_op jit(solution)/shard_map/ppermute | solution.py:558
  16.1 0.5 %collective-permute-start.8 = (bf16[32,384]{1,0:T(8,128)(2,1)S(1)}, bf16[32,384]{1,0:T(8,128)(2,1)S(1)}, u32[]{:S(2)}, u32[]{:S(2)}) collective-permute-start(bf16[32,384]{1,0:T(8,128)(2,1)S(1)} %get-tuple-element.51), channel_id=1, source_target_pairs={{0,4},{1,5},{2,6},{3,7},{4,0},{5,1},{6,2},{7,3},{8,12},{9,13},{10,... | collective-permute-start | bytes 73736 | tf_op jit(solution)/shard_map/ppermute | solution.py:558
  16.6 1.3 %collective-permute-start.3 = (bf16[128,512]{1,0:T(8,128)(2,1)S(1)}, bf16[128,512]{1,0:T(8,128)(2,1)S(1)}, u32[]{:S(2)}, u32[]{:S(2)}) collective-permute-start(bf16[128,512]{1,0:T(8,128)(2,1)S(1)} %get-tuple-element.44), channel_id=1, source_target_pairs={{0,2},{1,3},{2,0},{3,1},{4,6},{5,7},{6,4},{7,5},{8,10},{9,11},{10,... | collective-permute-start | bytes 393224 | tf_op jit(solution)/shard_map/ppermute | solution.py:558
  17.9 2.1 %collective-permute-done.8.refs_8_.refs_3_ = bf16[32,384]{1,0:T(8,128)(2,1)S(1)} collective-permute-done((bf16[32,384]{1,0:T(8,128)(2,1)S(1)}, bf16[32,384]{1,0:T(8,128)(2,1)S(1)}, u32[]{:S(2)}, u32[]{:S(2)}) %collective-permute-start.8) | collective-permute-done | bytes 24608 | tf_op jit(solution)/shard_map/ppermute | solution.py:558
  20.1 0.5 %collective-permute-start.15 = (bf16[48,1024]{1,0:T(8,128)(2,1)S(1)}, bf16[48,1024]{1,0:T(8,128)(2,1)S(1)}, u32[]{:S(2)}, u32[]{:S(2)}) collective-permute-start(bf16[48,1024]{1,0:T(8,128)(2,1)S(1)} %get-tuple-element.57), channel_id=1, source_target_pairs={{0,1},{1,0},{2,3},{3,2},{4,5},{5,4},{6,7},{7,6},{8,9},{9,8},{10,11... | collective-permute-start | bytes 294920 | tf_op jit(solution)/shard_map/ppermute | solution.py:558
  20.6 1.7 %qkv.1 = (bf16[384,1024]{1,0:T(8,128)(2,1)S(1)}, bf16[1024,768]{1,0:T(8,128)(2,1)S(1)}, bf16[768,384]{1,0:T(8,128)(2,1)S(1)}, bf16[16,384]{1,0:T(8,128)(2,1)S(1)}) custom-call(bf16[256,768]{1,0:T(8,128)(2,1)S(1)} %get-tuple-element.45.refs_0_, bf16[256,768]{1,0:T(8,128)(2,1)S(1)} %get-tuple-element.46.refs_1_, ...), custom_call_target="tpu_custom_call" | custom-call | flops 1 | bytes 1 | tf_op jit(solution)/shard_map/qkv/pallas_call | solution.py:179
  22.4 0.4 %collective-permute-start.13 = (bf16[32,256]{1,0:T(8,128)(2,1)S(1)}, bf16[32,256]{1,0:T(8,128)(2,1)S(1)}, u32[]{:S(2)}, u32[]{:S(2)}) collective-permute-start(bf16[32,256]{1,0:T(8,128)(2,1)S(1)} %get-tuple-element.55), channel_id=1, source_target_pairs={{0,1},{1,0},{2,3},{3,2},{4,5},{5,4},{6,7},{7,6},{8,9},{9,8},{10,11... | collective-permute-start | bytes 49160 | tf_op jit(solution)/shard_map/ppermute | solution.py:558
  22.9 0.8 %last_qkv.1 = (bf16[128,1024]{1,0:T(8,128)(2,1)S(1)}, bf16[768,512]{1,0:T(8,128)(2,1)S(1)}, bf16[16,512]{1,0:T(8,128)(2,1)S(1)}) custom-call(bf16[80,1024]{1,0:T(8,128)(2,1)S(1)} %collective-permute-done.14.refs_0_, bf16[48,1024]{1,0:T(8,128)(2,1)S(1)} %collective-permute-done.15.refs_1_, bf16[1024,768]{1,0:T(8,128)(2,1)S(1)} %get-tuple-element.58.refs_2_.refs_8_.w_all, ...), custom_call_target="tpu_custom_call" | custom-call | flops 1 | bytes 1 | tf_op jit(solution)/shard_map/last_qkv/pallas_call | solution.py:119
  23.7 4.6 %attention_grads.1 = (f32[128,1024]{1,0:T(8,128)S(1)}, bf16[128,1024]{1,0:T(8,128)(2,1)S(1)}, bf16[768,512]{1,0:T(8,128)(2,1)S(1)}, bf16[16,1280]{1,0:T(8,128)(2,1)S(1)}) custom-call(f32[4]{0:T(128)S(1)} %copy-done.3, bf16[128,256]{1,0:T(8,128)(2,1)S(1)} %get-tuple-element.42.refs_1_, bf16[128,256]{1,0:T(8,128)(2,1)S(1)} %get-tuple-element.43.refs_2_, ...), custom_call_target="tpu_custom_call" | custom-call | flops 1 | bytes 1 | tf_op jit(solution)/shard_map/attention_grads/pallas_call | solution.py:272
  28.3 0.4 %collective-permute-start.16 = (bf16[128,1024]{1,0:T(8,128)(2,1)S(1)}, bf16[128,1024]{1,0:T(8,128)(2,1)S(1)}, u32[]{:S(2)}, u32[]{:S(2)}) collective-permute-start(bf16[128,1024]{1,0:T(8,128)(2,1)S(1)} %get-tuple-element.65), channel_id=1, source_target_pairs={{0,1},{1,0},{2,3},{3,2},{4,5},{5,4},{6,7},{7,6},{8,9},{9,8},{10,11... | collective-permute-start | bytes 786440 | tf_op jit(solution)/shard_map/ppermute | solution.py:558
  28.7 1.4 %collective-permute-start.17 = (bf16[16,1280]{1,0:T(8,128)(2,1)S(1)}, bf16[16,1280]{1,0:T(8,128)(2,1)S(1)}, u32[]{:S(2)}, u32[]{:S(2)}) collective-permute-start(bf16[16,1280]{1,0:T(8,128)(2,1)S(1)} %get-tuple-element.63.pack.refs_0_), channel_id=1, source_target_pairs={{0,2},{1,3},{2,0},{3,1},{4,6},{5,7},{6,4},{7,5},{8,10},{9,11},{10,... | collective-permute-start | bytes 122888 | tf_op jit(solution)/shard_map/ppermute | solution.py:558
  30.1 1.2 %collective-permute-start.20 = (bf16[128,1024]{1,0:T(8,128)(2,1)S(1)}, bf16[128,1024]{1,0:T(8,128)(2,1)S(1)}, u32[]{:S(2)}, u32[]{:S(2)}) collective-permute-start(bf16[128,1024]{1,0:T(8,128)(2,1)S(1)} %add.1.refs_0_), channel_id=1, source_target_pairs={{0,2},{1,3},{2,0},{3,1},{4,6},{5,7},{6,4},{7,5},{8,10},{9,11},{10,... | collective-permute-start | bytes 786440 | tf_op jit(solution)/shard_map/ppermute | solution.py:558
  31.4 1.3 %collective-permute-done.17.refs_1_.refs_2_ = bf16[16,1280]{1,0:T(8,128)(2,1)S(1)} collective-permute-done((bf16[16,1280]{1,0:T(8,128)(2,1)S(1)}, bf16[16,1280]{1,0:T(8,128)(2,1)S(1)}, u32[]{:S(2)}, u32[]{:S(2)}) %collective-permute-start.17) | collective-permute-done | bytes 40992 | tf_op jit(solution)/shard_map/ppermute | solution.py:558
  32.7 0.7 %own_grads.1 = (f32[128,1024]{1,0:T(8,128)S(1)}, bf16[112,1024]{1,0:T(8,128)(2,1)S(1)}, bf16[16,1024]{1,0:T(8,128)(2,1)S(1)}) custom-call(bf16[768,512]{1,0:T(8,128)(2,1)S(1)} %get-tuple-element.62.grad_t, bf16[16,1280]{1,0:T(8,128)(2,1)S(1)} %get-tuple-element.63.pack.refs_0_, bf16[1024,768]{1,0:T(8,128)(2,1)S(1)} %get-tuple-element.58.refs_2_.refs_8_.w_all, ...), custom_call_target="tpu_custom_call" | custom-call | flops 1 | bytes 1 | tf_op jit(solution)/shard_map/own_grads/pallas_call | solution.py:337
  33.6 0.5 %collective-permute-start.21 = (bf16[16,1280]{1,0:T(8,128)(2,1)S(1)}, bf16[16,1280]{1,0:T(8,128)(2,1)S(1)}, u32[]{:S(2)}, u32[]{:S(2)}) collective-permute-start(bf16[16,1280]{1,0:T(8,128)(2,1)S(1)} %get-tuple-element.63.pack.refs_0_), channel_id=1, source_target_pairs={{0,1},{1,0},{2,3},{3,2},{4,5},{5,4},{6,7},{7,6},{8,9},{9,8},{10,11... | collective-permute-start | bytes 122888 | tf_op jit(solution)/shard_map/ppermute | solution.py:558
  34.1 0.4 %collective-permute-start.19 = (bf16[16,1024]{1,0:T(8,128)(2,1)S(1)}, bf16[16,1024]{1,0:T(8,128)(2,1)S(1)}, u32[]{:S(2)}, u32[]{:S(2)}) collective-permute-start(bf16[16,1024]{1,0:T(8,128)(2,1)S(1)} %get-tuple-element.68), channel_id=1, source_target_pairs={{0,1},{1,0},{2,3},{3,2},{4,5},{5,4},{6,7},{7,6},{8,9},{9,8},{10,11... | collective-permute-start | bytes 98312 | tf_op jit(solution)/shard_map/ppermute | solution.py:558
  34.6 0.5 %collective-permute-done.21.refs_1_ = bf16[16,1280]{1,0:T(8,128)(2,1)S(1)} collective-permute-done((bf16[16,1280]{1,0:T(8,128)(2,1)S(1)}, bf16[16,1280]{1,0:T(8,128)(2,1)S(1)}, u32[]{:S(2)}, u32[]{:S(2)}) %collective-permute-start.21) | collective-permute-done | bytes 40992 | tf_op jit(solution)/shard_map/ppermute | solution.py:558
  35.3 0.9 %adapter_grads.1 = (f32[16,1024]{1,0:T(8,128)}, f32[16,3072]{1,0:T(8,128)}) custom-call(bf16[16,1280]{1,0:T(8,128)(2,1)S(1)} %get-tuple-element.63.pack.refs_0_, bf16[16,1280]{1,0:T(8,128)(2,1)S(1)} %collective-permute-done.21.refs_1_, bf16[16,1280]{1,0:T(8,128)(2,1)S(1)} %collective-permute-done.17.refs_1_.refs_2_, ...), custom_call_target="tpu_custom_call" | custom-call | flops 1 | bytes 1 | tf_op jit(solution)/shard_map/adapter_grads/pallas_call | solution.py:370
  36.2 0.2 scale.1
  36.4 2.2 %collective-permute-done.20.refs_0_ = bf16[128,1024]{1,0:T(8,128)(2,1)S(1)} collective-permute-done((bf16[128,1024]{1,0:T(8,128)(2,1)S(1)}, bf16[128,1024]{1,0:T(8,128)(2,1)S(1)}, u32[]{:S(2)}, u32[]{:S(2)}) %collective-permute-start.20) | collective-permute-done | bytes 262176 | tf_op jit(solution)/shard_map/ppermute | solution.py:558
  38.6 0.8 %input_grads.1 = bf16[128,1024]{1,0:T(8,128)(2,1)} custom-call(f32[128,1024]{1,0:T(8,128)S(1)} %get-tuple-element.69.total, f32[128,1024]{1,0:T(8,128)S(1)} %get-tuple-element.70.token_gain, f32[128,1024]{1,0:T(8,128)S(1)} %get-tuple-element.71.scale, f32[128,1024]{1,0:T(8,128)S(1)} %get-tuple-element.72.slope, ...), custom_call_target="tpu_custom_call" | custom-call | flops 1 | bytes 1 | tf_op jit(solution)/shard_map/input_grads/pallas_call | solution.py:436
  (37 shorter events, 1.0 us)
Async XLA Ops:
  0.6 5.5 %collective-permute-start.1 = (bf16[256,3072]{1,0:T(8,128)(2,1)}, bf16[256,3072]{1,0:T(8,128)(2,1)S(1)}, u32[]{:S(2)}, u32[]{:S(2)}) collective-permute-start(bf16[256,3072]{1,0:T(8,128)(2,1)} %weight.1), channel_id=1, source_target_pairs={{0,1},{1,0},{2,3},{3,2},{4,5},{5,4},{6,7},{7,6},{8,9},{9,8},{10,11... | collective-permute-start | bytes 4718600 | tf_op jit(solution)/shard_map/ppermute | solution.py:558
  1.1 5.0 %collective-permute-start = (bf16[128,1024]{1,0:T(8,128)(2,1)}, bf16[128,1024]{1,0:T(8,128)(2,1)S(1)}, u32[]{:S(2)}, u32[]{:S(2)}) collective-permute-start(bf16[128,1024]{1,0:T(8,128)(2,1)} %tokens.3), channel_id=1, source_target_pairs={{0,1},{1,0},{2,3},{3,2},{4,5},{5,4},{6,7},{7,6},{8,9},{9,8},{10,11... | collective-permute-start | bytes 786440 | tf_op jit(solution)/shard_map/ppermute | solution.py:558
  1.2 4.9 %collective-permute-start.2 = (bf16[128,1024]{1,0:T(8,128)(2,1)}, bf16[128,1024]{1,0:T(8,128)(2,1)S(1)}, u32[]{:S(2)}, u32[]{:S(2)}) collective-permute-start(bf16[128,1024]{1,0:T(8,128)(2,1)} %refs_2_.1), channel_id=1, source_target_pairs={{0,1},{1,0},{2,3},{3,2},{4,5},{5,4},{6,7},{7,6},{8,9},{9,8},{10,11... | collective-permute-start | bytes 786440 | tf_op jit(solution)/shard_map/ppermute | solution.py:558
  2.7 7.2 %collective-permute-start.4 = (bf16[128,384]{1,0:T(8,128)(2,1)S(1)}, bf16[128,384]{1,0:T(8,128)(2,1)S(1)}, u32[]{:S(2)}, u32[]{:S(2)}) collective-permute-start(bf16[128,384]{1,0:T(8,128)(2,1)S(1)} %get-tuple-element.49), channel_id=1, source_target_pairs={{0,2},{1,3},{2,0},{3,1},{4,7},{5,6},{6,5},{7,4},{8,10},{9,11},{10,... | collective-permute-start | bytes 294920 | tf_op jit(solution)/shard_map/ppermute | solution.py:558
  5.3 7.9 %collective-permute-start.9 = (bf16[256,384]{1,0:T(8,128)(2,1)S(1)}, bf16[256,384]{1,0:T(8,128)(2,1)S(1)}, u32[]{:S(2)}, u32[]{:S(2)}) collective-permute-start(bf16[256,384]{1,0:T(8,128)(2,1)S(1)} %get-tuple-element.52), channel_id=1, source_target_pairs={{0,2},{1,3},{2,0},{3,1},{4,6},{5,7},{6,4},{7,5},{8,11},{9,10},{10,... | collective-permute-start | bytes 589832 | tf_op jit(solution)/shard_map/ppermute | solution.py:558
  6.1 14.5 %copy-start.1 = (bf16[16,3072]{1,0:T(8,128)(2,1)S(1)}, bf16[16,3072]{1,0:T(8,128)(2,1)}, u32[]{:S(2)}) copy-start(bf16[16,3072]{1,0:T(8,128)(2,1)} %refs_10_.1) | copy-start | bytes 294916
  6.1 14.4 %copy-start.2 = (bf16[1024,16]{0,1:T(8,128)(2,1)S(1)}, bf16[1024,16]{0,1:T(8,128)(2,1)}, u32[]{:S(2)}) copy-start(bf16[1024,16]{0,1:T(8,128)(2,1)} %param.12) | copy-start | bytes 98308
  7.9 12.1 %collective-permute-start.11 = (bf16[128,1024]{1,0:T(8,128)(2,1)S(1)}, bf16[128,1024]{1,0:T(8,128)(2,1)S(1)}, u32[]{:S(2)}, u32[]{:S(2)}) collective-permute-start(bf16[128,1024]{1,0:T(8,128)(2,1)S(1)} %get-tuple-element.47.refs_2_), channel_id=1, source_target_pairs={{0,2},{1,3},{2,0},{3,1},{4,6},{5,7},{6,4},{7,5},{8,10},{9,11},{10,... | collective-permute-start | bytes 786440 | tf_op jit(solution)/shard_map/ppermute | solution.py:558
  9.9 4.6 %collective-permute-start.6 = (bf16[128,384]{1,0:T(8,128)(2,1)S(1)}, bf16[128,384]{1,0:T(8,128)(2,1)S(1)}, u32[]{:S(2)}, u32[]{:S(2)}) collective-permute-start(bf16[128,384]{1,0:T(8,128)(2,1)S(1)} %collective-permute-done.4.refs_4_), channel_id=1, source_target_pairs={{0,8},{1,9},{2,10},{3,11},{4,12},{5,13},{6,14},{7,15},{8,0},{9,1},... | collective-permute-start | bytes 294920 | tf_op jit(solution)/shard_map/ppermute | solution.py:558
  11.4 5.2 %collective-permute-start.5 = (bf16[128,384]{1,0:T(8,128)(2,1)S(1)}, bf16[128,384]{1,0:T(8,128)(2,1)S(1)}, u32[]{:S(2)}, u32[]{:S(2)}) collective-permute-start(bf16[128,384]{1,0:T(8,128)(2,1)S(1)} %collective-permute-done.4.refs_4_), channel_id=1, source_target_pairs={{0,4},{1,5},{2,6},{3,7},{4,0},{5,1},{6,2},{7,3},{8,12},{9,13},{10,... | collective-permute-start | bytes 294920 | tf_op jit(solution)/shard_map/ppermute | solution.py:558
  13.2 7.4 %collective-permute-start.10 = (bf16[256,384]{1,0:T(8,128)(2,1)S(1)}, bf16[256,384]{1,0:T(8,128)(2,1)S(1)}, u32[]{:S(2)}, u32[]{:S(2)}) collective-permute-start(bf16[256,384]{1,0:T(8,128)(2,1)S(1)} %collective-permute-done.9.refs_9_), channel_id=1, source_target_pairs={{0,8},{1,9},{2,10},{3,11},{4,12},{5,13},{6,14},{7,15},{8,0},{9,1},... | collective-permute-start | bytes 589832 | tf_op jit(solution)/shard_map/ppermute | solution.py:558
  14.5 5.4 %collective-permute-start.7 = (bf16[96,384]{1,0:T(8,128)(2,1)S(1)}, bf16[96,384]{1,0:T(8,128)(2,1)S(1)}, u32[]{:S(2)}, u32[]{:S(2)}) collective-permute-start(bf16[96,384]{1,0:T(8,128)(2,1)S(1)} %get-tuple-element.50), channel_id=1, source_target_pairs={{0,4},{1,5},{2,6},{3,7},{4,0},{5,1},{6,2},{7,3},{8,12},{9,13},{10,... | collective-permute-start | bytes 221192 | tf_op jit(solution)/shard_map/ppermute | solution.py:558
  16.1 3.8 %collective-permute-start.8 = (bf16[32,384]{1,0:T(8,128)(2,1)S(1)}, bf16[32,384]{1,0:T(8,128)(2,1)S(1)}, u32[]{:S(2)}, u32[]{:S(2)}) collective-permute-start(bf16[32,384]{1,0:T(8,128)(2,1)S(1)} %get-tuple-element.51), channel_id=1, source_target_pairs={{0,4},{1,5},{2,6},{3,7},{4,0},{5,1},{6,2},{7,3},{8,12},{9,13},{10,... | collective-permute-start | bytes 73736 | tf_op jit(solution)/shard_map/ppermute | solution.py:558
  16.6 5.6 %collective-permute-start.3 = (bf16[128,512]{1,0:T(8,128)(2,1)S(1)}, bf16[128,512]{1,0:T(8,128)(2,1)S(1)}, u32[]{:S(2)}, u32[]{:S(2)}) collective-permute-start(bf16[128,512]{1,0:T(8,128)(2,1)S(1)} %get-tuple-element.44), channel_id=1, source_target_pairs={{0,2},{1,3},{2,0},{3,1},{4,6},{5,7},{6,4},{7,5},{8,10},{9,11},{10,... | collective-permute-start | bytes 393224 | tf_op jit(solution)/shard_map/ppermute | solution.py:558
  20.0 2.9 %collective-permute-start.14 = (bf16[80,1024]{1,0:T(8,128)(2,1)S(1)}, bf16[80,1024]{1,0:T(8,128)(2,1)S(1)}, u32[]{:S(2)}, u32[]{:S(2)}) collective-permute-start(bf16[80,1024]{1,0:T(8,128)(2,1)S(1)} %get-tuple-element.56), channel_id=1, source_target_pairs={{0,1},{1,0},{2,3},{3,2},{4,5},{5,4},{6,7},{7,6},{8,9},{9,8},{10,11... | collective-permute-start | bytes 491528 | tf_op jit(solution)/shard_map/ppermute | solution.py:558
  20.1 2.8 %collective-permute-start.15 = (bf16[48,1024]{1,0:T(8,128)(2,1)S(1)}, bf16[48,1024]{1,0:T(8,128)(2,1)S(1)}, u32[]{:S(2)}, u32[]{:S(2)}) collective-permute-start(bf16[48,1024]{1,0:T(8,128)(2,1)S(1)} %get-tuple-element.57), channel_id=1, source_target_pairs={{0,1},{1,0},{2,3},{3,2},{4,5},{5,4},{6,7},{7,6},{8,9},{9,8},{10,11... | collective-permute-start | bytes 294920 | tf_op jit(solution)/shard_map/ppermute | solution.py:558
  22.3 1.5 %copy-start.3 = (f32[4]{0:T(128)S(1)}, f32[4]{0:T(128)}, u32[]{:S(2)}) copy-start(f32[4]{0:T(128)} %refs_0_.3) | copy-start | bytes 52
  22.3 1.4 %collective-permute-start.12 = (bf16[96,256]{1,0:T(8,128)(2,1)S(1)}, bf16[96,256]{1,0:T(8,128)(2,1)S(1)}, u32[]{:S(2)}, u32[]{:S(2)}) collective-permute-start(bf16[96,256]{1,0:T(8,128)(2,1)S(1)} %get-tuple-element.54), channel_id=1, source_target_pairs={{0,1},{1,0},{2,3},{3,2},{4,5},{5,4},{6,7},{7,6},{8,9},{9,8},{10,11... | collective-permute-start | bytes 147464 | tf_op jit(solution)/shard_map/ppermute | solution.py:558
  22.4 1.3 %collective-permute-start.13 = (bf16[32,256]{1,0:T(8,128)(2,1)S(1)}, bf16[32,256]{1,0:T(8,128)(2,1)S(1)}, u32[]{:S(2)}, u32[]{:S(2)}) collective-permute-start(bf16[32,256]{1,0:T(8,128)(2,1)S(1)} %get-tuple-element.55), channel_id=1, source_target_pairs={{0,1},{1,0},{2,3},{3,2},{4,5},{5,4},{6,7},{7,6},{8,9},{9,8},{10,11... | collective-permute-start | bytes 49160 | tf_op jit(solution)/shard_map/ppermute | solution.py:558
  28.3 1.8 %collective-permute-start.16 = (bf16[128,1024]{1,0:T(8,128)(2,1)S(1)}, bf16[128,1024]{1,0:T(8,128)(2,1)S(1)}, u32[]{:S(2)}, u32[]{:S(2)}) collective-permute-start(bf16[128,1024]{1,0:T(8,128)(2,1)S(1)} %get-tuple-element.65), channel_id=1, source_target_pairs={{0,1},{1,0},{2,3},{3,2},{4,5},{5,4},{6,7},{7,6},{8,9},{9,8},{10,11... | collective-permute-start | bytes 786440 | tf_op jit(solution)/shard_map/ppermute | solution.py:558
  28.7 4.0 %collective-permute-start.17 = (bf16[16,1280]{1,0:T(8,128)(2,1)S(1)}, bf16[16,1280]{1,0:T(8,128)(2,1)S(1)}, u32[]{:S(2)}, u32[]{:S(2)}) collective-permute-start(bf16[16,1280]{1,0:T(8,128)(2,1)S(1)} %get-tuple-element.63.pack.refs_0_), channel_id=1, source_target_pairs={{0,2},{1,3},{2,0},{3,1},{4,6},{5,7},{6,4},{7,5},{8,10},{9,11},{10,... | collective-permute-start | bytes 122888 | tf_op jit(solution)/shard_map/ppermute | solution.py:558
  30.1 8.5 %collective-permute-start.20 = (bf16[128,1024]{1,0:T(8,128)(2,1)S(1)}, bf16[128,1024]{1,0:T(8,128)(2,1)S(1)}, u32[]{:S(2)}, u32[]{:S(2)}) collective-permute-start(bf16[128,1024]{1,0:T(8,128)(2,1)S(1)} %add.1.refs_0_), channel_id=1, source_target_pairs={{0,2},{1,3},{2,0},{3,1},{4,6},{5,7},{6,4},{7,5},{8,10},{9,11},{10,... | collective-permute-start | bytes 786440 | tf_op jit(solution)/shard_map/ppermute | solution.py:558
  32.7 3.4 %copy-start = (bf16[128,1024]{1,0:T(8,128)(2,1)S(1)}, bf16[128,1024]{1,0:T(8,128)(2,1)}, u32[]{:S(2)}) copy-start(bf16[128,1024]{1,0:T(8,128)(2,1)} %tokens.3) | copy-start | bytes 786436
  33.5 2.7 %collective-permute-start.18 = (bf16[112,1024]{1,0:T(8,128)(2,1)S(1)}, bf16[112,1024]{1,0:T(8,128)(2,1)S(1)}, u32[]{:S(2)}, u32[]{:S(2)}) collective-permute-start(bf16[112,1024]{1,0:T(8,128)(2,1)S(1)} %get-tuple-element.67), channel_id=1, source_target_pairs={{0,1},{1,0},{2,3},{3,2},{4,5},{5,4},{6,7},{7,6},{8,9},{9,8},{10,11... | collective-permute-start | bytes 688136 | tf_op jit(solution)/shard_map/ppermute | solution.py:558
  33.6 1.5 %collective-permute-start.21 = (bf16[16,1280]{1,0:T(8,128)(2,1)S(1)}, bf16[16,1280]{1,0:T(8,128)(2,1)S(1)}, u32[]{:S(2)}, u32[]{:S(2)}) collective-permute-start(bf16[16,1280]{1,0:T(8,128)(2,1)S(1)} %get-tuple-element.63.pack.refs_0_), channel_id=1, source_target_pairs={{0,1},{1,0},{2,3},{3,2},{4,5},{5,4},{6,7},{7,6},{8,9},{9,8},{10,11... | collective-permute-start | bytes 122888 | tf_op jit(solution)/shard_map/ppermute | solution.py:558
  34.0 1.2 %collective-permute-start.22 = (bf16[16,1280]{1,0:T(8,128)(2,1)S(1)}, bf16[16,1280]{1,0:T(8,128)(2,1)S(1)}, u32[]{:S(2)}, u32[]{:S(2)}) collective-permute-start(bf16[16,1280]{1,0:T(8,128)(2,1)S(1)} %collective-permute-done.17.refs_1_.refs_2_), channel_id=1, source_target_pairs={{0,1},{1,0},{2,3},{3,2},{4,5},{5,4},{6,7},{7,6},{8,9},{9,8},{10,11... | collective-permute-start | bytes 122888 | tf_op jit(solution)/shard_map/ppermute | solution.py:558
  34.1 2.0 %collective-permute-start.19 = (bf16[16,1024]{1,0:T(8,128)(2,1)S(1)}, bf16[16,1024]{1,0:T(8,128)(2,1)S(1)}, u32[]{:S(2)}, u32[]{:S(2)}) collective-permute-start(bf16[16,1024]{1,0:T(8,128)(2,1)S(1)} %get-tuple-element.68), channel_id=1, source_target_pairs={{0,1},{1,0},{2,3},{3,2},{4,5},{5,4},{6,7},{7,6},{8,9},{9,8},{10,11... | collective-permute-start | bytes 98312 | tf_op jit(solution)/shard_map/ppermute | solution.py:558

commit v11 on v10

--- a/solution.py
+++ b/solution.py
@@ -479,13 +479,34 @@
     )(*hbm([weight]))
 
 
+def own_columns(weight, cols):
+    def kernel(x, out, sem):
+        start = pl.multiple_of(lax.axis_index("rows") * cols, 128)
+        copy = pltpu.make_async_copy(x.at[:, pl.ds(start, cols)], out, sem)
+        copy.start()
+        copy.wait()
+
+    return pl.pallas_call(
+        kernel,
+        out_shape=in_vmem((weight.shape[0], cols), BF),
+        in_specs=[pl.BlockSpec(memory_space=pltpu.HBM)],
+        out_specs=whole_vmem(1)[0],
+        scratch_shapes=[pltpu.SemaphoreType.DMA],
+        compiler_params=pltpu.CompilerParams(vmem_limit_bytes=VMEM),
+        cost_estimate=SMALL,
+        name="own_columns",
+    )(*hbm([weight]))
+
+
 def prepare_kernel(chips, head_cols, sizes, features, gain_map, tokens, core_tokens, cot, *refs):
     count, outs = len(sizes), len(sizes) + len(chips)
     normed, core_normed, gain, inv_rms = refs[count : count + 4]
     cut = refs[count + 4 : count + 4 + outs]
     map_in, tokens_in, core_in, sems = refs[count + 4 + outs :]
     r = lax.axis_index("rows")
-    copies = [(tokens, tokens_in), (core_tokens, core_in), (gain_map, map_in)]
+    half = features.shape[1]
+    copies = [(tokens, tokens_in), (core_tokens, core_in)]
+    copies += [(gain_map.at[pl.ds(at, half)], map_in.at[pl.ds(at, half)]) for at in (0, half)]
     for x, size, out in zip(refs, sizes, cut):
         copies.append((x.at[:, pl.ds(pl.multiple_of(r * size, 128), size)] if size else x, out))
     for j, out in zip(chips, cut[count:]):
@@ -494,20 +515,21 @@
     copies = [pltpu.make_async_copy(a, b, sems.at[i]) for i, (a, b) in enumerate(copies)]
     for c in copies:
         c.start()
-    half = features.shape[1]
     col = features[...].T
-    for c in copies[:3]:
+    held = []
+    for c, x in zip(copies[:2], (tokens_in, core_in)):
         c.wait()
+        x = x[...].astype(F32)
+        held.append(lax.rsqrt(jnp.mean(x * x, -1, keepdims=True) + EPS))
+    inv_rms[...] = held[0]
+    copies[2].wait()
     total = jnp.sum(col[:, :1] * map_in[:half, :], 0, keepdims=True)
+    copies[3].wait()
     total = total + jnp.sum(col[:, 1:] * map_in[half:, :], 0, keepdims=True)
     gain[...] = 1.0 + total
-    for x, out in ((tokens_in, normed), (core_in, core_normed)):
-        x = x[...].astype(F32)
-        inv = lax.rsqrt(jnp.mean(x * x, -1, keepdims=True) + EPS)
-        if out is normed:
-            inv_rms[...] = inv
-        out[...] = (x * inv * gain[...]).astype(BF)
-    for c in copies[3:]:
+    for x, inv, out in ((tokens_in, held[0], normed), (core_in, held[1], core_normed)):
+        out[...] = (x[...].astype(F32) * inv * gain[...]).astype(BF)
+    for c in copies[4:]:
         c.wait()
 
 
@@ -516,7 +538,7 @@
     shapes = [((tok, width), BF), ((tok, width), BF), ((1, width), F32), ((tok, 1), F32)]
     shapes += [((x.shape[0], size or x.shape[1]), BF) for x, size in arrays]
     shapes += [((tok, 2 * head_cols), BF)] * len(chips)
-    copies = 3 + len(arrays) + len(chips)
+    copies = 4 + len(arrays) + len(chips)
     return pl.pallas_call(
         functools.partial(prepare_kernel, chips, head_cols, [size for _, size in arrays]),
         out_shape=[in_vmem(*shape) for shape in shapes],
@@ -586,10 +608,11 @@
         return (x, size) if size % 128 == 0 else (lax.dynamic_slice(x, (0, r * size), (x.shape[0], size)), 0)
 
     own_map, own_tokens, own_cot = hbm([timestep_gain_map, tokens, cot_all])
-    normed, core_normed, gain, inv_rms, own_w, core_w, own_cot, core_cot, *chip_cot = prepare_call(
+    normed, core_normed, gain, inv_rms, core_w, own_cot, core_cot, *chip_cot = prepare_call(
         time_features(timestep), own_map, own_tokens, core_tokens, own_cot, chips, head_cols,
-        [mine(weight, cols), mine(core_weight, cols), mine(cot_all, head_cols), mine(core_cot, head_cols)],
+        [mine(core_weight, cols), mine(cot_all, head_cols), mine(core_cot, head_cols)],
     )
+    own_w = own_columns(weight, cols) if cols % 128 == 0 else mine(weight, cols)[0]
     arrays = [own_w, core_w, normed, core_normed]
     w_from, x_from = [(0, 0, 0, 1, 0, 0), (1, 0, 1, 1, 0, 0)], [(2, tok), (3, tok)]
     def exchange(x, other):
@@ -613,7 +636,7 @@
 
     relay_rows = (tok * 5 // 8, tok * 3 // 8) if tok % 128 == 0 else (tok,)
     chip_normed = [to_row(normed, j) for j in chips]
-    later = list(gate(chip_normed, [relay_rows] * len(chips), *early))
+    later = list(gate(chip_normed, [relay_rows] * len(chips), *early, own_w))
     for x in chip_normed:
         x_from.append((len(arrays), x.shape[0]))
         arrays.append(x)

time: 39.6 us -> 39.6 us (level)
  waiting for transfers between devices: 6.99 us -> 5.97 us
  Pallas kernels: 12.4 us -> 13.4 us
    ppermute x23, waiting for transfers between devices: 6.99 us -> 5.97 us  [send(): return lax.ppermute(x, axes, perm)]
    pallas_call x0 -> x1, Pallas kernels: none -> 1 us  [own_columns(): pl.pallas_call(kernel, out_shape=in_vmem((weight.shape[0], cols), BF), in...]
  transfers between devices with their start and end apart: 23 -> 23, of which waited for: 8 -> 8; matrix products, arithmetic and copies ran while one was open for 0% -> 0% of each run, Pallas kernels for 18% -> 20%
where the time goes in v11:
time: 39.6 us; the launch traced here: 39.4 us
  starting transfers between devices  18.5 us (47%)
  Pallas kernels  13.4 us (34%)
  waiting for transfers between devices  5.97 us (15%)
  between operations  1.47 us (4%)
    ppermute x23, starting transfers between devices, send(): return lax.ppermute(x, axes, perm)  18.5 us
    ppermute x23, waiting for transfers between devices, send(): return lax.ppermute(x, axes, perm)  5.97 us
    pallas_call x1, Pallas kernels, attention_call(): pl.pallas_call(functools.partial(attention_kernel, cols // (3 * HEAD), to...  4.57 us
    pallas_call x1, Pallas kernels, prepare_call(): pl.pallas_call(functools.partial(prepare_kernel, chips, head_cols, [size...  1.71 us
    pallas_call x1, Pallas kernels, qkv_call(): pl.pallas_call(functools.partial(qkv_kernel, n, x_from, w_from), out_shap...  1.67 us
    pallas_call x1, Pallas kernels, own_columns(): pl.pallas_call(kernel, out_shape=in_vmem((weight.shape[0], cols), BF), in...  1 us
    pallas_call x1, Pallas kernels, shares_call(): pl.pallas_call(functools.partial(shares_kernel, chips, pair_cols), out_sh...  0.99 us
    pallas_call x1, Pallas kernels, adapter_call(): pl.pallas_call(functools.partial(adapter_kernel, tok, places), out_shape=...  0.89 us
  transfers between devices with their start and end apart: 23, of which 8 were waited for; matrix products, arithmetic and copies ran while one was open for 0% of the time, Pallas kernels for 20%

profile of v11, /device:TPU:0, one launch (start us, length us, event | category | flops | bytes accessed | tf_op | source)
XLA Modules:
  0.0 39.4 jit_solution(14498518792745021512)
XLA Ops:
  0.6 0.5 %collective-permute-start.1 = (bf16[256,3072]{1,0:T(8,128)(2,1)}, bf16[256,3072]{1,0:T(8,128)(2,1)S(1)}, u32[]{:S(2)}, u32[]{:S(2)}) collective-permute-start(bf16[256,3072]{1,0:T(8,128)(2,1)} %weight.1), channel_id=1, source_target_pairs={{0,1},{1,0},{2,3},{3,2},{4,5},{5,4},{6,7},{7,6},{8,9},{9,8},{10,11... | collective-permute-start | bytes 4718600 | tf_op jit(solution)/shard_map/ppermute | solution.py:580
  1.2 0.4 %collective-permute-start.2 = (bf16[128,1024]{1,0:T(8,128)(2,1)}, bf16[128,1024]{1,0:T(8,128)(2,1)S(1)}, u32[]{:S(2)}, u32[]{:S(2)}) collective-permute-start(bf16[128,1024]{1,0:T(8,128)(2,1)} %refs_1_.1), channel_id=1, source_target_pairs={{0,1},{1,0},{2,3},{3,2},{4,5},{5,4},{6,7},{7,6},{8,9},{9,8},{10,11... | collective-permute-start | bytes 786440 | tf_op jit(solution)/shard_map/ppermute | solution.py:580
  1.7 1.0 %shares.1 = (bf16[128,384]{1,0:T(8,128)(2,1)S(1)}, bf16[256,384]{1,0:T(8,128)(2,1)S(1)}) custom-call(bf16[256,3072]{1,0:T(8,128)(2,1)} %weight.1), custom_call_target="tpu_custom_call" | custom-call | flops 1 | bytes 1 | tf_op jit(solution)/shard_map/shares/pallas_call | solution.py:470
  2.7 2.7 %collective-permute-start.4 = (bf16[128,384]{1,0:T(8,128)(2,1)S(1)}, bf16[128,384]{1,0:T(8,128)(2,1)S(1)}, u32[]{:S(2)}, u32[]{:S(2)}) collective-permute-start(bf16[128,384]{1,0:T(8,128)(2,1)S(1)} %get-tuple-element.47), channel_id=1, source_target_pairs={{0,2},{1,3},{2,0},{3,1},{4,7},{5,6},{6,5},{7,4},{8,10},{9,11},{10,... | collective-permute-start | bytes 294920 | tf_op jit(solution)/shard_map/ppermute | solution.py:580
  6.2 1.7 %prepare.1 = (bf16[128,1024]{1,0:T(8,128)(2,1)S(1)}, bf16[128,1024]{1,0:T(8,128)(2,1)S(1)}, f32[1,1024]{1,0:T(1,128)S(1)}, f32[128,1]{1,0:T(8,128)S(1)}, bf16[25...) custom-call(f32[2,128]{1,0:T(2,128)S(1)} %pad_maximum_fusion.feature, ...), custom_call_target="tpu_custom_call" | custom-call | flops 1 | bytes 1 | tf_op jit(solution)/shard_map/prepare/pallas_call | solution.py:542
  7.9 2.0 %collective-permute-start.11 = (bf16[128,1024]{1,0:T(8,128)(2,1)S(1)}, bf16[128,1024]{1,0:T(8,128)(2,1)S(1)}, u32[]{:S(2)}, u32[]{:S(2)}) collective-permute-start(bf16[128,1024]{1,0:T(8,128)(2,1)S(1)} %get-tuple-element.45.refs_2_), channel_id=1, source_target_pairs={{0,2},{1,3},{2,0},{3,1},{4,6},{5,7},{6,4},{7,5},{8,10},{9,11},{10,... | collective-permute-start | bytes 786440 | tf_op jit(solution)/shard_map/ppermute | solution.py:580
  9.9 1.5 %collective-permute-start.6 = (bf16[128,384]{1,0:T(8,128)(2,1)S(1)}, bf16[128,384]{1,0:T(8,128)(2,1)S(1)}, u32[]{:S(2)}, u32[]{:S(2)}) collective-permute-start(bf16[128,384]{1,0:T(8,128)(2,1)S(1)} %collective-permute-done.4.refs_4_), channel_id=1, source_target_pairs={{0,8},{1,9},{2,10},{3,11},{4,12},{5,13},{6,14},{7,15},{8,0},{9,1},... | collective-permute-start | bytes 294920 | tf_op jit(solution)/shard_map/ppermute | solution.py:580
  11.4 1.5 %collective-permute-start.5 = (bf16[128,384]{1,0:T(8,128)(2,1)S(1)}, bf16[128,384]{1,0:T(8,128)(2,1)S(1)}, u32[]{:S(2)}, u32[]{:S(2)}) collective-permute-start(bf16[128,384]{1,0:T(8,128)(2,1)S(1)} %collective-permute-done.4.refs_4_), channel_id=1, source_target_pairs={{0,4},{1,5},{2,6},{3,7},{4,0},{5,1},{6,2},{7,3},{8,12},{9,13},{10,... | collective-permute-start | bytes 294920 | tf_op jit(solution)/shard_map/ppermute | solution.py:580
  12.9 0.3 collective-permute-done.9.refs_9_
  13.2 1.1 %collective-permute-start.10 = (bf16[256,384]{1,0:T(8,128)(2,1)S(1)}, bf16[256,384]{1,0:T(8,128)(2,1)S(1)}, u32[]{:S(2)}, u32[]{:S(2)}) collective-permute-start(bf16[256,384]{1,0:T(8,128)(2,1)S(1)} %collective-permute-done.9.refs_9_), channel_id=1, source_target_pairs={{0,8},{1,9},{2,10},{3,11},{4,12},{5,13},{6,14},{7,15},{8,0},{9,1},... | collective-permute-start | bytes 589832 | tf_op jit(solution)/shard_map/ppermute | solution.py:580
  14.3 0.2 collective-permute-done.6.refs_0_.refs_6_
  14.5 1.6 %collective-permute-start.7 = (bf16[96,384]{1,0:T(8,128)(2,1)S(1)}, bf16[96,384]{1,0:T(8,128)(2,1)S(1)}, u32[]{:S(2)}, u32[]{:S(2)}) collective-permute-start(bf16[96,384]{1,0:T(8,128)(2,1)S(1)} %get-tuple-element.48), channel_id=1, source_target_pairs={{0,4},{1,5},{2,6},{3,7},{4,0},{5,1},{6,2},{7,3},{8,12},{9,13},{10,... | collective-permute-start | bytes 221192 | tf_op jit(solution)/shard_map/ppermute | solution.py:580
  16.1 0.5 %collective-permute-start.8 = (bf16[32,384]{1,0:T(8,128)(2,1)S(1)}, bf16[32,384]{1,0:T(8,128)(2,1)S(1)}, u32[]{:S(2)}, u32[]{:S(2)}) collective-permute-start(bf16[32,384]{1,0:T(8,128)(2,1)S(1)} %get-tuple-element.49), channel_id=1, source_target_pairs={{0,4},{1,5},{2,6},{3,7},{4,0},{5,1},{6,2},{7,3},{8,12},{9,13},{10,... | collective-permute-start | bytes 73736 | tf_op jit(solution)/shard_map/ppermute | solution.py:580
  16.6 1.3 %collective-permute-start.3 = (bf16[128,512]{1,0:T(8,128)(2,1)S(1)}, bf16[128,512]{1,0:T(8,128)(2,1)S(1)}, u32[]{:S(2)}, u32[]{:S(2)}) collective-permute-start(bf16[128,512]{1,0:T(8,128)(2,1)S(1)} %get-tuple-element.43), channel_id=1, source_target_pairs={{0,2},{1,3},{2,0},{3,1},{4,6},{5,7},{6,4},{7,5},{8,10},{9,11},{10,... | collective-permute-start | bytes 393224 | tf_op jit(solution)/shard_map/ppermute | solution.py:580
  17.9 1.0 %own_columns.1.refs_0_.refs_4_ = bf16[256,768]{1,0:T(8,128)(2,1)S(1)} custom-call(bf16[256,3072]{1,0:T(8,128)(2,1)} %weight.1), custom_call_target="tpu_custom_call" | custom-call | flops 1 | bytes 1 | tf_op jit(solution)/shard_map/own_columns/pallas_call | solution.py:489
  18.9 1.0 %collective-permute-done.8.refs_8_.refs_3_ = bf16[32,384]{1,0:T(8,128)(2,1)S(1)} collective-permute-done((bf16[32,384]{1,0:T(8,128)(2,1)S(1)}, bf16[32,384]{1,0:T(8,128)(2,1)S(1)}, u32[]{:S(2)}, u32[]{:S(2)}) %collective-permute-start.8) | collective-permute-done | bytes 24608 | tf_op jit(solution)/shard_map/ppermute | solution.py:580
  20.1 0.5 %collective-permute-start.15 = (bf16[48,1024]{1,0:T(8,128)(2,1)S(1)}, bf16[48,1024]{1,0:T(8,128)(2,1)S(1)}, u32[]{:S(2)}, u32[]{:S(2)}) collective-permute-start(bf16[48,1024]{1,0:T(8,128)(2,1)S(1)} %get-tuple-element.55), channel_id=1, source_target_pairs={{0,1},{1,0},{2,3},{3,2},{4,5},{5,4},{6,7},{7,6},{8,9},{9,8},{10,11... | collective-permute-start | bytes 294920 | tf_op jit(solution)/shard_map/ppermute | solution.py:580
  20.6 1.7 %qkv.1 = (bf16[384,1024]{1,0:T(8,128)(2,1)S(1)}, bf16[1024,768]{1,0:T(8,128)(2,1)S(1)}, bf16[768,384]{1,0:T(8,128)(2,1)S(1)}, bf16[16,384]{1,0:T(8,128)(2,1)S(1)}) custom-call(bf16[256,768]{1,0:T(8,128)(2,1)S(1)} %own_columns.1.refs_0_.refs_4_, bf16[256,768]{1,0:T(8,128)(2,1)S(1)} %get-tuple-element.44.refs_1_, ...), custom_call_target="tpu_custom_call" | custom-call | flops 1 | bytes 1 | tf_op jit(solution)/shard_map/qkv/pallas_call | solution.py:179
  22.5 0.4 %collective-permute-start.13 = (bf16[32,256]{1,0:T(8,128)(2,1)S(1)}, bf16[32,256]{1,0:T(8,128)(2,1)S(1)}, u32[]{:S(2)}, u32[]{:S(2)}) collective-permute-start(bf16[32,256]{1,0:T(8,128)(2,1)S(1)} %get-tuple-element.53), channel_id=1, source_target_pairs={{0,1},{1,0},{2,3},{3,2},{4,5},{5,4},{6,7},{7,6},{8,9},{9,8},{10,11... | collective-permute-start | bytes 49160 | tf_op jit(solution)/shard_map/ppermute | solution.py:580
  22.9 0.8 %last_qkv.1 = (bf16[128,1024]{1,0:T(8,128)(2,1)S(1)}, bf16[768,512]{1,0:T(8,128)(2,1)S(1)}, bf16[16,512]{1,0:T(8,128)(2,1)S(1)}) custom-call(bf16[80,1024]{1,0:T(8,128)(2,1)S(1)} %collective-permute-done.14.refs_0_, bf16[48,1024]{1,0:T(8,128)(2,1)S(1)} %collective-permute-done.15.refs_1_, bf16[1024,768]{1,0:T(8,128)(2,1)S(1)} %get-tuple-element.56.refs_2_.refs_8_.w_all, ...), custom_call_target="tpu_custom_call" | custom-call | flops 1 | bytes 1 | tf_op jit(solution)/shard_map/last_qkv/pallas_call | solution.py:119
  23.7 4.6 %attention_grads.1 = (f32[128,1024]{1,0:T(8,128)S(1)}, bf16[128,1024]{1,0:T(8,128)(2,1)S(1)}, bf16[768,512]{1,0:T(8,128)(2,1)S(1)}, bf16[16,1280]{1,0:T(8,128)(2,1)S(1)}) custom-call(f32[4]{0:T(128)S(1)} %copy-done.3, bf16[128,256]{1,0:T(8,128)(2,1)S(1)} %get-tuple-element.41.refs_1_, bf16[128,256]{1,0:T(8,128)(2,1)S(1)} %get-tuple-element.42.refs_2_, ...), custom_call_target="tpu_custom_call" | custom-call | flops 1 | bytes 1 | tf_op jit(solution)/shard_map/attention_grads/pallas_call | solution.py:272
  28.3 0.4 %collective-permute-start.16 = (bf16[128,1024]{1,0:T(8,128)(2,1)S(1)}, bf16[128,1024]{1,0:T(8,128)(2,1)S(1)}, u32[]{:S(2)}, u32[]{:S(2)}) collective-permute-start(bf16[128,1024]{1,0:T(8,128)(2,1)S(1)} %get-tuple-element.63), channel_id=1, source_target_pairs={{0,1},{1,0},{2,3},{3,2},{4,5},{5,4},{6,7},{7,6},{8,9},{9,8},{10,11... | collective-permute-start | bytes 786440 | tf_op jit(solution)/shard_map/ppermute | solution.py:580
  28.7 1.4 %collective-permute-start.17 = (bf16[16,1280]{1,0:T(8,128)(2,1)S(1)}, bf16[16,1280]{1,0:T(8,128)(2,1)S(1)}, u32[]{:S(2)}, u32[]{:S(2)}) collective-permute-start(bf16[16,1280]{1,0:T(8,128)(2,1)S(1)} %get-tuple-element.61.pack.refs_0_), channel_id=1, source_target_pairs={{0,2},{1,3},{2,0},{3,1},{4,6},{5,7},{6,4},{7,5},{8,10},{9,11},{10,... | collective-permute-start | bytes 122888 | tf_op jit(solution)/shard_map/ppermute | solution.py:580
  30.1 1.2 %collective-permute-start.20 = (bf16[128,1024]{1,0:T(8,128)(2,1)S(1)}, bf16[128,1024]{1,0:T(8,128)(2,1)S(1)}, u32[]{:S(2)}, u32[]{:S(2)}) collective-permute-start(bf16[128,1024]{1,0:T(8,128)(2,1)S(1)} %add.1.refs_0_), channel_id=1, source_target_pairs={{0,2},{1,3},{2,0},{3,1},{4,6},{5,7},{6,4},{7,5},{8,10},{9,11},{10,... | collective-permute-start | bytes 786440 | tf_op jit(solution)/shard_map/ppermute | solution.py:580
  31.4 1.4 %collective-permute-done.17.refs_1_.refs_2_ = bf16[16,1280]{1,0:T(8,128)(2,1)S(1)} collective-permute-done((bf16[16,1280]{1,0:T(8,128)(2,1)S(1)}, bf16[16,1280]{1,0:T(8,128)(2,1)S(1)}, u32[]{:S(2)}, u32[]{:S(2)}) %collective-permute-start.17) | collective-permute-done | bytes 40992 | tf_op jit(solution)/shard_map/ppermute | solution.py:580
  32.7 0.7 %own_grads.1 = (f32[128,1024]{1,0:T(8,128)S(1)}, bf16[112,1024]{1,0:T(8,128)(2,1)S(1)}, bf16[16,1024]{1,0:T(8,128)(2,1)S(1)}) custom-call(bf16[768,512]{1,0:T(8,128)(2,1)S(1)} %get-tuple-element.60.grad_t, bf16[16,1280]{1,0:T(8,128)(2,1)S(1)} %get-tuple-element.61.pack.refs_0_, bf16[1024,768]{1,0:T(8,128)(2,1)S(1)} %get-tuple-element.56.refs_2_.refs_8_.w_all, ...), custom_call_target="tpu_custom_call" | custom-call | flops 1 | bytes 1 | tf_op jit(solution)/shard_map/own_grads/pallas_call | solution.py:337
  33.6 0.5 %collective-permute-start.21 = (bf16[16,1280]{1,0:T(8,128)(2,1)S(1)}, bf16[16,1280]{1,0:T(8,128)(2,1)S(1)}, u32[]{:S(2)}, u32[]{:S(2)}) collective-permute-start(bf16[16,1280]{1,0:T(8,128)(2,1)S(1)} %get-tuple-element.61.pack.refs_0_), channel_id=1, source_target_pairs={{0,1},{1,0},{2,3},{3,2},{4,5},{5,4},{6,7},{7,6},{8,9},{9,8},{10,11... | collective-permute-start | bytes 122888 | tf_op jit(solution)/shard_map/ppermute | solution.py:580
  34.1 0.4 %collective-permute-start.19 = (bf16[16,1024]{1,0:T(8,128)(2,1)S(1)}, bf16[16,1024]{1,0:T(8,128)(2,1)S(1)}, u32[]{:S(2)}, u32[]{:S(2)}) collective-permute-start(bf16[16,1024]{1,0:T(8,128)(2,1)S(1)} %get-tuple-element.66), channel_id=1, source_target_pairs={{0,1},{1,0},{2,3},{3,2},{4,5},{5,4},{6,7},{7,6},{8,9},{9,8},{10,11... | collective-permute-start | bytes 98312 | tf_op jit(solution)/shard_map/ppermute | solution.py:580
  34.6 0.5 %collective-permute-done.21.refs_1_ = bf16[16,1280]{1,0:T(8,128)(2,1)S(1)} collective-permute-done((bf16[16,1280]{1,0:T(8,128)(2,1)S(1)}, bf16[16,1280]{1,0:T(8,128)(2,1)S(1)}, u32[]{:S(2)}, u32[]{:S(2)}) %collective-permute-start.21) | collective-permute-done | bytes 40992 | tf_op jit(solution)/shard_map/ppermute | solution.py:580
  35.3 0.9 %adapter_grads.1 = (f32[16,1024]{1,0:T(8,128)}, f32[16,3072]{1,0:T(8,128)}) custom-call(bf16[16,1280]{1,0:T(8,128)(2,1)S(1)} %get-tuple-element.61.pack.refs_0_, bf16[16,1280]{1,0:T(8,128)(2,1)S(1)} %collective-permute-done.21.refs_1_, bf16[16,1280]{1,0:T(8,128)(2,1)S(1)} %collective-permute-done.17.refs_1_.refs_2_, ...), custom_call_target="tpu_custom_call" | custom-call | flops 1 | bytes 1 | tf_op jit(solution)/shard_map/adapter_grads/pallas_call | solution.py:370
  36.4 2.2 %collective-permute-done.20.refs_0_ = bf16[128,1024]{1,0:T(8,128)(2,1)S(1)} collective-permute-done((bf16[128,1024]{1,0:T(8,128)(2,1)S(1)}, bf16[128,1024]{1,0:T(8,128)(2,1)S(1)}, u32[]{:S(2)}, u32[]{:S(2)}) %collective-permute-start.20) | collective-permute-done | bytes 262176 | tf_op jit(solution)/shard_map/ppermute | solution.py:580
  38.6 0.8 %input_grads.1 = bf16[128,1024]{1,0:T(8,128)(2,1)} custom-call(f32[128,1024]{1,0:T(8,128)S(1)} %get-tuple-element.67.total, f32[128,1024]{1,0:T(8,128)S(1)} %get-tuple-element.68.token_gain, f32[128,1024]{1,0:T(8,128)S(1)} %get-tuple-element.69.scale, f32[128,1024]{1,0:T(8,128)S(1)} %get-tuple-element.70.slope, ...), custom_call_target="tpu_custom_call" | custom-call | flops 1 | bytes 1 | tf_op jit(solution)/shard_map/input_grads/pallas_call | solution.py:436
  (38 shorter events, 1.2 us)
Async XLA Ops:
  0.6 5.5 %collective-permute-start.1 = (bf16[256,3072]{1,0:T(8,128)(2,1)}, bf16[256,3072]{1,0:T(8,128)(2,1)S(1)}, u32[]{:S(2)}, u32[]{:S(2)}) collective-permute-start(bf16[256,3072]{1,0:T(8,128)(2,1)} %weight.1), channel_id=1, source_target_pairs={{0,1},{1,0},{2,3},{3,2},{4,5},{5,4},{6,7},{7,6},{8,9},{9,8},{10,11... | collective-permute-start | bytes 4718600 | tf_op jit(solution)/shard_map/ppermute | solution.py:580
  1.1 5.0 %collective-permute-start = (bf16[128,1024]{1,0:T(8,128)(2,1)}, bf16[128,1024]{1,0:T(8,128)(2,1)S(1)}, u32[]{:S(2)}, u32[]{:S(2)}) collective-permute-start(bf16[128,1024]{1,0:T(8,128)(2,1)} %tokens.3), channel_id=1, source_target_pairs={{0,1},{1,0},{2,3},{3,2},{4,5},{5,4},{6,7},{7,6},{8,9},{9,8},{10,11... | collective-permute-start | bytes 786440 | tf_op jit(solution)/shard_map/ppermute | solution.py:580
  1.2 4.9 %collective-permute-start.2 = (bf16[128,1024]{1,0:T(8,128)(2,1)}, bf16[128,1024]{1,0:T(8,128)(2,1)S(1)}, u32[]{:S(2)}, u32[]{:S(2)}) collective-permute-start(bf16[128,1024]{1,0:T(8,128)(2,1)} %refs_1_.1), channel_id=1, source_target_pairs={{0,1},{1,0},{2,3},{3,2},{4,5},{5,4},{6,7},{7,6},{8,9},{9,8},{10,11... | collective-permute-start | bytes 786440 | tf_op jit(solution)/shard_map/ppermute | solution.py:580
  2.7 7.2 %collective-permute-start.4 = (bf16[128,384]{1,0:T(8,128)(2,1)S(1)}, bf16[128,384]{1,0:T(8,128)(2,1)S(1)}, u32[]{:S(2)}, u32[]{:S(2)}) collective-permute-start(bf16[128,384]{1,0:T(8,128)(2,1)S(1)} %get-tuple-element.47), channel_id=1, source_target_pairs={{0,2},{1,3},{2,0},{3,1},{4,7},{5,6},{6,5},{7,4},{8,10},{9,11},{10,... | collective-permute-start | bytes 294920 | tf_op jit(solution)/shard_map/ppermute | solution.py:580
  5.3 7.9 %collective-permute-start.9 = (bf16[256,384]{1,0:T(8,128)(2,1)S(1)}, bf16[256,384]{1,0:T(8,128)(2,1)S(1)}, u32[]{:S(2)}, u32[]{:S(2)}) collective-permute-start(bf16[256,384]{1,0:T(8,128)(2,1)S(1)} %get-tuple-element.50), channel_id=1, source_target_pairs={{0,2},{1,3},{2,0},{3,1},{4,6},{5,7},{6,4},{7,5},{8,11},{9,10},{10,... | collective-permute-start | bytes 589832 | tf_op jit(solution)/shard_map/ppermute | solution.py:580
  7.9 12.7 %copy-start.1 = (bf16[16,3072]{1,0:T(8,128)(2,1)S(1)}, bf16[16,3072]{1,0:T(8,128)(2,1)}, u32[]{:S(2)}) copy-start(bf16[16,3072]{1,0:T(8,128)(2,1)} %refs_10_.1) | copy-start | bytes 294916
  7.9 12.7 %copy-start.2 = (bf16[1024,16]{0,1:T(8,128)(2,1)S(1)}, bf16[1024,16]{0,1:T(8,128)(2,1)}, u32[]{:S(2)}) copy-start(bf16[1024,16]{0,1:T(8,128)(2,1)} %param.12) | copy-start | bytes 98308
  7.9 12.1 %collective-permute-start.11 = (bf16[128,1024]{1,0:T(8,128)(2,1)S(1)}, bf16[128,1024]{1,0:T(8,128)(2,1)S(1)}, u32[]{:S(2)}, u32[]{:S(2)}) collective-permute-start(bf16[128,1024]{1,0:T(8,128)(2,1)S(1)} %get-tuple-element.45.refs_2_), channel_id=1, source_target_pairs={{0,2},{1,3},{2,0},{3,1},{4,6},{5,7},{6,4},{7,5},{8,10},{9,11},{10,... | collective-permute-start | bytes 786440 | tf_op jit(solution)/shard_map/ppermute | solution.py:580
  9.9 4.6 %collective-permute-start.6 = (bf16[128,384]{1,0:T(8,128)(2,1)S(1)}, bf16[128,384]{1,0:T(8,128)(2,1)S(1)}, u32[]{:S(2)}, u32[]{:S(2)}) collective-permute-start(bf16[128,384]{1,0:T(8,128)(2,1)S(1)} %collective-permute-done.4.refs_4_), channel_id=1, source_target_pairs={{0,8},{1,9},{2,10},{3,11},{4,12},{5,13},{6,14},{7,15},{8,0},{9,1},... | collective-permute-start | bytes 294920 | tf_op jit(solution)/shard_map/ppermute | solution.py:580
  11.4 5.2 %collective-permute-start.5 = (bf16[128,384]{1,0:T(8,128)(2,1)S(1)}, bf16[128,384]{1,0:T(8,128)(2,1)S(1)}, u32[]{:S(2)}, u32[]{:S(2)}) collective-permute-start(bf16[128,384]{1,0:T(8,128)(2,1)S(1)} %collective-permute-done.4.refs_4_), channel_id=1, source_target_pairs={{0,4},{1,5},{2,6},{3,7},{4,0},{5,1},{6,2},{7,3},{8,12},{9,13},{10,... | collective-permute-start | bytes 294920 | tf_op jit(solution)/shard_map/ppermute | solution.py:580
  13.2 7.4 %collective-permute-start.10 = (bf16[256,384]{1,0:T(8,128)(2,1)S(1)}, bf16[256,384]{1,0:T(8,128)(2,1)S(1)}, u32[]{:S(2)}, u32[]{:S(2)}) collective-permute-start(bf16[256,384]{1,0:T(8,128)(2,1)S(1)} %collective-permute-done.9.refs_9_), channel_id=1, source_target_pairs={{0,8},{1,9},{2,10},{3,11},{4,12},{5,13},{6,14},{7,15},{8,0},{9,1},... | collective-permute-start | bytes 589832 | tf_op jit(solution)/shard_map/ppermute | solution.py:580
  14.5 5.4 %collective-permute-start.7 = (bf16[96,384]{1,0:T(8,128)(2,1)S(1)}, bf16[96,384]{1,0:T(8,128)(2,1)S(1)}, u32[]{:S(2)}, u32[]{:S(2)}) collective-permute-start(bf16[96,384]{1,0:T(8,128)(2,1)S(1)} %get-tuple-element.48), channel_id=1, source_target_pairs={{0,4},{1,5},{2,6},{3,7},{4,0},{5,1},{6,2},{7,3},{8,12},{9,13},{10,... | collective-permute-start | bytes 221192 | tf_op jit(solution)/shard_map/ppermute | solution.py:580
  16.1 3.8 %collective-permute-start.8 = (bf16[32,384]{1,0:T(8,128)(2,1)S(1)}, bf16[32,384]{1,0:T(8,128)(2,1)S(1)}, u32[]{:S(2)}, u32[]{:S(2)}) collective-permute-start(bf16[32,384]{1,0:T(8,128)(2,1)S(1)} %get-tuple-element.49), channel_id=1, source_target_pairs={{0,4},{1,5},{2,6},{3,7},{4,0},{5,1},{6,2},{7,3},{8,12},{9,13},{10,... | collective-permute-start | bytes 73736 | tf_op jit(solution)/shard_map/ppermute | solution.py:580
  16.6 5.6 %collective-permute-start.3 = (bf16[128,512]{1,0:T(8,128)(2,1)S(1)}, bf16[128,512]{1,0:T(8,128)(2,1)S(1)}, u32[]{:S(2)}, u32[]{:S(2)}) collective-permute-start(bf16[128,512]{1,0:T(8,128)(2,1)S(1)} %get-tuple-element.43), channel_id=1, source_target_pairs={{0,2},{1,3},{2,0},{3,1},{4,6},{5,7},{6,4},{7,5},{8,10},{9,11},{10,... | collective-permute-start | bytes 393224 | tf_op jit(solution)/shard_map/ppermute | solution.py:580
  20.0 2.9 %collective-permute-start.14 = (bf16[80,1024]{1,0:T(8,128)(2,1)S(1)}, bf16[80,1024]{1,0:T(8,128)(2,1)S(1)}, u32[]{:S(2)}, u32[]{:S(2)}) collective-permute-start(bf16[80,1024]{1,0:T(8,128)(2,1)S(1)} %get-tuple-element.54), channel_id=1, source_target_pairs={{0,1},{1,0},{2,3},{3,2},{4,5},{5,4},{6,7},{7,6},{8,9},{9,8},{10,11... | collective-permute-start | bytes 491528 | tf_op jit(solution)/shard_map/ppermute | solution.py:580
  20.1 2.8 %collective-permute-start.15 = (bf16[48,1024]{1,0:T(8,128)(2,1)S(1)}, bf16[48,1024]{1,0:T(8,128)(2,1)S(1)}, u32[]{:S(2)}, u32[]{:S(2)}) collective-permute-start(bf16[48,1024]{1,0:T(8,128)(2,1)S(1)} %get-tuple-element.55), channel_id=1, source_target_pairs={{0,1},{1,0},{2,3},{3,2},{4,5},{5,4},{6,7},{7,6},{8,9},{9,8},{10,11... | collective-permute-start | bytes 294920 | tf_op jit(solution)/shard_map/ppermute | solution.py:580
  22.3 1.5 %copy-start.3 = (f32[4]{0:T(128)S(1)}, f32[4]{0:T(128)}, u32[]{:S(2)}) copy-start(f32[4]{0:T(128)} %refs_0_.1) | copy-start | bytes 52
  22.3 1.4 %collective-permute-start.12 = (bf16[96,256]{1,0:T(8,128)(2,1)S(1)}, bf16[96,256]{1,0:T(8,128)(2,1)S(1)}, u32[]{:S(2)}, u32[]{:S(2)}) collective-permute-start(bf16[96,256]{1,0:T(8,128)(2,1)S(1)} %get-tuple-element.52), channel_id=1, source_target_pairs={{0,1},{1,0},{2,3},{3,2},{4,5},{5,4},{6,7},{7,6},{8,9},{9,8},{10,11... | collective-permute-start | bytes 147464 | tf_op jit(solution)/shard_map/ppermute | solution.py:580
  22.5 1.3 %collective-permute-start.13 = (bf16[32,256]{1,0:T(8,128)(2,1)S(1)}, bf16[32,256]{1,0:T(8,128)(2,1)S(1)}, u32[]{:S(2)}, u32[]{:S(2)}) collective-permute-start(bf16[32,256]{1,0:T(8,128)(2,1)S(1)} %get-tuple-element.53), channel_id=1, source_target_pairs={{0,1},{1,0},{2,3},{3,2},{4,5},{5,4},{6,7},{7,6},{8,9},{9,8},{10,11... | collective-permute-start | bytes 49160 | tf_op jit(solution)/shard_map/ppermute | solution.py:580
  28.3 1.8 %collective-permute-start.16 = (bf16[128,1024]{1,0:T(8,128)(2,1)S(1)}, bf16[128,1024]{1,0:T(8,128)(2,1)S(1)}, u32[]{:S(2)}, u32[]{:S(2)}) collective-permute-start(bf16[128,1024]{1,0:T(8,128)(2,1)S(1)} %get-tuple-element.63), channel_id=1, source_target_pairs={{0,1},{1,0},{2,3},{3,2},{4,5},{5,4},{6,7},{7,6},{8,9},{9,8},{10,11... | collective-permute-start | bytes 786440 | tf_op jit(solution)/shard_map/ppermute | solution.py:580
  28.7 4.0 %collective-permute-start.17 = (bf16[16,1280]{1,0:T(8,128)(2,1)S(1)}, bf16[16,1280]{1,0:T(8,128)(2,1)S(1)}, u32[]{:S(2)}, u32[]{:S(2)}) collective-permute-start(bf16[16,1280]{1,0:T(8,128)(2,1)S(1)} %get-tuple-element.61.pack.refs_0_), channel_id=1, source_target_pairs={{0,2},{1,3},{2,0},{3,1},{4,6},{5,7},{6,4},{7,5},{8,10},{9,11},{10,... | collective-permute-start | bytes 122888 | tf_op jit(solution)/shard_map/ppermute | solution.py:580
  30.1 8.5 %collective-permute-start.20 = (bf16[128,1024]{1,0:T(8,128)(2,1)S(1)}, bf16[128,1024]{1,0:T(8,128)(2,1)S(1)}, u32[]{:S(2)}, u32[]{:S(2)}) collective-permute-start(bf16[128,1024]{1,0:T(8,128)(2,1)S(1)} %add.1.refs_0_), channel_id=1, source_target_pairs={{0,2},{1,3},{2,0},{3,1},{4,6},{5,7},{6,4},{7,5},{8,10},{9,11},{10,... | collective-permute-start | bytes 786440 | tf_op jit(solution)/shard_map/ppermute | solution.py:580
  32.7 3.4 %copy-start = (bf16[128,1024]{1,0:T(8,128)(2,1)S(1)}, bf16[128,1024]{1,0:T(8,128)(2,1)}, u32[]{:S(2)}) copy-start(bf16[128,1024]{1,0:T(8,128)(2,1)} %tokens.3) | copy-start | bytes 786436
  33.5 2.7 %collective-permute-start.18 = (bf16[112,1024]{1,0:T(8,128)(2,1)S(1)}, bf16[112,1024]{1,0:T(8,128)(2,1)S(1)}, u32[]{:S(2)}, u32[]{:S(2)}) collective-permute-start(bf16[112,1024]{1,0:T(8,128)(2,1)S(1)} %get-tuple-element.65), channel_id=1, source_target_pairs={{0,1},{1,0},{2,3},{3,2},{4,5},{5,4},{6,7},{7,6},{8,9},{9,8},{10,11... | collective-permute-start | bytes 688136 | tf_op jit(solution)/shard_map/ppermute | solution.py:580
  33.6 1.5 %collective-permute-start.21 = (bf16[16,1280]{1,0:T(8,128)(2,1)S(1)}, bf16[16,1280]{1,0:T(8,128)(2,1)S(1)}, u32[]{:S(2)}, u32[]{:S(2)}) collective-permute-start(bf16[16,1280]{1,0:T(8,128)(2,1)S(1)} %get-tuple-element.61.pack.refs_0_), channel_id=1, source_target_pairs={{0,1},{1,0},{2,3},{3,2},{4,5},{5,4},{6,7},{7,6},{8,9},{9,8},{10,11... | collective-permute-start | bytes 122888 | tf_op jit(solution)/shard_map/ppermute | solution.py:580
  34.1 1.2 %collective-permute-start.22 = (bf16[16,1280]{1,0:T(8,128)(2,1)S(1)}, bf16[16,1280]{1,0:T(8,128)(2,1)S(1)}, u32[]{:S(2)}, u32[]{:S(2)}) collective-permute-start(bf16[16,1280]{1,0:T(8,128)(2,1)S(1)} %collective-permute-done.17.refs_1_.refs_2_), channel_id=1, source_target_pairs={{0,1},{1,0},{2,3},{3,2},{4,5},{5,4},{6,7},{7,6},{8,9},{9,8},{10,11... | collective-permute-start | bytes 122888 | tf_op jit(solution)/shard_map/ppermute | solution.py:580
  34.1 2.0 %collective-permute-start.19 = (bf16[16,1024]{1,0:T(8,128)(2,1)S(1)}, bf16[16,1024]{1,0:T(8,128)(2,1)S(1)}, u32[]{:S(2)}, u32[]{:S(2)}) collective-permute-start(bf16[16,1024]{1,0:T(8,128)(2,1)S(1)} %get-tuple-element.66), channel_id=1, source_target_pairs={{0,1},{1,0},{2,3},{3,2},{4,5},{5,4},{6,7},{7,6},{8,9},{9,8},{10,11... | collective-permute-start | bytes 98312 | tf_op jit(solution)/shard_map/ppermute | solution.py:580

commit v12 on v10

--- a/solution.py
+++ b/solution.py
@@ -240,8 +240,8 @@
             delta = jnp.sum(e * grad_probs, 0, keepdims=True) * share
             attention = e * share
             grad_scores = (attention * (grad_probs - delta)).astype(BF)
-            gv_s = jnp.dot(attention.astype(BF), g.T, preferred_element_type=F32)
-            gk_s = jnp.dot(grad_scores, q_low.T, preferred_element_type=F32)
+            gv_s = contract(attention.astype(BF), g, 1, 1)
+            gk_s = contract(grad_scores, q_low, 1, 1)
             gq = sc * jnp.dot(k_low, grad_scores, preferred_element_type=F32)
             gq = q_inv * (gq - q_unit * jnp.sum(q_unit * gq, 0, keepdims=True))
             grad_t[pl.ds(o, HEAD), pl.ds(s, step)] = gq.astype(BF)

time: 39.6 us -> 39.6 us (level)
  no operation moved by 1% of the time
where the time goes in v12:
time: 39.6 us; the launch traced here: 39.4 us
  starting transfers between devices  18.5 us (47%)
  Pallas kernels  12.4 us (31%)
  waiting for transfers between devices  6.99 us (18%)
  between operations  1.47 us (4%)
    ppermute x23, starting transfers between devices, send(): return lax.ppermute(x, axes, perm)  18.5 us
    ppermute x23, waiting for transfers between devices, send(): return lax.ppermute(x, axes, perm)  6.99 us
    pallas_call x1, Pallas kernels, attention_call(): pl.pallas_call(functools.partial(attention_kernel, cols // (3 * HEAD), to...  4.58 us
    pallas_call x1, Pallas kernels, prepare_call(): pl.pallas_call(functools.partial(prepare_kernel, chips, head_cols, [size...  1.7 us
    pallas_call x1, Pallas kernels, qkv_call(): pl.pallas_call(functools.partial(qkv_kernel, n, x_from, w_from), out_shap...  1.67 us
    pallas_call x1, Pallas kernels, shares_call(): pl.pallas_call(functools.partial(shares_kernel, chips, pair_cols), out_sh...  0.99 us
    pallas_call x1, Pallas kernels, adapter_call(): pl.pallas_call(functools.partial(adapter_kernel, tok, places), out_shape=...  0.89 us
    pallas_call x1, Pallas kernels, final_call(): pl.pallas_call(final_kernel, out_shape=jax.ShapeDtypeStruct(shape, BF), i...  0.84 us
  transfers between devices with their start and end apart: 23, of which 8 were waited for; matrix products, arithmetic and copies ran while one was open for 0% of the time, Pallas kernels for 18%

profile of v12, /device:TPU:0, one launch (start us, length us, event | category | flops | bytes accessed | tf_op | source)
XLA Modules:
  0.0 39.4 jit_solution(6069164517960497135)
XLA Ops:
  0.6 0.5 %collective-permute-start.1 = (bf16[256,3072]{1,0:T(8,128)(2,1)}, bf16[256,3072]{1,0:T(8,128)(2,1)S(1)}, u32[]{:S(2)}, u32[]{:S(2)}) collective-permute-start(bf16[256,3072]{1,0:T(8,128)(2,1)} %weight.1), channel_id=1, source_target_pairs={{0,1},{1,0},{2,3},{3,2},{4,5},{5,4},{6,7},{7,6},{8,9},{9,8},{10,11... | collective-permute-start | bytes 4718600 | tf_op jit(solution)/shard_map/ppermute | solution.py:558
  1.2 0.4 %collective-permute-start.2 = (bf16[128,1024]{1,0:T(8,128)(2,1)}, bf16[128,1024]{1,0:T(8,128)(2,1)S(1)}, u32[]{:S(2)}, u32[]{:S(2)}) collective-permute-start(bf16[128,1024]{1,0:T(8,128)(2,1)} %refs_2_.1), channel_id=1, source_target_pairs={{0,1},{1,0},{2,3},{3,2},{4,5},{5,4},{6,7},{7,6},{8,9},{9,8},{10,11... | collective-permute-start | bytes 786440 | tf_op jit(solution)/shard_map/ppermute | solution.py:558
  1.7 1.0 %shares.1 = (bf16[128,384]{1,0:T(8,128)(2,1)S(1)}, bf16[256,384]{1,0:T(8,128)(2,1)S(1)}) custom-call(bf16[256,3072]{1,0:T(8,128)(2,1)} %weight.1), custom_call_target="tpu_custom_call" | custom-call | flops 1 | bytes 1 | tf_op jit(solution)/shard_map/shares/pallas_call | solution.py:470
  2.7 2.7 %collective-permute-start.4 = (bf16[128,384]{1,0:T(8,128)(2,1)S(1)}, bf16[128,384]{1,0:T(8,128)(2,1)S(1)}, u32[]{:S(2)}, u32[]{:S(2)}) collective-permute-start(bf16[128,384]{1,0:T(8,128)(2,1)S(1)} %get-tuple-element.49), channel_id=1, source_target_pairs={{0,2},{1,3},{2,0},{3,1},{4,7},{5,6},{6,5},{7,4},{8,10},{9,11},{10,... | collective-permute-start | bytes 294920 | tf_op jit(solution)/shard_map/ppermute | solution.py:558
  6.2 1.7 %prepare.1 = (bf16[128,1024]{1,0:T(8,128)(2,1)S(1)}, bf16[128,1024]{1,0:T(8,128)(2,1)S(1)}, f32[1,1024]{1,0:T(1,128)S(1)}, f32[128,1]{1,0:T(8,128)S(1)}, bf16[25...) custom-call(f32[2,128]{1,0:T(2,128)S(1)} %pad_maximum_fusion.feature, ...), custom_call_target="tpu_custom_call" | custom-call | flops 1 | bytes 1 | tf_op jit(solution)/shard_map/prepare/pallas_call | solution.py:520
  7.9 2.0 %collective-permute-start.11 = (bf16[128,1024]{1,0:T(8,128)(2,1)S(1)}, bf16[128,1024]{1,0:T(8,128)(2,1)S(1)}, u32[]{:S(2)}, u32[]{:S(2)}) collective-permute-start(bf16[128,1024]{1,0:T(8,128)(2,1)S(1)} %get-tuple-element.47.refs_2_), channel_id=1, source_target_pairs={{0,2},{1,3},{2,0},{3,1},{4,6},{5,7},{6,4},{7,5},{8,10},{9,11},{10,... | collective-permute-start | bytes 786440 | tf_op jit(solution)/shard_map/ppermute | solution.py:558
  9.9 1.5 %collective-permute-start.6 = (bf16[128,384]{1,0:T(8,128)(2,1)S(1)}, bf16[128,384]{1,0:T(8,128)(2,1)S(1)}, u32[]{:S(2)}, u32[]{:S(2)}) collective-permute-start(bf16[128,384]{1,0:T(8,128)(2,1)S(1)} %collective-permute-done.4.refs_4_), channel_id=1, source_target_pairs={{0,8},{1,9},{2,10},{3,11},{4,12},{5,13},{6,14},{7,15},{8,0},{9,1},... | collective-permute-start | bytes 294920 | tf_op jit(solution)/shard_map/ppermute | solution.py:558
  11.4 1.5 %collective-permute-start.5 = (bf16[128,384]{1,0:T(8,128)(2,1)S(1)}, bf16[128,384]{1,0:T(8,128)(2,1)S(1)}, u32[]{:S(2)}, u32[]{:S(2)}) collective-permute-start(bf16[128,384]{1,0:T(8,128)(2,1)S(1)} %collective-permute-done.4.refs_4_), channel_id=1, source_target_pairs={{0,4},{1,5},{2,6},{3,7},{4,0},{5,1},{6,2},{7,3},{8,12},{9,13},{10,... | collective-permute-start | bytes 294920 | tf_op jit(solution)/shard_map/ppermute | solution.py:558
  12.9 0.3 collective-permute-done.9.refs_9_
  13.2 1.1 %collective-permute-start.10 = (bf16[256,384]{1,0:T(8,128)(2,1)S(1)}, bf16[256,384]{1,0:T(8,128)(2,1)S(1)}, u32[]{:S(2)}, u32[]{:S(2)}) collective-permute-start(bf16[256,384]{1,0:T(8,128)(2,1)S(1)} %collective-permute-done.9.refs_9_), channel_id=1, source_target_pairs={{0,8},{1,9},{2,10},{3,11},{4,12},{5,13},{6,14},{7,15},{8,0},{9,1},... | collective-permute-start | bytes 589832 | tf_op jit(solution)/shard_map/ppermute | solution.py:558
  14.3 0.2 collective-permute-done.6.refs_0_.refs_6_
  14.5 1.6 %collective-permute-start.7 = (bf16[96,384]{1,0:T(8,128)(2,1)S(1)}, bf16[96,384]{1,0:T(8,128)(2,1)S(1)}, u32[]{:S(2)}, u32[]{:S(2)}) collective-permute-start(bf16[96,384]{1,0:T(8,128)(2,1)S(1)} %get-tuple-element.50), channel_id=1, source_target_pairs={{0,4},{1,5},{2,6},{3,7},{4,0},{5,1},{6,2},{7,3},{8,12},{9,13},{10,... | collective-permute-start | bytes 221192 | tf_op jit(solution)/shard_map/ppermute | solution.py:558
  16.1 0.5 %collective-permute-start.8 = (bf16[32,384]{1,0:T(8,128)(2,1)S(1)}, bf16[32,384]{1,0:T(8,128)(2,1)S(1)}, u32[]{:S(2)}, u32[]{:S(2)}) collective-permute-start(bf16[32,384]{1,0:T(8,128)(2,1)S(1)} %get-tuple-element.51), channel_id=1, source_target_pairs={{0,4},{1,5},{2,6},{3,7},{4,0},{5,1},{6,2},{7,3},{8,12},{9,13},{10,... | collective-permute-start | bytes 73736 | tf_op jit(solution)/shard_map/ppermute | solution.py:558
  16.6 1.3 %collective-permute-start.3 = (bf16[128,512]{1,0:T(8,128)(2,1)S(1)}, bf16[128,512]{1,0:T(8,128)(2,1)S(1)}, u32[]{:S(2)}, u32[]{:S(2)}) collective-permute-start(bf16[128,512]{1,0:T(8,128)(2,1)S(1)} %get-tuple-element.44), channel_id=1, source_target_pairs={{0,2},{1,3},{2,0},{3,1},{4,6},{5,7},{6,4},{7,5},{8,10},{9,11},{10,... | collective-permute-start | bytes 393224 | tf_op jit(solution)/shard_map/ppermute | solution.py:558
  17.9 2.1 %collective-permute-done.8.refs_8_.refs_3_ = bf16[32,384]{1,0:T(8,128)(2,1)S(1)} collective-permute-done((bf16[32,384]{1,0:T(8,128)(2,1)S(1)}, bf16[32,384]{1,0:T(8,128)(2,1)S(1)}, u32[]{:S(2)}, u32[]{:S(2)}) %collective-permute-start.8) | collective-permute-done | bytes 24608 | tf_op jit(solution)/shard_map/ppermute | solution.py:558
  20.1 0.5 %collective-permute-start.15 = (bf16[48,1024]{1,0:T(8,128)(2,1)S(1)}, bf16[48,1024]{1,0:T(8,128)(2,1)S(1)}, u32[]{:S(2)}, u32[]{:S(2)}) collective-permute-start(bf16[48,1024]{1,0:T(8,128)(2,1)S(1)} %get-tuple-element.57), channel_id=1, source_target_pairs={{0,1},{1,0},{2,3},{3,2},{4,5},{5,4},{6,7},{7,6},{8,9},{9,8},{10,11... | collective-permute-start | bytes 294920 | tf_op jit(solution)/shard_map/ppermute | solution.py:558
  20.6 1.7 %qkv.1 = (bf16[384,1024]{1,0:T(8,128)(2,1)S(1)}, bf16[1024,768]{1,0:T(8,128)(2,1)S(1)}, bf16[768,384]{1,0:T(8,128)(2,1)S(1)}, bf16[16,384]{1,0:T(8,128)(2,1)S(1)}) custom-call(bf16[256,768]{1,0:T(8,128)(2,1)S(1)} %get-tuple-element.45.refs_0_, bf16[256,768]{1,0:T(8,128)(2,1)S(1)} %get-tuple-element.46.refs_1_, ...), custom_call_target="tpu_custom_call" | custom-call | flops 1 | bytes 1 | tf_op jit(solution)/shard_map/qkv/pallas_call | solution.py:179
  22.4 0.4 %collective-permute-start.13 = (bf16[32,256]{1,0:T(8,128)(2,1)S(1)}, bf16[32,256]{1,0:T(8,128)(2,1)S(1)}, u32[]{:S(2)}, u32[]{:S(2)}) collective-permute-start(bf16[32,256]{1,0:T(8,128)(2,1)S(1)} %get-tuple-element.55), channel_id=1, source_target_pairs={{0,1},{1,0},{2,3},{3,2},{4,5},{5,4},{6,7},{7,6},{8,9},{9,8},{10,11... | collective-permute-start | bytes 49160 | tf_op jit(solution)/shard_map/ppermute | solution.py:558
  22.9 0.8 %last_qkv.1 = (bf16[128,1024]{1,0:T(8,128)(2,1)S(1)}, bf16[768,512]{1,0:T(8,128)(2,1)S(1)}, bf16[16,512]{1,0:T(8,128)(2,1)S(1)}) custom-call(bf16[80,1024]{1,0:T(8,128)(2,1)S(1)} %collective-permute-done.14.refs_0_, bf16[48,1024]{1,0:T(8,128)(2,1)S(1)} %collective-permute-done.15.refs_1_, bf16[1024,768]{1,0:T(8,128)(2,1)S(1)} %get-tuple-element.58.refs_2_.refs_8_.w_all, ...), custom_call_target="tpu_custom_call" | custom-call | flops 1 | bytes 1 | tf_op jit(solution)/shard_map/last_qkv/pallas_call | solution.py:119
  23.7 4.6 %attention_grads.1 = (f32[128,1024]{1,0:T(8,128)S(1)}, bf16[128,1024]{1,0:T(8,128)(2,1)S(1)}, bf16[768,512]{1,0:T(8,128)(2,1)S(1)}, bf16[16,1280]{1,0:T(8,128)(2,1)S(1)}) custom-call(f32[4]{0:T(128)S(1)} %copy-done.3, bf16[128,256]{1,0:T(8,128)(2,1)S(1)} %get-tuple-element.42.refs_1_, bf16[128,256]{1,0:T(8,128)(2,1)S(1)} %get-tuple-element.43.refs_2_, ...), custom_call_target="tpu_custom_call" | custom-call | flops 1 | bytes 1 | tf_op jit(solution)/shard_map/attention_grads/pallas_call | solution.py:272
  28.3 0.4 %collective-permute-start.16 = (bf16[128,1024]{1,0:T(8,128)(2,1)S(1)}, bf16[128,1024]{1,0:T(8,128)(2,1)S(1)}, u32[]{:S(2)}, u32[]{:S(2)}) collective-permute-start(bf16[128,1024]{1,0:T(8,128)(2,1)S(1)} %get-tuple-element.65), channel_id=1, source_target_pairs={{0,1},{1,0},{2,3},{3,2},{4,5},{5,4},{6,7},{7,6},{8,9},{9,8},{10,11... | collective-permute-start | bytes 786440 | tf_op jit(solution)/shard_map/ppermute | solution.py:558
  28.7 1.4 %collective-permute-start.17 = (bf16[16,1280]{1,0:T(8,128)(2,1)S(1)}, bf16[16,1280]{1,0:T(8,128)(2,1)S(1)}, u32[]{:S(2)}, u32[]{:S(2)}) collective-permute-start(bf16[16,1280]{1,0:T(8,128)(2,1)S(1)} %get-tuple-element.63.pack.refs_0_), channel_id=1, source_target_pairs={{0,2},{1,3},{2,0},{3,1},{4,6},{5,7},{6,4},{7,5},{8,10},{9,11},{10,... | collective-permute-start | bytes 122888 | tf_op jit(solution)/shard_map/ppermute | solution.py:558
  30.1 1.2 %collective-permute-start.20 = (bf16[128,1024]{1,0:T(8,128)(2,1)S(1)}, bf16[128,1024]{1,0:T(8,128)(2,1)S(1)}, u32[]{:S(2)}, u32[]{:S(2)}) collective-permute-start(bf16[128,1024]{1,0:T(8,128)(2,1)S(1)} %add.1.refs_0_), channel_id=1, source_target_pairs={{0,2},{1,3},{2,0},{3,1},{4,6},{5,7},{6,4},{7,5},{8,10},{9,11},{10,... | collective-permute-start | bytes 786440 | tf_op jit(solution)/shard_map/ppermute | solution.py:558
  31.4 1.3 %collective-permute-done.17.refs_1_.refs_2_ = bf16[16,1280]{1,0:T(8,128)(2,1)S(1)} collective-permute-done((bf16[16,1280]{1,0:T(8,128)(2,1)S(1)}, bf16[16,1280]{1,0:T(8,128)(2,1)S(1)}, u32[]{:S(2)}, u32[]{:S(2)}) %collective-permute-start.17) | collective-permute-done | bytes 40992 | tf_op jit(solution)/shard_map/ppermute | solution.py:558
  32.7 0.7 %own_grads.1 = (f32[128,1024]{1,0:T(8,128)S(1)}, bf16[112,1024]{1,0:T(8,128)(2,1)S(1)}, bf16[16,1024]{1,0:T(8,128)(2,1)S(1)}) custom-call(bf16[768,512]{1,0:T(8,128)(2,1)S(1)} %get-tuple-element.62.grad_t, bf16[16,1280]{1,0:T(8,128)(2,1)S(1)} %get-tuple-element.63.pack.refs_0_, bf16[1024,768]{1,0:T(8,128)(2,1)S(1)} %get-tuple-element.58.refs_2_.refs_8_.w_all, ...), custom_call_target="tpu_custom_call" | custom-call | flops 1 | bytes 1 | tf_op jit(solution)/shard_map/own_grads/pallas_call | solution.py:337
  33.6 0.5 %collective-permute-start.21 = (bf16[16,1280]{1,0:T(8,128)(2,1)S(1)}, bf16[16,1280]{1,0:T(8,128)(2,1)S(1)}, u32[]{:S(2)}, u32[]{:S(2)}) collective-permute-start(bf16[16,1280]{1,0:T(8,128)(2,1)S(1)} %get-tuple-element.63.pack.refs_0_), channel_id=1, source_target_pairs={{0,1},{1,0},{2,3},{3,2},{4,5},{5,4},{6,7},{7,6},{8,9},{9,8},{10,11... | collective-permute-start | bytes 122888 | tf_op jit(solution)/shard_map/ppermute | solution.py:558
  34.1 0.4 %collective-permute-start.19 = (bf16[16,1024]{1,0:T(8,128)(2,1)S(1)}, bf16[16,1024]{1,0:T(8,128)(2,1)S(1)}, u32[]{:S(2)}, u32[]{:S(2)}) collective-permute-start(bf16[16,1024]{1,0:T(8,128)(2,1)S(1)} %get-tuple-element.68), channel_id=1, source_target_pairs={{0,1},{1,0},{2,3},{3,2},{4,5},{5,4},{6,7},{7,6},{8,9},{9,8},{10,11... | collective-permute-start | bytes 98312 | tf_op jit(solution)/shard_map/ppermute | solution.py:558
  34.6 0.5 %collective-permute-done.21.refs_1_ = bf16[16,1280]{1,0:T(8,128)(2,1)S(1)} collective-permute-done((bf16[16,1280]{1,0:T(8,128)(2,1)S(1)}, bf16[16,1280]{1,0:T(8,128)(2,1)S(1)}, u32[]{:S(2)}, u32[]{:S(2)}) %collective-permute-start.21) | collective-permute-done | bytes 40992 | tf_op jit(solution)/shard_map/ppermute | solution.py:558
  35.3 0.9 %adapter_grads.1 = (f32[16,1024]{1,0:T(8,128)}, f32[16,3072]{1,0:T(8,128)}) custom-call(bf16[16,1280]{1,0:T(8,128)(2,1)S(1)} %get-tuple-element.63.pack.refs_0_, bf16[16,1280]{1,0:T(8,128)(2,1)S(1)} %collective-permute-done.21.refs_1_, bf16[16,1280]{1,0:T(8,128)(2,1)S(1)} %collective-permute-done.17.refs_1_.refs_2_, ...), custom_call_target="tpu_custom_call" | custom-call | flops 1 | bytes 1 | tf_op jit(solution)/shard_map/adapter_grads/pallas_call | solution.py:370
  36.2 0.2 scale.1
  36.4 2.2 %collective-permute-done.20.refs_0_ = bf16[128,1024]{1,0:T(8,128)(2,1)S(1)} collective-permute-done((bf16[128,1024]{1,0:T(8,128)(2,1)S(1)}, bf16[128,1024]{1,0:T(8,128)(2,1)S(1)}, u32[]{:S(2)}, u32[]{:S(2)}) %collective-permute-start.20) | collective-permute-done | bytes 262176 | tf_op jit(solution)/shard_map/ppermute | solution.py:558
  38.6 0.8 %input_grads.1 = bf16[128,1024]{1,0:T(8,128)(2,1)} custom-call(f32[128,1024]{1,0:T(8,128)S(1)} %get-tuple-element.69.total, f32[128,1024]{1,0:T(8,128)S(1)} %get-tuple-element.70.token_gain, f32[128,1024]{1,0:T(8,128)S(1)} %get-tuple-element.71.scale, f32[128,1024]{1,0:T(8,128)S(1)} %get-tuple-element.72.slope, ...), custom_call_target="tpu_custom_call" | custom-call | flops 1 | bytes 1 | tf_op jit(solution)/shard_map/input_grads/pallas_call | solution.py:436
  (37 shorter events, 1.0 us)
Async XLA Ops:
  0.6 5.5 %collective-permute-start.1 = (bf16[256,3072]{1,0:T(8,128)(2,1)}, bf16[256,3072]{1,0:T(8,128)(2,1)S(1)}, u32[]{:S(2)}, u32[]{:S(2)}) collective-permute-start(bf16[256,3072]{1,0:T(8,128)(2,1)} %weight.1), channel_id=1, source_target_pairs={{0,1},{1,0},{2,3},{3,2},{4,5},{5,4},{6,7},{7,6},{8,9},{9,8},{10,11... | collective-permute-start | bytes 4718600 | tf_op jit(solution)/shard_map/ppermute | solution.py:558
  1.1 5.0 %collective-permute-start = (bf16[128,1024]{1,0:T(8,128)(2,1)}, bf16[128,1024]{1,0:T(8,128)(2,1)S(1)}, u32[]{:S(2)}, u32[]{:S(2)}) collective-permute-start(bf16[128,1024]{1,0:T(8,128)(2,1)} %tokens.3), channel_id=1, source_target_pairs={{0,1},{1,0},{2,3},{3,2},{4,5},{5,4},{6,7},{7,6},{8,9},{9,8},{10,11... | collective-permute-start | bytes 786440 | tf_op jit(solution)/shard_map/ppermute | solution.py:558
  1.2 4.9 %collective-permute-start.2 = (bf16[128,1024]{1,0:T(8,128)(2,1)}, bf16[128,1024]{1,0:T(8,128)(2,1)S(1)}, u32[]{:S(2)}, u32[]{:S(2)}) collective-permute-start(bf16[128,1024]{1,0:T(8,128)(2,1)} %refs_2_.1), channel_id=1, source_target_pairs={{0,1},{1,0},{2,3},{3,2},{4,5},{5,4},{6,7},{7,6},{8,9},{9,8},{10,11... | collective-permute-start | bytes 786440 | tf_op jit(solution)/shard_map/ppermute | solution.py:558
  2.7 7.2 %collective-permute-start.4 = (bf16[128,384]{1,0:T(8,128)(2,1)S(1)}, bf16[128,384]{1,0:T(8,128)(2,1)S(1)}, u32[]{:S(2)}, u32[]{:S(2)}) collective-permute-start(bf16[128,384]{1,0:T(8,128)(2,1)S(1)} %get-tuple-element.49), channel_id=1, source_target_pairs={{0,2},{1,3},{2,0},{3,1},{4,7},{5,6},{6,5},{7,4},{8,10},{9,11},{10,... | collective-permute-start | bytes 294920 | tf_op jit(solution)/shard_map/ppermute | solution.py:558
  5.3 7.9 %collective-permute-start.9 = (bf16[256,384]{1,0:T(8,128)(2,1)S(1)}, bf16[256,384]{1,0:T(8,128)(2,1)S(1)}, u32[]{:S(2)}, u32[]{:S(2)}) collective-permute-start(bf16[256,384]{1,0:T(8,128)(2,1)S(1)} %get-tuple-element.52), channel_id=1, source_target_pairs={{0,2},{1,3},{2,0},{3,1},{4,6},{5,7},{6,4},{7,5},{8,11},{9,10},{10,... | collective-permute-start | bytes 589832 | tf_op jit(solution)/shard_map/ppermute | solution.py:558
  6.1 14.5 %copy-start.1 = (bf16[16,3072]{1,0:T(8,128)(2,1)S(1)}, bf16[16,3072]{1,0:T(8,128)(2,1)}, u32[]{:S(2)}) copy-start(bf16[16,3072]{1,0:T(8,128)(2,1)} %refs_10_.1) | copy-start | bytes 294916
  6.1 14.4 %copy-start.2 = (bf16[1024,16]{0,1:T(8,128)(2,1)S(1)}, bf16[1024,16]{0,1:T(8,128)(2,1)}, u32[]{:S(2)}) copy-start(bf16[1024,16]{0,1:T(8,128)(2,1)} %param.12) | copy-start | bytes 98308
  7.9 12.1 %collective-permute-start.11 = (bf16[128,1024]{1,0:T(8,128)(2,1)S(1)}, bf16[128,1024]{1,0:T(8,128)(2,1)S(1)}, u32[]{:S(2)}, u32[]{:S(2)}) collective-permute-start(bf16[128,1024]{1,0:T(8,128)(2,1)S(1)} %get-tuple-element.47.refs_2_), channel_id=1, source_target_pairs={{0,2},{1,3},{2,0},{3,1},{4,6},{5,7},{6,4},{7,5},{8,10},{9,11},{10,... | collective-permute-start | bytes 786440 | tf_op jit(solution)/shard_map/ppermute | solution.py:558
  9.9 4.6 %collective-permute-start.6 = (bf16[128,384]{1,0:T(8,128)(2,1)S(1)}, bf16[128,384]{1,0:T(8,128)(2,1)S(1)}, u32[]{:S(2)}, u32[]{:S(2)}) collective-permute-start(bf16[128,384]{1,0:T(8,128)(2,1)S(1)} %collective-permute-done.4.refs_4_), channel_id=1, source_target_pairs={{0,8},{1,9},{2,10},{3,11},{4,12},{5,13},{6,14},{7,15},{8,0},{9,1},... | collective-permute-start | bytes 294920 | tf_op jit(solution)/shard_map/ppermute | solution.py:558
  11.4 5.2 %collective-permute-start.5 = (bf16[128,384]{1,0:T(8,128)(2,1)S(1)}, bf16[128,384]{1,0:T(8,128)(2,1)S(1)}, u32[]{:S(2)}, u32[]{:S(2)}) collective-permute-start(bf16[128,384]{1,0:T(8,128)(2,1)S(1)} %collective-permute-done.4.refs_4_), channel_id=1, source_target_pairs={{0,4},{1,5},{2,6},{3,7},{4,0},{5,1},{6,2},{7,3},{8,12},{9,13},{10,... | collective-permute-start | bytes 294920 | tf_op jit(solution)/shard_map/ppermute | solution.py:558
  13.2 7.4 %collective-permute-start.10 = (bf16[256,384]{1,0:T(8,128)(2,1)S(1)}, bf16[256,384]{1,0:T(8,128)(2,1)S(1)}, u32[]{:S(2)}, u32[]{:S(2)}) collective-permute-start(bf16[256,384]{1,0:T(8,128)(2,1)S(1)} %collective-permute-done.9.refs_9_), channel_id=1, source_target_pairs={{0,8},{1,9},{2,10},{3,11},{4,12},{5,13},{6,14},{7,15},{8,0},{9,1},... | collective-permute-start | bytes 589832 | tf_op jit(solution)/shard_map/ppermute | solution.py:558
  14.5 5.4 %collective-permute-start.7 = (bf16[96,384]{1,0:T(8,128)(2,1)S(1)}, bf16[96,384]{1,0:T(8,128)(2,1)S(1)}, u32[]{:S(2)}, u32[]{:S(2)}) collective-permute-start(bf16[96,384]{1,0:T(8,128)(2,1)S(1)} %get-tuple-element.50), channel_id=1, source_target_pairs={{0,4},{1,5},{2,6},{3,7},{4,0},{5,1},{6,2},{7,3},{8,12},{9,13},{10,... | collective-permute-start | bytes 221192 | tf_op jit(solution)/shard_map/ppermute | solution.py:558
  16.1 3.8 %collective-permute-start.8 = (bf16[32,384]{1,0:T(8,128)(2,1)S(1)}, bf16[32,384]{1,0:T(8,128)(2,1)S(1)}, u32[]{:S(2)}, u32[]{:S(2)}) collective-permute-start(bf16[32,384]{1,0:T(8,128)(2,1)S(1)} %get-tuple-element.51), channel_id=1, source_target_pairs={{0,4},{1,5},{2,6},{3,7},{4,0},{5,1},{6,2},{7,3},{8,12},{9,13},{10,... | collective-permute-start | bytes 73736 | tf_op jit(solution)/shard_map/ppermute | solution.py:558
  16.6 5.6 %collective-permute-start.3 = (bf16[128,512]{1,0:T(8,128)(2,1)S(1)}, bf16[128,512]{1,0:T(8,128)(2,1)S(1)}, u32[]{:S(2)}, u32[]{:S(2)}) collective-permute-start(bf16[128,512]{1,0:T(8,128)(2,1)S(1)} %get-tuple-element.44), channel_id=1, source_target_pairs={{0,2},{1,3},{2,0},{3,1},{4,6},{5,7},{6,4},{7,5},{8,10},{9,11},{10,... | collective-permute-start | bytes 393224 | tf_op jit(solution)/shard_map/ppermute | solution.py:558
  20.0 2.9 %collective-permute-start.14 = (bf16[80,1024]{1,0:T(8,128)(2,1)S(1)}, bf16[80,1024]{1,0:T(8,128)(2,1)S(1)}, u32[]{:S(2)}, u32[]{:S(2)}) collective-permute-start(bf16[80,1024]{1,0:T(8,128)(2,1)S(1)} %get-tuple-element.56), channel_id=1, source_target_pairs={{0,1},{1,0},{2,3},{3,2},{4,5},{5,4},{6,7},{7,6},{8,9},{9,8},{10,11... | collective-permute-start | bytes 491528 | tf_op jit(solution)/shard_map/ppermute | solution.py:558
  20.1 2.8 %collective-permute-start.15 = (bf16[48,1024]{1,0:T(8,128)(2,1)S(1)}, bf16[48,1024]{1,0:T(8,128)(2,1)S(1)}, u32[]{:S(2)}, u32[]{:S(2)}) collective-permute-start(bf16[48,1024]{1,0:T(8,128)(2,1)S(1)} %get-tuple-element.57), channel_id=1, source_target_pairs={{0,1},{1,0},{2,3},{3,2},{4,5},{5,4},{6,7},{7,6},{8,9},{9,8},{10,11... | collective-permute-start | bytes 294920 | tf_op jit(solution)/shard_map/ppermute | solution.py:558
  22.3 1.5 %copy-start.3 = (f32[4]{0:T(128)S(1)}, f32[4]{0:T(128)}, u32[]{:S(2)}) copy-start(f32[4]{0:T(128)} %refs_0_.3) | copy-start | bytes 52
  22.3 1.4 %collective-permute-start.12 = (bf16[96,256]{1,0:T(8,128)(2,1)S(1)}, bf16[96,256]{1,0:T(8,128)(2,1)S(1)}, u32[]{:S(2)}, u32[]{:S(2)}) collective-permute-start(bf16[96,256]{1,0:T(8,128)(2,1)S(1)} %get-tuple-element.54), channel_id=1, source_target_pairs={{0,1},{1,0},{2,3},{3,2},{4,5},{5,4},{6,7},{7,6},{8,9},{9,8},{10,11... | collective-permute-start | bytes 147464 | tf_op jit(solution)/shard_map/ppermute | solution.py:558
  22.4 1.3 %collective-permute-start.13 = (bf16[32,256]{1,0:T(8,128)(2,1)S(1)}, bf16[32,256]{1,0:T(8,128)(2,1)S(1)}, u32[]{:S(2)}, u32[]{:S(2)}) collective-permute-start(bf16[32,256]{1,0:T(8,128)(2,1)S(1)} %get-tuple-element.55), channel_id=1, source_target_pairs={{0,1},{1,0},{2,3},{3,2},{4,5},{5,4},{6,7},{7,6},{8,9},{9,8},{10,11... | collective-permute-start | bytes 49160 | tf_op jit(solution)/shard_map/ppermute | solution.py:558
  28.3 1.8 %collective-permute-start.16 = (bf16[128,1024]{1,0:T(8,128)(2,1)S(1)}, bf16[128,1024]{1,0:T(8,128)(2,1)S(1)}, u32[]{:S(2)}, u32[]{:S(2)}) collective-permute-start(bf16[128,1024]{1,0:T(8,128)(2,1)S(1)} %get-tuple-element.65), channel_id=1, source_target_pairs={{0,1},{1,0},{2,3},{3,2},{4,5},{5,4},{6,7},{7,6},{8,9},{9,8},{10,11... | collective-permute-start | bytes 786440 | tf_op jit(solution)/shard_map/ppermute | solution.py:558
  28.7 4.0 %collective-permute-start.17 = (bf16[16,1280]{1,0:T(8,128)(2,1)S(1)}, bf16[16,1280]{1,0:T(8,128)(2,1)S(1)}, u32[]{:S(2)}, u32[]{:S(2)}) collective-permute-start(bf16[16,1280]{1,0:T(8,128)(2,1)S(1)} %get-tuple-element.63.pack.refs_0_), channel_id=1, source_target_pairs={{0,2},{1,3},{2,0},{3,1},{4,6},{5,7},{6,4},{7,5},{8,10},{9,11},{10,... | collective-permute-start | bytes 122888 | tf_op jit(solution)/shard_map/ppermute | solution.py:558
  30.1 8.5 %collective-permute-start.20 = (bf16[128,1024]{1,0:T(8,128)(2,1)S(1)}, bf16[128,1024]{1,0:T(8,128)(2,1)S(1)}, u32[]{:S(2)}, u32[]{:S(2)}) collective-permute-start(bf16[128,1024]{1,0:T(8,128)(2,1)S(1)} %add.1.refs_0_), channel_id=1, source_target_pairs={{0,2},{1,3},{2,0},{3,1},{4,6},{5,7},{6,4},{7,5},{8,10},{9,11},{10,... | collective-permute-start | bytes 786440 | tf_op jit(solution)/shard_map/ppermute | solution.py:558
  32.7 3.4 %copy-start = (bf16[128,1024]{1,0:T(8,128)(2,1)S(1)}, bf16[128,1024]{1,0:T(8,128)(2,1)}, u32[]{:S(2)}) copy-start(bf16[128,1024]{1,0:T(8,128)(2,1)} %tokens.3) | copy-start | bytes 786436
  33.5 2.7 %collective-permute-start.18 = (bf16[112,1024]{1,0:T(8,128)(2,1)S(1)}, bf16[112,1024]{1,0:T(8,128)(2,1)S(1)}, u32[]{:S(2)}, u32[]{:S(2)}) collective-permute-start(bf16[112,1024]{1,0:T(8,128)(2,1)S(1)} %get-tuple-element.67), channel_id=1, source_target_pairs={{0,1},{1,0},{2,3},{3,2},{4,5},{5,4},{6,7},{7,6},{8,9},{9,8},{10,11... | collective-permute-start | bytes 688136 | tf_op jit(solution)/shard_map/ppermute | solution.py:558
  33.6 1.5 %collective-permute-start.21 = (bf16[16,1280]{1,0:T(8,128)(2,1)S(1)}, bf16[16,1280]{1,0:T(8,128)(2,1)S(1)}, u32[]{:S(2)}, u32[]{:S(2)}) collective-permute-start(bf16[16,1280]{1,0:T(8,128)(2,1)S(1)} %get-tuple-element.63.pack.refs_0_), channel_id=1, source_target_pairs={{0,1},{1,0},{2,3},{3,2},{4,5},{5,4},{6,7},{7,6},{8,9},{9,8},{10,11... | collective-permute-start | bytes 122888 | tf_op jit(solution)/shard_map/ppermute | solution.py:558
  34.0 1.2 %collective-permute-start.22 = (bf16[16,1280]{1,0:T(8,128)(2,1)S(1)}, bf16[16,1280]{1,0:T(8,128)(2,1)S(1)}, u32[]{:S(2)}, u32[]{:S(2)}) collective-permute-start(bf16[16,1280]{1,0:T(8,128)(2,1)S(1)} %collective-permute-done.17.refs_1_.refs_2_), channel_id=1, source_target_pairs={{0,1},{1,0},{2,3},{3,2},{4,5},{5,4},{6,7},{7,6},{8,9},{9,8},{10,11... | collective-permute-start | bytes 122888 | tf_op jit(solution)/shard_map/ppermute | solution.py:558
  34.1 2.0 %collective-permute-start.19 = (bf16[16,1024]{1,0:T(8,128)(2,1)S(1)}, bf16[16,1024]{1,0:T(8,128)(2,1)S(1)}, u32[]{:S(2)}, u32[]{:S(2)}) collective-permute-start(bf16[16,1024]{1,0:T(8,128)(2,1)S(1)} %get-tuple-element.68), channel_id=1, source_target_pairs={{0,1},{1,0},{2,3},{3,2},{4,5},{5,4},{6,7},{7,6},{8,9},{9,8},{10,11... | collective-permute-start | bytes 98312 | tf_op jit(solution)/shard_map/ppermute | solution.py:558
